TPU v7x, 128 devices: a whole 4x4x4 slice. The times are simulated.
128 devices in a mesh: group: 8 (over z, core), tile: 16 (over y, x).
Axes of the slice: x: 4, y: 4, z: 4, core: 2. Of those that a mesh axis runs over, the one named last changes fastest.
Arguments:
- embeddings: float32 [32768, 512], P(('group', 'tile'))
- cluster_ids: int32 [32768, 1], P(('group', 'tile')), may hold values from 0 to 7; in each aligned block of 256 rows (0 to 255, 256 to 511, ...) at most 96 rows name the same one
- order_rank: int32 [32768], P(('group', 'tile')), may hold values from 0 to 32767, each once
Outputs:
- nearest_earlier: float32 [32768], P(('group', 'tile'))
Inputs may be any that keep to these rules, and one draw needn't show every extreme that they name: `cluster_ids`: in the rows of one device at most 96 name one cluster; some device has exactly 96 rows in one cluster. `order_rank`: all values differ.
All inputs are finite; a program needn't handle non-finite values.
Results may differ from a plain program's by a relative error of at most 0.00074.
Values may be sent and summed in bfloat16 or wider, within the bound.
No kernel may reach another device: no remote copies, remote signals or barrier semaphores. Data moves between devices by JAX's collectives and lax.ppermute only.
A program may use at most 64 MiB of HBM per device.

v0:
```python
import jax
import jax.numpy as jnp
from jax import lax
from jax.sharding import PartitionSpec as P

CAP = 96


unused_rank = 1073741824
block_rows = 1024


def score_block(queries, query_rank, key_block, rank_block):
    scores = lax.dot_general(
        queries, key_block, (((1,), (1,)), ((), ())), preferred_element_type=jnp.float32
    )
    earlier = rank_block[None, :] < query_rank[:, None]
    row_part = jnp.max(jnp.where(earlier, scores, -1.0), axis=1)
    column = jnp.full((key_block.shape[0],), -1.0, jnp.float32)
    return (row_part, column)


def block_max(queries, query_rank, keys, key_rank):
    total = keys.shape[0]
    padded = -(-total // block_rows) * block_rows
    extra = padded - total
    keys_full = jnp.concatenate([keys, jnp.zeros((extra, keys.shape[1]), keys.dtype)], axis=0)
    rank_full = jnp.concatenate([key_rank, jnp.full((extra,), unused_rank, jnp.int32)], axis=0)
    row_best = jnp.full((queries.shape[0],), -1.0, jnp.float32)
    col_best = jnp.full((padded,), -1.0, jnp.float32)

    def step(index, carry):
        row_part, col_part = carry
        start = index * block_rows
        key_block = lax.dynamic_slice_in_dim(keys_full, start, block_rows, 0)
        rank_block = lax.dynamic_slice_in_dim(rank_full, start, block_rows, 0)
        found, column = score_block(queries, query_rank, key_block, rank_block)
        row_part = jnp.maximum(row_part, found)
        col_part = lax.dynamic_update_slice_in_dim(col_part, column, start, 0)
        return (row_part, col_part)

    row_best, col_best = lax.fori_loop(0, padded // block_rows, step, (row_best, col_best))
    return (row_best, col_best)


def on_device(embeddings, cluster_ids, order_rank):
    groups = lax.axis_size("group")
    sums = jnp.sum(embeddings * embeddings, axis=1, keepdims=True)
    unit = (embeddings * lax.rsqrt(sums + 1e-06)).astype(jnp.bfloat16)
    labels = cluster_ids[:, 0]
    onehot = (labels[:, None] == jnp.arange(groups, dtype=jnp.int32)[None, :]).astype(jnp.int32)
    before = jnp.cumsum(onehot, axis=0) - onehot
    position = jnp.sum(before * onehot, axis=1)
    slot = labels * CAP + position
    slots = groups * CAP
    send_rows = jnp.zeros((slots, unit.shape[1]), jnp.bfloat16).at[slot].set(unit)
    send_rank = jnp.full((slots,), unused_rank, jnp.int32).at[slot].set(order_rank)
    members, member_rank = (
        lax.all_to_all(send_rows, "group", split_axis=0, concat_axis=0, tiled=True),
        lax.all_to_all(send_rank, "group", split_axis=0, concat_axis=0, tiled=True),
    )
    start_best = jnp.full((slots,), -1.0, jnp.float32)
    found, unused = block_max(
        members,
        member_rank,
        lax.all_gather(members, "tile", axis=0, tiled=True),
        lax.all_gather(member_rank, "tile", axis=0, tiled=True),
    )
    best = jnp.maximum(start_best, found)
    back = lax.all_to_all(best, "group", split_axis=0, concat_axis=0, tiled=True)
    return back[slot]


def solution(mesh):
    return jax.shard_map(
        on_device,
        mesh=mesh,
        in_specs=(P(("group", "tile"), None), P(("group", "tile"), None), P(("group", "tile"))),
        out_specs=P(("group", "tile")),
        check_vma=False,
    )
```

profile of v0, /device:TPU:1, one launch (start us, length us, event | category | flops | bytes accessed | tf_op | source)
XLA Modules:
  0.0 172.8 jit_solution(9625939509692648325)
XLA Ops:
  6.5 0.7 fusion.8
  8.0 0.8 fusion.7
  8.8 0.7 compare_select_fusion
  9.5 1.2 multiply_reduce_fusion
  10.7 2.3 %scatter_custom_fusion.1 = bf16[768,512]{1,0:T(8,128)(2,1)S(1)} fusion(s32[256]{0:T(256)S(1)} %bitcast.36, bf16[]{:T(256)} %constant.55.clone.1, f32[256,512]{1,0:T(8,128)} %param.5, f32[256]{0:T(256)S(1)} %add_rsqrt_fusion), kind=kCustom, calls=%fused_computation.10 | custom fusion | flops 262144 | bytes 1311746 | tf_op jit(solution)/shard_map/scatter | solution.py:56
  13.0 18.9 %all_to_all.36 = bf16[8,96,512]{2,1,0:T(8,128)(2,1)} all-to-all(bf16[8,96,512]{2,1,0:T(8,128)(2,1)S(1)} %bitcast.31), channel_id=1, replica_groups=mesh['group'=8,'tile'=16] {'group'}, dimensions={0} | all-to-all | bytes 1572864 | tf_op jit(solution)/shard_map/all_to_all | solution.py:59
  32.0 1.6 scatter_custom_fusion
  33.5 0.7 all_to_all.24
  34.2 4.3 %all-to-all-start = ((s32[8,96,1]{1,2,0:T(1,128)}), s32[8,96,1]{1,2,0:T(1,128)S(1)}, u32[]{:S(2)}, u32[]{:S(2)}) async-start(s32[8,96,1]{1,2,0:T(1,128)} %bitcast.6), calls=%async_computation | async-start | bytes 8192 | tf_op jit(solution)/shard_map/all_to_all | solution.py:60
  38.5 4.6 %all-to-all-done = s32[8,96,1]{1,2,0:T(1,128)S(1)} async-done(((s32[8,96,1]{1,2,0:T(1,128)}), s32[8,96,1]{1,2,0:T(1,128)S(1)}, u32[]{:S(2)}, u32[]{:S(2)}) %all-to-all-start) | async-done | bytes 3104 | tf_op jit(solution)/shard_map/all_to_all | solution.py:60
  43.1 0.6 broadcast.62
  43.6 0.7 reduce.10
  44.5 19.7 %all-gather = s32[16,1,768]{2,1,0:T(1,128)S(1)} all-gather(s32[1,1,768]{2,1,0:T(1,128)S(1)} %reshape.56), channel_id=1, replica_groups=mesh['group'=8,'tile'=16] {'tile'}, dimensions={0}, use_global_device_ids=true | all-gather | bytes 52224 | tf_op jit(solution)/shard_map/all_gather | solution.py:67
  64.2 57.8 %all-gather.3.cloned.1.call-done = bf16[12288,512]{1,0:T(8,128)(2,1)} async-done(((bf16[768,512]{1,0:T(8,128)(2,1)}), bf16[12288,512]{1,0:T(8,128)(2,1)}) %all-gather.3.cloned.1.call-update) | async-done | bytes 12582928 | tf_op jit(solution)/shard_map/all_gather | solution.py:66
  122.0 30.5 %while.14 = (s32[]{:T(128)}, f32[768]{0:T(1024)S(1)}, s32[12288]{0:T(1024)S(1)}, s32[768]{0:T(1024)S(1)}, bf16[12288,512]{1,0:T(8,128)(2,1)}, /*index=5*/bf16[76...) while((s32[]{:T(128)}, f32[768]{0:T(1024)S(1)}, s32[12288]{0:T(1024)S(1)}, ...), condition=%wide.region_8.9_spmd.clone, body=%wide.region_6.8_spmd.clone.sunk | while | flops 807666432 | bytes 1862821 | solution.py:42
  122.0 2.5 %fusion.17 = f32[768]{0:T(1024)S(1)} fusion(bf16[768,512]{1,0:T(8,128)(2,1)} %get-tuple-element.210, s32[768]{0:T(1024)S(1)} %get-tuple-element.208, s32[1024]{0:T(1024)S(1)} %dynamic_slice.21, bf16[12288,512]{1,0:T(8,128)(2,1)} %get-tuple-element.209, s32[]{:T(128)S(6)} %select_n.32), kind=kOutput, calls=%fused_computation.4.clone.1 | convolution fusion | flops 807664896 | bytes 1845252 | tf_op jit(solution)/shard_map/while/body/eval_jaxpr/dot_general | solution.py:14
  124.5 2.5 %fusion.17 = f32[768]{0:T(1024)S(1)} fusion(bf16[768,512]{1,0:T(8,128)(2,1)} %get-tuple-element.210, s32[768]{0:T(1024)S(1)} %get-tuple-element.208, s32[1024]{0:T(1024)S(1)} %dynamic_slice.21, bf16[12288,512]{1,0:T(8,128)(2,1)} %get-tuple-element.209, s32[]{:T(128)S(6)} %select_n.32), kind=kOutput, calls=%fused_computation.4.clone.1 | convolution fusion | flops 807664896 | bytes 1845252 | tf_op jit(solution)/shard_map/while/body/eval_jaxpr/dot_general | solution.py:14
  127.0 2.5 %fusion.17 = f32[768]{0:T(1024)S(1)} fusion(bf16[768,512]{1,0:T(8,128)(2,1)} %get-tuple-element.210, s32[768]{0:T(1024)S(1)} %get-tuple-element.208, s32[1024]{0:T(1024)S(1)} %dynamic_slice.21, bf16[12288,512]{1,0:T(8,128)(2,1)} %get-tuple-element.209, s32[]{:T(128)S(6)} %select_n.32), kind=kOutput, calls=%fused_computation.4.clone.1 | convolution fusion | flops 807664896 | bytes 1845252 | tf_op jit(solution)/shard_map/while/body/eval_jaxpr/dot_general | solution.py:14
  129.6 2.5 %fusion.17 = f32[768]{0:T(1024)S(1)} fusion(bf16[768,512]{1,0:T(8,128)(2,1)} %get-tuple-element.210, s32[768]{0:T(1024)S(1)} %get-tuple-element.208, s32[1024]{0:T(1024)S(1)} %dynamic_slice.21, bf16[12288,512]{1,0:T(8,128)(2,1)} %get-tuple-element.209, s32[]{:T(128)S(6)} %select_n.32), kind=kOutput, calls=%fused_computation.4.clone.1 | convolution fusion | flops 807664896 | bytes 1845252 | tf_op jit(solution)/shard_map/while/body/eval_jaxpr/dot_general | solution.py:14
  132.1 2.5 %fusion.17 = f32[768]{0:T(1024)S(1)} fusion(bf16[768,512]{1,0:T(8,128)(2,1)} %get-tuple-element.210, s32[768]{0:T(1024)S(1)} %get-tuple-element.208, s32[1024]{0:T(1024)S(1)} %dynamic_slice.21, bf16[12288,512]{1,0:T(8,128)(2,1)} %get-tuple-element.209, s32[]{:T(128)S(6)} %select_n.32), kind=kOutput, calls=%fused_computation.4.clone.1 | convolution fusion | flops 807664896 | bytes 1845252 | tf_op jit(solution)/shard_map/while/body/eval_jaxpr/dot_general | solution.py:14
  134.7 2.5 %fusion.17 = f32[768]{0:T(1024)S(1)} fusion(bf16[768,512]{1,0:T(8,128)(2,1)} %get-tuple-element.210, s32[768]{0:T(1024)S(1)} %get-tuple-element.208, s32[1024]{0:T(1024)S(1)} %dynamic_slice.21, bf16[12288,512]{1,0:T(8,128)(2,1)} %get-tuple-element.209, s32[]{:T(128)S(6)} %select_n.32), kind=kOutput, calls=%fused_computation.4.clone.1 | convolution fusion | flops 807664896 | bytes 1845252 | tf_op jit(solution)/shard_map/while/body/eval_jaxpr/dot_general | solution.py:14
  137.2 2.5 %fusion.17 = f32[768]{0:T(1024)S(1)} fusion(bf16[768,512]{1,0:T(8,128)(2,1)} %get-tuple-element.210, s32[768]{0:T(1024)S(1)} %get-tuple-element.208, s32[1024]{0:T(1024)S(1)} %dynamic_slice.21, bf16[12288,512]{1,0:T(8,128)(2,1)} %get-tuple-element.209, s32[]{:T(128)S(6)} %select_n.32), kind=kOutput, calls=%fused_computation.4.clone.1 | convolution fusion | flops 807664896 | bytes 1845252 | tf_op jit(solution)/shard_map/while/body/eval_jaxpr/dot_general | solution.py:14
  139.8 2.5 %fusion.17 = f32[768]{0:T(1024)S(1)} fusion(bf16[768,512]{1,0:T(8,128)(2,1)} %get-tuple-element.210, s32[768]{0:T(1024)S(1)} %get-tuple-element.208, s32[1024]{0:T(1024)S(1)} %dynamic_slice.21, bf16[12288,512]{1,0:T(8,128)(2,1)} %get-tuple-element.209, s32[]{:T(128)S(6)} %select_n.32), kind=kOutput, calls=%fused_computation.4.clone.1 | convolution fusion | flops 807664896 | bytes 1845252 | tf_op jit(solution)/shard_map/while/body/eval_jaxpr/dot_general | solution.py:14
  142.3 2.5 %fusion.17 = f32[768]{0:T(1024)S(1)} fusion(bf16[768,512]{1,0:T(8,128)(2,1)} %get-tuple-element.210, s32[768]{0:T(1024)S(1)} %get-tuple-element.208, s32[1024]{0:T(1024)S(1)} %dynamic_slice.21, bf16[12288,512]{1,0:T(8,128)(2,1)} %get-tuple-element.209, s32[]{:T(128)S(6)} %select_n.32), kind=kOutput, calls=%fused_computation.4.clone.1 | convolution fusion | flops 807664896 | bytes 1845252 | tf_op jit(solution)/shard_map/while/body/eval_jaxpr/dot_general | solution.py:14
  144.8 2.5 %fusion.17 = f32[768]{0:T(1024)S(1)} fusion(bf16[768,512]{1,0:T(8,128)(2,1)} %get-tuple-element.210, s32[768]{0:T(1024)S(1)} %get-tuple-element.208, s32[1024]{0:T(1024)S(1)} %dynamic_slice.21, bf16[12288,512]{1,0:T(8,128)(2,1)} %get-tuple-element.209, s32[]{:T(128)S(6)} %select_n.32), kind=kOutput, calls=%fused_computation.4.clone.1 | convolution fusion | flops 807664896 | bytes 1845252 | tf_op jit(solution)/shard_map/while/body/eval_jaxpr/dot_general | solution.py:14
  147.4 2.5 %fusion.17 = f32[768]{0:T(1024)S(1)} fusion(bf16[768,512]{1,0:T(8,128)(2,1)} %get-tuple-element.210, s32[768]{0:T(1024)S(1)} %get-tuple-element.208, s32[1024]{0:T(1024)S(1)} %dynamic_slice.21, bf16[12288,512]{1,0:T(8,128)(2,1)} %get-tuple-element.209, s32[]{:T(128)S(6)} %select_n.32), kind=kOutput, calls=%fused_computation.4.clone.1 | convolution fusion | flops 807664896 | bytes 1845252 | tf_op jit(solution)/shard_map/while/body/eval_jaxpr/dot_general | solution.py:14
  149.9 2.5 %fusion.17 = f32[768]{0:T(1024)S(1)} fusion(bf16[768,512]{1,0:T(8,128)(2,1)} %get-tuple-element.210, s32[768]{0:T(1024)S(1)} %get-tuple-element.208, s32[1024]{0:T(1024)S(1)} %dynamic_slice.21, bf16[12288,512]{1,0:T(8,128)(2,1)} %get-tuple-element.209, s32[]{:T(128)S(6)} %select_n.32), kind=kOutput, calls=%fused_computation.4.clone.1 | convolution fusion | flops 807664896 | bytes 1845252 | tf_op jit(solution)/shard_map/while/body/eval_jaxpr/dot_general | solution.py:14
  152.5 0.7 all_to_all.30
  153.1 5.1 %all-to-all-start.2 = ((f32[8,96,1]{1,2,0:T(1,128)}), f32[8,96,1]{1,2,0:T(1,128)S(1)}, u32[]{:S(2)}, u32[]{:S(2)}) async-start(f32[8,96,1]{1,2,0:T(1,128)} %bitcast.10), calls=%async_computation.2 | async-start | bytes 8192 | tf_op jit(solution)/shard_map/all_to_all | solution.py:70
  158.2 4.6 %all-to-all-done.2 = f32[8,96,1]{1,2,0:T(1,128)S(1)} async-done(((f32[8,96,1]{1,2,0:T(1,128)}), f32[8,96,1]{1,2,0:T(1,128)S(1)}, u32[]{:S(2)}, u32[]{:S(2)}) %all-to-all-start.2) | async-done | bytes 3104 | tf_op jit(solution)/shard_map/all_to_all | solution.py:70
  163.3 0.7 reduce.11
  164.1 1.9 %gather_fusion = f32[256]{0:T(256)} fusion(f32[768]{0:T(1024)S(1)} %all_to_all.32, s32[1024]{0:T(1024)S(1)} %pad_clamp_fusion), kind=kCustom, calls=%fused_computation | custom fusion | bytes 3072 | tf_op jit(solution)/shard_map/gather | solution.py:71
  (38 shorter events, 1.8 us)
Async XLA Ops:
  6.5 115.4 %all-gather.3.cloned.1.call-start = ((), (), s32[]{:S(2)}) async-start(), calls=%async_computation.3 | async-start | bytes 13369344 | tf_op jit(solution)/shard_map/all_gather | solution.py:66
  34.2 8.9 %all-to-all-start = ((s32[8,96,1]{1,2,0:T(1,128)}), s32[8,96,1]{1,2,0:T(1,128)S(1)}, u32[]{:S(2)}, u32[]{:S(2)}) async-start(s32[8,96,1]{1,2,0:T(1,128)} %bitcast.6), calls=%async_computation | async-start | bytes 8192 | tf_op jit(solution)/shard_map/all_to_all | solution.py:60
  153.1 9.7 %all-to-all-start.2 = ((f32[8,96,1]{1,2,0:T(1,128)}), f32[8,96,1]{1,2,0:T(1,128)S(1)}, u32[]{:S(2)}, u32[]{:S(2)}) async-start(f32[8,96,1]{1,2,0:T(1,128)} %bitcast.10), calls=%async_computation.2 | async-start | bytes 8192 | tf_op jit(solution)/shard_map/all_to_all | solution.py:70
Sparse Core Ops, SparseCore 0:
  32.1 89.8 all-gather.2
where the time goes:
time: 174 us; the launch traced here: 173 us
  waiting for transfers between devices  66.9 us (38%)
  blocking collectives  38.7 us (22%)
  matrix products  29.8 us (17%)
  between operations  13.5 us (8%)
  starting transfers between devices  9.36 us (5%)
  other arithmetic  7.68 us (4%)
  local copies, waits for them, and re-layouts  6.43 us (4%)
    all_gather x1, waiting for transfers between devices, on_device(): lax.all_gather(members, 'tile', axis=0, tiled=True)  57.8 us
    dot_general x12, matrix products, score_block(): lax.dot_general(queries, key_block, (((1,), (1,)), ((), ())), preferred_e...  29.8 us
    all_gather x1, blocking collectives, on_device(): lax.all_gather(member_rank, 'tile', axis=0, tiled=True)  19.7 us
    all_to_all x1, blocking collectives, on_device(): lax.all_to_all(send_rows, 'group', split_axis=0, concat_axis=0, tiled=True)  18.9 us
    all_to_all x1, starting transfers between devices, on_device(): lax.all_to_all(best, 'group', split_axis=0, concat_axis=0, tiled=True)  5.1 us
    all_to_all x1, waiting for transfers between devices, on_device(): lax.all_to_all(send_rank, 'group', split_axis=0, concat_axis=0, tiled=True)  4.59 us
    all_to_all x1, waiting for transfers between devices, on_device(): lax.all_to_all(best, 'group', split_axis=0, concat_axis=0, tiled=True)  4.57 us
    all_to_all x1, starting transfers between devices, on_device(): lax.all_to_all(send_rank, 'group', split_axis=0, concat_axis=0, tiled=True)  4.26 us
  transfers between devices with their start and end apart: 3, of which 3 were waited for; matrix products, arithmetic and copies ran while one was open for 2% of the time, Pallas kernels for 0%

commit v1 on v0

v1 whole, which is shorter than its diff:
```python
import functools

import jax
import jax.numpy as jnp
from jax import lax
from jax.experimental import pallas as pl
from jax.experimental.pallas import tpu as pltpu
from jax.sharding import PartitionSpec as P

AXES = ("group", "tile")
ROWS = 256
META = 16
PAY = ROWS + META
E = 512
LOW = -(2**31)
NEAR = (1, 0, 3, 2)
OTHER = (3, 2, 1, 0)
PLACES = [(x, y, z, c) for x in range(4) for y in range(4) for z in range(4) for c in range(2)]


def linear(x, y, z, c):
    return (z * 2 + c) * 16 + y * 4 + x


def across(place, mask, both):
    x, y, z, c = place
    step = OTHER if (c and both) else NEAR
    return (
        step[x] if mask & 1 else x,
        step[y] if mask & 2 else y,
        step[z] if mask & 4 else z,
        c,
    )


def exchange(array, mask):
    pairs = [(linear(*across(q, mask, True)), linear(*q)) for q in PLACES]
    return lax.ppermute(array, AXES, pairs)


def swap(array):
    pairs = [(linear(x, y, z, 1 - c), linear(x, y, z, c)) for x, y, z, c in PLACES]
    return lax.ppermute(array, AXES, pairs)


def cube_groups():
    groups = []
    for x, y, z, c in PLACES:
        if x % 2 == 0 and y % 2 == 0 and z % 2 == 0:
            groups.append([linear(x + (k & 1), y + (k >> 1 & 1), z + (k >> 2 & 1), c) for k in range(8)])
    return groups


def unit_kernel(emb_ref, cluster_ref, rank_ref, out_ref):
    emb = emb_ref[...]
    sums = jnp.sum(emb * emb, axis=1, keepdims=True)
    out_ref[0:ROWS, :] = (emb * lax.rsqrt(sums + 1e-06)).astype(jnp.bfloat16)
    rank = rank_ref[...]
    high = (rank >> 8).astype(jnp.float32)
    low = (rank & 255).astype(jnp.float32)
    cluster = cluster_ref[...].astype(jnp.float32)
    first = jnp.concatenate([high, low], axis=1)
    second = jnp.concatenate([cluster, jnp.zeros_like(cluster)], axis=1)
    row = lax.broadcasted_iota(jnp.int32, (META, E), 0)
    meta = jnp.where(row == 0, first, jnp.where(row == 1, second, 0.0))
    out_ref[ROWS:PAY, :] = meta.astype(jnp.bfloat16)


def unit_rows(embeddings, cluster_ids, order_rank):
    return pl.pallas_call(
        unit_kernel,
        out_shape=jax.ShapeDtypeStruct((PAY, E), jnp.bfloat16),
        in_specs=[pl.BlockSpec(memory_space=pltpu.VMEM)] * 3,
        out_specs=pl.BlockSpec(memory_space=pltpu.VMEM),
        cost_estimate=pl.CostEstimate(flops=1000000, bytes_accessed=800000, transcendentals=256),
    )(embeddings, cluster_ids.reshape(1, ROWS), order_rank.reshape(1, ROWS))


def match_kernel(old, new, *refs):
    count = len(old) + len(new)
    masks = old + new
    others = [m for m in masks if m]
    scalar_ref, own_ref = refs[0], refs[1]
    mine = dict(zip(others, refs[2 : 2 + len(others)]))
    theirs = dict(zip(others, refs[2 + len(others) : 2 + 2 * len(others)]))
    rest = refs[2 + 2 * len(others) :]
    prev_ref, out_ref, qbuf, kbuf, qsem, ksem, qkey, qrank, kkey, acc = rest
    core, code = scalar_ref[0], scalar_ref[1]
    at = {m: i for i, m in enumerate(masks)}

    def query_copy(m, source):
        return pltpu.make_async_copy(source, qbuf.at[at[m]], qsem.at[at[m]])

    def key_copy(m, source):
        return pltpu.make_async_copy(source, kbuf.at[at[m]], ksem.at[at[m]])

    def start_query(m):
        if m == 0:
            query_copy(m, own_ref.at[0]).start()
            return

        @pl.when(core == 0)
        def _():
            query_copy(m, mine[m].at[0]).start()

        @pl.when(core == 1)
        def _():
            query_copy(m, theirs[m].at[1]).start()

    def start_key(m):
        if m == 0:
            key_copy(m, own_ref).start()
            return

        @pl.when(core == 0)
        def _():
            key_copy(m, theirs[m]).start()

        @pl.when(core == 1)
        def _():
            key_copy(m, mine[m]).start()

    for m in new:
        start_query(m)
    for m in masks:
        start_key(m)
    for m in old:
        start_query(m)

    def load_query(m):
        i = at[m]
        query_copy(m, own_ref.at[0]).wait()
        meta = qbuf[i, ROWS:PAY, :].astype(jnp.float32)
        rank = meta[0:1, 0:ROWS] * 256.0 + meta[0:1, ROWS : 2 * ROWS]
        key = meta[1:2, 0:ROWS] * 32768.0 + rank
        both = jnp.concatenate([key, rank, jnp.zeros((6, ROWS), jnp.float32)], axis=0)
        columns = jnp.transpose(both)
        qkey[i] = jnp.broadcast_to(columns[:, 0:1], (ROWS, 128)).astype(jnp.int32)
        qrank[i] = jnp.broadcast_to(columns[:, 1:2], (ROWS, 128)).astype(jnp.int32) + LOW
        acc[i] = jnp.full((ROWS, 128), -1.0, jnp.float32)

    def load_key(m):
        i = at[m]
        key_copy(m, own_ref).wait()
        for h in range(2):
            meta = kbuf[i, h, ROWS:PAY, :].astype(jnp.float32)
            rank = meta[0:1, 0:ROWS] * 256.0 + meta[0:1, ROWS : 2 * ROWS]
            key = meta[1:2, 0:ROWS] * 32768.0 + rank
            kkey[i, h] = key.astype(jnp.int32) + (LOW + 1)

    def rect(queries, keys):
        q0, k0 = at[queries[0]], at[keys[0]]
        nq, nk = len(queries), len(keys)

        def step(t, carry):
            k = k0 + t // 2
            h = t % 2
            tile = kbuf[k, h, 0:ROWS, :]
            row = kkey[k, h]
            for q in range(q0, q0 + nq):
                score = lax.dot_general(
                    qbuf[q, 0:ROWS, :], tile, (((1,), (1,)), ((), ())), preferred_element_type=jnp.float32
                )
                best = acc[q]
                for half in range(2):
                    lanes = slice(half * 128, half * 128 + 128)
                    gap = qkey[q] - row[:, lanes]
                    best = jnp.maximum(best, jnp.where(gap < qrank[q], score[:, lanes], -1.0))
                acc[q] = best
            return carry

        lax.fori_loop(0, nk * 2, step, 0)

    for m in new:
        load_query(m)
    for m in masks:
        load_key(m)
    for m in old:
        load_query(m)
    rect(new, masks)
    if old:
        rect(old, new)
    out_ref[...] = prev_ref[...]
    for m in masks:
        found = jnp.max(jnp.transpose(acc[at[m]]), axis=0, keepdims=True)
        slot = code ^ m
        out_ref[slot] = jnp.maximum(out_ref[slot], found)


def match(old, new, scalars, own, mine, theirs, prev):
    masks = old + new
    others = [m for m in masks if m]
    count = len(masks)
    pairs = len(new) * count + len(old) * len(new)
    anywhere = pl.BlockSpec(memory_space=pl.ANY)
    return pl.pallas_call(
        functools.partial(match_kernel, old, new),
        out_shape=jax.ShapeDtypeStruct((8, 1, ROWS), jnp.float32),
        in_specs=[pl.BlockSpec(memory_space=pltpu.SMEM)]
        + [anywhere] * (1 + 2 * len(others))
        + [pl.BlockSpec(memory_space=pltpu.VMEM)],
        out_specs=pl.BlockSpec(memory_space=pltpu.VMEM),
        scratch_shapes=[
            pltpu.VMEM((count, PAY, E), jnp.bfloat16),
            pltpu.VMEM((count, 2, PAY, E), jnp.bfloat16),
            pltpu.SemaphoreType.DMA((count,)),
            pltpu.SemaphoreType.DMA((count,)),
            pltpu.VMEM((count, ROWS, 128), jnp.int32),
            pltpu.VMEM((count, ROWS, 128), jnp.int32),
            pltpu.VMEM((count, 2, 1, ROWS), jnp.int32),
            pltpu.VMEM((count, ROWS, 128), jnp.float32),
        ],
        compiler_params=pltpu.CompilerParams(vmem_limit_bytes=40 * 2**20),
        cost_estimate=pl.CostEstimate(
            flops=pairs * 2 * ROWS * 2 * ROWS * E, bytes_accessed=count * 3 * PAY * E * 2, transcendentals=0
        ),
    )(scalars, own, *[mine[m] for m in others], *[theirs[m] for m in others], prev)


def on_device(embeddings, cluster_ids, order_rank):
    group, tile = lax.axis_index("group"), lax.axis_index("tile")
    core = group % 2
    code = (tile % 2) + 2 * (tile // 4 % 2) + 4 * (group // 2 % 2)
    scalars = jnp.stack([core, code]).astype(jnp.int32)
    unit = unit_rows(embeddings, cluster_ids, order_rank)
    own = jnp.stack([unit, swap(unit)])
    mine = {m: exchange(own, m) for m in (1, 2, 4)}
    mine[3] = exchange(mine[1], 2)
    mine[6] = exchange(mine[2], 4)
    mine[5] = exchange(mine[4], 1)
    theirs = {m: swap(mine[m]) for m in (1, 2, 4)}
    mine[7] = exchange(mine[3], 4)
    theirs.update({m: swap(mine[m]) for m in (3, 6, 5, 7)})
    best = jnp.full((8, 1, ROWS), -1.0, jnp.float32)
    best = match((), (0, 1, 2, 4), scalars, own, mine, theirs, best)
    best = match((0, 1, 2, 4), (3, 6, 5), scalars, own, mine, theirs, best)
    best = match((0, 1, 2, 4, 3, 6, 5), (7,), scalars, own, mine, theirs, best)
    back = lax.all_to_all(best, AXES, split_axis=0, concat_axis=0, axis_index_groups=cube_groups())
    return jnp.max(back, axis=0)[0]


def solution(mesh):
    return jax.shard_map(
        on_device,
        mesh=mesh,
        in_specs=(P(AXES, None), P(AXES, None), P(AXES)),
        out_specs=P(AXES),
        check_vma=False,
    )
```

time: 174 us -> 77.1 us (0.44)
  waiting for transfers between devices: 66.9 us -> 6.92 us
  Pallas kernels: 0 us -> 31.8 us
  blocking collectives: 38.7 us -> 8.13 us
  matrix products: 29.8 us -> 0 us
  starting transfers between devices: 9.36 us -> 24.4 us
  between operations: 13.5 us -> 0.09 us
  other arithmetic: 7.68 us -> 1.67 us
  local copies, waits for them, and re-layouts: 6.43 us -> 3.73 us
    all_gather x1 -> x0, waiting for transfers between devices: 57.8 us -> none  [on_device(): lax.all_gather(members, 'tile', axis=0, tiled=True)]
    pallas_call x0 -> x4, Pallas kernels: none -> 31.8 us  [the longest x3 29.9 us: match(): pl.pallas_call(functools.partial(match_kernel, old, new), out_shape=jax.S...]
    dot_general x12 -> x0, matrix products: 29.8 us -> none  [score_block(): lax.dot_general(queries, key_block, (((1,), (1,)), ((), ())), preferred_e...]
    ppermute x0 -> x15, starting transfers between devices: none -> 24.4 us  [the longest x7 21.9 us: exchange(): return lax.ppermute(array, AXES, pairs)]
    all_gather x1 -> x0, blocking collectives: 19.7 us -> none  [on_device(): lax.all_gather(member_rank, 'tile', axis=0, tiled=True)]
    all_to_all x1, blocking collectives: 18.9 us -> 8.13 us  [on_device(): lax.all_to_all(best, AXES, split_axis=0, concat_axis=0, axis_index_groups...]
    all_to_all x2 -> x0, starting transfers between devices: 9.36 us -> none  [the longest x1 5.1 us: on_device(): lax.all_to_all(best, 'group', split_axis=0, concat_axis=0, tiled=True)]
    all_to_all x2 -> x0, waiting for transfers between devices: 9.16 us -> none  [the longest x1 4.59 us: on_device(): lax.all_to_all(send_rank, 'group', split_axis=0, concat_axis=0, tiled=True)]
  transfers between devices with their start and end apart: 3 -> 15, of which waited for: 3 -> 5; matrix products, arithmetic and copies ran while one was open for 2% -> 0% of each run, Pallas kernels for 0% -> 25%
where the time goes in v1:
time: 77.1 us; the launch traced here: 76.8 us
  Pallas kernels  31.8 us (41%)
  starting transfers between devices  24.4 us (32%)
  blocking collectives  8.13 us (11%)
  waiting for transfers between devices  6.92 us (9%)
  local copies, waits for them, and re-layouts  3.73 us (5%)
  other arithmetic  1.67 us (2%)
    pallas_call x3, Pallas kernels, match(): pl.pallas_call(functools.partial(match_kernel, old, new), out_shape=jax.S...  29.9 us
    ppermute x7, starting transfers between devices, exchange(): return lax.ppermute(array, AXES, pairs)  21.9 us
    all_to_all x1, blocking collectives, on_device(): lax.all_to_all(best, AXES, split_axis=0, concat_axis=0, axis_index_groups...  8.13 us
    ppermute x7, waiting for transfers between devices, exchange(): return lax.ppermute(array, AXES, pairs)  5.5 us
    unnamed x8, local copies, waits for them, and re-layouts  3.72 us
    ppermute x8, starting transfers between devices, swap(): return lax.ppermute(array, AXES, pairs)  2.45 us
    pallas_call x1, Pallas kernels, unit_rows(): pl.pallas_call(unit_kernel, out_shape=jax.ShapeDtypeStruct((PAY, E), jnp....  1.88 us
  transfers between devices with their start and end apart: 15, of which 5 were waited for; matrix products, arithmetic and copies ran while one was open for 0% of the time, Pallas kernels for 25%

profile of v1, /device:TPU:1, one launch (start us, length us, event | category | flops | bytes accessed | tf_op | source)
XLA Modules:
  0.0 76.8 jit_solution(13919000955161678756)
XLA Ops:
  0.0 1.9 %shard_map.37 = bf16[272,512]{1,0:T(8,128)(2,1)} custom-call(f32[256,512]{1,0:T(8,128)} %emb_ref.1, s32[1,256]{1,0:T(1,128)} %bitcast.8, s32[1,256]{1,0:T(1,128)} %bitcast.9), custom_call_target="tpu_custom_call" | custom-call | flops 1000000 | bytes 800000 | tf_op jit(solution)/shard_map/pallas_call | solution.py:70
  1.9 1.4 %collective-permute-start = (bf16[272,512]{1,0:T(8,128)(2,1)}, bf16[272,512]{1,0:T(8,128)(2,1)S(1)}, u32[]{:S(2)}, u32[]{:S(2)}) collective-permute-start(bf16[272,512]{1,0:T(8,128)(2,1)} %shard_map.37), channel_id=1, source_target_pairs={{16,0},{0,16},{48,32},{32,48},{80,64},{64,80},{112,96},{96,112},{2... | collective-permute-start | bytes 835592 | tf_op jit(solution)/shard_map/ppermute | solution.py:43
  3.3 1.4 %collective-permute-done = bf16[272,512]{1,0:T(8,128)(2,1)S(1)} collective-permute-done((bf16[272,512]{1,0:T(8,128)(2,1)}, bf16[272,512]{1,0:T(8,128)(2,1)S(1)}, u32[]{:S(2)}, u32[]{:S(2)}) %collective-permute-start) | collective-permute-done | bytes 278560 | tf_op jit(solution)/shard_map/ppermute | solution.py:43
  4.7 1.0 %pad_maximum_fusion.refs_1_ = bf16[2,272,512]{2,1,0:T(8,128)(2,1)S(1)} fusion(bf16[1,272,512]{2,1,0:T(8,128)(2,1)S(1)} %bitcast.7, bf16[1,272,512]{2,1,0:T(8,128)(2,1)} %bitcast.6), kind=kLoop, calls=%fused_computation | loop fusion | flops 278528 | bytes 1114112 | tf_op jit(solution)/shard_map/stack | solution.py:226
  5.7 2.6 %collective-permute-start.1 = (bf16[2,272,512]{2,1,0:T(8,128)(2,1)S(1)}, bf16[2,272,512]{2,1,0:T(8,128)(2,1)S(1)}, u32[]{:S(2)}, u32[]{:S(2)}) collective-permute-start(bf16[2,272,512]{2,1,0:T(8,128)(2,1)S(1)} %pad_maximum_fusion.refs_1_), channel_id=1, source_target_pairs={{1,0},{19,16},{33,32},{51,48},{65,64},{83,80},{97,96},{115,112},{5... | collective-permute-start | bytes 1671176 | tf_op jit(solution)/shard_map/ppermute | solution.py:38
  8.4 2.7 %collective-permute-start.2 = (bf16[2,272,512]{2,1,0:T(8,128)(2,1)S(1)}, bf16[2,272,512]{2,1,0:T(8,128)(2,1)S(1)}, u32[]{:S(2)}, u32[]{:S(2)}) collective-permute-start(bf16[2,272,512]{2,1,0:T(8,128)(2,1)S(1)} %pad_maximum_fusion.refs_1_), channel_id=1, source_target_pairs={{4,0},{28,16},{36,32},{60,48},{68,64},{92,80},{100,96},{124,112},{... | collective-permute-start | bytes 1671176 | tf_op jit(solution)/shard_map/ppermute | solution.py:38
  11.1 3.8 %collective-permute-start.3 = (bf16[2,272,512]{2,1,0:T(8,128)(2,1)S(1)}, bf16[2,272,512]{2,1,0:T(8,128)(2,1)S(1)}, u32[]{:S(2)}, u32[]{:S(2)}) collective-permute-start(bf16[2,272,512]{2,1,0:T(8,128)(2,1)S(1)} %pad_maximum_fusion.refs_1_), channel_id=1, source_target_pairs={{32,0},{112,16},{0,32},{80,48},{96,64},{48,80},{64,96},{16,112},{3... | collective-permute-start | bytes 1671176 | tf_op jit(solution)/shard_map/ppermute | solution.py:38
  14.8 0.5 collective-permute-done.1.refs_2_
  15.4 2.8 %collective-permute-start.4 = (bf16[2,272,512]{2,1,0:T(8,128)(2,1)S(1)}, bf16[2,272,512]{2,1,0:T(8,128)(2,1)S(1)}, u32[]{:S(2)}, u32[]{:S(2)}) collective-permute-start(bf16[2,272,512]{2,1,0:T(8,128)(2,1)S(1)} %collective-permute-done.1.refs_2_), channel_id=1, source_target_pairs={{4,0},{28,16},{36,32},{60,48},{68,64},{92,80},{100,96},{124,112},{... | collective-permute-start | bytes 1671176 | tf_op jit(solution)/shard_map/ppermute | solution.py:38
  18.2 0.0 collective-permute-done.2.refs_3_
  18.2 3.8 %collective-permute-start.5 = (bf16[2,272,512]{2,1,0:T(8,128)(2,1)S(1)}, bf16[2,272,512]{2,1,0:T(8,128)(2,1)S(1)}, u32[]{:S(2)}, u32[]{:S(2)}) collective-permute-start(bf16[2,272,512]{2,1,0:T(8,128)(2,1)S(1)} %collective-permute-done.2.refs_3_), channel_id=1, source_target_pairs={{32,0},{112,16},{0,32},{80,48},{96,64},{48,80},{64,96},{16,112},{3... | collective-permute-start | bytes 1671176 | tf_op jit(solution)/shard_map/ppermute | solution.py:38
  22.0 0.0 collective-permute-done.3.refs_4_
  22.0 2.5 %collective-permute-start.6 = (bf16[2,272,512]{2,1,0:T(8,128)(2,1)S(1)}, bf16[2,272,512]{2,1,0:T(8,128)(2,1)}, u32[]{:S(2)}, u32[]{:S(2)}) collective-permute-start(bf16[2,272,512]{2,1,0:T(8,128)(2,1)S(1)} %collective-permute-done.3.refs_4_), channel_id=1, source_target_pairs={{1,0},{19,16},{33,32},{51,48},{65,64},{83,80},{97,96},{115,112},{5... | collective-permute-start | bytes 1671176 | tf_op jit(solution)/shard_map/ppermute | solution.py:38
  24.4 0.5 collective-permute-start.9
  25.0 0.2 collective-permute-done.4.refs_5_
  25.1 3.8 %collective-permute-start.7 = (bf16[2,272,512]{2,1,0:T(8,128)(2,1)S(1)}, bf16[2,272,512]{2,1,0:T(8,128)(2,1)}, u32[]{:S(2)}, u32[]{:S(2)}) collective-permute-start(bf16[2,272,512]{2,1,0:T(8,128)(2,1)S(1)} %collective-permute-done.4.refs_5_), channel_id=1, source_target_pairs={{32,0},{112,16},{0,32},{80,48},{96,64},{48,80},{64,96},{16,112},{3... | collective-permute-start | bytes 1671176 | tf_op jit(solution)/shard_map/ppermute | solution.py:38
  28.9 0.0 collective-permute-done.5.refs_6_
  28.9 0.0 collective-permute-start.10
  28.9 2.8 %collective-permute-done.6.refs_7_ = bf16[2,272,512]{2,1,0:T(8,128)(2,1)} collective-permute-done((bf16[2,272,512]{2,1,0:T(8,128)(2,1)S(1)}, bf16[2,272,512]{2,1,0:T(8,128)(2,1)}, u32[]{:S(2)}, u32[]{:S(2)}) %collective-permute-start.6) | collective-permute-done | bytes 557088 | tf_op jit(solution)/shard_map/ppermute | solution.py:38
  31.7 0.8 %copy-done = bf16[2,272,512]{2,1,0:T(8,128)(2,1)} copy-done((bf16[2,272,512]{2,1,0:T(8,128)(2,1)}, bf16[2,272,512]{2,1,0:T(8,128)(2,1)S(1)}, u32[]{:S(2)}) %copy-start) | copy-done | bytes 557080
  32.5 0.5 collective-permute-start.12
  33.0 0.8 %copy-done.2 = bf16[2,272,512]{2,1,0:T(8,128)(2,1)} copy-done((bf16[2,272,512]{2,1,0:T(8,128)(2,1)}, bf16[2,272,512]{2,1,0:T(8,128)(2,1)S(1)}, u32[]{:S(2)}) %copy-start.2) | copy-done | bytes 557080
  33.8 0.0 collective-permute-start.13
  33.8 0.1 pad_add_fusion.refs_0_
  33.9 2.0 %collective-permute-done.7.refs_8_ = bf16[2,272,512]{2,1,0:T(8,128)(2,1)} collective-permute-done((bf16[2,272,512]{2,1,0:T(8,128)(2,1)S(1)}, bf16[2,272,512]{2,1,0:T(8,128)(2,1)}, u32[]{:S(2)}, u32[]{:S(2)}) %collective-permute-start.7) | collective-permute-done | bytes 557088 | tf_op jit(solution)/shard_map/ppermute | solution.py:38
  35.9 1.0 %copy-done.1 = bf16[2,272,512]{2,1,0:T(8,128)(2,1)S(1)} copy-done((bf16[2,272,512]{2,1,0:T(8,128)(2,1)S(1)}, bf16[2,272,512]{2,1,0:T(8,128)(2,1)}, u32[]{:S(2)}) %copy-start.1) | copy-done | bytes 557080
  37.0 1.1 %copy-done.3 = bf16[2,272,512]{2,1,0:T(8,128)(2,1)S(1)} copy-done((bf16[2,272,512]{2,1,0:T(8,128)(2,1)S(1)}, bf16[2,272,512]{2,1,0:T(8,128)(2,1)}, u32[]{:S(2)}) %copy-start.3) | copy-done | bytes 557080
  38.0 6.4 %shard_map.38.refs_14_ = f32[8,1,256]{2,1,0:T(1,128)S(1)} custom-call(s32[2]{0:T(128)S(1)} %pad_add_fusion.refs_0_, bf16[2,272,512]{2,1,0:T(8,128)(2,1)S(1)} %pad_maximum_fusion.refs_1_, bf16[2,272,512]{2,1,0:T(8,128)(2,1)S(1)} %collective-permute-done.1.refs_2_, bf16[2,272,512]{2,1,0:T(8,128)(2,1)S(1)} %collective-permute-done.2.refs_3_, ...), custom_call_target="tpu_custom_call" | custom-call | flops 2147483648 | bytes 3342336 | tf_op jit(solution)/shard_map/pallas_call | solution.py:196
  44.5 12.9 %shard_map.39.refs_16_ = f32[8,1,256]{2,1,0:T(1,128)S(1)} custom-call(s32[2]{0:T(128)S(1)} %pad_add_fusion.refs_0_, bf16[2,272,512]{2,1,0:T(8,128)(2,1)S(1)} %pad_maximum_fusion.refs_1_, bf16[2,272,512]{2,1,0:T(8,128)(2,1)S(1)} %collective-permute-done.1.refs_2_, bf16[2,272,512]{2,1,0:T(8,128)(2,1)S(1)} %collective-permute-done.2.refs_3_, ...), custom_call_target="tpu_custom_call" | custom-call | flops 4429185024 | bytes 5849088 | tf_op jit(solution)/shard_map/pallas_call | solution.py:196
  57.4 10.6 %shard_map.40 = f32[8,1,256]{2,1,0:T(1,128)S(1)} custom-call(s32[2]{0:T(128)S(1)} %pad_add_fusion.refs_0_, bf16[2,272,512]{2,1,0:T(8,128)(2,1)S(1)} %pad_maximum_fusion.refs_1_, bf16[2,272,512]{2,1,0:T(8,128)(2,1)S(1)} %collective-permute-done.1.refs_2_, bf16[2,272,512]{2,1,0:T(8,128)(2,1)S(1)} %collective-permute-done.2.refs_3_, ...), custom_call_target="tpu_custom_call" | custom-call | flops 2013265920 | bytes 6684672 | tf_op jit(solution)/shard_map/pallas_call | solution.py:196
  68.0 8.1 %all_to_all.5 = f32[8,1,256]{2,1,0:T(1,128)S(1)} all-to-all(f32[8,1,256]{2,1,0:T(1,128)S(1)} %shard_map.40), channel_id=1, replica_groups={{0,1,4,5,32,33,36,37},{16,17,20,21,48,49,52,53},{64,65,68,69,96,97,100,..., dimensions={0} | all-to-all | bytes 16384 | tf_op jit(solution)/shard_map/all_to_all | solution.py:238
  76.2 0.6 reduce_max.9
  (15 shorter events, 0.0 us)
Async XLA Ops:
  1.9 2.8 %collective-permute-start = (bf16[272,512]{1,0:T(8,128)(2,1)}, bf16[272,512]{1,0:T(8,128)(2,1)S(1)}, u32[]{:S(2)}, u32[]{:S(2)}) collective-permute-start(bf16[272,512]{1,0:T(8,128)(2,1)} %shard_map.37), channel_id=1, source_target_pairs={{16,0},{0,16},{48,32},{32,48},{80,64},{64,80},{112,96},{96,112},{2... | collective-permute-start | bytes 835592 | tf_op jit(solution)/shard_map/ppermute | solution.py:43
  5.7 9.7 %collective-permute-start.1 = (bf16[2,272,512]{2,1,0:T(8,128)(2,1)S(1)}, bf16[2,272,512]{2,1,0:T(8,128)(2,1)S(1)}, u32[]{:S(2)}, u32[]{:S(2)}) collective-permute-start(bf16[2,272,512]{2,1,0:T(8,128)(2,1)S(1)} %pad_maximum_fusion.refs_1_), channel_id=1, source_target_pairs={{1,0},{19,16},{33,32},{51,48},{65,64},{83,80},{97,96},{115,112},{5... | collective-permute-start | bytes 1671176 | tf_op jit(solution)/shard_map/ppermute | solution.py:38
  8.4 9.9 %collective-permute-start.2 = (bf16[2,272,512]{2,1,0:T(8,128)(2,1)S(1)}, bf16[2,272,512]{2,1,0:T(8,128)(2,1)S(1)}, u32[]{:S(2)}, u32[]{:S(2)}) collective-permute-start(bf16[2,272,512]{2,1,0:T(8,128)(2,1)S(1)} %pad_maximum_fusion.refs_1_), channel_id=1, source_target_pairs={{4,0},{28,16},{36,32},{60,48},{68,64},{92,80},{100,96},{124,112},{... | collective-permute-start | bytes 1671176 | tf_op jit(solution)/shard_map/ppermute | solution.py:38
  11.1 10.9 %collective-permute-start.3 = (bf16[2,272,512]{2,1,0:T(8,128)(2,1)S(1)}, bf16[2,272,512]{2,1,0:T(8,128)(2,1)S(1)}, u32[]{:S(2)}, u32[]{:S(2)}) collective-permute-start(bf16[2,272,512]{2,1,0:T(8,128)(2,1)S(1)} %pad_maximum_fusion.refs_1_), channel_id=1, source_target_pairs={{32,0},{112,16},{0,32},{80,48},{96,64},{48,80},{64,96},{16,112},{3... | collective-permute-start | bytes 1671176 | tf_op jit(solution)/shard_map/ppermute | solution.py:38
  15.4 9.7 %collective-permute-start.4 = (bf16[2,272,512]{2,1,0:T(8,128)(2,1)S(1)}, bf16[2,272,512]{2,1,0:T(8,128)(2,1)S(1)}, u32[]{:S(2)}, u32[]{:S(2)}) collective-permute-start(bf16[2,272,512]{2,1,0:T(8,128)(2,1)S(1)} %collective-permute-done.1.refs_2_), channel_id=1, source_target_pairs={{4,0},{28,16},{36,32},{60,48},{68,64},{92,80},{100,96},{124,112},{... | collective-permute-start | bytes 1671176 | tf_op jit(solution)/shard_map/ppermute | solution.py:38
  18.2 10.7 %collective-permute-start.5 = (bf16[2,272,512]{2,1,0:T(8,128)(2,1)S(1)}, bf16[2,272,512]{2,1,0:T(8,128)(2,1)S(1)}, u32[]{:S(2)}, u32[]{:S(2)}) collective-permute-start(bf16[2,272,512]{2,1,0:T(8,128)(2,1)S(1)} %collective-permute-done.2.refs_3_), channel_id=1, source_target_pairs={{32,0},{112,16},{0,32},{80,48},{96,64},{48,80},{64,96},{16,112},{3... | collective-permute-start | bytes 1671176 | tf_op jit(solution)/shard_map/ppermute | solution.py:38
  22.0 9.7 %collective-permute-start.6 = (bf16[2,272,512]{2,1,0:T(8,128)(2,1)S(1)}, bf16[2,272,512]{2,1,0:T(8,128)(2,1)}, u32[]{:S(2)}, u32[]{:S(2)}) collective-permute-start(bf16[2,272,512]{2,1,0:T(8,128)(2,1)S(1)} %collective-permute-done.3.refs_4_), channel_id=1, source_target_pairs={{1,0},{19,16},{33,32},{51,48},{65,64},{83,80},{97,96},{115,112},{5... | collective-permute-start | bytes 1671176 | tf_op jit(solution)/shard_map/ppermute | solution.py:38
  24.4 7.2 %collective-permute-start.8 = (bf16[2,272,512]{2,1,0:T(8,128)(2,1)S(1)}, bf16[2,272,512]{2,1,0:T(8,128)(2,1)S(1)}, u32[]{:S(2)}, u32[]{:S(2)}) collective-permute-start(bf16[2,272,512]{2,1,0:T(8,128)(2,1)S(1)} %collective-permute-done.1.refs_2_), channel_id=1, source_target_pairs={{16,0},{0,16},{48,32},{32,48},{80,64},{64,80},{112,96},{96,112},{2... | collective-permute-start | bytes 1671176 | tf_op jit(solution)/shard_map/ppermute | solution.py:43
  24.4 8.6 %collective-permute-start.9 = (bf16[2,272,512]{2,1,0:T(8,128)(2,1)S(1)}, bf16[2,272,512]{2,1,0:T(8,128)(2,1)S(1)}, u32[]{:S(2)}, u32[]{:S(2)}) collective-permute-start(bf16[2,272,512]{2,1,0:T(8,128)(2,1)S(1)} %collective-permute-done.2.refs_3_), channel_id=1, source_target_pairs={{16,0},{0,16},{48,32},{32,48},{80,64},{64,80},{112,96},{96,112},{2... | collective-permute-start | bytes 1671176 | tf_op jit(solution)/shard_map/ppermute | solution.py:43
  25.1 10.8 %collective-permute-start.7 = (bf16[2,272,512]{2,1,0:T(8,128)(2,1)S(1)}, bf16[2,272,512]{2,1,0:T(8,128)(2,1)}, u32[]{:S(2)}, u32[]{:S(2)}) collective-permute-start(bf16[2,272,512]{2,1,0:T(8,128)(2,1)S(1)} %collective-permute-done.4.refs_5_), channel_id=1, source_target_pairs={{32,0},{112,16},{0,32},{80,48},{96,64},{48,80},{64,96},{16,112},{3... | collective-permute-start | bytes 1671176 | tf_op jit(solution)/shard_map/ppermute | solution.py:38
  28.9 7.0 %collective-permute-start.10 = (bf16[2,272,512]{2,1,0:T(8,128)(2,1)S(1)}, bf16[2,272,512]{2,1,0:T(8,128)(2,1)}, u32[]{:S(2)}, u32[]{:S(2)}) collective-permute-start(bf16[2,272,512]{2,1,0:T(8,128)(2,1)S(1)} %collective-permute-done.3.refs_4_), channel_id=1, source_target_pairs={{16,0},{0,16},{48,32},{32,48},{80,64},{64,80},{112,96},{96,112},{2... | collective-permute-start | bytes 1671176 | tf_op jit(solution)/shard_map/ppermute | solution.py:43
  31.7 12.8 %collective-permute-start.11 = (bf16[2,272,512]{2,1,0:T(8,128)(2,1)S(1)}, bf16[2,272,512]{2,1,0:T(8,128)(2,1)}, u32[]{:S(2)}, u32[]{:S(2)}) collective-permute-start(bf16[2,272,512]{2,1,0:T(8,128)(2,1)S(1)} %collective-permute-done.4.refs_5_), channel_id=1, source_target_pairs={{16,0},{0,16},{48,32},{32,48},{80,64},{64,80},{112,96},{96,112},{2... | collective-permute-start | bytes 1671176 | tf_op jit(solution)/shard_map/ppermute | solution.py:43
  31.7 0.8 %copy-start = (bf16[2,272,512]{2,1,0:T(8,128)(2,1)}, bf16[2,272,512]{2,1,0:T(8,128)(2,1)S(1)}, u32[]{:S(2)}) copy-start(bf16[2,272,512]{2,1,0:T(8,128)(2,1)S(1)} %collective-permute-done.8.refs_5_.refs_8_.refs_9_) | copy-start | bytes 1671172
  32.5 12.0 %collective-permute-start.12 = (bf16[2,272,512]{2,1,0:T(8,128)(2,1)S(1)}, bf16[2,272,512]{2,1,0:T(8,128)(2,1)}, u32[]{:S(2)}, u32[]{:S(2)}) collective-permute-start(bf16[2,272,512]{2,1,0:T(8,128)(2,1)S(1)} %collective-permute-done.5.refs_6_), channel_id=1, source_target_pairs={{16,0},{0,16},{48,32},{32,48},{80,64},{64,80},{112,96},{96,112},{2... | collective-permute-start | bytes 1671176 | tf_op jit(solution)/shard_map/ppermute | solution.py:43
  33.0 0.8 %copy-start.2 = (bf16[2,272,512]{2,1,0:T(8,128)(2,1)}, bf16[2,272,512]{2,1,0:T(8,128)(2,1)S(1)}, u32[]{:S(2)}) copy-start(bf16[2,272,512]{2,1,0:T(8,128)(2,1)S(1)} %collective-permute-done.9.refs_6_.refs_9_.refs_10_) | copy-start | bytes 1671172
  33.8 10.7 %collective-permute-start.13 = (bf16[2,272,512]{2,1,0:T(8,128)(2,1)}, bf16[2,272,512]{2,1,0:T(8,128)(2,1)}, u32[]{:S(2)}, u32[]{:S(2)}) collective-permute-start(bf16[2,272,512]{2,1,0:T(8,128)(2,1)} %collective-permute-done.6.refs_7_), channel_id=1, source_target_pairs={{16,0},{0,16},{48,32},{32,48},{80,64},{64,80},{112,96},{96,112},{2... | collective-permute-start | bytes 1671176 | tf_op jit(solution)/shard_map/ppermute | solution.py:43
  35.9 21.5 %collective-permute-start.14 = (bf16[2,272,512]{2,1,0:T(8,128)(2,1)}, bf16[2,272,512]{2,1,0:T(8,128)(2,1)S(1)}, u32[]{:S(2)}, u32[]{:S(2)}) collective-permute-start(bf16[2,272,512]{2,1,0:T(8,128)(2,1)} %collective-permute-done.7.refs_8_), channel_id=1, source_target_pairs={{16,0},{0,16},{48,32},{32,48},{80,64},{64,80},{112,96},{96,112},{2... | collective-permute-start | bytes 1671176 | tf_op jit(solution)/shard_map/ppermute | solution.py:43
  35.9 1.1 %copy-start.1 = (bf16[2,272,512]{2,1,0:T(8,128)(2,1)S(1)}, bf16[2,272,512]{2,1,0:T(8,128)(2,1)}, u32[]{:S(2)}) copy-start(bf16[2,272,512]{2,1,0:T(8,128)(2,1)} %copy-done) | copy-start | bytes 1671172
  37.0 1.1 %copy-start.3 = (bf16[2,272,512]{2,1,0:T(8,128)(2,1)S(1)}, bf16[2,272,512]{2,1,0:T(8,128)(2,1)}, u32[]{:S(2)}) copy-start(bf16[2,272,512]{2,1,0:T(8,128)(2,1)} %copy-done.2) | copy-start | bytes 1671172

commit v2 on v1

v2 whole, which is shorter than its diff:
```python
import functools

import jax
import jax.numpy as jnp
from jax import lax
from jax.experimental import pallas as pl
from jax.experimental.pallas import tpu as pltpu
from jax.sharding import PartitionSpec as P

AXES = ("group", "tile")
ROWS = 256
META = 16
PAY = ROWS + META
E = 512
LOW = -(2**31)
NEAR = (1, 0, 3, 2)
OTHER = (3, 2, 1, 0)
PLACES = [(x, y, z, c) for x in range(4) for y in range(4) for z in range(4) for c in range(2)]


def linear(x, y, z, c):
    return (z * 2 + c) * 16 + y * 4 + x


def across(place, mask):
    x, y, z, c = place
    step = OTHER if c else NEAR
    return (
        step[x] if mask & 1 else x,
        step[y] if mask & 2 else y,
        step[z] if mask & 4 else z,
        c,
    )


def exchange(array, mask):
    pairs = [(linear(*across(q, mask)), linear(*q)) for q in PLACES]
    return lax.ppermute(array, AXES, pairs)


def swap(array):
    pairs = [(linear(x, y, z, 1 - c), linear(x, y, z, c)) for x, y, z, c in PLACES]
    return lax.ppermute(array, AXES, pairs)


def cube_groups():
    groups = []
    for place in PLACES:
        starts = (0, 1) if place[3] else (0, 2)
        if all(p in starts for p in place[:3]):
            groups.append([linear(*across(place, k)) for k in range(8)])
    return groups


def unit_kernel(emb_ref, cluster_ref, rank_ref, out_ref):
    emb = emb_ref[...]
    sums = jnp.sum(emb * emb, axis=1, keepdims=True)
    out_ref[0:ROWS, :] = (emb * lax.rsqrt(sums + 1e-06)).astype(jnp.bfloat16)
    rank = rank_ref[...]
    high = (rank >> 8).astype(jnp.float32)
    low = (rank & 255).astype(jnp.float32)
    cluster = cluster_ref[...].astype(jnp.float32)
    first = jnp.concatenate([high, low], axis=1)
    second = jnp.concatenate([cluster, jnp.zeros_like(cluster)], axis=1)
    row = lax.broadcasted_iota(jnp.int32, (META, E), 0)
    meta = jnp.where(row == 0, first, jnp.where(row == 1, second, 0.0))
    out_ref[ROWS:PAY, :] = meta.astype(jnp.bfloat16)


def unit_rows(embeddings, cluster_ids, order_rank):
    return pl.pallas_call(
        unit_kernel,
        out_shape=jax.ShapeDtypeStruct((PAY, E), jnp.bfloat16),
        in_specs=[pl.BlockSpec(memory_space=pltpu.VMEM)] * 3,
        out_specs=pl.BlockSpec(memory_space=pltpu.VMEM),
        cost_estimate=pl.CostEstimate(flops=1000000, bytes_accessed=800000, transcendentals=256),
    )(embeddings, cluster_ids.reshape(1, ROWS), order_rank.reshape(1, ROWS))


def match_kernel(old, new, *refs):
    masks = old + new
    others = [m for m in masks if m]
    code_ref, own_ref = refs[0], refs[1]
    mine = dict(zip(others, refs[2 : 2 + len(others)]))
    theirs = dict(zip(others, refs[2 + len(others) : 2 + 2 * len(others)]))
    mine[0] = theirs[0] = own_ref
    prev_ref, out_ref, qkey, qrank, kkey = refs[2 + 2 * len(others) :]
    fresh = {m: i for i, m in enumerate(new)}

    def numbers(meta):
        meta = meta.astype(jnp.float32)
        rank = meta[0:1, 0:ROWS] * 256.0 + meta[0:1, ROWS : 2 * ROWS]
        return rank, meta[1:2, 0:ROWS] * 32768.0 + rank

    def columns(row):
        return jnp.broadcast_to(jnp.transpose(jnp.broadcast_to(row, (8, ROWS)))[:, 0:1], (ROWS, 128)).astype(jnp.int32)

    def product(left, right):
        return lax.dot_general(left, right, (((1,), (1,)), ((), ())), preferred_element_type=jnp.float32)

    code = code_ref[0]
    out_ref[...] = prev_ref[...]
    found = {}
    rows = {}
    for m in new:
        rank, key = numbers(mine[m][0, ROWS:PAY, :])
        qkey[fresh[m]] = columns(key)
        qrank[fresh[m]] = columns(rank) + LOW
    for m in masks:
        for h in range(2):
            key = numbers(theirs[m][h, ROWS:PAY, :])[1]
            rows[m, h] = key.astype(jnp.int32) + (LOW + 1)
            if old and m in new:
                kkey[fresh[m], h * ROWS : h * ROWS + ROWS, :] = columns(key) + (LOW + 1)
    for m in new:
        best = jnp.full((ROWS, 128), -1.0, jnp.float32)
        column, limit = qkey[fresh[m]], qrank[fresh[m]]
        for n in masks:
            for h in range(2):
                score = product(mine[m][0, 0:ROWS, :], theirs[n][h, 0:ROWS, :])
                for lanes in (slice(0, 128), slice(128, 256)):
                    valid = column - rows[n, h][:, lanes] < limit
                    best = jnp.maximum(best, jnp.where(valid, score[:, lanes], -1.0))
        found[m] = jnp.max(jnp.transpose(best), axis=0, keepdims=True)
    for m in old:
        rank, key = numbers(mine[m][0, ROWS:PAY, :])
        row = jnp.broadcast_to(key.astype(jnp.int32), (8, ROWS))
        limit = jnp.broadcast_to(rank.astype(jnp.int32) + LOW, (8, ROWS))
        best = jnp.full((8, ROWS), -1.0, jnp.float32)
        for n in new:
            for h in range(2):
                score = product(theirs[n][h, 0:ROWS, :], mine[m][0, 0:ROWS, :])
                for r in range(0, ROWS, 8):
                    column = kkey[fresh[n], h * ROWS + r : h * ROWS + r + 8, :]
                    valid = row - jnp.concatenate([column, column], axis=1) < limit
                    best = jnp.maximum(best, jnp.where(valid, score[r : r + 8, :], -1.0))
        found[m] = jnp.max(best, axis=0, keepdims=True)
    for m in masks:
        slot = code ^ m
        out_ref[slot] = jnp.maximum(out_ref[slot], found[m])


def match(old, new, code, own, mine, theirs, prev):
    masks = old + new
    others = [m for m in masks if m]
    count = len(masks)
    pairs = len(new) * count + len(old) * len(new)
    vmem = pl.BlockSpec(memory_space=pltpu.VMEM)
    return pl.pallas_call(
        functools.partial(match_kernel, old, new),
        out_shape=jax.ShapeDtypeStruct((8, 1, ROWS), jnp.float32),
        in_specs=[pl.BlockSpec(memory_space=pltpu.SMEM)] + [vmem] * (2 + 2 * len(others)),
        out_specs=vmem,
        scratch_shapes=[
            pltpu.VMEM((len(new), ROWS, 128), jnp.int32),
            pltpu.VMEM((len(new), ROWS, 128), jnp.int32),
            pltpu.VMEM((len(new), 2 * ROWS, 128), jnp.int32),
        ],
        compiler_params=pltpu.CompilerParams(vmem_limit_bytes=24 * 2**20),
        cost_estimate=pl.CostEstimate(
            flops=pairs * 2 * ROWS * 2 * ROWS * E, bytes_accessed=count * 3 * PAY * E * 2, transcendentals=0
        ),
    )(code, own, *[mine[m] for m in others], *[theirs[m] for m in others], prev)


def on_device(embeddings, cluster_ids, order_rank):
    group, tile = lax.axis_index("group"), lax.axis_index("tile")
    places = (tile % 4, tile // 4, group // 2)
    code = sum(jnp.where(group % 2 == 0, p % 2, p // 2) << i for i, p in enumerate(places))
    code = code.astype(jnp.int32).reshape(1)
    unit = unit_rows(embeddings, cluster_ids, order_rank)
    own = jnp.stack([unit, swap(unit)])
    best = jnp.full((8, 1, ROWS), -1.0, jnp.float32)
    mine = {m: exchange(own, m) for m in (1, 2, 4)}
    mine[3] = exchange(mine[1], 2)
    mine[6] = exchange(mine[2], 4)
    mine[5] = exchange(mine[4], 1)
    theirs = {m: swap(mine[m]) for m in (1, 2, 4)}
    best = match((), (0, 1, 2, 4), code, own, mine, theirs, best)
    mine[3], mine[6], mine[5], best = lax.optimization_barrier((mine[3], mine[6], mine[5], best))
    mine[7] = exchange(mine[3], 4)
    theirs.update({m: swap(mine[m]) for m in (3, 6, 5)})
    best = match((0, 1, 2, 4), (3, 6, 5), code, own, mine, theirs, best)
    mine[7], best = lax.optimization_barrier((mine[7], best))
    theirs[7] = swap(mine[7])
    best = match((0, 1, 2, 4, 3, 6, 5), (7,), code, own, mine, theirs, best)
    back = lax.all_to_all(best, AXES, split_axis=0, concat_axis=0, axis_index_groups=cube_groups())
    return jnp.max(back, axis=0)[0]


def solution(mesh):
    return jax.shard_map(
        on_device,
        mesh=mesh,
        in_specs=(P(AXES, None), P(AXES, None), P(AXES)),
        out_specs=P(AXES),
        check_vma=False,
    )
```

time: 77.1 us -> 63.7 us (0.83)
  Pallas kernels: 31.8 us -> 16.2 us
  waiting for transfers between devices: 6.92 us -> 15.5 us
  starting transfers between devices: 24.4 us -> 17.9 us
  blocking collectives: 8.13 us -> 12.2 us
  local copies, waits for them, and re-layouts: 3.73 us -> 0.01 us
    pallas_call x3, Pallas kernels: 29.9 us -> 14.3 us  [match(): pl.pallas_call(functools.partial(match_kernel, old, new), out_shape=jax.S...]
    ppermute x7, starting transfers between devices: 21.9 us -> 15.7 us  [exchange(): return lax.ppermute(array, AXES, pairs)]
    ppermute x7, waiting for transfers between devices: 5.5 us -> 11.7 us  [exchange(): return lax.ppermute(array, AXES, pairs)]
    all_to_all x1, blocking collectives: 8.13 us -> 12.2 us  [on_device(): lax.all_to_all(best, AXES, split_axis=0, concat_axis=0, axis_index_groups...]
    unnamed x8 -> x0, local copies, waits for them, and re-layouts: 3.72 us -> none
    ppermute x8, waiting for transfers between devices: 1.41 us -> 3.76 us  [swap(): return lax.ppermute(array, AXES, pairs)]
  transfers between devices with their start and end apart: 15 -> 15, of which waited for: 5 -> 9; matrix products, arithmetic and copies ran while one was open for 0% -> 0% of each run, Pallas kernels for 25% -> 16%
where the time goes in v2:
time: 63.7 us; the launch traced here: 63.4 us
  starting transfers between devices  17.9 us (28%)
  Pallas kernels  16.2 us (25%)
  waiting for transfers between devices  15.5 us (24%)
  blocking collectives  12.2 us (19%)
  other arithmetic  1.6 us (3%)
    ppermute x7, starting transfers between devices, exchange(): return lax.ppermute(array, AXES, pairs)  15.7 us
    pallas_call x3, Pallas kernels, match(): pl.pallas_call(functools.partial(match_kernel, old, new), out_shape=jax.S...  14.3 us
    all_to_all x1, blocking collectives, on_device(): lax.all_to_all(best, AXES, split_axis=0, concat_axis=0, axis_index_groups...  12.2 us
    ppermute x7, waiting for transfers between devices, exchange(): return lax.ppermute(array, AXES, pairs)  11.7 us
    ppermute x8, waiting for transfers between devices, swap(): return lax.ppermute(array, AXES, pairs)  3.76 us
    ppermute x8, starting transfers between devices, swap(): return lax.ppermute(array, AXES, pairs)  2.29 us
    pallas_call x1, Pallas kernels, unit_rows(): pl.pallas_call(unit_kernel, out_shape=jax.ShapeDtypeStruct((PAY, E), jnp....  1.89 us
  transfers between devices with their start and end apart: 15, of which 9 were waited for; matrix products, arithmetic and copies ran while one was open for 0% of the time, Pallas kernels for 16%

profile of v2, /device:TPU:1, one launch (start us, length us, event | category | flops | bytes accessed | tf_op | source)
XLA Modules:
  0.0 63.4 jit_solution(7826281256007766609)
XLA Ops:
  0.0 1.9 %shard_map.37 = bf16[272,512]{1,0:T(8,128)(2,1)} custom-call(f32[256,512]{1,0:T(8,128)} %emb_ref.1, s32[1,256]{1,0:T(1,128)} %bitcast.7, s32[1,256]{1,0:T(1,128)} %bitcast.8), custom_call_target="tpu_custom_call" | custom-call | flops 1000000 | bytes 800000 | tf_op jit(solution)/shard_map/pallas_call | solution.py:71
  1.9 1.4 %collective-permute-start = (bf16[272,512]{1,0:T(8,128)(2,1)}, bf16[272,512]{1,0:T(8,128)(2,1)S(1)}, u32[]{:S(2)}, u32[]{:S(2)}) collective-permute-start(bf16[272,512]{1,0:T(8,128)(2,1)} %shard_map.37), channel_id=1, source_target_pairs={{16,0},{0,16},{48,32},{32,48},{80,64},{64,80},{112,96},{96,112},{2... | collective-permute-start | bytes 835592 | tf_op jit(solution)/shard_map/ppermute | solution.py:43
  3.3 1.4 %collective-permute-done = bf16[272,512]{1,0:T(8,128)(2,1)S(1)} collective-permute-done((bf16[272,512]{1,0:T(8,128)(2,1)}, bf16[272,512]{1,0:T(8,128)(2,1)S(1)}, u32[]{:S(2)}, u32[]{:S(2)}) %collective-permute-start) | collective-permute-done | bytes 278560 | tf_op jit(solution)/shard_map/ppermute | solution.py:43
  4.7 1.0 %pad_maximum_fusion.refs_1_ = bf16[2,272,512]{2,1,0:T(8,128)(2,1)S(1)} fusion(bf16[1,272,512]{2,1,0:T(8,128)(2,1)S(1)} %bitcast.6, bf16[1,272,512]{2,1,0:T(8,128)(2,1)} %bitcast.5), kind=kLoop, calls=%fused_computation | loop fusion | flops 278528 | bytes 1114112 | tf_op jit(solution)/shard_map/stack | solution.py:172
  5.7 3.9 %collective-permute-start.3 = (bf16[2,272,512]{2,1,0:T(8,128)(2,1)S(1)}, bf16[2,272,512]{2,1,0:T(8,128)(2,1)S(1)}, u32[]{:S(2)}, u32[]{:S(2)}) collective-permute-start(bf16[2,272,512]{2,1,0:T(8,128)(2,1)S(1)} %pad_maximum_fusion.refs_1_), channel_id=1, source_target_pairs={{32,0},{112,16},{0,32},{80,48},{96,64},{48,80},{64,96},{16,112},{3... | collective-permute-start | bytes 1671176 | tf_op jit(solution)/shard_map/ppermute | solution.py:38
  9.6 2.7 %collective-permute-start.2 = (bf16[2,272,512]{2,1,0:T(8,128)(2,1)S(1)}, bf16[2,272,512]{2,1,0:T(8,128)(2,1)S(1)}, u32[]{:S(2)}, u32[]{:S(2)}) collective-permute-start(bf16[2,272,512]{2,1,0:T(8,128)(2,1)S(1)} %pad_maximum_fusion.refs_1_), channel_id=1, source_target_pairs={{4,0},{28,16},{36,32},{60,48},{68,64},{92,80},{100,96},{124,112},{... | collective-permute-start | bytes 1671176 | tf_op jit(solution)/shard_map/ppermute | solution.py:38
  12.4 2.5 %collective-permute-start.1 = (bf16[2,272,512]{2,1,0:T(8,128)(2,1)S(1)}, bf16[2,272,512]{2,1,0:T(8,128)(2,1)S(1)}, u32[]{:S(2)}, u32[]{:S(2)}) collective-permute-start(bf16[2,272,512]{2,1,0:T(8,128)(2,1)S(1)} %pad_maximum_fusion.refs_1_), channel_id=1, source_target_pairs={{1,0},{19,16},{33,32},{51,48},{65,64},{83,80},{97,96},{115,112},{5... | collective-permute-start | bytes 1671176 | tf_op jit(solution)/shard_map/ppermute | solution.py:38
  14.9 1.7 %collective-permute-done.3.refs_4_ = bf16[2,272,512]{2,1,0:T(8,128)(2,1)S(1)} collective-permute-done((bf16[2,272,512]{2,1,0:T(8,128)(2,1)S(1)}, bf16[2,272,512]{2,1,0:T(8,128)(2,1)S(1)}, u32[]{:S(2)}, u32[]{:S(2)}) %collective-permute-start.3) | collective-permute-done | bytes 557088 | tf_op jit(solution)/shard_map/ppermute | solution.py:38
  16.6 0.0 collective-permute-start.9
  16.6 2.7 %collective-permute-done.2.refs_3_ = bf16[2,272,512]{2,1,0:T(8,128)(2,1)S(1)} collective-permute-done((bf16[2,272,512]{2,1,0:T(8,128)(2,1)S(1)}, bf16[2,272,512]{2,1,0:T(8,128)(2,1)S(1)}, u32[]{:S(2)}, u32[]{:S(2)}) %collective-permute-start.2) | collective-permute-done | bytes 557088 | tf_op jit(solution)/shard_map/ppermute | solution.py:38
  19.3 0.0 collective-permute-start.8
  19.3 2.7 %collective-permute-done.1.refs_2_ = bf16[2,272,512]{2,1,0:T(8,128)(2,1)S(1)} collective-permute-done((bf16[2,272,512]{2,1,0:T(8,128)(2,1)S(1)}, bf16[2,272,512]{2,1,0:T(8,128)(2,1)S(1)}, u32[]{:S(2)}, u32[]{:S(2)}) %collective-permute-start.1) | collective-permute-done | bytes 557088 | tf_op jit(solution)/shard_map/ppermute | solution.py:38
  22.0 0.0 collective-permute-start.7
  22.0 2.5 %collective-permute-start.6 = (bf16[2,272,512]{2,1,0:T(8,128)(2,1)S(1)}, bf16[2,272,512]{2,1,0:T(8,128)(2,1)}, u32[]{:S(2)}, u32[]{:S(2)}) collective-permute-start(bf16[2,272,512]{2,1,0:T(8,128)(2,1)S(1)} %collective-permute-done.3.refs_4_), channel_id=1, source_target_pairs={{1,0},{19,16},{33,32},{51,48},{65,64},{83,80},{97,96},{115,112},{5... | collective-permute-start | bytes 1671176 | tf_op jit(solution)/shard_map/ppermute | solution.py:38
  24.5 0.1 collective-permute-start.5
  24.5 1.4 %collective-permute-start.4 = (bf16[2,272,512]{2,1,0:T(8,128)(2,1)S(1)}, bf16[2,272,512]{2,1,0:T(8,128)(2,1)}, u32[]{:S(2)}, u32[]{:S(2)}) collective-permute-start(bf16[2,272,512]{2,1,0:T(8,128)(2,1)S(1)} %collective-permute-done.1.refs_2_), channel_id=1, source_target_pairs={{4,0},{28,16},{36,32},{60,48},{68,64},{92,80},{100,96},{124,112},{... | collective-permute-start | bytes 1671176 | tf_op jit(solution)/shard_map/ppermute | solution.py:38
  25.9 3.7 %shard_map.38.refs_14_ = f32[8,1,256]{2,1,0:T(1,128)S(1)} custom-call(s32[1]{0:T(128)} %bitcast.refs_0_, bf16[2,272,512]{2,1,0:T(8,128)(2,1)S(1)} %pad_maximum_fusion.refs_1_, bf16[2,272,512]{2,1,0:T(8,128)(2,1)S(1)} %collective-permute-done.1.refs_2_, bf16[2,272,512]{2,1,0:T(8,128)(2,1)S(1)} %collective-permute-done.2.refs_3_, ...), custom_call_target="tpu_custom_call" | custom-call | flops 2147483648 | bytes 3342336 | tf_op jit(solution)/shard_map/pallas_call | solution.py:149
  29.6 2.1 %collective-permute-done.6.refs_7_ = bf16[2,272,512]{2,1,0:T(8,128)(2,1)} collective-permute-done((bf16[2,272,512]{2,1,0:T(8,128)(2,1)S(1)}, bf16[2,272,512]{2,1,0:T(8,128)(2,1)}, u32[]{:S(2)}, u32[]{:S(2)}) %collective-permute-start.6) | collective-permute-done | bytes 557088 | tf_op jit(solution)/shard_map/ppermute | solution.py:38
  31.7 2.5 %collective-permute-done.5.refs_6_ = bf16[2,272,512]{2,1,0:T(8,128)(2,1)} collective-permute-done((bf16[2,272,512]{2,1,0:T(8,128)(2,1)S(1)}, bf16[2,272,512]{2,1,0:T(8,128)(2,1)}, u32[]{:S(2)}, u32[]{:S(2)}) %collective-permute-start.5) | collective-permute-done | bytes 557088 | tf_op jit(solution)/shard_map/ppermute | solution.py:38
  34.2 0.1 collective-permute-done.4.refs_5_
  34.2 0.0 collective-permute-start.12
  34.3 0.5 collective-permute-start.13
  34.8 0.0 collective-permute-start.11
  34.8 2.6 %collective-permute-start.10 = (bf16[2,272,512]{2,1,0:T(8,128)(2,1)}, bf16[2,272,512]{2,1,0:T(8,128)(2,1)S(1)}, u32[]{:S(2)}, u32[]{:S(2)}) collective-permute-start(bf16[2,272,512]{2,1,0:T(8,128)(2,1)} %collective-permute-done.4.refs_5_), channel_id=1, source_target_pairs={{32,0},{112,16},{0,32},{80,48},{96,64},{48,80},{64,96},{16,112},{3... | collective-permute-start | bytes 1671176 | tf_op jit(solution)/shard_map/ppermute | solution.py:38
  37.4 0.0 collective-permute-done.13.refs_13_.refs_14_
  37.4 0.7 %collective-permute-done.11.refs_11_.refs_12_ = bf16[2,272,512]{2,1,0:T(8,128)(2,1)S(1)} collective-permute-done((bf16[2,272,512]{2,1,0:T(8,128)(2,1)}, bf16[2,272,512]{2,1,0:T(8,128)(2,1)S(1)}, u32[]{:S(2)}, u32[]{:S(2)}) %collective-permute-start.11) | collective-permute-done | bytes 557088 | tf_op jit(solution)/shard_map/ppermute | solution.py:43
  38.0 6.6 %shard_map.39.refs_16_ = f32[8,1,256]{2,1,0:T(1,128)S(1)} custom-call(s32[1]{0:T(128)} %bitcast.refs_0_, bf16[2,272,512]{2,1,0:T(8,128)(2,1)S(1)} %pad_maximum_fusion.refs_1_, bf16[2,272,512]{2,1,0:T(8,128)(2,1)S(1)} %collective-permute-done.1.refs_2_, bf16[2,272,512]{2,1,0:T(8,128)(2,1)S(1)} %collective-permute-done.2.refs_3_, ...), custom_call_target="tpu_custom_call" | custom-call | flops 4429185024 | bytes 5849088 | tf_op jit(solution)/shard_map/pallas_call | solution.py:149
  44.7 0.3 collective-permute-start.14
  45.0 1.7 %collective-permute-done.14.refs_15_ = bf16[2,272,512]{2,1,0:T(8,128)(2,1)S(1)} collective-permute-done((bf16[2,272,512]{2,1,0:T(8,128)(2,1)S(1)}, bf16[2,272,512]{2,1,0:T(8,128)(2,1)S(1)}, u32[]{:S(2)}, u32[]{:S(2)}) %collective-permute-start.14) | collective-permute-done | bytes 557088 | tf_op jit(solution)/shard_map/ppermute | solution.py:43
  46.7 4.0 %shard_map.40 = f32[8,1,256]{2,1,0:T(1,128)S(1)} custom-call(s32[1]{0:T(128)} %bitcast.refs_0_, bf16[2,272,512]{2,1,0:T(8,128)(2,1)S(1)} %pad_maximum_fusion.refs_1_, bf16[2,272,512]{2,1,0:T(8,128)(2,1)S(1)} %collective-permute-done.1.refs_2_, bf16[2,272,512]{2,1,0:T(8,128)(2,1)S(1)} %collective-permute-done.2.refs_3_, ...), custom_call_target="tpu_custom_call" | custom-call | flops 2013265920 | bytes 6684672 | tf_op jit(solution)/shard_map/pallas_call | solution.py:149
  50.7 12.2 %all_to_all.5 = f32[8,1,256]{2,1,0:T(1,128)S(1)} all-to-all(f32[8,1,256]{2,1,0:T(1,128)S(1)} %shard_map.40), channel_id=1, replica_groups={{0,1,4,5,32,33,36,37},{16,19,28,31,112,115,124,127},{48,51,60,63,80,83,..., dimensions={0} | all-to-all | bytes 16384 | tf_op jit(solution)/shard_map/all_to_all | solution.py:187
  62.8 0.6 reduce_max.9
  (6 shorter events, 0.0 us)
Async XLA Ops:
  1.9 2.8 %collective-permute-start = (bf16[272,512]{1,0:T(8,128)(2,1)}, bf16[272,512]{1,0:T(8,128)(2,1)S(1)}, u32[]{:S(2)}, u32[]{:S(2)}) collective-permute-start(bf16[272,512]{1,0:T(8,128)(2,1)} %shard_map.37), channel_id=1, source_target_pairs={{16,0},{0,16},{48,32},{32,48},{80,64},{64,80},{112,96},{96,112},{2... | collective-permute-start | bytes 835592 | tf_op jit(solution)/shard_map/ppermute | solution.py:43
  5.7 10.8 %collective-permute-start.3 = (bf16[2,272,512]{2,1,0:T(8,128)(2,1)S(1)}, bf16[2,272,512]{2,1,0:T(8,128)(2,1)S(1)}, u32[]{:S(2)}, u32[]{:S(2)}) collective-permute-start(bf16[2,272,512]{2,1,0:T(8,128)(2,1)S(1)} %pad_maximum_fusion.refs_1_), channel_id=1, source_target_pairs={{32,0},{112,16},{0,32},{80,48},{96,64},{48,80},{64,96},{16,112},{3... | collective-permute-start | bytes 1671176 | tf_op jit(solution)/shard_map/ppermute | solution.py:38
  9.6 9.7 %collective-permute-start.2 = (bf16[2,272,512]{2,1,0:T(8,128)(2,1)S(1)}, bf16[2,272,512]{2,1,0:T(8,128)(2,1)S(1)}, u32[]{:S(2)}, u32[]{:S(2)}) collective-permute-start(bf16[2,272,512]{2,1,0:T(8,128)(2,1)S(1)} %pad_maximum_fusion.refs_1_), channel_id=1, source_target_pairs={{4,0},{28,16},{36,32},{60,48},{68,64},{92,80},{100,96},{124,112},{... | collective-permute-start | bytes 1671176 | tf_op jit(solution)/shard_map/ppermute | solution.py:38
  12.4 9.6 %collective-permute-start.1 = (bf16[2,272,512]{2,1,0:T(8,128)(2,1)S(1)}, bf16[2,272,512]{2,1,0:T(8,128)(2,1)S(1)}, u32[]{:S(2)}, u32[]{:S(2)}) collective-permute-start(bf16[2,272,512]{2,1,0:T(8,128)(2,1)S(1)} %pad_maximum_fusion.refs_1_), channel_id=1, source_target_pairs={{1,0},{19,16},{33,32},{51,48},{65,64},{83,80},{97,96},{115,112},{5... | collective-permute-start | bytes 1671176 | tf_op jit(solution)/shard_map/ppermute | solution.py:38
  16.6 8.0 %collective-permute-start.9 = (bf16[2,272,512]{2,1,0:T(8,128)(2,1)S(1)}, bf16[2,272,512]{2,1,0:T(8,128)(2,1)S(1)}, u32[]{:S(2)}, u32[]{:S(2)}) collective-permute-start(bf16[2,272,512]{2,1,0:T(8,128)(2,1)S(1)} %collective-permute-done.3.refs_4_), channel_id=1, source_target_pairs={{16,0},{0,16},{48,32},{32,48},{80,64},{64,80},{112,96},{96,112},{2... | collective-permute-start | bytes 1671176 | tf_op jit(solution)/shard_map/ppermute | solution.py:43
  19.3 6.6 %collective-permute-start.8 = (bf16[2,272,512]{2,1,0:T(8,128)(2,1)S(1)}, bf16[2,272,512]{2,1,0:T(8,128)(2,1)S(1)}, u32[]{:S(2)}, u32[]{:S(2)}) collective-permute-start(bf16[2,272,512]{2,1,0:T(8,128)(2,1)S(1)} %collective-permute-done.2.refs_3_), channel_id=1, source_target_pairs={{16,0},{0,16},{48,32},{32,48},{80,64},{64,80},{112,96},{96,112},{2... | collective-permute-start | bytes 1671176 | tf_op jit(solution)/shard_map/ppermute | solution.py:43
  22.0 3.9 %collective-permute-start.7 = (bf16[2,272,512]{2,1,0:T(8,128)(2,1)S(1)}, bf16[2,272,512]{2,1,0:T(8,128)(2,1)}, u32[]{:S(2)}, u32[]{:S(2)}) collective-permute-start(bf16[2,272,512]{2,1,0:T(8,128)(2,1)S(1)} %collective-permute-done.1.refs_2_), channel_id=1, source_target_pairs={{16,0},{0,16},{48,32},{32,48},{80,64},{64,80},{112,96},{96,112},{2... | collective-permute-start | bytes 1671176 | tf_op jit(solution)/shard_map/ppermute | solution.py:43
  22.0 9.7 %collective-permute-start.6 = (bf16[2,272,512]{2,1,0:T(8,128)(2,1)S(1)}, bf16[2,272,512]{2,1,0:T(8,128)(2,1)}, u32[]{:S(2)}, u32[]{:S(2)}) collective-permute-start(bf16[2,272,512]{2,1,0:T(8,128)(2,1)S(1)} %collective-permute-done.3.refs_4_), channel_id=1, source_target_pairs={{1,0},{19,16},{33,32},{51,48},{65,64},{83,80},{97,96},{115,112},{5... | collective-permute-start | bytes 1671176 | tf_op jit(solution)/shard_map/ppermute | solution.py:38
  24.5 9.7 %collective-permute-start.5 = (bf16[2,272,512]{2,1,0:T(8,128)(2,1)S(1)}, bf16[2,272,512]{2,1,0:T(8,128)(2,1)}, u32[]{:S(2)}, u32[]{:S(2)}) collective-permute-start(bf16[2,272,512]{2,1,0:T(8,128)(2,1)S(1)} %collective-permute-done.2.refs_3_), channel_id=1, source_target_pairs={{32,0},{112,16},{0,32},{80,48},{96,64},{48,80},{64,96},{16,112},{3... | collective-permute-start | bytes 1671176 | tf_op jit(solution)/shard_map/ppermute | solution.py:38
  24.5 9.7 %collective-permute-start.4 = (bf16[2,272,512]{2,1,0:T(8,128)(2,1)S(1)}, bf16[2,272,512]{2,1,0:T(8,128)(2,1)}, u32[]{:S(2)}, u32[]{:S(2)}) collective-permute-start(bf16[2,272,512]{2,1,0:T(8,128)(2,1)S(1)} %collective-permute-done.1.refs_2_), channel_id=1, source_target_pairs={{4,0},{28,16},{36,32},{60,48},{68,64},{92,80},{100,96},{124,112},{... | collective-permute-start | bytes 1671176 | tf_op jit(solution)/shard_map/ppermute | solution.py:38
  34.2 3.1 %collective-permute-start.12 = (bf16[2,272,512]{2,1,0:T(8,128)(2,1)}, bf16[2,272,512]{2,1,0:T(8,128)(2,1)S(1)}, u32[]{:S(2)}, u32[]{:S(2)}) collective-permute-start(bf16[2,272,512]{2,1,0:T(8,128)(2,1)} %collective-permute-done.5.refs_6_), channel_id=1, source_target_pairs={{16,0},{0,16},{48,32},{32,48},{80,64},{64,80},{112,96},{96,112},{2... | collective-permute-start | bytes 1671176 | tf_op jit(solution)/shard_map/ppermute | solution.py:43
  34.3 3.1 %collective-permute-start.13 = (bf16[2,272,512]{2,1,0:T(8,128)(2,1)}, bf16[2,272,512]{2,1,0:T(8,128)(2,1)S(1)}, u32[]{:S(2)}, u32[]{:S(2)}) collective-permute-start(bf16[2,272,512]{2,1,0:T(8,128)(2,1)} %collective-permute-done.6.refs_7_), channel_id=1, source_target_pairs={{16,0},{0,16},{48,32},{32,48},{80,64},{64,80},{112,96},{96,112},{2... | collective-permute-start | bytes 1671176 | tf_op jit(solution)/shard_map/ppermute | solution.py:43
  34.8 3.3 %collective-permute-start.11 = (bf16[2,272,512]{2,1,0:T(8,128)(2,1)}, bf16[2,272,512]{2,1,0:T(8,128)(2,1)S(1)}, u32[]{:S(2)}, u32[]{:S(2)}) collective-permute-start(bf16[2,272,512]{2,1,0:T(8,128)(2,1)} %collective-permute-done.4.refs_5_), channel_id=1, source_target_pairs={{16,0},{0,16},{48,32},{32,48},{80,64},{64,80},{112,96},{96,112},{2... | collective-permute-start | bytes 1671176 | tf_op jit(solution)/shard_map/ppermute | solution.py:43
  34.8 9.9 %collective-permute-start.10 = (bf16[2,272,512]{2,1,0:T(8,128)(2,1)}, bf16[2,272,512]{2,1,0:T(8,128)(2,1)S(1)}, u32[]{:S(2)}, u32[]{:S(2)}) collective-permute-start(bf16[2,272,512]{2,1,0:T(8,128)(2,1)} %collective-permute-done.4.refs_5_), channel_id=1, source_target_pairs={{32,0},{112,16},{0,32},{80,48},{96,64},{48,80},{64,96},{16,112},{3... | collective-permute-start | bytes 1671176 | tf_op jit(solution)/shard_map/ppermute | solution.py:38
  44.7 2.0 %collective-permute-start.14 = (bf16[2,272,512]{2,1,0:T(8,128)(2,1)S(1)}, bf16[2,272,512]{2,1,0:T(8,128)(2,1)S(1)}, u32[]{:S(2)}, u32[]{:S(2)}) collective-permute-start(bf16[2,272,512]{2,1,0:T(8,128)(2,1)S(1)} %collective-permute-done.10.refs_8_), channel_id=1, source_target_pairs={{16,0},{0,16},{48,32},{32,48},{80,64},{64,80},{112,96},{96,112},{2... | collective-permute-start | bytes 1671176 | tf_op jit(solution)/shard_map/ppermute | solution.py:43

commit v3 on v2

v3 whole, which is shorter than its diff:
```python
import functools

import jax
import jax.numpy as jnp
from jax import lax
from jax.experimental import pallas as pl
from jax.experimental.pallas import tpu as pltpu
from jax.sharding import PartitionSpec as P

AXES = ("group", "tile")
ROWS = 256
META = 16
PAY = ROWS + META
E = 512
LOW = -(2**31)
GRANT = 12 * 2**20
NEAR = (1, 0, 3, 2)
OTHER = (3, 2, 1, 0)
PLACES = [(x, y, z, c) for x in range(4) for y in range(4) for z in range(4) for c in range(2)]


def linear(x, y, z, c):
    return (z * 2 + c) * 16 + y * 4 + x


def across(place, mask):
    x, y, z, c = place
    step = OTHER if c else NEAR
    return (
        step[x] if mask & 1 else x,
        step[y] if mask & 2 else y,
        step[z] if mask & 4 else z,
        c,
    )


def exchange(array, mask):
    pairs = [(linear(*across(q, mask)), linear(*q)) for q in PLACES]
    return lax.ppermute(array, AXES, pairs)


def swap(array):
    pairs = [(linear(x, y, z, 1 - c), linear(x, y, z, c)) for x, y, z, c in PLACES]
    return lax.ppermute(array, AXES, pairs)


def cube_groups():
    groups = []
    for place in PLACES:
        starts = (0, 1) if place[3] else (0, 2)
        if all(p in starts for p in place[:3]):
            groups.append([linear(*across(place, k)) for k in range(8)])
    return groups


def unit_kernel(*refs):
    out_ref = refs[-1]
    for h in range(2):
        emb_ref, cluster_ref, rank_ref = refs[3 * h : 3 * h + 3]
        emb = emb_ref[...]
        sums = jnp.sum(emb * emb, axis=1, keepdims=True)
        out_ref[h, 0:ROWS, :] = (emb * lax.rsqrt(sums + 1e-06)).astype(jnp.bfloat16)
        rank = rank_ref[...]
        high = (rank >> 8).astype(jnp.float32)
        low = (rank & 255).astype(jnp.float32)
        cluster = cluster_ref[...].astype(jnp.float32)
        first = jnp.concatenate([high, low], axis=1)
        second = jnp.concatenate([cluster, jnp.zeros_like(cluster)], axis=1)
        row = lax.broadcasted_iota(jnp.int32, (META, E), 0)
        meta = jnp.where(row == 0, first, jnp.where(row == 1, second, 0.0))
        out_ref[h, ROWS:PAY, :] = meta.astype(jnp.bfloat16)


def payload(*halves):
    vmem = pl.BlockSpec(memory_space=pltpu.VMEM)
    return pl.pallas_call(
        unit_kernel,
        out_shape=jax.ShapeDtypeStruct((2, PAY, E), jnp.bfloat16),
        in_specs=[vmem] * 6,
        out_specs=vmem,
        compiler_params=pltpu.CompilerParams(vmem_limit_bytes=GRANT),
        cost_estimate=pl.CostEstimate(flops=2000000, bytes_accessed=1600000, transcendentals=512),
    )(*halves)


def match_kernel(queries, keys, *refs):
    code_ref = refs[0]
    mine = dict(zip(queries, refs[1 : 1 + len(queries)]))
    theirs = dict(zip(keys, refs[1 + len(queries) : 1 + len(queries) + len(keys)]))
    prev_ref, out_ref, first, second = refs[1 + len(queries) + len(keys) :]

    def numbers(meta):
        meta = meta.astype(jnp.float32)
        rank = meta[0:1, 0:ROWS] * 256.0 + meta[0:1, ROWS : 2 * ROWS]
        return rank, meta[1:2, 0:ROWS] * 32768.0 + rank

    def columns(row):
        return jnp.broadcast_to(jnp.transpose(jnp.broadcast_to(row, (8, ROWS)))[:, 0:1], (ROWS, 128)).astype(jnp.int32)

    def product(left, right):
        return lax.dot_general(left, right, (((1,), (1,)), ((), ())), preferred_element_type=jnp.float32)

    found = {}
    sides = [(n, h) for n in keys for h in range(2)]
    limits = {m: numbers(mine[m][0, ROWS:PAY, :]) for m in queries}
    wanted = {(n, h): numbers(theirs[n][h, ROWS:PAY, :])[1] for n, h in sides}
    if len(queries) < len(keys):
        for i, m in enumerate(queries):
            first[i] = columns(limits[m][1])
            second[i] = columns(limits[m][0]) + LOW
        rows = {side: wanted[side].astype(jnp.int32) + (LOW + 1) for side in sides}
        for i, m in enumerate(queries):
            best = jnp.full((ROWS, 128), -1.0, jnp.float32)
            for n, h in sides:
                score = product(mine[m][0, 0:ROWS, :], theirs[n][h, 0:ROWS, :])
                for lanes in (slice(0, 128), slice(128, 256)):
                    valid = first[i] - rows[n, h][:, lanes] < second[i]
                    best = jnp.maximum(best, jnp.where(valid, score[:, lanes], -1.0))
            found[m] = jnp.max(jnp.transpose(best), axis=0, keepdims=True)
    else:
        for i, side in enumerate(sides):
            first[i] = columns(wanted[side]) + (LOW + 1)
        for m in queries:
            row = jnp.broadcast_to(limits[m][1].astype(jnp.int32), (8, ROWS))
            limit = jnp.broadcast_to(limits[m][0].astype(jnp.int32) + LOW, (8, ROWS))
            best = jnp.full((8, ROWS), -1.0, jnp.float32)
            for i, (n, h) in enumerate(sides):
                score = product(theirs[n][h, 0:ROWS, :], mine[m][0, 0:ROWS, :])
                for r in range(0, ROWS, 8):
                    column = first[i, r : r + 8, :]
                    valid = row - jnp.concatenate([column, column], axis=1) < limit
                    best = jnp.maximum(best, jnp.where(valid, score[r : r + 8, :], -1.0))
            found[m] = jnp.max(best, axis=0, keepdims=True)
    code = code_ref[0]
    out_ref[...] = prev_ref[...]
    for m in queries:
        slot = code ^ m
        out_ref[slot] = jnp.maximum(out_ref[slot], found[m])


def match(queries, keys, code, mine, theirs, prev):
    columns = len(queries) if len(queries) < len(keys) else 2 * len(keys)
    vmem = pl.BlockSpec(memory_space=pltpu.VMEM)
    return pl.pallas_call(
        functools.partial(match_kernel, queries, keys),
        out_shape=jax.ShapeDtypeStruct((8, 1, ROWS), jnp.float32),
        in_specs=[pl.BlockSpec(memory_space=pltpu.SMEM)] + [vmem] * (len(queries) + len(keys) + 1),
        out_specs=vmem,
        scratch_shapes=[pltpu.VMEM((columns, ROWS, 128), jnp.int32)] * 2,
        compiler_params=pltpu.CompilerParams(vmem_limit_bytes=GRANT),
        cost_estimate=pl.CostEstimate(
            flops=len(queries) * len(keys) * 2 * ROWS * 2 * ROWS * E, bytes_accessed=1000, transcendentals=0
        ),
    )(code, *[mine[m] for m in queries], *[theirs[m] for m in keys], prev)


def on_device(embeddings, cluster_ids, order_rank):
    group, tile = lax.axis_index("group"), lax.axis_index("tile")
    places = (tile % 4, tile // 4, group // 2)
    code = sum(jnp.where(group % 2 == 0, p % 2, p // 2) << i for i, p in enumerate(places))
    code = code.astype(jnp.int32).reshape(1)
    half = (embeddings, cluster_ids.reshape(1, ROWS), order_rank.reshape(1, ROWS))
    own = payload(*half, *[swap(part) for part in half])
    best = jnp.full((8, 1, ROWS), -1.0, jnp.float32)
    mine, theirs = {0: own}, {0: own}
    for m in (1, 2, 4):
        mine[m] = exchange(own, m)
    mine[3] = exchange(mine[1], 2)
    mine[6] = exchange(mine[2], 4)
    mine[5] = exchange(mine[4], 1)
    best = match((0, 1, 2, 4), (0,), code, mine, theirs, best)
    theirs.update({m: swap(mine[m]) for m in (1, 2, 4)})
    best = match((0, 1, 2, 4), (1, 2, 4), code, mine, theirs, best)
    mine[3], mine[6], mine[5], best = lax.optimization_barrier((mine[3], mine[6], mine[5], best))
    mine[7] = exchange(mine[3], 4)
    best = match((3, 6, 5), (0, 1, 2, 4), code, mine, theirs, best)
    theirs.update({m: swap(mine[m]) for m in (3, 6, 5)})
    best = match((0, 1, 2, 4, 3, 6, 5), (3, 6, 5), code, mine, theirs, best)
    mine[7], best = lax.optimization_barrier((mine[7], best))
    theirs[7] = swap(mine[7])
    best = match((7,), (0, 1, 2, 4, 3, 6, 5), code, mine, theirs, best)
    best = match((0, 1, 2, 4, 3, 6, 5, 7), (7,), code, mine, theirs, best)
    back = lax.all_to_all(best, AXES, split_axis=0, concat_axis=0, axis_index_groups=cube_groups())
    return jnp.max(back, axis=0)[0]


def solution(mesh):
    return jax.shard_map(
        on_device,
        mesh=mesh,
        in_specs=(P(AXES, None), P(AXES, None), P(AXES)),
        out_specs=P(AXES),
        check_vma=False,
    )
```

time: 63.7 us -> 62.4 us (0.980)
  waiting for transfers between devices: 15.5 us -> 12.3 us
  Pallas kernels: 16.2 us -> 18.1 us
  blocking collectives: 12.2 us -> 10.8 us
  starting transfers between devices: 17.9 us -> 19 us
  local copies, waits for them, and re-layouts: 0.01 us -> 1.06 us
  other arithmetic: 1.6 us -> 0.59 us
    ppermute x8 -> x10, waiting for transfers between devices: 3.76 us -> 0.84 us  [swap(): return lax.ppermute(array, AXES, pairs)]
    pallas_call x4 -> x7, Pallas kernels: 16.2 us -> 18.1 us  [the longest x6 18 us: match(): pl.pallas_call(functools.partial(match_kernel, queries, keys), out_shape=...]
    all_to_all x1, blocking collectives: 12.2 us -> 10.8 us  [on_device(): lax.all_to_all(best, AXES, split_axis=0, concat_axis=0, axis_index_groups...]
    ppermute x8 -> x10, starting transfers between devices: 2.29 us -> 3.38 us  [swap(): return lax.ppermute(array, AXES, pairs)]
    unnamed x0 -> x6, local copies, waits for them, and re-layouts: none -> 1.05 us
    another operation x1 -> x0, other arithmetic: 1.01 us -> none  [on_device(): own = jnp.stack([unit, swap(unit)])]
  transfers between devices with their start and end apart: 15 -> 17, of which waited for: 9 -> 8; matrix products, arithmetic and copies ran while one was open for 0% -> 0% of each run, Pallas kernels for 16% -> 24%
where the time goes in v3:
time: 62.4 us; the launch traced here: 62 us
  starting transfers between devices  19 us (30%)
  Pallas kernels  18.1 us (29%)
  waiting for transfers between devices  12.3 us (20%)
  blocking collectives  10.8 us (17%)
  local copies, waits for them, and re-layouts  1.06 us (2%)
    pallas_call x6, Pallas kernels, match(): pl.pallas_call(functools.partial(match_kernel, queries, keys), out_shape=...  18 us
    ppermute x7, starting transfers between devices, exchange(): return lax.ppermute(array, AXES, pairs)  15.6 us
    ppermute x7, waiting for transfers between devices, exchange(): return lax.ppermute(array, AXES, pairs)  11.5 us
    all_to_all x1, blocking collectives, on_device(): lax.all_to_all(best, AXES, split_axis=0, concat_axis=0, axis_index_groups...  10.8 us
    ppermute x10, starting transfers between devices, swap(): return lax.ppermute(array, AXES, pairs)  3.38 us
  transfers between devices with their start and end apart: 17, of which 8 were waited for; matrix products, arithmetic and copies ran while one was open for 0% of the time, Pallas kernels for 24%

profile of v3, /device:TPU:1, one launch (start us, length us, event | category | flops | bytes accessed | tf_op | source)
XLA Modules:
  0.0 62.0 jit_solution(17731228568038467865)
XLA Ops:
  0.0 1.4 %collective-permute-start = (f32[256,512]{1,0:T(8,128)}, f32[256,512]{1,0:T(8,128)S(1)}, u32[]{:S(2)}, u32[]{:S(2)}) collective-permute-start(f32[256,512]{1,0:T(8,128)} %refs_0_.1), channel_id=1, source_target_pairs={{16,0},{0,16},{48,32},{32,48},{80,64},{64,80},{112,96},{96,112},{2... | collective-permute-start | bytes 1572872 | tf_op jit(solution)/shard_map/ppermute | solution.py:44
  1.4 0.7 %collective-permute-start.1 = (s32[1,256]{1,0:T(1,128)S(1)}, s32[1,256]{1,0:T(1,128)S(1)}, u32[]{:S(2)}, u32[]{:S(2)}) collective-permute-start(s32[1,256]{1,0:T(1,128)S(1)} %bitcast.3), channel_id=1, source_target_pairs={{16,0},{0,16},{48,32},{32,48},{80,64},{64,80},{112,96},{96,112},{2... | collective-permute-start | bytes 3080 | tf_op jit(solution)/shard_map/ppermute | solution.py:44
  2.1 0.0 copy-done.2
  2.1 0.7 %collective-permute-start.2 = (s32[1,256]{1,0:T(1,128)S(1)}, s32[1,256]{1,0:T(1,128)S(1)}, u32[]{:S(2)}, u32[]{:S(2)}) collective-permute-start(s32[1,256]{1,0:T(1,128)S(1)} %bitcast.5), channel_id=1, source_target_pairs={{16,0},{0,16},{48,32},{32,48},{80,64},{64,80},{112,96},{96,112},{2... | collective-permute-start | bytes 3080 | tf_op jit(solution)/shard_map/ppermute | solution.py:44
  2.8 0.2 collective-permute-done.1.refs_4_
  3.0 0.6 %collective-permute-done.2.refs_5_ = s32[1,256]{1,0:T(1,128)S(1)} collective-permute-done((s32[1,256]{1,0:T(1,128)S(1)}, s32[1,256]{1,0:T(1,128)S(1)}, u32[]{:S(2)}, u32[]{:S(2)}) %collective-permute-start.2) | collective-permute-done | bytes 1056 | tf_op jit(solution)/shard_map/ppermute | solution.py:44
  3.6 1.0 %copy-done = f32[256,512]{1,0:T(8,128)S(1)} copy-done((f32[256,512]{1,0:T(8,128)S(1)}, f32[256,512]{1,0:T(8,128)}, u32[]{:S(2)}) %copy-start) | copy-done | bytes 524312
  4.6 0.2 shard_map.37.refs_1_.refs_5_.refs_4_.refs_2_
  4.8 3.9 %collective-permute-start.5 = (bf16[2,272,512]{2,1,0:T(8,128)(2,1)S(1)}, bf16[2,272,512]{2,1,0:T(8,128)(2,1)S(1)}, u32[]{:S(2)}, u32[]{:S(2)}) collective-permute-start(bf16[2,272,512]{2,1,0:T(8,128)(2,1)S(1)} %shard_map.37.refs_1_.refs_5_.refs_4_.refs_2_), channel_id=1, source_target_pairs={{32,0},{112,16},{0,32},{80,48},{96,64},{48,80},{64,96},{16,112},{3... | collective-permute-start | bytes 1671176 | tf_op jit(solution)/shard_map/ppermute | solution.py:39
  8.7 2.7 %collective-permute-start.4 = (bf16[2,272,512]{2,1,0:T(8,128)(2,1)S(1)}, bf16[2,272,512]{2,1,0:T(8,128)(2,1)S(1)}, u32[]{:S(2)}, u32[]{:S(2)}) collective-permute-start(bf16[2,272,512]{2,1,0:T(8,128)(2,1)S(1)} %shard_map.37.refs_1_.refs_5_.refs_4_.refs_2_), channel_id=1, source_target_pairs={{4,0},{28,16},{36,32},{60,48},{68,64},{92,80},{100,96},{124,112},{... | collective-permute-start | bytes 1671176 | tf_op jit(solution)/shard_map/ppermute | solution.py:39
  11.5 2.5 %collective-permute-start.3 = (bf16[2,272,512]{2,1,0:T(8,128)(2,1)S(1)}, bf16[2,272,512]{2,1,0:T(8,128)(2,1)S(1)}, u32[]{:S(2)}, u32[]{:S(2)}) collective-permute-start(bf16[2,272,512]{2,1,0:T(8,128)(2,1)S(1)} %shard_map.37.refs_1_.refs_5_.refs_4_.refs_2_), channel_id=1, source_target_pairs={{1,0},{19,16},{33,32},{51,48},{65,64},{83,80},{97,96},{115,112},{5... | collective-permute-start | bytes 1671176 | tf_op jit(solution)/shard_map/ppermute | solution.py:39
  13.9 1.7 %collective-permute-done.5.refs_4_ = bf16[2,272,512]{2,1,0:T(8,128)(2,1)S(1)} collective-permute-done((bf16[2,272,512]{2,1,0:T(8,128)(2,1)S(1)}, bf16[2,272,512]{2,1,0:T(8,128)(2,1)S(1)}, u32[]{:S(2)}, u32[]{:S(2)}) %collective-permute-start.5) | collective-permute-done | bytes 557088 | tf_op jit(solution)/shard_map/ppermute | solution.py:39
  15.7 2.7 %collective-permute-done.4.refs_3_ = bf16[2,272,512]{2,1,0:T(8,128)(2,1)S(1)} collective-permute-done((bf16[2,272,512]{2,1,0:T(8,128)(2,1)S(1)}, bf16[2,272,512]{2,1,0:T(8,128)(2,1)S(1)}, u32[]{:S(2)}, u32[]{:S(2)}) %collective-permute-start.4) | collective-permute-done | bytes 557088 | tf_op jit(solution)/shard_map/ppermute | solution.py:39
  18.4 2.7 %collective-permute-done.3.refs_2_ = bf16[2,272,512]{2,1,0:T(8,128)(2,1)S(1)} collective-permute-done((bf16[2,272,512]{2,1,0:T(8,128)(2,1)S(1)}, bf16[2,272,512]{2,1,0:T(8,128)(2,1)S(1)}, u32[]{:S(2)}, u32[]{:S(2)}) %collective-permute-start.3) | collective-permute-done | bytes 557088 | tf_op jit(solution)/shard_map/ppermute | solution.py:39
  21.1 2.5 %collective-permute-start.8 = (bf16[2,272,512]{2,1,0:T(8,128)(2,1)S(1)}, bf16[2,272,512]{2,1,0:T(8,128)(2,1)}, u32[]{:S(2)}, u32[]{:S(2)}) collective-permute-start(bf16[2,272,512]{2,1,0:T(8,128)(2,1)S(1)} %collective-permute-done.5.refs_4_), channel_id=1, source_target_pairs={{1,0},{19,16},{33,32},{51,48},{65,64},{83,80},{97,96},{115,112},{5... | collective-permute-start | bytes 1671176 | tf_op jit(solution)/shard_map/ppermute | solution.py:39
  23.5 0.1 collective-permute-start.7
  23.6 1.3 %collective-permute-start.6 = (bf16[2,272,512]{2,1,0:T(8,128)(2,1)S(1)}, bf16[2,272,512]{2,1,0:T(8,128)(2,1)}, u32[]{:S(2)}, u32[]{:S(2)}) collective-permute-start(bf16[2,272,512]{2,1,0:T(8,128)(2,1)S(1)} %collective-permute-done.3.refs_2_), channel_id=1, source_target_pairs={{4,0},{28,16},{36,32},{60,48},{68,64},{92,80},{100,96},{124,112},{... | collective-permute-start | bytes 1671176 | tf_op jit(solution)/shard_map/ppermute | solution.py:39
  25.0 0.8 %shard_map.38.refs_8_ = f32[8,1,256]{2,1,0:T(1,128)S(1)} custom-call(s32[1]{0:T(128)} %bitcast.refs_0_, bf16[2,272,512]{2,1,0:T(8,128)(2,1)S(1)} %shard_map.37.refs_1_.refs_5_.refs_4_.refs_2_, bf16[2,272,512]{2,1,0:T(8,128)(2,1)S(1)} %collective-permute-done.3.refs_2_, bf16[2,272,512]{2,1,0:T(8,128)(2,1)S(1)} %collective-permute-done.4.refs_3_, ...), custom_call_target="tpu_custom_call" | custom-call | flops 536870912 | bytes 1000 | tf_op jit(solution)/shard_map/pallas_call | solution.py:144
  25.8 3.1 %shard_map.39.refs_8_ = f32[8,1,256]{2,1,0:T(1,128)S(1)} custom-call(s32[1]{0:T(128)} %bitcast.refs_0_, bf16[2,272,512]{2,1,0:T(8,128)(2,1)S(1)} %shard_map.37.refs_1_.refs_5_.refs_4_.refs_2_, bf16[2,272,512]{2,1,0:T(8,128)(2,1)S(1)} %collective-permute-done.3.refs_2_, bf16[2,272,512]{2,1,0:T(8,128)(2,1)S(1)} %collective-permute-done.4.refs_3_, ...), custom_call_target="tpu_custom_call" | custom-call | flops 1610612736 | bytes 1000 | tf_op jit(solution)/shard_map/pallas_call | solution.py:144
  29.0 1.8 %collective-permute-done.8.refs_3_.refs_7_ = bf16[2,272,512]{2,1,0:T(8,128)(2,1)} collective-permute-done((bf16[2,272,512]{2,1,0:T(8,128)(2,1)S(1)}, bf16[2,272,512]{2,1,0:T(8,128)(2,1)}, u32[]{:S(2)}, u32[]{:S(2)}) %collective-permute-start.8) | collective-permute-done | bytes 557088 | tf_op jit(solution)/shard_map/ppermute | solution.py:39
  30.8 2.5 %collective-permute-done.7.refs_2_.refs_6_ = bf16[2,272,512]{2,1,0:T(8,128)(2,1)} collective-permute-done((bf16[2,272,512]{2,1,0:T(8,128)(2,1)S(1)}, bf16[2,272,512]{2,1,0:T(8,128)(2,1)}, u32[]{:S(2)}, u32[]{:S(2)}) %collective-permute-start.7) | collective-permute-done | bytes 557088 | tf_op jit(solution)/shard_map/ppermute | solution.py:39
  33.2 0.1 collective-permute-done.6.refs_1_.refs_5_
  33.3 0.5 collective-permute-start.15
  33.9 0.0 collective-permute-start.13
  33.9 2.6 %collective-permute-start.12 = (bf16[2,272,512]{2,1,0:T(8,128)(2,1)}, bf16[2,272,512]{2,1,0:T(8,128)(2,1)S(1)}, u32[]{:S(2)}, u32[]{:S(2)}) collective-permute-start(bf16[2,272,512]{2,1,0:T(8,128)(2,1)} %collective-permute-done.6.refs_1_.refs_5_), channel_id=1, source_target_pairs={{32,0},{112,16},{0,32},{80,48},{96,64},{48,80},{64,96},{16,112},{3... | collective-permute-start | bytes 1671176 | tf_op jit(solution)/shard_map/ppermute | solution.py:39
  36.4 3.6 %shard_map.40.refs_11_ = f32[8,1,256]{2,1,0:T(1,128)S(1)} custom-call(s32[1]{0:T(128)} %bitcast.refs_0_, bf16[2,272,512]{2,1,0:T(8,128)(2,1)} %collective-permute-done.6.refs_1_.refs_5_, bf16[2,272,512]{2,1,0:T(8,128)(2,1)} %collective-permute-done.7.refs_2_.refs_6_, bf16[2,272,512]{2,1,0:T(8,128)(2,1)} %collective-permute-done.8.refs_3_.refs_7_, ...), custom_call_target="tpu_custom_call" | custom-call | flops 1610612736 | bytes 1000 | tf_op jit(solution)/shard_map/pallas_call | solution.py:144
  40.1 5.0 %shard_map.41.refs_9_ = f32[8,1,256]{2,1,0:T(1,128)S(1)} custom-call(s32[1]{0:T(128)} %bitcast.refs_0_, bf16[2,272,512]{2,1,0:T(8,128)(2,1)S(1)} %shard_map.37.refs_1_.refs_5_.refs_4_.refs_2_, bf16[2,272,512]{2,1,0:T(8,128)(2,1)S(1)} %collective-permute-done.3.refs_2_, bf16[2,272,512]{2,1,0:T(8,128)(2,1)S(1)} %collective-permute-done.4.refs_3_, ...), custom_call_target="tpu_custom_call" | custom-call | flops 2818572288 | bytes 1000 | tf_op jit(solution)/shard_map/pallas_call | solution.py:144
  45.2 0.1 collective-permute-start.16
  45.3 2.4 %shard_map.42.refs_10_ = f32[8,1,256]{2,1,0:T(1,128)S(1)} custom-call(s32[1]{0:T(128)} %bitcast.refs_0_, bf16[2,272,512]{2,1,0:T(8,128)(2,1)S(1)} %collective-permute-done.12.refs_1_.refs_8_, bf16[2,272,512]{2,1,0:T(8,128)(2,1)S(1)} %shard_map.37.refs_1_.refs_5_.refs_4_.refs_2_, bf16[2,272,512]{2,1,0:T(8,128)(2,1)} %collective-permute-done.9.refs_5_.refs_3_, ...), custom_call_target="tpu_custom_call" | custom-call | flops 939524096 | bytes 1000 | tf_op jit(solution)/shard_map/pallas_call | solution.py:144
  47.7 2.9 %shard_map.43 = f32[8,1,256]{2,1,0:T(1,128)S(1)} custom-call(s32[1]{0:T(128)} %bitcast.refs_0_, bf16[2,272,512]{2,1,0:T(8,128)(2,1)S(1)} %shard_map.37.refs_1_.refs_5_.refs_4_.refs_2_, bf16[2,272,512]{2,1,0:T(8,128)(2,1)S(1)} %collective-permute-done.3.refs_2_, bf16[2,272,512]{2,1,0:T(8,128)(2,1)S(1)} %collective-permute-done.4.refs_3_, ...), custom_call_target="tpu_custom_call" | custom-call | flops 1073741824 | bytes 1000 | tf_op jit(solution)/shard_map/pallas_call | solution.py:144
  50.6 10.8 %all_to_all.5 = f32[8,1,256]{2,1,0:T(1,128)S(1)} all-to-all(f32[8,1,256]{2,1,0:T(1,128)S(1)} %shard_map.43), channel_id=1, replica_groups={{0,1,4,5,32,33,36,37},{16,19,28,31,112,115,124,127},{48,51,60,63,80,83,..., dimensions={0} | all-to-all | bytes 16384 | tf_op jit(solution)/shard_map/all_to_all | solution.py:183
  61.4 0.6 reduce_max.9
  (18 shorter events, 0.0 us)
Async XLA Ops:
  0.0 1.4 %copy-start.1 = (s32[256,1]{0,1:T(1,128)S(1)}, s32[256,1]{0,1:T(1,128)}, u32[]{:S(2)}) copy-start(s32[256,1]{0,1:T(1,128)} %param.4) | copy-start | bytes 3076
  0.0 3.6 %collective-permute-start = (f32[256,512]{1,0:T(8,128)}, f32[256,512]{1,0:T(8,128)S(1)}, u32[]{:S(2)}, u32[]{:S(2)}) collective-permute-start(f32[256,512]{1,0:T(8,128)} %refs_0_.1), channel_id=1, source_target_pairs={{16,0},{0,16},{48,32},{32,48},{80,64},{64,80},{112,96},{96,112},{2... | collective-permute-start | bytes 1572872 | tf_op jit(solution)/shard_map/ppermute | solution.py:44
  1.4 0.7 %copy-start.2 = (s32[256]{0:T(256)S(1)}, s32[256]{0:T(256)}, u32[]{:S(2)}) copy-start(s32[256]{0:T(256)} %param.5) | copy-start | bytes 3076
  1.4 1.5 %collective-permute-start.1 = (s32[1,256]{1,0:T(1,128)S(1)}, s32[1,256]{1,0:T(1,128)S(1)}, u32[]{:S(2)}, u32[]{:S(2)}) collective-permute-start(s32[1,256]{1,0:T(1,128)S(1)} %bitcast.3), channel_id=1, source_target_pairs={{16,0},{0,16},{48,32},{32,48},{80,64},{64,80},{112,96},{96,112},{2... | collective-permute-start | bytes 3080 | tf_op jit(solution)/shard_map/ppermute | solution.py:44
  2.1 1.5 %collective-permute-start.2 = (s32[1,256]{1,0:T(1,128)S(1)}, s32[1,256]{1,0:T(1,128)S(1)}, u32[]{:S(2)}, u32[]{:S(2)}) collective-permute-start(s32[1,256]{1,0:T(1,128)S(1)} %bitcast.5), channel_id=1, source_target_pairs={{16,0},{0,16},{48,32},{32,48},{80,64},{64,80},{112,96},{96,112},{2... | collective-permute-start | bytes 3080 | tf_op jit(solution)/shard_map/ppermute | solution.py:44
  3.6 1.0 %copy-start = (f32[256,512]{1,0:T(8,128)S(1)}, f32[256,512]{1,0:T(8,128)}, u32[]{:S(2)}) copy-start(f32[256,512]{1,0:T(8,128)} %refs_0_.1) | copy-start | bytes 1572868
  4.8 10.8 %collective-permute-start.5 = (bf16[2,272,512]{2,1,0:T(8,128)(2,1)S(1)}, bf16[2,272,512]{2,1,0:T(8,128)(2,1)S(1)}, u32[]{:S(2)}, u32[]{:S(2)}) collective-permute-start(bf16[2,272,512]{2,1,0:T(8,128)(2,1)S(1)} %shard_map.37.refs_1_.refs_5_.refs_4_.refs_2_), channel_id=1, source_target_pairs={{32,0},{112,16},{0,32},{80,48},{96,64},{48,80},{64,96},{16,112},{3... | collective-permute-start | bytes 1671176 | tf_op jit(solution)/shard_map/ppermute | solution.py:39
  8.7 9.7 %collective-permute-start.4 = (bf16[2,272,512]{2,1,0:T(8,128)(2,1)S(1)}, bf16[2,272,512]{2,1,0:T(8,128)(2,1)S(1)}, u32[]{:S(2)}, u32[]{:S(2)}) collective-permute-start(bf16[2,272,512]{2,1,0:T(8,128)(2,1)S(1)} %shard_map.37.refs_1_.refs_5_.refs_4_.refs_2_), channel_id=1, source_target_pairs={{4,0},{28,16},{36,32},{60,48},{68,64},{92,80},{100,96},{124,112},{... | collective-permute-start | bytes 1671176 | tf_op jit(solution)/shard_map/ppermute | solution.py:39
  11.5 9.6 %collective-permute-start.3 = (bf16[2,272,512]{2,1,0:T(8,128)(2,1)S(1)}, bf16[2,272,512]{2,1,0:T(8,128)(2,1)S(1)}, u32[]{:S(2)}, u32[]{:S(2)}) collective-permute-start(bf16[2,272,512]{2,1,0:T(8,128)(2,1)S(1)} %shard_map.37.refs_1_.refs_5_.refs_4_.refs_2_), channel_id=1, source_target_pairs={{1,0},{19,16},{33,32},{51,48},{65,64},{83,80},{97,96},{115,112},{5... | collective-permute-start | bytes 1671176 | tf_op jit(solution)/shard_map/ppermute | solution.py:39
  15.7 8.0 %collective-permute-start.11 = (bf16[2,272,512]{2,1,0:T(8,128)(2,1)S(1)}, bf16[2,272,512]{2,1,0:T(8,128)(2,1)S(1)}, u32[]{:S(2)}, u32[]{:S(2)}) collective-permute-start(bf16[2,272,512]{2,1,0:T(8,128)(2,1)S(1)} %collective-permute-done.5.refs_4_), channel_id=1, source_target_pairs={{16,0},{0,16},{48,32},{32,48},{80,64},{64,80},{112,96},{96,112},{2... | collective-permute-start | bytes 1671176 | tf_op jit(solution)/shard_map/ppermute | solution.py:44
  18.4 7.4 %collective-permute-start.10 = (bf16[2,272,512]{2,1,0:T(8,128)(2,1)S(1)}, bf16[2,272,512]{2,1,0:T(8,128)(2,1)S(1)}, u32[]{:S(2)}, u32[]{:S(2)}) collective-permute-start(bf16[2,272,512]{2,1,0:T(8,128)(2,1)S(1)} %collective-permute-done.4.refs_3_), channel_id=1, source_target_pairs={{16,0},{0,16},{48,32},{32,48},{80,64},{64,80},{112,96},{96,112},{2... | collective-permute-start | bytes 1671176 | tf_op jit(solution)/shard_map/ppermute | solution.py:44
  21.1 4.7 %collective-permute-start.9 = (bf16[2,272,512]{2,1,0:T(8,128)(2,1)S(1)}, bf16[2,272,512]{2,1,0:T(8,128)(2,1)}, u32[]{:S(2)}, u32[]{:S(2)}) collective-permute-start(bf16[2,272,512]{2,1,0:T(8,128)(2,1)S(1)} %collective-permute-done.3.refs_2_), channel_id=1, source_target_pairs={{16,0},{0,16},{48,32},{32,48},{80,64},{64,80},{112,96},{96,112},{2... | collective-permute-start | bytes 1671176 | tf_op jit(solution)/shard_map/ppermute | solution.py:44
  21.1 9.7 %collective-permute-start.8 = (bf16[2,272,512]{2,1,0:T(8,128)(2,1)S(1)}, bf16[2,272,512]{2,1,0:T(8,128)(2,1)}, u32[]{:S(2)}, u32[]{:S(2)}) collective-permute-start(bf16[2,272,512]{2,1,0:T(8,128)(2,1)S(1)} %collective-permute-done.5.refs_4_), channel_id=1, source_target_pairs={{1,0},{19,16},{33,32},{51,48},{65,64},{83,80},{97,96},{115,112},{5... | collective-permute-start | bytes 1671176 | tf_op jit(solution)/shard_map/ppermute | solution.py:39
  23.5 9.7 %collective-permute-start.7 = (bf16[2,272,512]{2,1,0:T(8,128)(2,1)S(1)}, bf16[2,272,512]{2,1,0:T(8,128)(2,1)}, u32[]{:S(2)}, u32[]{:S(2)}) collective-permute-start(bf16[2,272,512]{2,1,0:T(8,128)(2,1)S(1)} %collective-permute-done.4.refs_3_), channel_id=1, source_target_pairs={{32,0},{112,16},{0,32},{80,48},{96,64},{48,80},{64,96},{16,112},{3... | collective-permute-start | bytes 1671176 | tf_op jit(solution)/shard_map/ppermute | solution.py:39
  23.6 9.7 %collective-permute-start.6 = (bf16[2,272,512]{2,1,0:T(8,128)(2,1)S(1)}, bf16[2,272,512]{2,1,0:T(8,128)(2,1)}, u32[]{:S(2)}, u32[]{:S(2)}) collective-permute-start(bf16[2,272,512]{2,1,0:T(8,128)(2,1)S(1)} %collective-permute-done.3.refs_2_), channel_id=1, source_target_pairs={{4,0},{28,16},{36,32},{60,48},{68,64},{92,80},{100,96},{124,112},{... | collective-permute-start | bytes 1671176 | tf_op jit(solution)/shard_map/ppermute | solution.py:39
  33.3 6.8 %collective-permute-start.14 = (bf16[2,272,512]{2,1,0:T(8,128)(2,1)}, bf16[2,272,512]{2,1,0:T(8,128)(2,1)S(1)}, u32[]{:S(2)}, u32[]{:S(2)}) collective-permute-start(bf16[2,272,512]{2,1,0:T(8,128)(2,1)} %collective-permute-done.7.refs_2_.refs_6_), channel_id=1, source_target_pairs={{16,0},{0,16},{48,32},{32,48},{80,64},{64,80},{112,96},{96,112},{2... | collective-permute-start | bytes 1671176 | tf_op jit(solution)/shard_map/ppermute | solution.py:44
  33.3 6.8 %collective-permute-start.15 = (bf16[2,272,512]{2,1,0:T(8,128)(2,1)}, bf16[2,272,512]{2,1,0:T(8,128)(2,1)S(1)}, u32[]{:S(2)}, u32[]{:S(2)}) collective-permute-start(bf16[2,272,512]{2,1,0:T(8,128)(2,1)} %collective-permute-done.8.refs_3_.refs_7_), channel_id=1, source_target_pairs={{16,0},{0,16},{48,32},{32,48},{80,64},{64,80},{112,96},{96,112},{2... | collective-permute-start | bytes 1671176 | tf_op jit(solution)/shard_map/ppermute | solution.py:44
  33.9 6.3 %collective-permute-start.13 = (bf16[2,272,512]{2,1,0:T(8,128)(2,1)}, bf16[2,272,512]{2,1,0:T(8,128)(2,1)S(1)}, u32[]{:S(2)}, u32[]{:S(2)}) collective-permute-start(bf16[2,272,512]{2,1,0:T(8,128)(2,1)} %collective-permute-done.6.refs_1_.refs_5_), channel_id=1, source_target_pairs={{16,0},{0,16},{48,32},{32,48},{80,64},{64,80},{112,96},{96,112},{2... | collective-permute-start | bytes 1671176 | tf_op jit(solution)/shard_map/ppermute | solution.py:44
  33.9 11.3 %collective-permute-start.12 = (bf16[2,272,512]{2,1,0:T(8,128)(2,1)}, bf16[2,272,512]{2,1,0:T(8,128)(2,1)S(1)}, u32[]{:S(2)}, u32[]{:S(2)}) collective-permute-start(bf16[2,272,512]{2,1,0:T(8,128)(2,1)} %collective-permute-done.6.refs_1_.refs_5_), channel_id=1, source_target_pairs={{32,0},{112,16},{0,32},{80,48},{96,64},{48,80},{64,96},{16,112},{3... | collective-permute-start | bytes 1671176 | tf_op jit(solution)/shard_map/ppermute | solution.py:39
  45.2 2.5 %collective-permute-start.16 = (bf16[2,272,512]{2,1,0:T(8,128)(2,1)S(1)}, bf16[2,272,512]{2,1,0:T(8,128)(2,1)S(1)}, u32[]{:S(2)}, u32[]{:S(2)}) collective-permute-start(bf16[2,272,512]{2,1,0:T(8,128)(2,1)S(1)} %collective-permute-done.12.refs_1_.refs_8_), channel_id=1, source_target_pairs={{16,0},{0,16},{48,32},{32,48},{80,64},{64,80},{112,96},{96,112},{2... | collective-permute-start | bytes 1671176 | tf_op jit(solution)/shard_map/ppermute | solution.py:44

commit v4 on v3

--- a/solution.py
+++ b/solution.py
@@ -83,11 +83,17 @@
     )(*halves)
 
 
-def match_kernel(queries, keys, *refs):
-    code_ref = refs[0]
-    mine = dict(zip(queries, refs[1 : 1 + len(queries)]))
-    theirs = dict(zip(keys, refs[1 + len(queries) : 1 + len(queries) + len(keys)]))
-    prev_ref, out_ref, first, second = refs[1 + len(queries) + len(keys) :]
+def cube_code():
+    group, tile = lax.axis_index("group"), lax.axis_index("tile")
+    side = group & 1
+    bits = [(place >> side) & 1 for place in (tile & 3, tile >> 2, group >> 1)]
+    return bits[0] | (bits[1] << 1) | (bits[2] << 2)
+
+
+def match_kernel(queries, keys, begin, *refs):
+    mine = dict(zip(queries, refs[0 : len(queries)]))
+    theirs = dict(zip(keys, refs[len(queries) : len(queries) + len(keys)]))
+    out_ref, first, second = refs[-3:]
 
     def numbers(meta):
         meta = meta.astype(jnp.float32)
@@ -131,55 +137,50 @@
                     valid = row - jnp.concatenate([column, column], axis=1) < limit
                     best = jnp.maximum(best, jnp.where(valid, score[r : r + 8, :], -1.0))
             found[m] = jnp.max(best, axis=0, keepdims=True)
-    code = code_ref[0]
-    out_ref[...] = prev_ref[...]
+    code = cube_code()
+    out_ref[...] = jnp.full(out_ref.shape, -1.0, jnp.float32) if begin else refs[-4][...]
     for m in queries:
         slot = code ^ m
         out_ref[slot] = jnp.maximum(out_ref[slot], found[m])
 
 
-def match(queries, keys, code, mine, theirs, prev):
+def match(queries, keys, mine, theirs, *prev):
     columns = len(queries) if len(queries) < len(keys) else 2 * len(keys)
     vmem = pl.BlockSpec(memory_space=pltpu.VMEM)
     return pl.pallas_call(
-        functools.partial(match_kernel, queries, keys),
+        functools.partial(match_kernel, queries, keys, not prev),
         out_shape=jax.ShapeDtypeStruct((8, 1, ROWS), jnp.float32),
-        in_specs=[pl.BlockSpec(memory_space=pltpu.SMEM)] + [vmem] * (len(queries) + len(keys) + 1),
+        in_specs=[vmem] * (len(queries) + len(keys) + len(prev)),
         out_specs=vmem,
         scratch_shapes=[pltpu.VMEM((columns, ROWS, 128), jnp.int32)] * 2,
         compiler_params=pltpu.CompilerParams(vmem_limit_bytes=GRANT),
         cost_estimate=pl.CostEstimate(
             flops=len(queries) * len(keys) * 2 * ROWS * 2 * ROWS * E, bytes_accessed=1000, transcendentals=0
         ),
-    )(code, *[mine[m] for m in queries], *[theirs[m] for m in keys], prev)
+    )(*[mine[m] for m in queries], *[theirs[m] for m in keys], *prev)
 
 
 def on_device(embeddings, cluster_ids, order_rank):
-    group, tile = lax.axis_index("group"), lax.axis_index("tile")
-    places = (tile % 4, tile // 4, group // 2)
-    code = sum(jnp.where(group % 2 == 0, p % 2, p // 2) << i for i, p in enumerate(places))
-    code = code.astype(jnp.int32).reshape(1)
     half = (embeddings, cluster_ids.reshape(1, ROWS), order_rank.reshape(1, ROWS))
     own = payload(*half, *[swap(part) for part in half])
-    best = jnp.full((8, 1, ROWS), -1.0, jnp.float32)
     mine, theirs = {0: own}, {0: own}
     for m in (1, 2, 4):
         mine[m] = exchange(own, m)
     mine[3] = exchange(mine[1], 2)
     mine[6] = exchange(mine[2], 4)
     mine[5] = exchange(mine[4], 1)
-    best = match((0, 1, 2, 4), (0,), code, mine, theirs, best)
+    best = match((0, 1, 2, 4), (0,), mine, theirs)
     theirs.update({m: swap(mine[m]) for m in (1, 2, 4)})
-    best = match((0, 1, 2, 4), (1, 2, 4), code, mine, theirs, best)
+    best = match((0, 1, 2, 4), (1, 2, 4), mine, theirs, best)
     mine[3], mine[6], mine[5], best = lax.optimization_barrier((mine[3], mine[6], mine[5], best))
     mine[7] = exchange(mine[3], 4)
-    best = match((3, 6, 5), (0, 1, 2, 4), code, mine, theirs, best)
+    best = match((3, 6, 5), (0, 1, 2, 4), mine, theirs, best)
     theirs.update({m: swap(mine[m]) for m in (3, 6, 5)})
-    best = match((0, 1, 2, 4, 3, 6, 5), (3, 6, 5), code, mine, theirs, best)
+    best = match((0, 1, 2, 4, 3, 6, 5), (3, 6, 5), mine, theirs, best)
     mine[7], best = lax.optimization_barrier((mine[7], best))
     theirs[7] = swap(mine[7])
-    best = match((7,), (0, 1, 2, 4, 3, 6, 5), code, mine, theirs, best)
-    best = match((0, 1, 2, 4, 3, 6, 5, 7), (7,), code, mine, theirs, best)
+    best = match((7,), (0, 1, 2, 4, 3, 6, 5), mine, theirs, best)
+    best = match((0, 1, 2, 4, 3, 6, 5, 7), (7,), mine, theirs, best)
     back = lax.all_to_all(best, AXES, split_axis=0, concat_axis=0, axis_index_groups=cube_groups())
     return jnp.max(back, axis=0)[0]
 

time: 62.4 us -> 59.8 us (0.958)
  Pallas kernels: 18.1 us -> 11.2 us
  waiting for transfers between devices: 12.3 us -> 15.1 us
  blocking collectives: 10.8 us -> 12.2 us
    pallas_call x6, Pallas kernels: 18 us -> 11.1 us  [match(): pl.pallas_call(functools.partial(match_kernel, queries, keys, not prev),...]
    ppermute x7, waiting for transfers between devices: 11.5 us -> 14 us  [exchange(): return lax.ppermute(array, AXES, pairs)]
    all_to_all x1, blocking collectives: 10.8 us -> 12.2 us  [on_device(): lax.all_to_all(best, AXES, split_axis=0, concat_axis=0, axis_index_groups...]
  transfers between devices with their start and end apart: 17 -> 17, of which waited for: 8 -> 10; matrix products, arithmetic and copies ran while one was open for 0% -> 0% of each run, Pallas kernels for 24% -> 16%
where the time goes in v4:
time: 59.8 us; the launch traced here: 59.6 us
  starting transfers between devices  19.3 us (32%)
  waiting for transfers between devices  15.1 us (25%)
  blocking collectives  12.2 us (20%)
  Pallas kernels  11.2 us (19%)
  local copies, waits for them, and re-layouts  1.05 us (2%)
    ppermute x7, starting transfers between devices, exchange(): return lax.ppermute(array, AXES, pairs)  15.6 us
    ppermute x7, waiting for transfers between devices, exchange(): return lax.ppermute(array, AXES, pairs)  14 us
    all_to_all x1, blocking collectives, on_device(): lax.all_to_all(best, AXES, split_axis=0, concat_axis=0, axis_index_groups...  12.2 us
    pallas_call x6, Pallas kernels, match(): pl.pallas_call(functools.partial(match_kernel, queries, keys, not prev),...  11.1 us
    ppermute x10, starting transfers between devices, swap(): return lax.ppermute(array, AXES, pairs)  3.74 us
  transfers between devices with their start and end apart: 17, of which 10 were waited for; matrix products, arithmetic and copies ran while one was open for 0% of the time, Pallas kernels for 16%

profile of v4, /device:TPU:1, one launch (start us, length us, event | category | flops | bytes accessed | tf_op | source)
XLA Modules:
  0.0 59.6 jit_solution(9985531699052664708)
XLA Ops:
  0.0 1.4 %collective-permute-start = (f32[256,512]{1,0:T(8,128)}, f32[256,512]{1,0:T(8,128)S(1)}, u32[]{:S(2)}, u32[]{:S(2)}) collective-permute-start(f32[256,512]{1,0:T(8,128)} %refs_0_.1), channel_id=1, source_target_pairs={{16,0},{0,16},{48,32},{32,48},{80,64},{64,80},{112,96},{96,112},{2... | collective-permute-start | bytes 1572872 | tf_op jit(solution)/shard_map/ppermute | solution.py:44
  1.4 0.7 %collective-permute-start.1 = (s32[1,256]{1,0:T(1,128)S(1)}, s32[1,256]{1,0:T(1,128)S(1)}, u32[]{:S(2)}, u32[]{:S(2)}) collective-permute-start(s32[1,256]{1,0:T(1,128)S(1)} %bitcast.2), channel_id=1, source_target_pairs={{16,0},{0,16},{48,32},{32,48},{80,64},{64,80},{112,96},{96,112},{2... | collective-permute-start | bytes 3080 | tf_op jit(solution)/shard_map/ppermute | solution.py:44
  2.1 0.7 %collective-permute-start.2 = (s32[1,256]{1,0:T(1,128)S(1)}, s32[1,256]{1,0:T(1,128)S(1)}, u32[]{:S(2)}, u32[]{:S(2)}) collective-permute-start(s32[1,256]{1,0:T(1,128)S(1)} %bitcast.4), channel_id=1, source_target_pairs={{16,0},{0,16},{48,32},{32,48},{80,64},{64,80},{112,96},{96,112},{2... | collective-permute-start | bytes 3080 | tf_op jit(solution)/shard_map/ppermute | solution.py:44
  2.8 0.2 collective-permute-done.1.refs_4_
  3.0 0.6 %collective-permute-done.2.refs_5_ = s32[1,256]{1,0:T(1,128)S(1)} collective-permute-done((s32[1,256]{1,0:T(1,128)S(1)}, s32[1,256]{1,0:T(1,128)S(1)}, u32[]{:S(2)}, u32[]{:S(2)}) %collective-permute-start.2) | collective-permute-done | bytes 1056 | tf_op jit(solution)/shard_map/ppermute | solution.py:44
  3.6 1.0 %copy-done = f32[256,512]{1,0:T(8,128)S(1)} copy-done((f32[256,512]{1,0:T(8,128)S(1)}, f32[256,512]{1,0:T(8,128)}, u32[]{:S(2)}) %copy-start) | copy-done | bytes 524312
  4.6 0.2 shard_map.37.refs_0_.refs_4_.refs_3_.refs_1_
  4.8 3.9 %collective-permute-start.5 = (bf16[2,272,512]{2,1,0:T(8,128)(2,1)S(1)}, bf16[2,272,512]{2,1,0:T(8,128)(2,1)S(1)}, u32[]{:S(2)}, u32[]{:S(2)}) collective-permute-start(bf16[2,272,512]{2,1,0:T(8,128)(2,1)S(1)} %shard_map.37.refs_0_.refs_4_.refs_3_.refs_1_), channel_id=1, source_target_pairs={{32,0},{112,16},{0,32},{80,48},{96,64},{48,80},{64,96},{16,112},{3... | collective-permute-start | bytes 1671176 | tf_op jit(solution)/shard_map/ppermute | solution.py:39
  8.7 2.7 %collective-permute-start.4 = (bf16[2,272,512]{2,1,0:T(8,128)(2,1)S(1)}, bf16[2,272,512]{2,1,0:T(8,128)(2,1)S(1)}, u32[]{:S(2)}, u32[]{:S(2)}) collective-permute-start(bf16[2,272,512]{2,1,0:T(8,128)(2,1)S(1)} %shard_map.37.refs_0_.refs_4_.refs_3_.refs_1_), channel_id=1, source_target_pairs={{4,0},{28,16},{36,32},{60,48},{68,64},{92,80},{100,96},{124,112},{... | collective-permute-start | bytes 1671176 | tf_op jit(solution)/shard_map/ppermute | solution.py:39
  11.5 2.5 %collective-permute-start.3 = (bf16[2,272,512]{2,1,0:T(8,128)(2,1)S(1)}, bf16[2,272,512]{2,1,0:T(8,128)(2,1)S(1)}, u32[]{:S(2)}, u32[]{:S(2)}) collective-permute-start(bf16[2,272,512]{2,1,0:T(8,128)(2,1)S(1)} %shard_map.37.refs_0_.refs_4_.refs_3_.refs_1_), channel_id=1, source_target_pairs={{1,0},{19,16},{33,32},{51,48},{65,64},{83,80},{97,96},{115,112},{5... | collective-permute-start | bytes 1671176 | tf_op jit(solution)/shard_map/ppermute | solution.py:39
  13.9 1.7 %collective-permute-done.5.refs_3_ = bf16[2,272,512]{2,1,0:T(8,128)(2,1)S(1)} collective-permute-done((bf16[2,272,512]{2,1,0:T(8,128)(2,1)S(1)}, bf16[2,272,512]{2,1,0:T(8,128)(2,1)S(1)}, u32[]{:S(2)}, u32[]{:S(2)}) %collective-permute-start.5) | collective-permute-done | bytes 557088 | tf_op jit(solution)/shard_map/ppermute | solution.py:39
  15.7 2.7 %collective-permute-done.4.refs_2_ = bf16[2,272,512]{2,1,0:T(8,128)(2,1)S(1)} collective-permute-done((bf16[2,272,512]{2,1,0:T(8,128)(2,1)S(1)}, bf16[2,272,512]{2,1,0:T(8,128)(2,1)S(1)}, u32[]{:S(2)}, u32[]{:S(2)}) %collective-permute-start.4) | collective-permute-done | bytes 557088 | tf_op jit(solution)/shard_map/ppermute | solution.py:39
  18.4 2.7 %collective-permute-done.3.refs_1_ = bf16[2,272,512]{2,1,0:T(8,128)(2,1)S(1)} collective-permute-done((bf16[2,272,512]{2,1,0:T(8,128)(2,1)S(1)}, bf16[2,272,512]{2,1,0:T(8,128)(2,1)S(1)}, u32[]{:S(2)}, u32[]{:S(2)}) %collective-permute-start.3) | collective-permute-done | bytes 557088 | tf_op jit(solution)/shard_map/ppermute | solution.py:39
  21.1 2.5 %collective-permute-start.8 = (bf16[2,272,512]{2,1,0:T(8,128)(2,1)S(1)}, bf16[2,272,512]{2,1,0:T(8,128)(2,1)S(1)}, u32[]{:S(2)}, u32[]{:S(2)}) collective-permute-start(bf16[2,272,512]{2,1,0:T(8,128)(2,1)S(1)} %collective-permute-done.5.refs_3_), channel_id=1, source_target_pairs={{1,0},{19,16},{33,32},{51,48},{65,64},{83,80},{97,96},{115,112},{5... | collective-permute-start | bytes 1671176 | tf_op jit(solution)/shard_map/ppermute | solution.py:39
  23.5 0.1 collective-permute-start.7
  23.6 1.3 %collective-permute-start.6 = (bf16[2,272,512]{2,1,0:T(8,128)(2,1)S(1)}, bf16[2,272,512]{2,1,0:T(8,128)(2,1)S(1)}, u32[]{:S(2)}, u32[]{:S(2)}) collective-permute-start(bf16[2,272,512]{2,1,0:T(8,128)(2,1)S(1)} %collective-permute-done.3.refs_1_), channel_id=1, source_target_pairs={{4,0},{28,16},{36,32},{60,48},{68,64},{92,80},{100,96},{124,112},{... | collective-permute-start | bytes 1671176 | tf_op jit(solution)/shard_map/ppermute | solution.py:39
  25.0 0.8 %shard_map.38.refs_7_ = f32[8,1,256]{2,1,0:T(1,128)S(1)} custom-call(bf16[2,272,512]{2,1,0:T(8,128)(2,1)S(1)} %shard_map.37.refs_0_.refs_4_.refs_3_.refs_1_, bf16[2,272,512]{2,1,0:T(8,128)(2,1)S(1)} %collective-permute-done.3.refs_1_, bf16[2,272,512]{2,1,0:T(8,128)(2,1)S(1)} %collective-permute-done.4.refs_2_, ...), custom_call_target="tpu_custom_call" | custom-call | flops 536870912 | bytes 1000 | tf_op jit(solution)/shard_map/pallas_call | solution.py:150
  25.8 2.1 %shard_map.39.refs_7_ = f32[8,1,256]{2,1,0:T(1,128)S(1)} custom-call(bf16[2,272,512]{2,1,0:T(8,128)(2,1)S(1)} %shard_map.37.refs_0_.refs_4_.refs_3_.refs_1_, bf16[2,272,512]{2,1,0:T(8,128)(2,1)S(1)} %collective-permute-done.3.refs_1_, bf16[2,272,512]{2,1,0:T(8,128)(2,1)S(1)} %collective-permute-done.4.refs_2_, ...), custom_call_target="tpu_custom_call" | custom-call | flops 1610612736 | bytes 1000 | tf_op jit(solution)/shard_map/pallas_call | solution.py:150
  27.9 2.8 %collective-permute-done.8.refs_2_.refs_6_ = bf16[2,272,512]{2,1,0:T(8,128)(2,1)S(1)} collective-permute-done((bf16[2,272,512]{2,1,0:T(8,128)(2,1)S(1)}, bf16[2,272,512]{2,1,0:T(8,128)(2,1)S(1)}, u32[]{:S(2)}, u32[]{:S(2)}) %collective-permute-start.8) | collective-permute-done | bytes 557088 | tf_op jit(solution)/shard_map/ppermute | solution.py:39
  30.7 2.5 %collective-permute-done.7.refs_1_.refs_5_ = bf16[2,272,512]{2,1,0:T(8,128)(2,1)S(1)} collective-permute-done((bf16[2,272,512]{2,1,0:T(8,128)(2,1)S(1)}, bf16[2,272,512]{2,1,0:T(8,128)(2,1)S(1)}, u32[]{:S(2)}, u32[]{:S(2)}) %collective-permute-start.7) | collective-permute-done | bytes 557088 | tf_op jit(solution)/shard_map/ppermute | solution.py:39
  33.1 0.1 collective-permute-done.6.refs_0_.refs_4_
  33.2 0.5 collective-permute-start.15
  33.8 2.6 %collective-permute-start.12 = (bf16[2,272,512]{2,1,0:T(8,128)(2,1)S(1)}, bf16[2,272,512]{2,1,0:T(8,128)(2,1)S(1)}, u32[]{:S(2)}, u32[]{:S(2)}) collective-permute-start(bf16[2,272,512]{2,1,0:T(8,128)(2,1)S(1)} %collective-permute-done.6.refs_0_.refs_4_), channel_id=1, source_target_pairs={{32,0},{112,16},{0,32},{80,48},{96,64},{48,80},{64,96},{16,112},{3... | collective-permute-start | bytes 1671176 | tf_op jit(solution)/shard_map/ppermute | solution.py:39
  36.3 2.1 %shard_map.40.refs_10_ = f32[8,1,256]{2,1,0:T(1,128)S(1)} custom-call(bf16[2,272,512]{2,1,0:T(8,128)(2,1)S(1)} %collective-permute-done.6.refs_0_.refs_4_, bf16[2,272,512]{2,1,0:T(8,128)(2,1)S(1)} %collective-permute-done.7.refs_1_.refs_5_, bf16[2,272,512]{2,1,0:T(8,128)(2,1)S(1)} %collective-permute-done.8.refs_2_.refs_6_, ...), custom_call_target="tpu_custom_call" | custom-call | flops 1610612736 | bytes 1000 | tf_op jit(solution)/shard_map/pallas_call | solution.py:150
  38.5 3.4 %shard_map.41.refs_8_ = f32[8,1,256]{2,1,0:T(1,128)S(1)} custom-call(bf16[2,272,512]{2,1,0:T(8,128)(2,1)S(1)} %shard_map.37.refs_0_.refs_4_.refs_3_.refs_1_, bf16[2,272,512]{2,1,0:T(8,128)(2,1)S(1)} %collective-permute-done.3.refs_1_, bf16[2,272,512]{2,1,0:T(8,128)(2,1)S(1)} %collective-permute-done.4.refs_2_, ...), custom_call_target="tpu_custom_call" | custom-call | flops 2818572288 | bytes 1000 | tf_op jit(solution)/shard_map/pallas_call | solution.py:150
  41.8 1.5 %collective-permute-done.12.refs_0_.refs_7_ = bf16[2,272,512]{2,1,0:T(8,128)(2,1)S(1)} collective-permute-done((bf16[2,272,512]{2,1,0:T(8,128)(2,1)S(1)}, bf16[2,272,512]{2,1,0:T(8,128)(2,1)S(1)}, u32[]{:S(2)}, u32[]{:S(2)}) %collective-permute-start.12) | collective-permute-done | bytes 557088 | tf_op jit(solution)/shard_map/ppermute | solution.py:39
  43.3 0.4 collective-permute-start.16
  43.8 1.3 %shard_map.42.refs_9_ = f32[8,1,256]{2,1,0:T(1,128)S(1)} custom-call(bf16[2,272,512]{2,1,0:T(8,128)(2,1)S(1)} %collective-permute-done.12.refs_0_.refs_7_, bf16[2,272,512]{2,1,0:T(8,128)(2,1)S(1)} %shard_map.37.refs_0_.refs_4_.refs_3_.refs_1_, bf16[2,272,512]{2,1,0:T(8,128)(2,1)S(1)} %collective-permute-done.9.refs_4_.refs_2_, ...), custom_call_target="tpu_custom_call" | custom-call | flops 939524096 | bytes 1000 | tf_op jit(solution)/shard_map/pallas_call | solution.py:150
  45.1 0.3 collective-permute-done.16.refs_8_
  45.4 1.4 %shard_map.43 = f32[8,1,256]{2,1,0:T(1,128)S(1)} custom-call(bf16[2,272,512]{2,1,0:T(8,128)(2,1)S(1)} %shard_map.37.refs_0_.refs_4_.refs_3_.refs_1_, bf16[2,272,512]{2,1,0:T(8,128)(2,1)S(1)} %collective-permute-done.3.refs_1_, bf16[2,272,512]{2,1,0:T(8,128)(2,1)S(1)} %collective-permute-done.4.refs_2_, ...), custom_call_target="tpu_custom_call" | custom-call | flops 1073741824 | bytes 1000 | tf_op jit(solution)/shard_map/pallas_call | solution.py:150
  46.8 12.2 %all_to_all.5 = f32[8,1,256]{2,1,0:T(1,128)S(1)} all-to-all(f32[8,1,256]{2,1,0:T(1,128)S(1)} %shard_map.43), channel_id=1, replica_groups={{0,1,4,5,32,33,36,37},{16,19,28,31,112,115,124,127},{48,51,60,63,80,83,..., dimensions={0} | all-to-all | bytes 16384 | tf_op jit(solution)/shard_map/all_to_all | solution.py:184
  59.0 0.6 reduce_max.9
  (17 shorter events, 0.0 us)
Async XLA Ops:
  0.0 1.4 %copy-start.1 = (s32[256,1]{0,1:T(1,128)S(1)}, s32[256,1]{0,1:T(1,128)}, u32[]{:S(2)}) copy-start(s32[256,1]{0,1:T(1,128)} %param.4) | copy-start | bytes 3076
  0.0 3.6 %collective-permute-start = (f32[256,512]{1,0:T(8,128)}, f32[256,512]{1,0:T(8,128)S(1)}, u32[]{:S(2)}, u32[]{:S(2)}) collective-permute-start(f32[256,512]{1,0:T(8,128)} %refs_0_.1), channel_id=1, source_target_pairs={{16,0},{0,16},{48,32},{32,48},{80,64},{64,80},{112,96},{96,112},{2... | collective-permute-start | bytes 1572872 | tf_op jit(solution)/shard_map/ppermute | solution.py:44
  1.4 0.7 %copy-start.2 = (s32[256]{0:T(256)S(1)}, s32[256]{0:T(256)}, u32[]{:S(2)}) copy-start(s32[256]{0:T(256)} %param.5) | copy-start | bytes 3076
  1.4 1.5 %collective-permute-start.1 = (s32[1,256]{1,0:T(1,128)S(1)}, s32[1,256]{1,0:T(1,128)S(1)}, u32[]{:S(2)}, u32[]{:S(2)}) collective-permute-start(s32[1,256]{1,0:T(1,128)S(1)} %bitcast.2), channel_id=1, source_target_pairs={{16,0},{0,16},{48,32},{32,48},{80,64},{64,80},{112,96},{96,112},{2... | collective-permute-start | bytes 3080 | tf_op jit(solution)/shard_map/ppermute | solution.py:44
  2.1 1.5 %collective-permute-start.2 = (s32[1,256]{1,0:T(1,128)S(1)}, s32[1,256]{1,0:T(1,128)S(1)}, u32[]{:S(2)}, u32[]{:S(2)}) collective-permute-start(s32[1,256]{1,0:T(1,128)S(1)} %bitcast.4), channel_id=1, source_target_pairs={{16,0},{0,16},{48,32},{32,48},{80,64},{64,80},{112,96},{96,112},{2... | collective-permute-start | bytes 3080 | tf_op jit(solution)/shard_map/ppermute | solution.py:44
  3.6 1.0 %copy-start = (f32[256,512]{1,0:T(8,128)S(1)}, f32[256,512]{1,0:T(8,128)}, u32[]{:S(2)}) copy-start(f32[256,512]{1,0:T(8,128)} %refs_0_.1) | copy-start | bytes 1572868
  4.8 10.8 %collective-permute-start.5 = (bf16[2,272,512]{2,1,0:T(8,128)(2,1)S(1)}, bf16[2,272,512]{2,1,0:T(8,128)(2,1)S(1)}, u32[]{:S(2)}, u32[]{:S(2)}) collective-permute-start(bf16[2,272,512]{2,1,0:T(8,128)(2,1)S(1)} %shard_map.37.refs_0_.refs_4_.refs_3_.refs_1_), channel_id=1, source_target_pairs={{32,0},{112,16},{0,32},{80,48},{96,64},{48,80},{64,96},{16,112},{3... | collective-permute-start | bytes 1671176 | tf_op jit(solution)/shard_map/ppermute | solution.py:39
  8.7 9.7 %collective-permute-start.4 = (bf16[2,272,512]{2,1,0:T(8,128)(2,1)S(1)}, bf16[2,272,512]{2,1,0:T(8,128)(2,1)S(1)}, u32[]{:S(2)}, u32[]{:S(2)}) collective-permute-start(bf16[2,272,512]{2,1,0:T(8,128)(2,1)S(1)} %shard_map.37.refs_0_.refs_4_.refs_3_.refs_1_), channel_id=1, source_target_pairs={{4,0},{28,16},{36,32},{60,48},{68,64},{92,80},{100,96},{124,112},{... | collective-permute-start | bytes 1671176 | tf_op jit(solution)/shard_map/ppermute | solution.py:39
  11.5 9.6 %collective-permute-start.3 = (bf16[2,272,512]{2,1,0:T(8,128)(2,1)S(1)}, bf16[2,272,512]{2,1,0:T(8,128)(2,1)S(1)}, u32[]{:S(2)}, u32[]{:S(2)}) collective-permute-start(bf16[2,272,512]{2,1,0:T(8,128)(2,1)S(1)} %shard_map.37.refs_0_.refs_4_.refs_3_.refs_1_), channel_id=1, source_target_pairs={{1,0},{19,16},{33,32},{51,48},{65,64},{83,80},{97,96},{115,112},{5... | collective-permute-start | bytes 1671176 | tf_op jit(solution)/shard_map/ppermute | solution.py:39
  15.7 8.0 %collective-permute-start.11 = (bf16[2,272,512]{2,1,0:T(8,128)(2,1)S(1)}, bf16[2,272,512]{2,1,0:T(8,128)(2,1)S(1)}, u32[]{:S(2)}, u32[]{:S(2)}) collective-permute-start(bf16[2,272,512]{2,1,0:T(8,128)(2,1)S(1)} %collective-permute-done.5.refs_3_), channel_id=1, source_target_pairs={{16,0},{0,16},{48,32},{32,48},{80,64},{64,80},{112,96},{96,112},{2... | collective-permute-start | bytes 1671176 | tf_op jit(solution)/shard_map/ppermute | solution.py:44
  18.4 7.4 %collective-permute-start.10 = (bf16[2,272,512]{2,1,0:T(8,128)(2,1)S(1)}, bf16[2,272,512]{2,1,0:T(8,128)(2,1)S(1)}, u32[]{:S(2)}, u32[]{:S(2)}) collective-permute-start(bf16[2,272,512]{2,1,0:T(8,128)(2,1)S(1)} %collective-permute-done.4.refs_2_), channel_id=1, source_target_pairs={{16,0},{0,16},{48,32},{32,48},{80,64},{64,80},{112,96},{96,112},{2... | collective-permute-start | bytes 1671176 | tf_op jit(solution)/shard_map/ppermute | solution.py:44
  21.1 4.7 %collective-permute-start.9 = (bf16[2,272,512]{2,1,0:T(8,128)(2,1)S(1)}, bf16[2,272,512]{2,1,0:T(8,128)(2,1)S(1)}, u32[]{:S(2)}, u32[]{:S(2)}) collective-permute-start(bf16[2,272,512]{2,1,0:T(8,128)(2,1)S(1)} %collective-permute-done.3.refs_1_), channel_id=1, source_target_pairs={{16,0},{0,16},{48,32},{32,48},{80,64},{64,80},{112,96},{96,112},{2... | collective-permute-start | bytes 1671176 | tf_op jit(solution)/shard_map/ppermute | solution.py:44
  21.1 9.6 %collective-permute-start.8 = (bf16[2,272,512]{2,1,0:T(8,128)(2,1)S(1)}, bf16[2,272,512]{2,1,0:T(8,128)(2,1)S(1)}, u32[]{:S(2)}, u32[]{:S(2)}) collective-permute-start(bf16[2,272,512]{2,1,0:T(8,128)(2,1)S(1)} %collective-permute-done.5.refs_3_), channel_id=1, source_target_pairs={{1,0},{19,16},{33,32},{51,48},{65,64},{83,80},{97,96},{115,112},{5... | collective-permute-start | bytes 1671176 | tf_op jit(solution)/shard_map/ppermute | solution.py:39
  23.5 9.6 %collective-permute-start.7 = (bf16[2,272,512]{2,1,0:T(8,128)(2,1)S(1)}, bf16[2,272,512]{2,1,0:T(8,128)(2,1)S(1)}, u32[]{:S(2)}, u32[]{:S(2)}) collective-permute-start(bf16[2,272,512]{2,1,0:T(8,128)(2,1)S(1)} %collective-permute-done.4.refs_2_), channel_id=1, source_target_pairs={{32,0},{112,16},{0,32},{80,48},{96,64},{48,80},{64,96},{16,112},{3... | collective-permute-start | bytes 1671176 | tf_op jit(solution)/shard_map/ppermute | solution.py:39
  23.6 9.6 %collective-permute-start.6 = (bf16[2,272,512]{2,1,0:T(8,128)(2,1)S(1)}, bf16[2,272,512]{2,1,0:T(8,128)(2,1)S(1)}, u32[]{:S(2)}, u32[]{:S(2)}) collective-permute-start(bf16[2,272,512]{2,1,0:T(8,128)(2,1)S(1)} %collective-permute-done.3.refs_1_), channel_id=1, source_target_pairs={{4,0},{28,16},{36,32},{60,48},{68,64},{92,80},{100,96},{124,112},{... | collective-permute-start | bytes 1671176 | tf_op jit(solution)/shard_map/ppermute | solution.py:39
  33.2 5.2 %collective-permute-start.14 = (bf16[2,272,512]{2,1,0:T(8,128)(2,1)S(1)}, bf16[2,272,512]{2,1,0:T(8,128)(2,1)S(1)}, u32[]{:S(2)}, u32[]{:S(2)}) collective-permute-start(bf16[2,272,512]{2,1,0:T(8,128)(2,1)S(1)} %collective-permute-done.7.refs_1_.refs_5_), channel_id=1, source_target_pairs={{16,0},{0,16},{48,32},{32,48},{80,64},{64,80},{112,96},{96,112},{2... | collective-permute-start | bytes 1671176 | tf_op jit(solution)/shard_map/ppermute | solution.py:44
  33.2 5.2 %collective-permute-start.15 = (bf16[2,272,512]{2,1,0:T(8,128)(2,1)S(1)}, bf16[2,272,512]{2,1,0:T(8,128)(2,1)S(1)}, u32[]{:S(2)}, u32[]{:S(2)}) collective-permute-start(bf16[2,272,512]{2,1,0:T(8,128)(2,1)S(1)} %collective-permute-done.8.refs_2_.refs_6_), channel_id=1, source_target_pairs={{16,0},{0,16},{48,32},{32,48},{80,64},{64,80},{112,96},{96,112},{2... | collective-permute-start | bytes 1671176 | tf_op jit(solution)/shard_map/ppermute | solution.py:44
  33.7 4.7 %collective-permute-start.13 = (bf16[2,272,512]{2,1,0:T(8,128)(2,1)S(1)}, bf16[2,272,512]{2,1,0:T(8,128)(2,1)S(1)}, u32[]{:S(2)}, u32[]{:S(2)}) collective-permute-start(bf16[2,272,512]{2,1,0:T(8,128)(2,1)S(1)} %collective-permute-done.6.refs_0_.refs_4_), channel_id=1, source_target_pairs={{16,0},{0,16},{48,32},{32,48},{80,64},{64,80},{112,96},{96,112},{2... | collective-permute-start | bytes 1671176 | tf_op jit(solution)/shard_map/ppermute | solution.py:44
  33.8 9.6 %collective-permute-start.12 = (bf16[2,272,512]{2,1,0:T(8,128)(2,1)S(1)}, bf16[2,272,512]{2,1,0:T(8,128)(2,1)S(1)}, u32[]{:S(2)}, u32[]{:S(2)}) collective-permute-start(bf16[2,272,512]{2,1,0:T(8,128)(2,1)S(1)} %collective-permute-done.6.refs_0_.refs_4_), channel_id=1, source_target_pairs={{32,0},{112,16},{0,32},{80,48},{96,64},{48,80},{64,96},{16,112},{3... | collective-permute-start | bytes 1671176 | tf_op jit(solution)/shard_map/ppermute | solution.py:39
  43.3 2.0 %collective-permute-start.16 = (bf16[2,272,512]{2,1,0:T(8,128)(2,1)S(1)}, bf16[2,272,512]{2,1,0:T(8,128)(2,1)S(1)}, u32[]{:S(2)}, u32[]{:S(2)}) collective-permute-start(bf16[2,272,512]{2,1,0:T(8,128)(2,1)S(1)} %collective-permute-done.12.refs_0_.refs_7_), channel_id=1, source_target_pairs={{16,0},{0,16},{48,32},{32,48},{80,64},{64,80},{112,96},{96,112},{2... | collective-permute-start | bytes 1671176 | tf_op jit(solution)/shard_map/ppermute | solution.py:44

commit v5 on v4

v5 whole, which is shorter than its diff:
```python
import functools

import jax
import jax.numpy as jnp
from jax import lax
from jax.experimental import pallas as pl
from jax.experimental.pallas import tpu as pltpu
from jax.sharding import PartitionSpec as P

AXES = ("group", "tile")
ROWS = 256
META = 16
PAY = ROWS + META
E = 512
LOW = -(2**31)
GRANT = 12 * 2**20
SMALL = pl.CostEstimate(flops=1000, bytes_accessed=1000, transcendentals=0)
NEAR = (1, 0, 3, 2)
OTHER = (3, 2, 1, 0)
PLACES = [(x, y, z, c) for x in range(4) for y in range(4) for z in range(4) for c in range(2)]


def linear(x, y, z, c):
    return (z * 2 + c) * 16 + y * 4 + x


def across(place, mask):
    x, y, z, c = place
    step = OTHER if c else NEAR
    return (
        step[x] if mask & 1 else x,
        step[y] if mask & 2 else y,
        step[z] if mask & 4 else z,
        c,
    )


def exchange(array, mask):
    pairs = [(linear(*across(q, mask)), linear(*q)) for q in PLACES]
    return lax.ppermute(array, AXES, pairs)


def swap(array):
    pairs = [(linear(x, y, z, 1 - c), linear(x, y, z, c)) for x, y, z, c in PLACES]
    return lax.ppermute(array, AXES, pairs)


def cube_groups():
    groups = []
    for place in PLACES:
        starts = (0, 1) if place[3] else (0, 2)
        if all(p in starts for p in place[:3]):
            groups.append([linear(*across(place, k)) for k in range(8)])
    return groups


def unit_kernel(emb_hbm, cluster_hbm, rank_hbm, out_ref, emb_ref, cluster_ref, rank_ref, sem):
    sources = (cluster_hbm, rank_hbm, emb_hbm)
    targets = (cluster_ref, rank_ref, emb_ref)
    copies = [pltpu.make_async_copy(a, b, sem.at[i]) for i, (a, b) in enumerate(zip(sources, targets))]
    for copy in copies:
        copy.start()
    for copy in copies:
        copy.wait()
    emb = emb_ref[...]
    sums = jnp.sum(emb * emb, axis=1, keepdims=True)
    out_ref[0:ROWS, :] = (emb * lax.rsqrt(sums + 1e-06)).astype(jnp.bfloat16)
    rank = rank_ref[...]
    high = (rank >> 8).astype(jnp.float32)
    low = (rank & 255).astype(jnp.float32)
    cluster = cluster_ref[...].astype(jnp.float32)
    first = jnp.concatenate([high, low], axis=1)
    second = jnp.concatenate([cluster, jnp.zeros_like(cluster)], axis=1)
    row = lax.broadcasted_iota(jnp.int32, (META, E), 0)
    meta = jnp.where(row == 0, first, jnp.where(row == 1, second, 0.0))
    out_ref[ROWS:PAY, :] = meta.astype(jnp.bfloat16)


def payload(embeddings, cluster_ids, order_rank):
    anywhere = pl.BlockSpec(memory_space=pl.ANY)
    return pl.pallas_call(
        unit_kernel,
        out_shape=jax.ShapeDtypeStruct((PAY, E), jnp.bfloat16),
        in_specs=[anywhere] * 3,
        out_specs=pl.BlockSpec(memory_space=pltpu.VMEM),
        scratch_shapes=[
            pltpu.VMEM((ROWS, E), jnp.float32),
            pltpu.VMEM((1, ROWS), jnp.int32),
            pltpu.VMEM((1, ROWS), jnp.int32),
            pltpu.SemaphoreType.DMA((3,)),
        ],
        compiler_params=pltpu.CompilerParams(vmem_limit_bytes=GRANT),
        cost_estimate=SMALL,
    )(embeddings, cluster_ids.reshape(1, ROWS), order_rank.reshape(1, ROWS))


def join_kernel(first_ref, second_ref, out_ref):
    out_ref[0] = first_ref[...]
    out_ref[1] = second_ref[...]


def join(first, second):
    vmem = pl.BlockSpec(memory_space=pltpu.VMEM)
    return pl.pallas_call(
        join_kernel,
        out_shape=jax.ShapeDtypeStruct((2, PAY, E), jnp.bfloat16),
        in_specs=[vmem] * 2,
        out_specs=vmem,
        compiler_params=pltpu.CompilerParams(vmem_limit_bytes=GRANT),
        cost_estimate=SMALL,
    )(first, second)


def pack_kernel(*refs):
    half = len(refs) // 2
    for source, out in zip(refs[:half], refs[half:]):
        out[0:ROWS, :] = source[0, 0:ROWS, :]
        out[ROWS : 2 * ROWS, :] = source[1, 0:ROWS, :]
        one = source[0, ROWS:PAY, :].astype(jnp.float32)
        two = source[1, ROWS:PAY, :].astype(jnp.float32)
        both = jnp.concatenate([one[0:2], two[0:2], jnp.zeros((META - 4, E), jnp.float32)], axis=0)
        out[2 * ROWS : 2 * ROWS + META, :] = both.astype(jnp.bfloat16)


def pack(*blocks):
    vmem = pl.BlockSpec(memory_space=pltpu.VMEM)
    return pl.pallas_call(
        pack_kernel,
        out_shape=[jax.ShapeDtypeStruct((2 * ROWS + META, E), jnp.bfloat16)] * len(blocks),
        in_specs=[vmem] * len(blocks),
        out_specs=[vmem] * len(blocks),
        compiler_params=pltpu.CompilerParams(vmem_limit_bytes=GRANT),
        cost_estimate=SMALL,
    )(*blocks)


def cube_code():
    group, tile = lax.axis_index("group"), lax.axis_index("tile")
    side = group & 1
    bits = [(place >> side) & 1 for place in (tile & 3, tile >> 2, group >> 1)]
    return bits[0] | (bits[1] << 1) | (bits[2] << 2)


def match_kernel(queries, keys, masks, begin, *refs):
    mine = dict(zip(masks, refs[0 : len(masks)]))
    others = [n for n in keys if n]
    theirs = dict(zip(others, refs[len(masks) : len(masks) + len(others)]))
    out_ref, first, second = refs[-3:]

    def numbers(meta, at):
        rank = meta[at : at + 1, 0:ROWS] * 256.0 + meta[at : at + 1, ROWS : 2 * ROWS]
        return rank, meta[at + 1 : at + 2, 0:ROWS] * 32768.0 + rank

    def columns(row):
        return jnp.broadcast_to(jnp.transpose(jnp.broadcast_to(row, (8, ROWS)))[:, 0:1], (ROWS, 128)).astype(jnp.int32)

    def product(left, right):
        return lax.dot_general(left, right, (((1,), (1,)), ((), ())), preferred_element_type=jnp.float32)

    def ask(m):
        return mine[m][0, 0:ROWS, :]

    def give(n, h):
        return theirs[n][h * ROWS : h * ROWS + ROWS, :] if n else mine[0][h, 0:ROWS, :]

    def given(n, h):
        meta = theirs[n][2 * ROWS : 2 * ROWS + META, :] if n else mine[0][h, ROWS:PAY, :]
        return numbers(meta.astype(jnp.float32), 2 * h if n else 0)[1]

    found = {}
    sides = [(n, h) for n in keys for h in range(2)]
    limits = {m: numbers(mine[m][0, ROWS:PAY, :].astype(jnp.float32), 0) for m in queries}
    wanted = {side: given(*side) for side in sides}
    if len(queries) < len(keys):
        for i, m in enumerate(queries):
            first[i] = columns(limits[m][1])
            second[i] = columns(limits[m][0]) + LOW
        rows = {side: wanted[side].astype(jnp.int32) + (LOW + 1) for side in sides}
        for i, m in enumerate(queries):
            best = jnp.full((ROWS, 128), -1.0, jnp.float32)
            for side in sides:
                score = product(ask(m), give(*side))
                for lanes in (slice(0, 128), slice(128, 256)):
                    valid = first[i] - rows[side][:, lanes] < second[i]
                    best = jnp.maximum(best, jnp.where(valid, score[:, lanes], -1.0))
            found[m] = jnp.max(jnp.transpose(best), axis=0, keepdims=True)
    else:
        for i, side in enumerate(sides):
            first[i] = columns(wanted[side]) + (LOW + 1)
        for m in queries:
            row = jnp.broadcast_to(limits[m][1].astype(jnp.int32), (8, ROWS))
            limit = jnp.broadcast_to(limits[m][0].astype(jnp.int32) + LOW, (8, ROWS))
            best = jnp.full((8, ROWS), -1.0, jnp.float32)
            for i, side in enumerate(sides):
                score = product(give(*side), ask(m))
                for r in range(0, ROWS, 8):
                    column = first[i, r : r + 8, :]
                    valid = row - jnp.concatenate([column, column], axis=1) < limit
                    best = jnp.maximum(best, jnp.where(valid, score[r : r + 8, :], -1.0))
            found[m] = jnp.max(best, axis=0, keepdims=True)
    code = cube_code()
    out_ref[...] = jnp.full(out_ref.shape, -1.0, jnp.float32) if begin else refs[-4][...]
    for m in queries:
        slot = code ^ m
        out_ref[slot] = jnp.maximum(out_ref[slot], found[m])


def match(queries, keys, mine, theirs, *prev):
    masks = sorted(set(queries) | ({0} & set(keys)))
    others = [n for n in keys if n]
    columns = len(queries) if len(queries) < len(keys) else 2 * len(keys)
    vmem = pl.BlockSpec(memory_space=pltpu.VMEM)
    return pl.pallas_call(
        functools.partial(match_kernel, queries, keys, masks, not prev),
        out_shape=jax.ShapeDtypeStruct((8, 1, ROWS), jnp.float32),
        in_specs=[vmem] * (len(masks) + len(others) + len(prev)),
        out_specs=vmem,
        scratch_shapes=[pltpu.VMEM((columns, ROWS, 128), jnp.int32)] * 2,
        compiler_params=pltpu.CompilerParams(vmem_limit_bytes=GRANT),
        cost_estimate=SMALL,
    )(*[mine[m] for m in masks], *[theirs[n] for n in others], *prev)


def on_device(embeddings, cluster_ids, order_rank):
    unit = payload(embeddings, cluster_ids, order_rank)
    mine, theirs = {0: join(unit, swap(unit))}, {}
    near, far = (0, 1, 2, 4), (3, 6, 5)
    for m in (1, 2, 4):
        mine[m] = exchange(mine[0], m)
    mine[3] = exchange(mine[1], 2)
    mine[6] = exchange(mine[2], 4)
    mine[5] = exchange(mine[4], 1)
    theirs.update({m: swap(pack(mine[m])[0]) for m in (1, 2, 4)})
    best = match(near, near, mine, theirs)
    best, mine[3] = lax.optimization_barrier((best, mine[3]))
    mine[7] = exchange(mine[3], 4)
    theirs.update({m: swap(pack(mine[m])[0]) for m in far})
    best = match(far, near, mine, theirs, best)
    best = match((*near, *far), far, mine, theirs, best)
    best, mine[7] = lax.optimization_barrier((best, mine[7]))
    theirs[7] = swap(pack(mine[7])[0])
    best = match((7,), (*near, *far), mine, theirs, best)
    best = match((*near, *far, 7), (7,), mine, theirs, best)
    back = lax.all_to_all(best, AXES, split_axis=0, concat_axis=0, axis_index_groups=cube_groups())
    return jnp.max(back, axis=0)[0]


def solution(mesh):
    return jax.shard_map(
        on_device,
        mesh=mesh,
        in_specs=(P(AXES, None), P(AXES, None), P(AXES)),
        out_specs=P(AXES),
        check_vma=False,
    )
```

time: 59.8 us -> 56.1 us (0.938)
  waiting for transfers between devices: 15.1 us -> 10.8 us
  local copies, waits for them, and re-layouts: 1.05 us -> 1.73 us
    ppermute x7, waiting for transfers between devices: 14 us -> 7.93 us  [exchange(): return lax.ppermute(array, AXES, pairs)]
    ppermute x10 -> x8, waiting for transfers between devices: 1.1 us -> 2.85 us  [swap(): return lax.ppermute(array, AXES, pairs)]
    unnamed x6, local copies, waits for them, and re-layouts: 1.05 us -> 1.73 us
    ppermute x10 -> x8, starting transfers between devices: 3.74 us -> 3.48 us  [swap(): return lax.ppermute(array, AXES, pairs)]
    pallas_call x7 -> x14, Pallas kernels: 11.2 us -> 11.3 us  [the longest x5 10.8 us: match(): pl.pallas_call(functools.partial(match_kernel, queries, keys, masks, not...]
  transfers between devices with their start and end apart: 17 -> 15, of which waited for: 10 -> 7; matrix products, arithmetic and copies ran while one was open for 0% -> 0% of each run, Pallas kernels for 16% -> 17%
where the time goes in v5:
time: 56.1 us; the launch traced here: 55.9 us
  starting transfers between devices  19.3 us (34%)
  blocking collectives  11.9 us (21%)
  Pallas kernels  11.3 us (20%)
  waiting for transfers between devices  10.8 us (19%)
  local copies, waits for them, and re-layouts  1.73 us (3%)
  other arithmetic  0.59 us (1%)
    ppermute x7, starting transfers between devices, exchange(): return lax.ppermute(array, AXES, pairs)  15.9 us
    all_to_all x1, blocking collectives, on_device(): lax.all_to_all(best, AXES, split_axis=0, concat_axis=0, axis_index_groups...  11.9 us
    pallas_call x5, Pallas kernels, match(): pl.pallas_call(functools.partial(match_kernel, queries, keys, masks, not...  10.8 us
    ppermute x7, waiting for transfers between devices, exchange(): return lax.ppermute(array, AXES, pairs)  7.93 us
    ppermute x8, starting transfers between devices, swap(): return lax.ppermute(array, AXES, pairs)  3.48 us
    ppermute x8, waiting for transfers between devices, swap(): return lax.ppermute(array, AXES, pairs)  2.85 us
    unnamed x6, local copies, waits for them, and re-layouts  1.73 us
  transfers between devices with their start and end apart: 15, of which 7 were waited for; matrix products, arithmetic and copies ran while one was open for 0% of the time, Pallas kernels for 17%

profile of v5, /device:TPU:1, one launch (start us, length us, event | category | flops | bytes accessed | tf_op | source)
XLA Modules:
  0.0 55.9 jit_solution(12498094930305846154)
XLA Ops:
  0.0 0.7 %copy-done.2 = s32[256]{0:T(256)S(1)} copy-done((s32[256]{0:T(256)S(1)}, s32[256]{0:T(256)}, u32[]{:S(2)}) %copy-start.2) | copy-done | bytes 1048
  0.7 1.0 %copy-done = f32[256,512]{1,0:T(8,128)S(1)} copy-done((f32[256,512]{1,0:T(8,128)S(1)}, f32[256,512]{1,0:T(8,128)}, u32[]{:S(2)}) %copy-start) | copy-done | bytes 524312
  1.7 0.2 shard_map.37.first_ref
  1.9 1.5 %collective-permute-start = (bf16[272,512]{1,0:T(8,128)(2,1)S(1)}, bf16[272,512]{1,0:T(8,128)(2,1)S(1)}, u32[]{:S(2)}, u32[]{:S(2)}) collective-permute-start(bf16[272,512]{1,0:T(8,128)(2,1)S(1)} %shard_map.37.first_ref), channel_id=1, source_target_pairs={{16,0},{0,16},{48,32},{32,48},{80,64},{64,80},{112,96},{96,112},{2... | collective-permute-start | bytes 835592 | tf_op jit(solution)/shard_map/ppermute | solution.py:45
  3.4 1.2 %collective-permute-done.second_ref = bf16[272,512]{1,0:T(8,128)(2,1)S(1)} collective-permute-done((bf16[272,512]{1,0:T(8,128)(2,1)S(1)}, bf16[272,512]{1,0:T(8,128)(2,1)S(1)}, u32[]{:S(2)}, u32[]{:S(2)}) %collective-permute-start) | collective-permute-done | bytes 278560 | tf_op jit(solution)/shard_map/ppermute | solution.py:45
  4.7 3.9 %collective-permute-start.3 = (bf16[2,272,512]{2,1,0:T(8,128)(2,1)S(1)}, bf16[2,272,512]{2,1,0:T(8,128)(2,1)S(1)}, u32[]{:S(2)}, u32[]{:S(2)}) collective-permute-start(bf16[2,272,512]{2,1,0:T(8,128)(2,1)S(1)} %shard_map.38.refs_0_), channel_id=1, source_target_pairs={{32,0},{112,16},{0,32},{80,48},{96,64},{48,80},{64,96},{16,112},{3... | collective-permute-start | bytes 1671176 | tf_op jit(solution)/shard_map/ppermute | solution.py:40
  8.6 2.5 %collective-permute-start.1 = (bf16[2,272,512]{2,1,0:T(8,128)(2,1)S(1)}, bf16[2,272,512]{2,1,0:T(8,128)(2,1)S(1)}, u32[]{:S(2)}, u32[]{:S(2)}) collective-permute-start(bf16[2,272,512]{2,1,0:T(8,128)(2,1)S(1)} %shard_map.38.refs_0_), channel_id=1, source_target_pairs={{1,0},{19,16},{33,32},{51,48},{65,64},{83,80},{97,96},{115,112},{5... | collective-permute-start | bytes 1671176 | tf_op jit(solution)/shard_map/ppermute | solution.py:40
  11.1 2.7 %collective-permute-start.2 = (bf16[2,272,512]{2,1,0:T(8,128)(2,1)S(1)}, bf16[2,272,512]{2,1,0:T(8,128)(2,1)S(1)}, u32[]{:S(2)}, u32[]{:S(2)}) collective-permute-start(bf16[2,272,512]{2,1,0:T(8,128)(2,1)S(1)} %shard_map.38.refs_0_), channel_id=1, source_target_pairs={{4,0},{28,16},{36,32},{60,48},{68,64},{92,80},{100,96},{124,112},{... | collective-permute-start | bytes 1671176 | tf_op jit(solution)/shard_map/ppermute | solution.py:40
  13.8 1.7 %collective-permute-done.3.refs_0_.refs_3_.refs_4_ = bf16[2,272,512]{2,1,0:T(8,128)(2,1)S(1)} collective-permute-done((bf16[2,272,512]{2,1,0:T(8,128)(2,1)S(1)}, bf16[2,272,512]{2,1,0:T(8,128)(2,1)S(1)}, u32[]{:S(2)}, u32[]{:S(2)}) %collective-permute-start.3) | collective-permute-done | bytes 557088 | tf_op jit(solution)/shard_map/ppermute | solution.py:40
  15.6 0.1 collective-permute-start.6
  15.7 2.5 %collective-permute-done.1.refs_0_.refs_1_ = bf16[2,272,512]{2,1,0:T(8,128)(2,1)S(1)} collective-permute-done((bf16[2,272,512]{2,1,0:T(8,128)(2,1)S(1)}, bf16[2,272,512]{2,1,0:T(8,128)(2,1)S(1)}, u32[]{:S(2)}, u32[]{:S(2)}) %collective-permute-start.1) | collective-permute-done | bytes 557088 | tf_op jit(solution)/shard_map/ppermute | solution.py:40
  18.2 2.7 %collective-permute-start.7 = (bf16[2,272,512]{2,1,0:T(8,128)(2,1)S(1)}, bf16[2,272,512]{2,1,0:T(8,128)(2,1)S(1)}, u32[]{:S(2)}, u32[]{:S(2)}) collective-permute-start(bf16[2,272,512]{2,1,0:T(8,128)(2,1)S(1)} %collective-permute-done.1.refs_0_.refs_1_), channel_id=1, source_target_pairs={{4,0},{28,16},{36,32},{60,48},{68,64},{92,80},{100,96},{124,112},{... | collective-permute-start | bytes 1671176 | tf_op jit(solution)/shard_map/ppermute | solution.py:40
  21.0 0.1 collective-permute-start.5
  21.1 2.6 %collective-permute-start.8 = (bf16[2,272,512]{2,1,0:T(8,128)(2,1)S(1)}, bf16[2,272,512]{2,1,0:T(8,128)(2,1)S(1)}, u32[]{:S(2)}, u32[]{:S(2)}) collective-permute-start(bf16[2,272,512]{2,1,0:T(8,128)(2,1)S(1)} %collective-permute-done.3.refs_0_.refs_3_.refs_4_), channel_id=1, source_target_pairs={{1,0},{19,16},{33,32},{51,48},{65,64},{83,80},{97,96},{115,112},{5... | collective-permute-start | bytes 1671176 | tf_op jit(solution)/shard_map/ppermute | solution.py:40
  23.7 0.1 collective-permute-start.4
  23.8 0.5 collective-permute-start.9
  24.3 1.4 %collective-permute-done.4.refs_4_.refs_2_ = bf16[528,512]{1,0:T(8,128)(2,1)S(1)} collective-permute-done((bf16[528,512]{1,0:T(8,128)(2,1)S(1)}, bf16[528,512]{1,0:T(8,128)(2,1)S(1)}, u32[]{:S(2)}, u32[]{:S(2)}) %collective-permute-start.4) | collective-permute-done | bytes 540704 | tf_op jit(solution)/shard_map/ppermute | solution.py:45
  25.7 2.7 %shard_map.42.refs_7_ = f32[8,1,256]{2,1,0:T(1,128)S(1)} custom-call(bf16[2,272,512]{2,1,0:T(8,128)(2,1)S(1)} %shard_map.38.refs_0_, bf16[2,272,512]{2,1,0:T(8,128)(2,1)S(1)} %collective-permute-done.1.refs_0_.refs_1_, bf16[2,272,512]{2,1,0:T(8,128)(2,1)S(1)} %collective-permute-done.2.refs_0_.refs_2_, ...), custom_call_target="tpu_custom_call" | custom-call | flops 1000 | bytes 1000 | tf_op jit(solution)/shard_map/pallas_call | solution.py:213
  28.4 0.9 %collective-permute-start.13 = (bf16[2,272,512]{2,1,0:T(8,128)(2,1)S(1)}, bf16[2,272,512]{2,1,0:T(8,128)(2,1)S(1)}, u32[]{:S(2)}, u32[]{:S(2)}) collective-permute-start(bf16[2,272,512]{2,1,0:T(8,128)(2,1)S(1)} %collective-permute-done.7.refs_0_.refs_1_.refs_3_), channel_id=1, source_target_pairs={{32,0},{112,16},{0,32},{80,48},{96,64},{48,80},{64,96},{16,112},{3... | collective-permute-start | bytes 1671176 | tf_op jit(solution)/shard_map/ppermute | solution.py:40
  29.3 1.5 %collective-permute-done.8.refs_0_.refs_2_.refs_5_ = bf16[2,272,512]{2,1,0:T(8,128)(2,1)S(1)} collective-permute-done((bf16[2,272,512]{2,1,0:T(8,128)(2,1)S(1)}, bf16[2,272,512]{2,1,0:T(8,128)(2,1)S(1)}, u32[]{:S(2)}, u32[]{:S(2)}) %collective-permute-start.8) | collective-permute-done | bytes 557088 | tf_op jit(solution)/shard_map/ppermute | solution.py:40
  30.8 0.4 collective-permute-start.12
  31.2 2.2 %collective-permute-done.9.refs_0_.refs_3_.refs_6_ = bf16[2,272,512]{2,1,0:T(8,128)(2,1)S(1)} collective-permute-done((bf16[2,272,512]{2,1,0:T(8,128)(2,1)S(1)}, bf16[2,272,512]{2,1,0:T(8,128)(2,1)S(1)}, u32[]{:S(2)}, u32[]{:S(2)}) %collective-permute-start.9) | collective-permute-done | bytes 557088 | tf_op jit(solution)/shard_map/ppermute | solution.py:40
  33.5 0.4 collective-permute-start.11
  34.0 0.2 collective-permute-start.10
  34.2 2.1 %shard_map.46.refs_10_ = f32[8,1,256]{2,1,0:T(1,128)S(1)} custom-call(bf16[2,272,512]{2,1,0:T(8,128)(2,1)S(1)} %shard_map.38.refs_0_, bf16[2,272,512]{2,1,0:T(8,128)(2,1)S(1)} %collective-permute-done.7.refs_0_.refs_1_.refs_3_, bf16[2,272,512]{2,1,0:T(8,128)(2,1)S(1)} %collective-permute-done.8.refs_0_.refs_2_.refs_5_, ...), custom_call_target="tpu_custom_call" | custom-call | flops 1000 | bytes 1000 | tf_op jit(solution)/shard_map/pallas_call | solution.py:213
  36.3 3.4 %shard_map.47.refs_8_ = f32[8,1,256]{2,1,0:T(1,128)S(1)} custom-call(bf16[2,272,512]{2,1,0:T(8,128)(2,1)S(1)} %shard_map.38.refs_0_, bf16[2,272,512]{2,1,0:T(8,128)(2,1)S(1)} %collective-permute-done.1.refs_0_.refs_1_, bf16[2,272,512]{2,1,0:T(8,128)(2,1)S(1)} %collective-permute-done.2.refs_0_.refs_2_, ...), custom_call_target="tpu_custom_call" | custom-call | flops 1000 | bytes 1000 | tf_op jit(solution)/shard_map/pallas_call | solution.py:213
  39.7 0.6 %collective-permute-start.14 = (bf16[528,512]{1,0:T(8,128)(2,1)S(1)}, bf16[528,512]{1,0:T(8,128)(2,1)S(1)}, u32[]{:S(2)}, u32[]{:S(2)}) collective-permute-start(bf16[528,512]{1,0:T(8,128)(2,1)S(1)} %shard_map.48), channel_id=1, source_target_pairs={{16,0},{0,16},{48,32},{32,48},{80,64},{64,80},{112,96},{96,112},{2... | collective-permute-start | bytes 1622024 | tf_op jit(solution)/shard_map/ppermute | solution.py:45
  40.3 1.3 %shard_map.49.refs_9_ = f32[8,1,256]{2,1,0:T(1,128)S(1)} custom-call(bf16[2,272,512]{2,1,0:T(8,128)(2,1)S(1)} %shard_map.38.refs_0_, bf16[2,272,512]{2,1,0:T(8,128)(2,1)S(1)} %collective-permute-done.13.refs_0_.refs_1_.refs_7_, bf16[528,512]{1,0:T(8,128)(2,1)S(1)} %collective-permute-done.4.refs_4_.refs_2_, ...), custom_call_target="tpu_custom_call" | custom-call | flops 1000 | bytes 1000 | tf_op jit(solution)/shard_map/pallas_call | solution.py:213
  41.7 0.3 collective-permute-done.14.refs_8_
  41.9 1.4 %shard_map.50 = f32[8,1,256]{2,1,0:T(1,128)S(1)} custom-call(bf16[2,272,512]{2,1,0:T(8,128)(2,1)S(1)} %shard_map.38.refs_0_, bf16[2,272,512]{2,1,0:T(8,128)(2,1)S(1)} %collective-permute-done.1.refs_0_.refs_1_, bf16[2,272,512]{2,1,0:T(8,128)(2,1)S(1)} %collective-permute-done.2.refs_0_.refs_2_, ...), custom_call_target="tpu_custom_call" | custom-call | flops 1000 | bytes 1000 | tf_op jit(solution)/shard_map/pallas_call | solution.py:213
  43.3 11.9 %all_to_all.5 = f32[8,1,256]{2,1,0:T(1,128)S(1)} all-to-all(f32[8,1,256]{2,1,0:T(1,128)S(1)} %shard_map.50), channel_id=1, replica_groups={{0,1,4,5,32,33,36,37},{16,19,28,31,112,115,124,127},{48,51,60,63,80,83,..., dimensions={0} | all-to-all | bytes 16384 | tf_op jit(solution)/shard_map/all_to_all | solution.py:244
  55.3 0.6 %reduce_max.9 = f32[256]{0:T(256)} reduce(f32[8,1,256]{2,1,0:T(1,128)S(1)} %all_to_all.5, f32[]{:T(128)} %constant.0.clone.1), dimensions={0,1}, to_apply=%region_0.0 | reduce | flops 1792 | bytes 9220 | tf_op jit(solution)/shard_map/reduce_max | solution.py:245
  (20 shorter events, 0.4 us)
Async XLA Ops:
  0.0 0.7 %copy-start.2 = (s32[256]{0:T(256)S(1)}, s32[256]{0:T(256)}, u32[]{:S(2)}) copy-start(s32[256]{0:T(256)} %param.5) | copy-start | bytes 3076
  0.0 0.7 %copy-start.1 = (s32[256,1]{0,1:T(1,128)S(1)}, s32[256,1]{0,1:T(1,128)}, u32[]{:S(2)}) copy-start(s32[256,1]{0,1:T(1,128)} %param.4) | copy-start | bytes 3076
  0.7 1.0 %copy-start = (f32[256,512]{1,0:T(8,128)S(1)}, f32[256,512]{1,0:T(8,128)}, u32[]{:S(2)}) copy-start(f32[256,512]{1,0:T(8,128)} %emb_hbm.1) | copy-start | bytes 1572868
  1.9 2.7 %collective-permute-start = (bf16[272,512]{1,0:T(8,128)(2,1)S(1)}, bf16[272,512]{1,0:T(8,128)(2,1)S(1)}, u32[]{:S(2)}, u32[]{:S(2)}) collective-permute-start(bf16[272,512]{1,0:T(8,128)(2,1)S(1)} %shard_map.37.first_ref), channel_id=1, source_target_pairs={{16,0},{0,16},{48,32},{32,48},{80,64},{64,80},{112,96},{96,112},{2... | collective-permute-start | bytes 835592 | tf_op jit(solution)/shard_map/ppermute | solution.py:45
  4.7 10.8 %collective-permute-start.3 = (bf16[2,272,512]{2,1,0:T(8,128)(2,1)S(1)}, bf16[2,272,512]{2,1,0:T(8,128)(2,1)S(1)}, u32[]{:S(2)}, u32[]{:S(2)}) collective-permute-start(bf16[2,272,512]{2,1,0:T(8,128)(2,1)S(1)} %shard_map.38.refs_0_), channel_id=1, source_target_pairs={{32,0},{112,16},{0,32},{80,48},{96,64},{48,80},{64,96},{16,112},{3... | collective-permute-start | bytes 1671176 | tf_op jit(solution)/shard_map/ppermute | solution.py:40
  8.6 9.6 %collective-permute-start.1 = (bf16[2,272,512]{2,1,0:T(8,128)(2,1)S(1)}, bf16[2,272,512]{2,1,0:T(8,128)(2,1)S(1)}, u32[]{:S(2)}, u32[]{:S(2)}) collective-permute-start(bf16[2,272,512]{2,1,0:T(8,128)(2,1)S(1)} %shard_map.38.refs_0_), channel_id=1, source_target_pairs={{1,0},{19,16},{33,32},{51,48},{65,64},{83,80},{97,96},{115,112},{5... | collective-permute-start | bytes 1671176 | tf_op jit(solution)/shard_map/ppermute | solution.py:40
  11.1 9.9 %collective-permute-start.2 = (bf16[2,272,512]{2,1,0:T(8,128)(2,1)S(1)}, bf16[2,272,512]{2,1,0:T(8,128)(2,1)S(1)}, u32[]{:S(2)}, u32[]{:S(2)}) collective-permute-start(bf16[2,272,512]{2,1,0:T(8,128)(2,1)S(1)} %shard_map.38.refs_0_), channel_id=1, source_target_pairs={{4,0},{28,16},{36,32},{60,48},{68,64},{92,80},{100,96},{124,112},{... | collective-permute-start | bytes 1671176 | tf_op jit(solution)/shard_map/ppermute | solution.py:40
  15.6 8.2 %collective-permute-start.6 = (bf16[528,512]{1,0:T(8,128)(2,1)S(1)}, bf16[528,512]{1,0:T(8,128)(2,1)S(1)}, u32[]{:S(2)}, u32[]{:S(2)}) collective-permute-start(bf16[528,512]{1,0:T(8,128)(2,1)S(1)} %shard_map.41), channel_id=1, source_target_pairs={{16,0},{0,16},{48,32},{32,48},{80,64},{64,80},{112,96},{96,112},{2... | collective-permute-start | bytes 1622024 | tf_op jit(solution)/shard_map/ppermute | solution.py:45
  18.2 10.2 %collective-permute-start.7 = (bf16[2,272,512]{2,1,0:T(8,128)(2,1)S(1)}, bf16[2,272,512]{2,1,0:T(8,128)(2,1)S(1)}, u32[]{:S(2)}, u32[]{:S(2)}) collective-permute-start(bf16[2,272,512]{2,1,0:T(8,128)(2,1)S(1)} %collective-permute-done.1.refs_0_.refs_1_), channel_id=1, source_target_pairs={{4,0},{28,16},{36,32},{60,48},{68,64},{92,80},{100,96},{124,112},{... | collective-permute-start | bytes 1671176 | tf_op jit(solution)/shard_map/ppermute | solution.py:40
  21.0 3.3 %collective-permute-start.5 = (bf16[528,512]{1,0:T(8,128)(2,1)S(1)}, bf16[528,512]{1,0:T(8,128)(2,1)S(1)}, u32[]{:S(2)}, u32[]{:S(2)}) collective-permute-start(bf16[528,512]{1,0:T(8,128)(2,1)S(1)} %shard_map.40), channel_id=1, source_target_pairs={{16,0},{0,16},{48,32},{32,48},{80,64},{64,80},{112,96},{96,112},{2... | collective-permute-start | bytes 1622024 | tf_op jit(solution)/shard_map/ppermute | solution.py:45
  21.1 9.7 %collective-permute-start.8 = (bf16[2,272,512]{2,1,0:T(8,128)(2,1)S(1)}, bf16[2,272,512]{2,1,0:T(8,128)(2,1)S(1)}, u32[]{:S(2)}, u32[]{:S(2)}) collective-permute-start(bf16[2,272,512]{2,1,0:T(8,128)(2,1)S(1)} %collective-permute-done.3.refs_0_.refs_3_.refs_4_), channel_id=1, source_target_pairs={{1,0},{19,16},{33,32},{51,48},{65,64},{83,80},{97,96},{115,112},{5... | collective-permute-start | bytes 1671176 | tf_op jit(solution)/shard_map/ppermute | solution.py:40
  23.7 2.0 %collective-permute-start.4 = (bf16[528,512]{1,0:T(8,128)(2,1)S(1)}, bf16[528,512]{1,0:T(8,128)(2,1)S(1)}, u32[]{:S(2)}, u32[]{:S(2)}) collective-permute-start(bf16[528,512]{1,0:T(8,128)(2,1)S(1)} %shard_map.39), channel_id=1, source_target_pairs={{16,0},{0,16},{48,32},{32,48},{80,64},{64,80},{112,96},{96,112},{2... | collective-permute-start | bytes 1622024 | tf_op jit(solution)/shard_map/ppermute | solution.py:45
  23.8 9.7 %collective-permute-start.9 = (bf16[2,272,512]{2,1,0:T(8,128)(2,1)S(1)}, bf16[2,272,512]{2,1,0:T(8,128)(2,1)S(1)}, u32[]{:S(2)}, u32[]{:S(2)}) collective-permute-start(bf16[2,272,512]{2,1,0:T(8,128)(2,1)S(1)} %collective-permute-done.2.refs_0_.refs_2_), channel_id=1, source_target_pairs={{32,0},{112,16},{0,32},{80,48},{96,64},{48,80},{64,96},{16,112},{3... | collective-permute-start | bytes 1671176 | tf_op jit(solution)/shard_map/ppermute | solution.py:40
  28.4 11.3 %collective-permute-start.13 = (bf16[2,272,512]{2,1,0:T(8,128)(2,1)S(1)}, bf16[2,272,512]{2,1,0:T(8,128)(2,1)S(1)}, u32[]{:S(2)}, u32[]{:S(2)}) collective-permute-start(bf16[2,272,512]{2,1,0:T(8,128)(2,1)S(1)} %collective-permute-done.7.refs_0_.refs_1_.refs_3_), channel_id=1, source_target_pairs={{32,0},{112,16},{0,32},{80,48},{96,64},{48,80},{64,96},{16,112},{3... | collective-permute-start | bytes 1671176 | tf_op jit(solution)/shard_map/ppermute | solution.py:40
  30.8 5.5 %collective-permute-start.12 = (bf16[528,512]{1,0:T(8,128)(2,1)S(1)}, bf16[528,512]{1,0:T(8,128)(2,1)S(1)}, u32[]{:S(2)}, u32[]{:S(2)}) collective-permute-start(bf16[528,512]{1,0:T(8,128)(2,1)S(1)} %shard_map.45), channel_id=1, source_target_pairs={{16,0},{0,16},{48,32},{32,48},{80,64},{64,80},{112,96},{96,112},{2... | collective-permute-start | bytes 1622024 | tf_op jit(solution)/shard_map/ppermute | solution.py:45
  33.5 2.8 %collective-permute-start.11 = (bf16[528,512]{1,0:T(8,128)(2,1)S(1)}, bf16[528,512]{1,0:T(8,128)(2,1)S(1)}, u32[]{:S(2)}, u32[]{:S(2)}) collective-permute-start(bf16[528,512]{1,0:T(8,128)(2,1)S(1)} %shard_map.44), channel_id=1, source_target_pairs={{16,0},{0,16},{48,32},{32,48},{80,64},{64,80},{112,96},{96,112},{2... | collective-permute-start | bytes 1622024 | tf_op jit(solution)/shard_map/ppermute | solution.py:45
  34.0 2.3 %collective-permute-start.10 = (bf16[528,512]{1,0:T(8,128)(2,1)S(1)}, bf16[528,512]{1,0:T(8,128)(2,1)S(1)}, u32[]{:S(2)}, u32[]{:S(2)}) collective-permute-start(bf16[528,512]{1,0:T(8,128)(2,1)S(1)} %shard_map.43), channel_id=1, source_target_pairs={{16,0},{0,16},{48,32},{32,48},{80,64},{64,80},{112,96},{96,112},{2... | collective-permute-start | bytes 1622024 | tf_op jit(solution)/shard_map/ppermute | solution.py:45
  39.7 2.2 %collective-permute-start.14 = (bf16[528,512]{1,0:T(8,128)(2,1)S(1)}, bf16[528,512]{1,0:T(8,128)(2,1)S(1)}, u32[]{:S(2)}, u32[]{:S(2)}) collective-permute-start(bf16[528,512]{1,0:T(8,128)(2,1)S(1)} %shard_map.48), channel_id=1, source_target_pairs={{16,0},{0,16},{48,32},{32,48},{80,64},{64,80},{112,96},{96,112},{2... | collective-permute-start | bytes 1622024 | tf_op jit(solution)/shard_map/ppermute | solution.py:45

commit v6 on v5

--- a/solution.py
+++ b/solution.py
@@ -43,15 +43,6 @@
 def swap(array):
     pairs = [(linear(x, y, z, 1 - c), linear(x, y, z, c)) for x, y, z, c in PLACES]
     return lax.ppermute(array, AXES, pairs)
-
-
-def cube_groups():
-    groups = []
-    for place in PLACES:
-        starts = (0, 1) if place[3] else (0, 2)
-        if all(p in starts for p in place[:3]):
-            groups.append([linear(*across(place, k)) for k in range(8)])
-    return groups
 
 
 def unit_kernel(emb_hbm, cluster_hbm, rank_hbm, out_ref, emb_ref, cluster_ref, rank_ref, sem):
@@ -77,11 +68,11 @@
 
 
 def payload(embeddings, cluster_ids, order_rank):
-    anywhere = pl.BlockSpec(memory_space=pl.ANY)
+    outside = pl.BlockSpec(memory_space=pltpu.HBM)
     return pl.pallas_call(
         unit_kernel,
         out_shape=jax.ShapeDtypeStruct((PAY, E), jnp.bfloat16),
-        in_specs=[anywhere] * 3,
+        in_specs=[outside] * 3,
         out_specs=pl.BlockSpec(memory_space=pltpu.VMEM),
         scratch_shapes=[
             pltpu.VMEM((ROWS, E), jnp.float32),
@@ -91,7 +82,7 @@
         ],
         compiler_params=pltpu.CompilerParams(vmem_limit_bytes=GRANT),
         cost_estimate=SMALL,
-    )(embeddings, cluster_ids.reshape(1, ROWS), order_rank.reshape(1, ROWS))
+    )(*[pltpu.with_memory_space_constraint(x, pltpu.HBM) for x in (embeddings, cluster_ids.reshape(1, ROWS), order_rank.reshape(1, ROWS))])
 
 
 def join_kernel(first_ref, second_ref, out_ref):
@@ -134,18 +125,11 @@
     )(*blocks)
 
 
-def cube_code():
-    group, tile = lax.axis_index("group"), lax.axis_index("tile")
-    side = group & 1
-    bits = [(place >> side) & 1 for place in (tile & 3, tile >> 2, group >> 1)]
-    return bits[0] | (bits[1] << 1) | (bits[2] << 2)
-
-
-def match_kernel(queries, keys, masks, begin, *refs):
+def match_kernel(queries, keys, masks, begin, last, *refs):
     mine = dict(zip(masks, refs[0 : len(masks)]))
     others = [n for n in keys if n]
     theirs = dict(zip(others, refs[len(masks) : len(masks) + len(others)]))
-    out_ref, first, second = refs[-3:]
+    out_ref, first, second = refs[-4 if last else -3], *refs[-2:]
 
     def numbers(meta, at):
         rank = meta[at : at + 1, 0:ROWS] * 256.0 + meta[at : at + 1, ROWS : 2 * ROWS]
@@ -198,27 +182,54 @@
                     valid = row - jnp.concatenate([column, column], axis=1) < limit
                     best = jnp.maximum(best, jnp.where(valid, score[r : r + 8, :], -1.0))
             found[m] = jnp.max(best, axis=0, keepdims=True)
-    code = cube_code()
-    out_ref[...] = jnp.full(out_ref.shape, -1.0, jnp.float32) if begin else refs[-4][...]
-    for m in queries:
-        slot = code ^ m
-        out_ref[slot] = jnp.maximum(out_ref[slot], found[m])
-
-
-def match(queries, keys, mine, theirs, *prev):
+    old = None if begin else refs[-5 if last else -4]
+    for m in range(8):
+        best = jnp.full((1, ROWS), -1.0, jnp.float32) if begin else old[m]
+        best = jnp.maximum(best, found[m]) if m in found else best
+        out_ref[m] = best
+        if last and m > 3:
+            refs[-3][m - 4] = best
+
+
+def match(queries, keys, mine, theirs, *prev, last=False):
     masks = sorted(set(queries) | ({0} & set(keys)))
     others = [n for n in keys if n]
     columns = len(queries) if len(queries) < len(keys) else 2 * len(keys)
     vmem = pl.BlockSpec(memory_space=pltpu.VMEM)
-    return pl.pallas_call(
-        functools.partial(match_kernel, queries, keys, masks, not prev),
-        out_shape=jax.ShapeDtypeStruct((8, 1, ROWS), jnp.float32),
+    found = pl.pallas_call(
+        functools.partial(match_kernel, queries, keys, masks, not prev, last),
+        out_shape=[jax.ShapeDtypeStruct((k, 1, ROWS), jnp.float32) for k in ((8, 4) if last else (8,))],
         in_specs=[vmem] * (len(masks) + len(others) + len(prev)),
-        out_specs=vmem,
+        out_specs=[vmem] * (2 if last else 1),
         scratch_shapes=[pltpu.VMEM((columns, ROWS, 128), jnp.int32)] * 2,
         compiler_params=pltpu.CompilerParams(vmem_limit_bytes=GRANT),
         cost_estimate=SMALL,
     )(*[mine[m] for m in masks], *[theirs[n] for n in others], *prev)
+    return found if last else found[0]
+
+
+def fold_kernel(held_ref, come_ref, *outs):
+    rows = come_ref.shape[0]
+    total = jnp.maximum(held_ref[0:rows], come_ref[...])
+    if len(outs) == 1:
+        outs[0][...] = total[0]
+    else:
+        outs[0][...] = total
+        outs[1][...] = total[rows // 2 :]
+
+
+def fold(held, come):
+    rows = come.shape[0]
+    vmem = pl.BlockSpec(memory_space=pltpu.VMEM)
+    shapes = [jax.ShapeDtypeStruct((k, 1, ROWS), jnp.float32) for k in (rows, rows // 2)]
+    return pl.pallas_call(
+        fold_kernel,
+        out_shape=shapes if rows > 1 else [jax.ShapeDtypeStruct((1, ROWS), jnp.float32)],
+        in_specs=[vmem] * 2,
+        out_specs=[vmem] * (2 if rows > 1 else 1),
+        compiler_params=pltpu.CompilerParams(vmem_limit_bytes=GRANT),
+        cost_estimate=SMALL,
+    )(held, come)
 
 
 def on_device(embeddings, cluster_ids, order_rank):
@@ -236,13 +247,15 @@
     mine[7] = exchange(mine[3], 4)
     theirs.update({m: swap(pack(mine[m])[0]) for m in far})
     best = match(far, near, mine, theirs, best)
-    best = match((*near, *far), far, mine, theirs, best)
+    best = match((4, 6, 5), far, mine, theirs, best)
     best, mine[7] = lax.optimization_barrier((best, mine[7]))
     theirs[7] = swap(pack(mine[7])[0])
     best = match((7,), (*near, *far), mine, theirs, best)
-    best = match((*near, *far, 7), (7,), mine, theirs, best)
-    back = lax.all_to_all(best, AXES, split_axis=0, concat_axis=0, axis_index_groups=cube_groups())
-    return jnp.max(back, axis=0)[0]
+    best, send = match((4, 6, 5, 7), (7,), mine, theirs, best, last=True)
+    held = match((0, 1, 2, 3), (3, 6, 5, 7), mine, theirs, best)
+    for mask in (4, 2):
+        held, send = fold(held, exchange(send, mask))
+    return fold(held, exchange(send, 1))[0].reshape(ROWS)
 
 
 def solution(mesh):

time: 56.1 us -> 53.5 us (0.954)
  blocking collectives: 11.9 us -> 0 us
  waiting for transfers between devices: 10.8 us -> 18.7 us
  Pallas kernels: 11.3 us -> 13.3 us
  starting transfers between devices: 19.3 us -> 21.2 us
  local copies, waits for them, and re-layouts: 1.73 us -> 0 us
  other arithmetic: 0.59 us -> 0 us
    all_to_all x1 -> x0, blocking collectives: 11.9 us -> none  [on_device(): lax.all_to_all(best, AXES, split_axis=0, concat_axis=0, axis_index_groups...]
    ppermute x7 -> x10, waiting for transfers between devices: 7.93 us -> 15.9 us  [exchange(): return lax.ppermute(array, AXES, pairs)]
    ppermute x7 -> x10, starting transfers between devices: 15.9 us -> 17.7 us  [exchange(): return lax.ppermute(array, AXES, pairs)]
    unnamed x6 -> x0, local copies, waits for them, and re-layouts: 1.73 us -> none
    pallas_call x1, Pallas kernels: 0.2 us -> 1.23 us  [payload(): pl.pallas_call(unit_kernel, out_shape=jax.ShapeDtypeStruct((PAY, E), jnp....]
    reduce_max x1 -> x0, other arithmetic: 0.59 us -> none  [on_device(): return jnp.max(back, axis=0)[0]]
    pallas_call x0 -> x3, Pallas kernels: none -> 0.57 us  [fold(): pl.pallas_call(fold_kernel, out_shape=shapes if rows > 1 else [jax.ShapeD...]
    pallas_call x5 -> x6, Pallas kernels: 10.8 us -> 11.2 us  [match(): pl.pallas_call(functools.partial(match_kernel, queries, keys, masks, not...]
  transfers between devices with their start and end apart: 15 -> 18, of which waited for: 7 -> 11; matrix products, arithmetic and copies ran while one was open for 0% -> 0% of each run, Pallas kernels for 17% -> 20%
where the time goes in v6:
time: 53.5 us; the launch traced here: 53.4 us
  starting transfers between devices  21.2 us (40%)
  waiting for transfers between devices  18.7 us (35%)
  Pallas kernels  13.3 us (25%)
    ppermute x10, starting transfers between devices, exchange(): return lax.ppermute(array, AXES, pairs)  17.7 us
    ppermute x10, waiting for transfers between devices, exchange(): return lax.ppermute(array, AXES, pairs)  15.9 us
    pallas_call x6, Pallas kernels, match(): pl.pallas_call(functools.partial(match_kernel, queries, keys, masks, not...  11.2 us
    ppermute x8, starting transfers between devices, swap(): return lax.ppermute(array, AXES, pairs)  3.47 us
    ppermute x8, waiting for transfers between devices, swap(): return lax.ppermute(array, AXES, pairs)  2.85 us
    pallas_call x1, Pallas kernels, payload(): pl.pallas_call(unit_kernel, out_shape=jax.ShapeDtypeStruct((PAY, E), jnp....  1.23 us
  transfers between devices with their start and end apart: 18, of which 11 were waited for; matrix products, arithmetic and copies ran while one was open for 0% of the time, Pallas kernels for 20%

profile of v6, /device:TPU:1, one launch (start us, length us, event | category | flops | bytes accessed | tf_op | source)
XLA Modules:
  0.0 53.4 jit_solution(5093155216481582258)
XLA Ops:
  0.0 1.2 %shard_map.37.first_ref = bf16[272,512]{1,0:T(8,128)(2,1)S(1)} custom-call(f32[256,512]{1,0:T(8,128)} %emb_hbm.1, s32[1,256]{1,0:T(1,128)} %bitcast.3, s32[1,256]{1,0:T(1,128)} %bitcast.4), custom_call_target="tpu_custom_call" | custom-call | flops 1000 | bytes 1000 | tf_op jit(solution)/shard_map/pallas_call | solution.py:72
  1.2 1.5 %collective-permute-start = (bf16[272,512]{1,0:T(8,128)(2,1)S(1)}, bf16[272,512]{1,0:T(8,128)(2,1)S(1)}, u32[]{:S(2)}, u32[]{:S(2)}) collective-permute-start(bf16[272,512]{1,0:T(8,128)(2,1)S(1)} %shard_map.37.first_ref), channel_id=1, source_target_pairs={{16,0},{0,16},{48,32},{32,48},{80,64},{64,80},{112,96},{96,112},{2... | collective-permute-start | bytes 835592 | tf_op jit(solution)/shard_map/ppermute | solution.py:45
  2.7 1.2 %collective-permute-done.second_ref = bf16[272,512]{1,0:T(8,128)(2,1)S(1)} collective-permute-done((bf16[272,512]{1,0:T(8,128)(2,1)S(1)}, bf16[272,512]{1,0:T(8,128)(2,1)S(1)}, u32[]{:S(2)}, u32[]{:S(2)}) %collective-permute-start) | collective-permute-done | bytes 278560 | tf_op jit(solution)/shard_map/ppermute | solution.py:45
  4.0 3.9 %collective-permute-start.3 = (bf16[2,272,512]{2,1,0:T(8,128)(2,1)S(1)}, bf16[2,272,512]{2,1,0:T(8,128)(2,1)S(1)}, u32[]{:S(2)}, u32[]{:S(2)}) collective-permute-start(bf16[2,272,512]{2,1,0:T(8,128)(2,1)S(1)} %shard_map.38.refs_0_), channel_id=1, source_target_pairs={{32,0},{112,16},{0,32},{80,48},{96,64},{48,80},{64,96},{16,112},{3... | collective-permute-start | bytes 1671176 | tf_op jit(solution)/shard_map/ppermute | solution.py:40
  7.9 2.5 %collective-permute-start.1 = (bf16[2,272,512]{2,1,0:T(8,128)(2,1)S(1)}, bf16[2,272,512]{2,1,0:T(8,128)(2,1)S(1)}, u32[]{:S(2)}, u32[]{:S(2)}) collective-permute-start(bf16[2,272,512]{2,1,0:T(8,128)(2,1)S(1)} %shard_map.38.refs_0_), channel_id=1, source_target_pairs={{1,0},{19,16},{33,32},{51,48},{65,64},{83,80},{97,96},{115,112},{5... | collective-permute-start | bytes 1671176 | tf_op jit(solution)/shard_map/ppermute | solution.py:40
  10.4 2.7 %collective-permute-start.2 = (bf16[2,272,512]{2,1,0:T(8,128)(2,1)S(1)}, bf16[2,272,512]{2,1,0:T(8,128)(2,1)S(1)}, u32[]{:S(2)}, u32[]{:S(2)}) collective-permute-start(bf16[2,272,512]{2,1,0:T(8,128)(2,1)S(1)} %shard_map.38.refs_0_), channel_id=1, source_target_pairs={{4,0},{28,16},{36,32},{60,48},{68,64},{92,80},{100,96},{124,112},{... | collective-permute-start | bytes 1671176 | tf_op jit(solution)/shard_map/ppermute | solution.py:40
  13.1 1.7 %collective-permute-done.3.refs_0_.refs_3_ = bf16[2,272,512]{2,1,0:T(8,128)(2,1)S(1)} collective-permute-done((bf16[2,272,512]{2,1,0:T(8,128)(2,1)S(1)}, bf16[2,272,512]{2,1,0:T(8,128)(2,1)S(1)}, u32[]{:S(2)}, u32[]{:S(2)}) %collective-permute-start.3) | collective-permute-done | bytes 557088 | tf_op jit(solution)/shard_map/ppermute | solution.py:40
  14.9 2.5 %collective-permute-done.1.refs_0_.refs_1_ = bf16[2,272,512]{2,1,0:T(8,128)(2,1)S(1)} collective-permute-done((bf16[2,272,512]{2,1,0:T(8,128)(2,1)S(1)}, bf16[2,272,512]{2,1,0:T(8,128)(2,1)S(1)}, u32[]{:S(2)}, u32[]{:S(2)}) %collective-permute-start.1) | collective-permute-done | bytes 557088 | tf_op jit(solution)/shard_map/ppermute | solution.py:40
  17.5 2.7 %collective-permute-start.7 = (bf16[2,272,512]{2,1,0:T(8,128)(2,1)S(1)}, bf16[2,272,512]{2,1,0:T(8,128)(2,1)S(1)}, u32[]{:S(2)}, u32[]{:S(2)}) collective-permute-start(bf16[2,272,512]{2,1,0:T(8,128)(2,1)S(1)} %collective-permute-done.1.refs_0_.refs_1_), channel_id=1, source_target_pairs={{4,0},{28,16},{36,32},{60,48},{68,64},{92,80},{100,96},{124,112},{... | collective-permute-start | bytes 1671176 | tf_op jit(solution)/shard_map/ppermute | solution.py:40
  20.4 2.6 %collective-permute-start.11 = (bf16[2,272,512]{2,1,0:T(8,128)(2,1)S(1)}, bf16[2,272,512]{2,1,0:T(8,128)(2,1)S(1)}, u32[]{:S(2)}, u32[]{:S(2)}) collective-permute-start(bf16[2,272,512]{2,1,0:T(8,128)(2,1)S(1)} %collective-permute-done.3.refs_0_.refs_3_), channel_id=1, source_target_pairs={{1,0},{19,16},{33,32},{51,48},{65,64},{83,80},{97,96},{115,112},{5... | collective-permute-start | bytes 1671176 | tf_op jit(solution)/shard_map/ppermute | solution.py:40
  23.1 0.5 collective-permute-start.9
  23.6 1.4 %collective-permute-done.4.refs_4_.refs_2_ = bf16[528,512]{1,0:T(8,128)(2,1)S(1)} collective-permute-done((bf16[528,512]{1,0:T(8,128)(2,1)S(1)}, bf16[528,512]{1,0:T(8,128)(2,1)S(1)}, u32[]{:S(2)}, u32[]{:S(2)}) %collective-permute-start.4) | collective-permute-done | bytes 540704 | tf_op jit(solution)/shard_map/ppermute | solution.py:45
  25.0 2.7 %shard_map.42.refs_7_ = f32[8,1,256]{2,1,0:T(1,128)S(1)} custom-call(bf16[2,272,512]{2,1,0:T(8,128)(2,1)S(1)} %shard_map.38.refs_0_, bf16[2,272,512]{2,1,0:T(8,128)(2,1)S(1)} %collective-permute-done.1.refs_0_.refs_1_, bf16[2,272,512]{2,1,0:T(8,128)(2,1)S(1)} %collective-permute-done.2.refs_0_.refs_2_, ...), custom_call_target="tpu_custom_call" | custom-call | flops 1000 | bytes 1000 | tf_op jit(solution)/shard_map/pallas_call | solution.py:199
  27.6 0.9 %collective-permute-start.13 = (bf16[2,272,512]{2,1,0:T(8,128)(2,1)S(1)}, bf16[2,272,512]{2,1,0:T(8,128)(2,1)S(1)}, u32[]{:S(2)}, u32[]{:S(2)}) collective-permute-start(bf16[2,272,512]{2,1,0:T(8,128)(2,1)S(1)} %collective-permute-done.7.refs_0_.refs_1_.refs_3_), channel_id=1, source_target_pairs={{32,0},{112,16},{0,32},{80,48},{96,64},{48,80},{64,96},{16,112},{3... | collective-permute-start | bytes 1671176 | tf_op jit(solution)/shard_map/ppermute | solution.py:40
  28.6 1.5 %collective-permute-done.11.refs_0_.refs_2_.refs_1_ = bf16[2,272,512]{2,1,0:T(8,128)(2,1)S(1)} collective-permute-done((bf16[2,272,512]{2,1,0:T(8,128)(2,1)S(1)}, bf16[2,272,512]{2,1,0:T(8,128)(2,1)S(1)}, u32[]{:S(2)}, u32[]{:S(2)}) %collective-permute-start.11) | collective-permute-done | bytes 557088 | tf_op jit(solution)/shard_map/ppermute | solution.py:40
  30.1 0.4 collective-permute-start.12
  30.5 2.2 %collective-permute-done.9.refs_0_.refs_3_.refs_2_ = bf16[2,272,512]{2,1,0:T(8,128)(2,1)S(1)} collective-permute-done((bf16[2,272,512]{2,1,0:T(8,128)(2,1)S(1)}, bf16[2,272,512]{2,1,0:T(8,128)(2,1)S(1)}, u32[]{:S(2)}, u32[]{:S(2)}) %collective-permute-start.9) | collective-permute-done | bytes 557088 | tf_op jit(solution)/shard_map/ppermute | solution.py:40
  32.8 0.4 collective-permute-start.10
  33.5 2.1 %shard_map.46.refs_6_ = f32[8,1,256]{2,1,0:T(1,128)S(1)} custom-call(bf16[2,272,512]{2,1,0:T(8,128)(2,1)S(1)} %shard_map.38.refs_0_, bf16[2,272,512]{2,1,0:T(8,128)(2,1)S(1)} %collective-permute-done.7.refs_0_.refs_1_.refs_3_, bf16[2,272,512]{2,1,0:T(8,128)(2,1)S(1)} %collective-permute-done.11.refs_0_.refs_2_.refs_1_, ...), custom_call_target="tpu_custom_call" | custom-call | flops 1000 | bytes 1000 | tf_op jit(solution)/shard_map/pallas_call | solution.py:199
  35.6 1.6 %shard_map.47.refs_8_ = f32[8,1,256]{2,1,0:T(1,128)S(1)} custom-call(bf16[2,272,512]{2,1,0:T(8,128)(2,1)S(1)} %collective-permute-done.3.refs_0_.refs_3_, bf16[2,272,512]{2,1,0:T(8,128)(2,1)S(1)} %collective-permute-done.11.refs_0_.refs_2_.refs_1_, bf16[2,272,512]{2,1,0:T(8,128)(2,1)S(1)} %collective-permute-done.9.refs_0_.refs_3_.refs_2_, ...), custom_call_target="tpu_custom_call" | custom-call | flops 1000 | bytes 1000 | tf_op jit(solution)/shard_map/pallas_call | solution.py:199
  37.2 1.5 %collective-permute-done.13.refs_0_.refs_1_.refs_3_ = bf16[2,272,512]{2,1,0:T(8,128)(2,1)S(1)} collective-permute-done((bf16[2,272,512]{2,1,0:T(8,128)(2,1)S(1)}, bf16[2,272,512]{2,1,0:T(8,128)(2,1)S(1)}, u32[]{:S(2)}, u32[]{:S(2)}) %collective-permute-start.13) | collective-permute-done | bytes 557088 | tf_op jit(solution)/shard_map/ppermute | solution.py:40
  38.7 0.6 %collective-permute-start.14 = (bf16[528,512]{1,0:T(8,128)(2,1)S(1)}, bf16[528,512]{1,0:T(8,128)(2,1)S(1)}, u32[]{:S(2)}, u32[]{:S(2)}) collective-permute-start(bf16[528,512]{1,0:T(8,128)(2,1)S(1)} %shard_map.48), channel_id=1, source_target_pairs={{16,0},{0,16},{48,32},{32,48},{80,64},{64,80},{112,96},{96,112},{2... | collective-permute-start | bytes 1622024 | tf_op jit(solution)/shard_map/ppermute | solution.py:45
  39.4 1.3 %shard_map.49.refs_5_ = f32[8,1,256]{2,1,0:T(1,128)S(1)} custom-call(bf16[2,272,512]{2,1,0:T(8,128)(2,1)S(1)} %shard_map.38.refs_0_, bf16[2,272,512]{2,1,0:T(8,128)(2,1)S(1)} %collective-permute-done.13.refs_0_.refs_1_.refs_3_, bf16[528,512]{1,0:T(8,128)(2,1)S(1)} %collective-permute-done.4.refs_4_.refs_2_, ...), custom_call_target="tpu_custom_call" | custom-call | flops 1000 | bytes 1000 | tf_op jit(solution)/shard_map/pallas_call | solution.py:199
  40.9 0.8 %shard_map.50 = (f32[8,1,256]{2,1,0:T(1,128)S(1)}, f32[4,1,256]{2,1,0:T(1,128)S(1)}) custom-call(bf16[2,272,512]{2,1,0:T(8,128)(2,1)S(1)} %collective-permute-done.3.refs_0_.refs_3_, bf16[2,272,512]{2,1,0:T(8,128)(2,1)S(1)} %collective-permute-done.11.refs_0_.refs_2_.refs_1_, bf16[2,272,512]{2,1,0:T(8,128)(2,1)S(1)} %collective-permute-done.9.refs_0_.refs_3_.refs_2_, ...), custom_call_target="tpu_custom_call" | custom-call | flops 1000 | bytes 1000 | tf_op jit(solution)/shard_map/pallas_call | solution.py:199
  41.8 0.5 collective-permute-start.15
  42.3 2.7 %shard_map.51.held_ref = f32[8,1,256]{2,1,0:T(1,128)S(1)} custom-call(bf16[2,272,512]{2,1,0:T(8,128)(2,1)S(1)} %shard_map.38.refs_0_, bf16[2,272,512]{2,1,0:T(8,128)(2,1)S(1)} %collective-permute-done.1.refs_0_.refs_1_, bf16[2,272,512]{2,1,0:T(8,128)(2,1)S(1)} %collective-permute-done.2.refs_0_.refs_2_, ...), custom_call_target="tpu_custom_call" | custom-call | flops 1000 | bytes 1000 | tf_op jit(solution)/shard_map/pallas_call | solution.py:199
  45.0 0.6 %collective-permute-done.15.come_ref = f32[4,1,256]{2,1,0:T(1,128)S(1)} collective-permute-done((f32[4,1,256]{2,1,0:T(1,128)S(1)}, f32[4,1,256]{2,1,0:T(1,128)S(1)}, u32[]{:S(2)}, u32[]{:S(2)}) %collective-permute-start.15) | collective-permute-done | bytes 4128 | tf_op jit(solution)/shard_map/ppermute | solution.py:40
  45.5 0.7 %collective-permute-start.16 = (f32[2,1,256]{2,1,0:T(1,128)S(1)}, f32[2,1,256]{2,1,0:T(1,128)S(1)}, u32[]{:S(2)}, u32[]{:S(2)}) collective-permute-start(f32[2,1,256]{2,1,0:T(1,128)S(1)} %get-tuple-element.22), channel_id=1, source_target_pairs={{4,0},{28,16},{36,32},{60,48},{68,64},{92,80},{100,96},{124,112},{... | collective-permute-start | bytes 6152 | tf_op jit(solution)/shard_map/ppermute | solution.py:40
  46.2 3.0 %collective-permute-done.16.come_ref = f32[2,1,256]{2,1,0:T(1,128)S(1)} collective-permute-done((f32[2,1,256]{2,1,0:T(1,128)S(1)}, f32[2,1,256]{2,1,0:T(1,128)S(1)}, u32[]{:S(2)}, u32[]{:S(2)}) %collective-permute-start.16) | collective-permute-done | bytes 2080 | tf_op jit(solution)/shard_map/ppermute | solution.py:40
  49.2 0.7 %collective-permute-start.17 = (f32[1,1,256]{2,1,0:T(1,128)S(1)}, f32[1,1,256]{2,1,0:T(1,128)S(1)}, u32[]{:S(2)}, u32[]{:S(2)}) collective-permute-start(f32[1,1,256]{2,1,0:T(1,128)S(1)} %get-tuple-element.24), channel_id=1, source_target_pairs={{1,0},{19,16},{33,32},{51,48},{65,64},{83,80},{97,96},{115,112},{5... | collective-permute-start | bytes 3080 | tf_op jit(solution)/shard_map/ppermute | solution.py:40
  49.9 3.0 %collective-permute-done.17.come_ref = f32[1,1,256]{2,1,0:T(1,128)S(1)} collective-permute-done((f32[1,1,256]{2,1,0:T(1,128)S(1)}, f32[1,1,256]{2,1,0:T(1,128)S(1)}, u32[]{:S(2)}, u32[]{:S(2)}) %collective-permute-start.17) | collective-permute-done | bytes 1056 | tf_op jit(solution)/shard_map/ppermute | solution.py:40
  52.8 0.6 %shard_map.54 = f32[1,256]{1,0:T(1,128)} custom-call(f32[2,1,256]{2,1,0:T(1,128)S(1)} %get-tuple-element.23.held_ref, f32[1,1,256]{2,1,0:T(1,128)S(1)} %collective-permute-done.17.come_ref), custom_call_target="tpu_custom_call" | custom-call | flops 1000 | bytes 1000 | tf_op jit(solution)/shard_map/pallas_call | solution.py:225
  (22 shorter events, 1.1 us)
Async XLA Ops:
  1.2 2.7 %collective-permute-start = (bf16[272,512]{1,0:T(8,128)(2,1)S(1)}, bf16[272,512]{1,0:T(8,128)(2,1)S(1)}, u32[]{:S(2)}, u32[]{:S(2)}) collective-permute-start(bf16[272,512]{1,0:T(8,128)(2,1)S(1)} %shard_map.37.first_ref), channel_id=1, source_target_pairs={{16,0},{0,16},{48,32},{32,48},{80,64},{64,80},{112,96},{96,112},{2... | collective-permute-start | bytes 835592 | tf_op jit(solution)/shard_map/ppermute | solution.py:45
  4.0 10.8 %collective-permute-start.3 = (bf16[2,272,512]{2,1,0:T(8,128)(2,1)S(1)}, bf16[2,272,512]{2,1,0:T(8,128)(2,1)S(1)}, u32[]{:S(2)}, u32[]{:S(2)}) collective-permute-start(bf16[2,272,512]{2,1,0:T(8,128)(2,1)S(1)} %shard_map.38.refs_0_), channel_id=1, source_target_pairs={{32,0},{112,16},{0,32},{80,48},{96,64},{48,80},{64,96},{16,112},{3... | collective-permute-start | bytes 1671176 | tf_op jit(solution)/shard_map/ppermute | solution.py:40
  7.9 9.6 %collective-permute-start.1 = (bf16[2,272,512]{2,1,0:T(8,128)(2,1)S(1)}, bf16[2,272,512]{2,1,0:T(8,128)(2,1)S(1)}, u32[]{:S(2)}, u32[]{:S(2)}) collective-permute-start(bf16[2,272,512]{2,1,0:T(8,128)(2,1)S(1)} %shard_map.38.refs_0_), channel_id=1, source_target_pairs={{1,0},{19,16},{33,32},{51,48},{65,64},{83,80},{97,96},{115,112},{5... | collective-permute-start | bytes 1671176 | tf_op jit(solution)/shard_map/ppermute | solution.py:40
  10.4 9.9 %collective-permute-start.2 = (bf16[2,272,512]{2,1,0:T(8,128)(2,1)S(1)}, bf16[2,272,512]{2,1,0:T(8,128)(2,1)S(1)}, u32[]{:S(2)}, u32[]{:S(2)}) collective-permute-start(bf16[2,272,512]{2,1,0:T(8,128)(2,1)S(1)} %shard_map.38.refs_0_), channel_id=1, source_target_pairs={{4,0},{28,16},{36,32},{60,48},{68,64},{92,80},{100,96},{124,112},{... | collective-permute-start | bytes 1671176 | tf_op jit(solution)/shard_map/ppermute | solution.py:40
  14.8 8.2 %collective-permute-start.6 = (bf16[528,512]{1,0:T(8,128)(2,1)S(1)}, bf16[528,512]{1,0:T(8,128)(2,1)S(1)}, u32[]{:S(2)}, u32[]{:S(2)}) collective-permute-start(bf16[528,512]{1,0:T(8,128)(2,1)S(1)} %shard_map.41), channel_id=1, source_target_pairs={{16,0},{0,16},{48,32},{32,48},{80,64},{64,80},{112,96},{96,112},{2... | collective-permute-start | bytes 1622024 | tf_op jit(solution)/shard_map/ppermute | solution.py:45
  17.5 10.2 %collective-permute-start.7 = (bf16[2,272,512]{2,1,0:T(8,128)(2,1)S(1)}, bf16[2,272,512]{2,1,0:T(8,128)(2,1)S(1)}, u32[]{:S(2)}, u32[]{:S(2)}) collective-permute-start(bf16[2,272,512]{2,1,0:T(8,128)(2,1)S(1)} %collective-permute-done.1.refs_0_.refs_1_), channel_id=1, source_target_pairs={{4,0},{28,16},{36,32},{60,48},{68,64},{92,80},{100,96},{124,112},{... | collective-permute-start | bytes 1671176 | tf_op jit(solution)/shard_map/ppermute | solution.py:40
  20.3 3.3 %collective-permute-start.5 = (bf16[528,512]{1,0:T(8,128)(2,1)S(1)}, bf16[528,512]{1,0:T(8,128)(2,1)S(1)}, u32[]{:S(2)}, u32[]{:S(2)}) collective-permute-start(bf16[528,512]{1,0:T(8,128)(2,1)S(1)} %shard_map.40), channel_id=1, source_target_pairs={{16,0},{0,16},{48,32},{32,48},{80,64},{64,80},{112,96},{96,112},{2... | collective-permute-start | bytes 1622024 | tf_op jit(solution)/shard_map/ppermute | solution.py:45
  20.4 9.7 %collective-permute-start.11 = (bf16[2,272,512]{2,1,0:T(8,128)(2,1)S(1)}, bf16[2,272,512]{2,1,0:T(8,128)(2,1)S(1)}, u32[]{:S(2)}, u32[]{:S(2)}) collective-permute-start(bf16[2,272,512]{2,1,0:T(8,128)(2,1)S(1)} %collective-permute-done.3.refs_0_.refs_3_), channel_id=1, source_target_pairs={{1,0},{19,16},{33,32},{51,48},{65,64},{83,80},{97,96},{115,112},{5... | collective-permute-start | bytes 1671176 | tf_op jit(solution)/shard_map/ppermute | solution.py:40
  23.0 2.0 %collective-permute-start.4 = (bf16[528,512]{1,0:T(8,128)(2,1)S(1)}, bf16[528,512]{1,0:T(8,128)(2,1)S(1)}, u32[]{:S(2)}, u32[]{:S(2)}) collective-permute-start(bf16[528,512]{1,0:T(8,128)(2,1)S(1)} %shard_map.39), channel_id=1, source_target_pairs={{16,0},{0,16},{48,32},{32,48},{80,64},{64,80},{112,96},{96,112},{2... | collective-permute-start | bytes 1622024 | tf_op jit(solution)/shard_map/ppermute | solution.py:45
  23.1 9.7 %collective-permute-start.9 = (bf16[2,272,512]{2,1,0:T(8,128)(2,1)S(1)}, bf16[2,272,512]{2,1,0:T(8,128)(2,1)S(1)}, u32[]{:S(2)}, u32[]{:S(2)}) collective-permute-start(bf16[2,272,512]{2,1,0:T(8,128)(2,1)S(1)} %collective-permute-done.2.refs_0_.refs_2_), channel_id=1, source_target_pairs={{32,0},{112,16},{0,32},{80,48},{96,64},{48,80},{64,96},{16,112},{3... | collective-permute-start | bytes 1671176 | tf_op jit(solution)/shard_map/ppermute | solution.py:40
  27.6 11.1 %collective-permute-start.13 = (bf16[2,272,512]{2,1,0:T(8,128)(2,1)S(1)}, bf16[2,272,512]{2,1,0:T(8,128)(2,1)S(1)}, u32[]{:S(2)}, u32[]{:S(2)}) collective-permute-start(bf16[2,272,512]{2,1,0:T(8,128)(2,1)S(1)} %collective-permute-done.7.refs_0_.refs_1_.refs_3_), channel_id=1, source_target_pairs={{32,0},{112,16},{0,32},{80,48},{96,64},{48,80},{64,96},{16,112},{3... | collective-permute-start | bytes 1671176 | tf_op jit(solution)/shard_map/ppermute | solution.py:40
  30.1 5.5 %collective-permute-start.12 = (bf16[528,512]{1,0:T(8,128)(2,1)S(1)}, bf16[528,512]{1,0:T(8,128)(2,1)S(1)}, u32[]{:S(2)}, u32[]{:S(2)}) collective-permute-start(bf16[528,512]{1,0:T(8,128)(2,1)S(1)} %shard_map.45), channel_id=1, source_target_pairs={{16,0},{0,16},{48,32},{32,48},{80,64},{64,80},{112,96},{96,112},{2... | collective-permute-start | bytes 1622024 | tf_op jit(solution)/shard_map/ppermute | solution.py:45
  32.8 2.8 %collective-permute-start.10 = (bf16[528,512]{1,0:T(8,128)(2,1)S(1)}, bf16[528,512]{1,0:T(8,128)(2,1)S(1)}, u32[]{:S(2)}, u32[]{:S(2)}) collective-permute-start(bf16[528,512]{1,0:T(8,128)(2,1)S(1)} %shard_map.44), channel_id=1, source_target_pairs={{16,0},{0,16},{48,32},{32,48},{80,64},{64,80},{112,96},{96,112},{2... | collective-permute-start | bytes 1622024 | tf_op jit(solution)/shard_map/ppermute | solution.py:45
  33.2 2.3 %collective-permute-start.8 = (bf16[528,512]{1,0:T(8,128)(2,1)S(1)}, bf16[528,512]{1,0:T(8,128)(2,1)S(1)}, u32[]{:S(2)}, u32[]{:S(2)}) collective-permute-start(bf16[528,512]{1,0:T(8,128)(2,1)S(1)} %shard_map.43), channel_id=1, source_target_pairs={{16,0},{0,16},{48,32},{32,48},{80,64},{64,80},{112,96},{96,112},{2... | collective-permute-start | bytes 1622024 | tf_op jit(solution)/shard_map/ppermute | solution.py:45
  38.7 2.2 %collective-permute-start.14 = (bf16[528,512]{1,0:T(8,128)(2,1)S(1)}, bf16[528,512]{1,0:T(8,128)(2,1)S(1)}, u32[]{:S(2)}, u32[]{:S(2)}) collective-permute-start(bf16[528,512]{1,0:T(8,128)(2,1)S(1)} %shard_map.48), channel_id=1, source_target_pairs={{16,0},{0,16},{48,32},{32,48},{80,64},{64,80},{112,96},{96,112},{2... | collective-permute-start | bytes 1622024 | tf_op jit(solution)/shard_map/ppermute | solution.py:45
  41.8 3.7 %collective-permute-start.15 = (f32[4,1,256]{2,1,0:T(1,128)S(1)}, f32[4,1,256]{2,1,0:T(1,128)S(1)}, u32[]{:S(2)}, u32[]{:S(2)}) collective-permute-start(f32[4,1,256]{2,1,0:T(1,128)S(1)} %get-tuple-element.20), channel_id=1, source_target_pairs={{32,0},{112,16},{0,32},{80,48},{96,64},{48,80},{64,96},{16,112},{3... | collective-permute-start | bytes 12296 | tf_op jit(solution)/shard_map/ppermute | solution.py:40
  45.5 3.6 %collective-permute-start.16 = (f32[2,1,256]{2,1,0:T(1,128)S(1)}, f32[2,1,256]{2,1,0:T(1,128)S(1)}, u32[]{:S(2)}, u32[]{:S(2)}) collective-permute-start(f32[2,1,256]{2,1,0:T(1,128)S(1)} %get-tuple-element.22), channel_id=1, source_target_pairs={{4,0},{28,16},{36,32},{60,48},{68,64},{92,80},{100,96},{124,112},{... | collective-permute-start | bytes 6152 | tf_op jit(solution)/shard_map/ppermute | solution.py:40
  49.2 3.6 %collective-permute-start.17 = (f32[1,1,256]{2,1,0:T(1,128)S(1)}, f32[1,1,256]{2,1,0:T(1,128)S(1)}, u32[]{:S(2)}, u32[]{:S(2)}) collective-permute-start(f32[1,1,256]{2,1,0:T(1,128)S(1)} %get-tuple-element.24), channel_id=1, source_target_pairs={{1,0},{19,16},{33,32},{51,48},{65,64},{83,80},{97,96},{115,112},{5... | collective-permute-start | bytes 3080 | tf_op jit(solution)/shard_map/ppermute | solution.py:40

commit v7 on v6

--- a/solution.py
+++ b/solution.py
@@ -208,28 +208,25 @@
     return found if last else found[0]
 
 
-def fold_kernel(held_ref, come_ref, *outs):
-    rows = come_ref.shape[0]
-    total = jnp.maximum(held_ref[0:rows], come_ref[...])
-    if len(outs) == 1:
-        outs[0][...] = total[0]
-    else:
-        outs[0][...] = total
-        outs[1][...] = total[rows // 2 :]
-
-
-def fold(held, come):
-    rows = come.shape[0]
-    vmem = pl.BlockSpec(memory_space=pltpu.VMEM)
-    shapes = [jax.ShapeDtypeStruct((k, 1, ROWS), jnp.float32) for k in (rows, rows // 2)]
-    return pl.pallas_call(
-        fold_kernel,
-        out_shape=shapes if rows > 1 else [jax.ShapeDtypeStruct((1, ROWS), jnp.float32)],
-        in_specs=[vmem] * 2,
-        out_specs=[vmem] * (2 if rows > 1 else 1),
-        compiler_params=pltpu.CompilerParams(vmem_limit_bytes=GRANT),
-        cost_estimate=SMALL,
-    )(held, come)
+def fold_kernel(row, *refs):
+    out_ref = refs[-1]
+    total = refs[0][row : row + 1] if row < 2 else refs[0][row : row + 2]
+    for come_ref in refs[1:-1]:
+        total = jnp.maximum(total, come_ref[row : row + total.shape[0]])
+    out_ref[...] = total if row else total[0]
+
+
+def fold(row, *parts):
+    vmem = pl.BlockSpec(memory_space=pltpu.VMEM)
+    shape = {0: (1, ROWS), 1: (1, 1, ROWS), 2: (2, 1, ROWS)}[row]
+    return pl.pallas_call(
+        functools.partial(fold_kernel, row),
+        out_shape=jax.ShapeDtypeStruct(shape, jnp.float32),
+        in_specs=[vmem] * len(parts),
+        out_specs=vmem,
+        compiler_params=pltpu.CompilerParams(vmem_limit_bytes=GRANT),
+        cost_estimate=SMALL,
+    )(*parts)
 
 
 def on_device(embeddings, cluster_ids, order_rank):
@@ -242,20 +239,24 @@
     mine[6] = exchange(mine[2], 4)
     mine[5] = exchange(mine[4], 1)
     theirs.update({m: swap(pack(mine[m])[0]) for m in (1, 2, 4)})
-    best = match(near, near, mine, theirs)
-    best, mine[3] = lax.optimization_barrier((best, mine[3]))
     mine[7] = exchange(mine[3], 4)
     theirs.update({m: swap(pack(mine[m])[0]) for m in far})
-    best = match(far, near, mine, theirs, best)
+    every = (*near, *far, 7)
+    best = match((4, 6, 5), near, mine, theirs)
     best = match((4, 6, 5), far, mine, theirs, best)
     best, mine[7] = lax.optimization_barrier((best, mine[7]))
     theirs[7] = swap(pack(mine[7])[0])
     best = match((7,), (*near, *far), mine, theirs, best)
     best, send = match((4, 6, 5, 7), (7,), mine, theirs, best, last=True)
-    held = match((0, 1, 2, 3), (3, 6, 5, 7), mine, theirs, best)
-    for mask in (4, 2):
-        held, send = fold(held, exchange(send, mask))
-    return fold(held, exchange(send, 1))[0].reshape(ROWS)
+    send, mine[0] = lax.optimization_barrier((send, mine[0]))
+    first = exchange(send, 4)
+    send = fold(2, match((2, 3), every, mine, theirs), first)
+    send, mine[0] = lax.optimization_barrier((send, mine[0]))
+    second = exchange(send, 2)
+    send = fold(1, match((1,), every, mine, theirs), first, second)
+    send, mine[0] = lax.optimization_barrier((send, mine[0]))
+    third = exchange(send, 1)
+    return fold(0, match((0,), every, mine, theirs), first, second, third).reshape(ROWS)
 
 
 def solution(mesh):

time: 53.5 us -> 51.9 us (0.970)
  waiting for transfers between devices: 18.7 us -> 5.47 us
  starting transfers between devices: 21.2 us -> 31.9 us
  Pallas kernels: 13.3 us -> 14.2 us
    ppermute x10, waiting for transfers between devices: 15.9 us -> 3.18 us  [exchange(): return lax.ppermute(array, AXES, pairs)]
    ppermute x10, starting transfers between devices: 17.7 us -> 28.8 us  [exchange(): return lax.ppermute(array, AXES, pairs)]
    pallas_call x6 -> x7, Pallas kernels: 11.2 us -> 12 us  [match(): pl.pallas_call(functools.partial(match_kernel, queries, keys, masks, not...]
    ppermute x8, waiting for transfers between devices: 2.85 us -> 2.29 us  [swap(): return lax.ppermute(array, AXES, pairs)]
  transfers between devices with their start and end apart: 18 -> 18, of which waited for: 11 -> 6; matrix products, arithmetic and copies ran while one was open for 0% -> 0% of each run, Pallas kernels for 20% -> 21%
where the time goes in v7:
time: 51.9 us; the launch traced here: 51.7 us
  starting transfers between devices  31.9 us (61%)
  Pallas kernels  14.2 us (27%)
  waiting for transfers between devices  5.47 us (11%)
    ppermute x10, starting transfers between devices, exchange(): return lax.ppermute(array, AXES, pairs)  28.8 us
    pallas_call x7, Pallas kernels, match(): pl.pallas_call(functools.partial(match_kernel, queries, keys, masks, not...  12 us
    ppermute x10, waiting for transfers between devices, exchange(): return lax.ppermute(array, AXES, pairs)  3.18 us
    ppermute x8, starting transfers between devices, swap(): return lax.ppermute(array, AXES, pairs)  3.15 us
    ppermute x8, waiting for transfers between devices, swap(): return lax.ppermute(array, AXES, pairs)  2.29 us
    pallas_call x1, Pallas kernels, payload(): pl.pallas_call(unit_kernel, out_shape=jax.ShapeDtypeStruct((PAY, E), jnp....  1.23 us
  transfers between devices with their start and end apart: 18, of which 6 were waited for; matrix products, arithmetic and copies ran while one was open for 0% of the time, Pallas kernels for 21%

profile of v7, /device:TPU:1, one launch (start us, length us, event | category | flops | bytes accessed | tf_op | source)
XLA Modules:
  0.0 51.7 jit_solution(14251493249895969704)
XLA Ops:
  0.0 1.2 %shard_map.37.first_ref = bf16[272,512]{1,0:T(8,128)(2,1)S(1)} custom-call(f32[256,512]{1,0:T(8,128)} %emb_hbm.1, s32[1,256]{1,0:T(1,128)} %bitcast.3, s32[1,256]{1,0:T(1,128)} %bitcast.4), custom_call_target="tpu_custom_call" | custom-call | flops 1000 | bytes 1000 | tf_op jit(solution)/shard_map/pallas_call | solution.py:72
  1.2 1.5 %collective-permute-start = (bf16[272,512]{1,0:T(8,128)(2,1)S(1)}, bf16[272,512]{1,0:T(8,128)(2,1)S(1)}, u32[]{:S(2)}, u32[]{:S(2)}) collective-permute-start(bf16[272,512]{1,0:T(8,128)(2,1)S(1)} %shard_map.37.first_ref), channel_id=1, source_target_pairs={{16,0},{0,16},{48,32},{32,48},{80,64},{64,80},{112,96},{96,112},{2... | collective-permute-start | bytes 835592 | tf_op jit(solution)/shard_map/ppermute | solution.py:45
  2.7 1.2 %collective-permute-done.second_ref = bf16[272,512]{1,0:T(8,128)(2,1)S(1)} collective-permute-done((bf16[272,512]{1,0:T(8,128)(2,1)S(1)}, bf16[272,512]{1,0:T(8,128)(2,1)S(1)}, u32[]{:S(2)}, u32[]{:S(2)}) %collective-permute-start) | collective-permute-done | bytes 278560 | tf_op jit(solution)/shard_map/ppermute | solution.py:45
  4.0 2.6 %collective-permute-start.5 = (bf16[2,272,512]{2,1,0:T(8,128)(2,1)S(1)}, bf16[2,272,512]{2,1,0:T(8,128)(2,1)S(1)}, u32[]{:S(2)}, u32[]{:S(2)}) collective-permute-start(bf16[2,272,512]{2,1,0:T(8,128)(2,1)S(1)} %shard_map.38.refs_0_), channel_id=1, source_target_pairs={{1,0},{19,16},{33,32},{51,48},{65,64},{83,80},{97,96},{115,112},{5... | collective-permute-start | bytes 1671176 | tf_op jit(solution)/shard_map/ppermute | solution.py:40
  6.6 2.7 %collective-permute-start.3 = (bf16[2,272,512]{2,1,0:T(8,128)(2,1)S(1)}, bf16[2,272,512]{2,1,0:T(8,128)(2,1)S(1)}, u32[]{:S(2)}, u32[]{:S(2)}) collective-permute-start(bf16[2,272,512]{2,1,0:T(8,128)(2,1)S(1)} %shard_map.38.refs_0_), channel_id=1, source_target_pairs={{4,0},{28,16},{36,32},{60,48},{68,64},{92,80},{100,96},{124,112},{... | collective-permute-start | bytes 1671176 | tf_op jit(solution)/shard_map/ppermute | solution.py:40
  9.3 3.8 %collective-permute-start.1 = (bf16[2,272,512]{2,1,0:T(8,128)(2,1)S(1)}, bf16[2,272,512]{2,1,0:T(8,128)(2,1)S(1)}, u32[]{:S(2)}, u32[]{:S(2)}) collective-permute-start(bf16[2,272,512]{2,1,0:T(8,128)(2,1)S(1)} %shard_map.38.refs_0_), channel_id=1, source_target_pairs={{32,0},{112,16},{0,32},{80,48},{96,64},{48,80},{64,96},{16,112},{3... | collective-permute-start | bytes 1671176 | tf_op jit(solution)/shard_map/ppermute | solution.py:40
  13.1 0.5 %collective-permute-done.5.refs_0_.refs_1_ = bf16[2,272,512]{2,1,0:T(8,128)(2,1)S(1)} collective-permute-done((bf16[2,272,512]{2,1,0:T(8,128)(2,1)S(1)}, bf16[2,272,512]{2,1,0:T(8,128)(2,1)S(1)}, u32[]{:S(2)}, u32[]{:S(2)}) %collective-permute-start.5) | collective-permute-done | bytes 557088 | tf_op jit(solution)/shard_map/ppermute | solution.py:40
  13.6 2.8 %collective-permute-start.6 = (bf16[2,272,512]{2,1,0:T(8,128)(2,1)S(1)}, bf16[2,272,512]{2,1,0:T(8,128)(2,1)S(1)}, u32[]{:S(2)}, u32[]{:S(2)}) collective-permute-start(bf16[2,272,512]{2,1,0:T(8,128)(2,1)S(1)} %collective-permute-done.5.refs_0_.refs_1_), channel_id=1, source_target_pairs={{4,0},{28,16},{36,32},{60,48},{68,64},{92,80},{100,96},{124,112},{... | collective-permute-start | bytes 1671176 | tf_op jit(solution)/shard_map/ppermute | solution.py:40
  16.5 3.8 %collective-permute-start.4 = (bf16[2,272,512]{2,1,0:T(8,128)(2,1)S(1)}, bf16[2,272,512]{2,1,0:T(8,128)(2,1)S(1)}, u32[]{:S(2)}, u32[]{:S(2)}) collective-permute-start(bf16[2,272,512]{2,1,0:T(8,128)(2,1)S(1)} %collective-permute-done.3.refs_0_.refs_1_), channel_id=1, source_target_pairs={{32,0},{112,16},{0,32},{80,48},{96,64},{48,80},{64,96},{16,112},{3... | collective-permute-start | bytes 1671176 | tf_op jit(solution)/shard_map/ppermute | solution.py:40
  20.2 2.5 %collective-permute-start.2 = (bf16[2,272,512]{2,1,0:T(8,128)(2,1)S(1)}, bf16[2,272,512]{2,1,0:T(8,128)(2,1)S(1)}, u32[]{:S(2)}, u32[]{:S(2)}) collective-permute-start(bf16[2,272,512]{2,1,0:T(8,128)(2,1)S(1)} %collective-permute-done.1.refs_0_.refs_1_), channel_id=1, source_target_pairs={{1,0},{19,16},{33,32},{51,48},{65,64},{83,80},{97,96},{115,112},{5... | collective-permute-start | bytes 1671176 | tf_op jit(solution)/shard_map/ppermute | solution.py:40
  22.7 0.1 collective-permute-start.10
  22.9 0.6 %collective-permute-start.11 = (bf16[528,512]{1,0:T(8,128)(2,1)S(1)}, bf16[528,512]{1,0:T(8,128)(2,1)S(1)}, u32[]{:S(2)}, u32[]{:S(2)}) collective-permute-start(bf16[528,512]{1,0:T(8,128)(2,1)S(1)} %shard_map.43), channel_id=1, source_target_pairs={{16,0},{0,16},{48,32},{32,48},{80,64},{64,80},{112,96},{96,112},{2... | collective-permute-start | bytes 1622024 | tf_op jit(solution)/shard_map/ppermute | solution.py:45
  23.5 3.7 %collective-permute-start.13 = (bf16[2,272,512]{2,1,0:T(8,128)(2,1)S(1)}, bf16[2,272,512]{2,1,0:T(8,128)(2,1)S(1)}, u32[]{:S(2)}, u32[]{:S(2)}) collective-permute-start(bf16[2,272,512]{2,1,0:T(8,128)(2,1)S(1)} %collective-permute-done.6.refs_0_.refs_2_), channel_id=1, source_target_pairs={{32,0},{112,16},{0,32},{80,48},{96,64},{48,80},{64,96},{16,112},{3... | collective-permute-start | bytes 1671176 | tf_op jit(solution)/shard_map/ppermute | solution.py:40
  27.2 0.1 collective-permute-start.12
  27.4 2.4 %collective-permute-done.2.refs_0_.refs_2_.refs_1_ = bf16[2,272,512]{2,1,0:T(8,128)(2,1)S(1)} collective-permute-done((bf16[2,272,512]{2,1,0:T(8,128)(2,1)S(1)}, bf16[2,272,512]{2,1,0:T(8,128)(2,1)S(1)}, u32[]{:S(2)}, u32[]{:S(2)}) %collective-permute-start.2) | collective-permute-done | bytes 557088 | tf_op jit(solution)/shard_map/ppermute | solution.py:40
  29.9 0.6 %collective-permute-start.8 = (bf16[528,512]{1,0:T(8,128)(2,1)S(1)}, bf16[528,512]{1,0:T(8,128)(2,1)S(1)}, u32[]{:S(2)}, u32[]{:S(2)}) collective-permute-start(bf16[528,512]{1,0:T(8,128)(2,1)S(1)} %shard_map.40), channel_id=1, source_target_pairs={{16,0},{0,16},{48,32},{32,48},{80,64},{64,80},{112,96},{96,112},{2... | collective-permute-start | bytes 1622024 | tf_op jit(solution)/shard_map/ppermute | solution.py:45
  30.5 0.1 collective-permute-start.9
  30.6 2.1 %shard_map.45.refs_6_ = f32[8,1,256]{2,1,0:T(1,128)S(1)} custom-call(bf16[2,272,512]{2,1,0:T(8,128)(2,1)S(1)} %shard_map.38.refs_0_, bf16[2,272,512]{2,1,0:T(8,128)(2,1)S(1)} %collective-permute-done.1.refs_0_.refs_1_, bf16[2,272,512]{2,1,0:T(8,128)(2,1)S(1)} %collective-permute-done.2.refs_0_.refs_2_.refs_1_, ...), custom_call_target="tpu_custom_call" | custom-call | flops 1000 | bytes 1000 | tf_op jit(solution)/shard_map/pallas_call | solution.py:199
  32.7 0.6 %collective-permute-done.9.refs_5_.refs_7_.refs_8_.refs_6_ = bf16[528,512]{1,0:T(8,128)(2,1)S(1)} collective-permute-done((bf16[528,512]{1,0:T(8,128)(2,1)S(1)}, bf16[528,512]{1,0:T(8,128)(2,1)S(1)}, u32[]{:S(2)}, u32[]{:S(2)}) %collective-permute-start.9) | collective-permute-done | bytes 540704 | tf_op jit(solution)/shard_map/ppermute | solution.py:45
  33.3 1.6 %shard_map.46.refs_8_ = f32[8,1,256]{2,1,0:T(1,128)S(1)} custom-call(bf16[2,272,512]{2,1,0:T(8,128)(2,1)S(1)} %collective-permute-done.1.refs_0_.refs_1_, bf16[2,272,512]{2,1,0:T(8,128)(2,1)S(1)} %collective-permute-done.2.refs_0_.refs_2_.refs_1_, bf16[2,272,512]{2,1,0:T(8,128)(2,1)S(1)} %collective-permute-done.4.refs_0_.refs_3_.refs_2_, ...), custom_call_target="tpu_custom_call" | custom-call | flops 1000 | bytes 1000 | tf_op jit(solution)/shard_map/pallas_call | solution.py:199
  35.0 0.2 collective-permute-start.14
  35.2 1.3 %shard_map.48.refs_5_ = f32[8,1,256]{2,1,0:T(1,128)S(1)} custom-call(bf16[2,272,512]{2,1,0:T(8,128)(2,1)S(1)} %shard_map.38.refs_0_, bf16[2,272,512]{2,1,0:T(8,128)(2,1)S(1)} %collective-permute-done.13.refs_0_.refs_1_.refs_3_, bf16[528,512]{1,0:T(8,128)(2,1)S(1)} %collective-permute-done.10.refs_4_.refs_2_.refs_3_.refs_1_, ...), custom_call_target="tpu_custom_call" | custom-call | flops 1000 | bytes 1000 | tf_op jit(solution)/shard_map/pallas_call | solution.py:199
  36.5 0.5 collective-permute-done.14.refs_4_.refs_9_.refs_8_.refs_7_
  37.0 1.5 %shard_map.49 = (f32[8,1,256]{2,1,0:T(1,128)}, f32[4,1,256]{2,1,0:T(1,128)S(1)}) custom-call(bf16[2,272,512]{2,1,0:T(8,128)(2,1)S(1)} %collective-permute-done.1.refs_0_.refs_1_, bf16[2,272,512]{2,1,0:T(8,128)(2,1)S(1)} %collective-permute-done.2.refs_0_.refs_2_.refs_1_, bf16[2,272,512]{2,1,0:T(8,128)(2,1)S(1)} %collective-permute-done.4.refs_0_.refs_3_.refs_2_, ...), custom_call_target="tpu_custom_call" | custom-call | flops 1000 | bytes 1000 | tf_op jit(solution)/shard_map/pallas_call | solution.py:199
  38.5 2.5 %collective-permute-start.15 = (f32[4,1,256]{2,1,0:T(1,128)S(1)}, f32[4,1,256]{2,1,0:T(1,128)S(1)}, u32[]{:S(2)}, u32[]{:S(2)}) collective-permute-start(f32[4,1,256]{2,1,0:T(1,128)S(1)} %get-tuple-element.18), channel_id=1, source_target_pairs={{32,0},{112,16},{0,32},{80,48},{96,64},{48,80},{64,96},{16,112},{3... | collective-permute-start | bytes 12296 | tf_op jit(solution)/shard_map/ppermute | solution.py:40
  40.9 2.6 %shard_map.50.refs_0_ = f32[8,1,256]{2,1,0:T(1,128)S(1)} custom-call(bf16[2,272,512]{2,1,0:T(8,128)(2,1)S(1)} %shard_map.38.refs_0_, bf16[2,272,512]{2,1,0:T(8,128)(2,1)S(1)} %collective-permute-done.3.refs_0_.refs_1_, bf16[2,272,512]{2,1,0:T(8,128)(2,1)S(1)} %collective-permute-done.6.refs_0_.refs_2_, ...), custom_call_target="tpu_custom_call" | custom-call | flops 1000 | bytes 1000 | tf_op jit(solution)/shard_map/pallas_call | solution.py:199
  43.6 2.1 %collective-permute-start.16 = (f32[2,1,256]{2,1,0:T(1,128)S(1)}, f32[2,1,256]{2,1,0:T(1,128)S(1)}, u32[]{:S(2)}, u32[]{:S(2)}) collective-permute-start(f32[2,1,256]{2,1,0:T(1,128)S(1)} %shard_map.51), channel_id=1, source_target_pairs={{4,0},{28,16},{36,32},{60,48},{68,64},{92,80},{100,96},{124,112},{... | collective-permute-start | bytes 6152 | tf_op jit(solution)/shard_map/ppermute | solution.py:40
  45.6 1.5 %shard_map.52.refs_0_ = f32[8,1,256]{2,1,0:T(1,128)S(1)} custom-call(bf16[2,272,512]{2,1,0:T(8,128)(2,1)S(1)} %shard_map.38.refs_0_, bf16[2,272,512]{2,1,0:T(8,128)(2,1)S(1)} %collective-permute-done.5.refs_0_.refs_1_, bf16[528,512]{1,0:T(8,128)(2,1)S(1)} %collective-permute-done.10.refs_4_.refs_2_.refs_3_.refs_1_, ...), custom_call_target="tpu_custom_call" | custom-call | flops 1000 | bytes 1000 | tf_op jit(solution)/shard_map/pallas_call | solution.py:199
  47.1 0.2 collective-permute-done.16.refs_2_
  47.3 2.4 %collective-permute-start.17 = (f32[1,1,256]{2,1,0:T(1,128)S(1)}, f32[1,1,256]{2,1,0:T(1,128)S(1)}, u32[]{:S(2)}, u32[]{:S(2)}) collective-permute-start(f32[1,1,256]{2,1,0:T(1,128)S(1)} %shard_map.53), channel_id=1, source_target_pairs={{1,0},{19,16},{33,32},{51,48},{65,64},{83,80},{97,96},{115,112},{5... | collective-permute-start | bytes 3080 | tf_op jit(solution)/shard_map/ppermute | solution.py:40
  49.7 1.5 %shard_map.54.refs_0_ = f32[8,1,256]{2,1,0:T(1,128)S(1)} custom-call(bf16[2,272,512]{2,1,0:T(8,128)(2,1)S(1)} %shard_map.38.refs_0_, bf16[528,512]{1,0:T(8,128)(2,1)S(1)} %collective-permute-done.10.refs_4_.refs_2_.refs_3_.refs_1_, bf16[528,512]{1,0:T(8,128)(2,1)S(1)} %collective-permute-done.11.refs_5_.refs_3_.refs_4_.refs_2_, ...), custom_call_target="tpu_custom_call" | custom-call | flops 1000 | bytes 1000 | tf_op jit(solution)/shard_map/pallas_call | solution.py:199
  51.2 0.6 %shard_map.55 = f32[1,256]{1,0:T(1,128)} custom-call(f32[8,1,256]{2,1,0:T(1,128)S(1)} %shard_map.54.refs_0_, f32[4,1,256]{2,1,0:T(1,128)S(1)} %collective-permute-done.15.refs_1_, f32[2,1,256]{2,1,0:T(1,128)S(1)} %collective-permute-done.16.refs_2_, f32[1,1,256]{2,1,0:T(1,128)S(1)} %collective-permute-done.17.refs_3_), custom_call_target="tpu_custom_call" | custom-call | flops 1000 | bytes 1000 | tf_op jit(solution)/shard_map/pallas_call | solution.py:222
  (23 shorter events, 0.4 us)
Async XLA Ops:
  1.2 2.7 %collective-permute-start = (bf16[272,512]{1,0:T(8,128)(2,1)S(1)}, bf16[272,512]{1,0:T(8,128)(2,1)S(1)}, u32[]{:S(2)}, u32[]{:S(2)}) collective-permute-start(bf16[272,512]{1,0:T(8,128)(2,1)S(1)} %shard_map.37.first_ref), channel_id=1, source_target_pairs={{16,0},{0,16},{48,32},{32,48},{80,64},{64,80},{112,96},{96,112},{2... | collective-permute-start | bytes 835592 | tf_op jit(solution)/shard_map/ppermute | solution.py:45
  4.0 9.7 %collective-permute-start.5 = (bf16[2,272,512]{2,1,0:T(8,128)(2,1)S(1)}, bf16[2,272,512]{2,1,0:T(8,128)(2,1)S(1)}, u32[]{:S(2)}, u32[]{:S(2)}) collective-permute-start(bf16[2,272,512]{2,1,0:T(8,128)(2,1)S(1)} %shard_map.38.refs_0_), channel_id=1, source_target_pairs={{1,0},{19,16},{33,32},{51,48},{65,64},{83,80},{97,96},{115,112},{5... | collective-permute-start | bytes 1671176 | tf_op jit(solution)/shard_map/ppermute | solution.py:40
  6.6 9.9 %collective-permute-start.3 = (bf16[2,272,512]{2,1,0:T(8,128)(2,1)S(1)}, bf16[2,272,512]{2,1,0:T(8,128)(2,1)S(1)}, u32[]{:S(2)}, u32[]{:S(2)}) collective-permute-start(bf16[2,272,512]{2,1,0:T(8,128)(2,1)S(1)} %shard_map.38.refs_0_), channel_id=1, source_target_pairs={{4,0},{28,16},{36,32},{60,48},{68,64},{92,80},{100,96},{124,112},{... | collective-permute-start | bytes 1671176 | tf_op jit(solution)/shard_map/ppermute | solution.py:40
  9.3 10.9 %collective-permute-start.1 = (bf16[2,272,512]{2,1,0:T(8,128)(2,1)S(1)}, bf16[2,272,512]{2,1,0:T(8,128)(2,1)S(1)}, u32[]{:S(2)}, u32[]{:S(2)}) collective-permute-start(bf16[2,272,512]{2,1,0:T(8,128)(2,1)S(1)} %shard_map.38.refs_0_), channel_id=1, source_target_pairs={{32,0},{112,16},{0,32},{80,48},{96,64},{48,80},{64,96},{16,112},{3... | collective-permute-start | bytes 1671176 | tf_op jit(solution)/shard_map/ppermute | solution.py:40
  13.6 9.8 %collective-permute-start.6 = (bf16[2,272,512]{2,1,0:T(8,128)(2,1)S(1)}, bf16[2,272,512]{2,1,0:T(8,128)(2,1)S(1)}, u32[]{:S(2)}, u32[]{:S(2)}) collective-permute-start(bf16[2,272,512]{2,1,0:T(8,128)(2,1)S(1)} %collective-permute-done.5.refs_0_.refs_1_), channel_id=1, source_target_pairs={{4,0},{28,16},{36,32},{60,48},{68,64},{92,80},{100,96},{124,112},{... | collective-permute-start | bytes 1671176 | tf_op jit(solution)/shard_map/ppermute | solution.py:40
  16.5 10.8 %collective-permute-start.4 = (bf16[2,272,512]{2,1,0:T(8,128)(2,1)S(1)}, bf16[2,272,512]{2,1,0:T(8,128)(2,1)S(1)}, u32[]{:S(2)}, u32[]{:S(2)}) collective-permute-start(bf16[2,272,512]{2,1,0:T(8,128)(2,1)S(1)} %collective-permute-done.3.refs_0_.refs_1_), channel_id=1, source_target_pairs={{32,0},{112,16},{0,32},{80,48},{96,64},{48,80},{64,96},{16,112},{3... | collective-permute-start | bytes 1671176 | tf_op jit(solution)/shard_map/ppermute | solution.py:40
  20.2 9.6 %collective-permute-start.2 = (bf16[2,272,512]{2,1,0:T(8,128)(2,1)S(1)}, bf16[2,272,512]{2,1,0:T(8,128)(2,1)S(1)}, u32[]{:S(2)}, u32[]{:S(2)}) collective-permute-start(bf16[2,272,512]{2,1,0:T(8,128)(2,1)S(1)} %collective-permute-done.1.refs_0_.refs_1_), channel_id=1, source_target_pairs={{1,0},{19,16},{33,32},{51,48},{65,64},{83,80},{97,96},{115,112},{5... | collective-permute-start | bytes 1671176 | tf_op jit(solution)/shard_map/ppermute | solution.py:40
  22.7 7.1 %collective-permute-start.10 = (bf16[528,512]{1,0:T(8,128)(2,1)S(1)}, bf16[528,512]{1,0:T(8,128)(2,1)S(1)}, u32[]{:S(2)}, u32[]{:S(2)}) collective-permute-start(bf16[528,512]{1,0:T(8,128)(2,1)S(1)} %shard_map.42), channel_id=1, source_target_pairs={{16,0},{0,16},{48,32},{32,48},{80,64},{64,80},{112,96},{96,112},{2... | collective-permute-start | bytes 1622024 | tf_op jit(solution)/shard_map/ppermute | solution.py:45
  22.9 7.6 %collective-permute-start.11 = (bf16[528,512]{1,0:T(8,128)(2,1)S(1)}, bf16[528,512]{1,0:T(8,128)(2,1)S(1)}, u32[]{:S(2)}, u32[]{:S(2)}) collective-permute-start(bf16[528,512]{1,0:T(8,128)(2,1)S(1)} %shard_map.43), channel_id=1, source_target_pairs={{16,0},{0,16},{48,32},{32,48},{80,64},{64,80},{112,96},{96,112},{2... | collective-permute-start | bytes 1622024 | tf_op jit(solution)/shard_map/ppermute | solution.py:45
  23.5 11.5 %collective-permute-start.13 = (bf16[2,272,512]{2,1,0:T(8,128)(2,1)S(1)}, bf16[2,272,512]{2,1,0:T(8,128)(2,1)S(1)}, u32[]{:S(2)}, u32[]{:S(2)}) collective-permute-start(bf16[2,272,512]{2,1,0:T(8,128)(2,1)S(1)} %collective-permute-done.6.refs_0_.refs_2_), channel_id=1, source_target_pairs={{32,0},{112,16},{0,32},{80,48},{96,64},{48,80},{64,96},{16,112},{3... | collective-permute-start | bytes 1671176 | tf_op jit(solution)/shard_map/ppermute | solution.py:40
  27.2 3.3 %collective-permute-start.12 = (bf16[528,512]{1,0:T(8,128)(2,1)S(1)}, bf16[528,512]{1,0:T(8,128)(2,1)S(1)}, u32[]{:S(2)}, u32[]{:S(2)}) collective-permute-start(bf16[528,512]{1,0:T(8,128)(2,1)S(1)} %shard_map.44), channel_id=1, source_target_pairs={{16,0},{0,16},{48,32},{32,48},{80,64},{64,80},{112,96},{96,112},{2... | collective-permute-start | bytes 1622024 | tf_op jit(solution)/shard_map/ppermute | solution.py:45
  29.8 2.9 %collective-permute-start.7 = (bf16[528,512]{1,0:T(8,128)(2,1)S(1)}, bf16[528,512]{1,0:T(8,128)(2,1)S(1)}, u32[]{:S(2)}, u32[]{:S(2)}) collective-permute-start(bf16[528,512]{1,0:T(8,128)(2,1)S(1)} %shard_map.39), channel_id=1, source_target_pairs={{16,0},{0,16},{48,32},{32,48},{80,64},{64,80},{112,96},{96,112},{2... | collective-permute-start | bytes 1622024 | tf_op jit(solution)/shard_map/ppermute | solution.py:45
  29.9 2.8 %collective-permute-start.8 = (bf16[528,512]{1,0:T(8,128)(2,1)S(1)}, bf16[528,512]{1,0:T(8,128)(2,1)S(1)}, u32[]{:S(2)}, u32[]{:S(2)}) collective-permute-start(bf16[528,512]{1,0:T(8,128)(2,1)S(1)} %shard_map.40), channel_id=1, source_target_pairs={{16,0},{0,16},{48,32},{32,48},{80,64},{64,80},{112,96},{96,112},{2... | collective-permute-start | bytes 1622024 | tf_op jit(solution)/shard_map/ppermute | solution.py:45
  30.5 2.8 %collective-permute-start.9 = (bf16[528,512]{1,0:T(8,128)(2,1)S(1)}, bf16[528,512]{1,0:T(8,128)(2,1)S(1)}, u32[]{:S(2)}, u32[]{:S(2)}) collective-permute-start(bf16[528,512]{1,0:T(8,128)(2,1)S(1)} %shard_map.41), channel_id=1, source_target_pairs={{16,0},{0,16},{48,32},{32,48},{80,64},{64,80},{112,96},{96,112},{2... | collective-permute-start | bytes 1622024 | tf_op jit(solution)/shard_map/ppermute | solution.py:45
  35.0 2.0 %collective-permute-start.14 = (bf16[528,512]{1,0:T(8,128)(2,1)S(1)}, bf16[528,512]{1,0:T(8,128)(2,1)S(1)}, u32[]{:S(2)}, u32[]{:S(2)}) collective-permute-start(bf16[528,512]{1,0:T(8,128)(2,1)S(1)} %shard_map.47), channel_id=1, source_target_pairs={{16,0},{0,16},{48,32},{32,48},{80,64},{64,80},{112,96},{96,112},{2... | collective-permute-start | bytes 1622024 | tf_op jit(solution)/shard_map/ppermute | solution.py:45
  38.5 5.1 %collective-permute-start.15 = (f32[4,1,256]{2,1,0:T(1,128)S(1)}, f32[4,1,256]{2,1,0:T(1,128)S(1)}, u32[]{:S(2)}, u32[]{:S(2)}) collective-permute-start(f32[4,1,256]{2,1,0:T(1,128)S(1)} %get-tuple-element.18), channel_id=1, source_target_pairs={{32,0},{112,16},{0,32},{80,48},{96,64},{48,80},{64,96},{16,112},{3... | collective-permute-start | bytes 12296 | tf_op jit(solution)/shard_map/ppermute | solution.py:40
  43.6 3.7 %collective-permute-start.16 = (f32[2,1,256]{2,1,0:T(1,128)S(1)}, f32[2,1,256]{2,1,0:T(1,128)S(1)}, u32[]{:S(2)}, u32[]{:S(2)}) collective-permute-start(f32[2,1,256]{2,1,0:T(1,128)S(1)} %shard_map.51), channel_id=1, source_target_pairs={{4,0},{28,16},{36,32},{60,48},{68,64},{92,80},{100,96},{124,112},{... | collective-permute-start | bytes 6152 | tf_op jit(solution)/shard_map/ppermute | solution.py:40
  47.3 3.9 %collective-permute-start.17 = (f32[1,1,256]{2,1,0:T(1,128)S(1)}, f32[1,1,256]{2,1,0:T(1,128)S(1)}, u32[]{:S(2)}, u32[]{:S(2)}) collective-permute-start(f32[1,1,256]{2,1,0:T(1,128)S(1)} %shard_map.53), channel_id=1, source_target_pairs={{1,0},{19,16},{33,32},{51,48},{65,64},{83,80},{97,96},{115,112},{5... | collective-permute-start | bytes 3080 | tf_op jit(solution)/shard_map/ppermute | solution.py:40

commit v8 on v7

--- a/solution.py
+++ b/solution.py
@@ -129,7 +129,7 @@
     mine = dict(zip(masks, refs[0 : len(masks)]))
     others = [n for n in keys if n]
     theirs = dict(zip(others, refs[len(masks) : len(masks) + len(others)]))
-    out_ref, first, second = refs[-4 if last else -3], *refs[-2:]
+    out_ref, first, second = refs[-3:]
 
     def numbers(meta, at):
         rank = meta[at : at + 1, 0:ROWS] * 256.0 + meta[at : at + 1, ROWS : 2 * ROWS]
@@ -182,13 +182,12 @@
                     valid = row - jnp.concatenate([column, column], axis=1) < limit
                     best = jnp.maximum(best, jnp.where(valid, score[r : r + 8, :], -1.0))
             found[m] = jnp.max(best, axis=0, keepdims=True)
-    old = None if begin else refs[-5 if last else -4]
-    for m in range(8):
+    old = None if begin else refs[-4]
+    skip = 4 if last else 0
+    for m in range(skip, 8):
         best = jnp.full((1, ROWS), -1.0, jnp.float32) if begin else old[m]
         best = jnp.maximum(best, found[m]) if m in found else best
-        out_ref[m] = best
-        if last and m > 3:
-            refs[-3][m - 4] = best
+        out_ref[m - skip] = best
 
 
 def match(queries, keys, mine, theirs, *prev, last=False):
@@ -196,16 +195,15 @@
     others = [n for n in keys if n]
     columns = len(queries) if len(queries) < len(keys) else 2 * len(keys)
     vmem = pl.BlockSpec(memory_space=pltpu.VMEM)
-    found = pl.pallas_call(
+    return pl.pallas_call(
         functools.partial(match_kernel, queries, keys, masks, not prev, last),
-        out_shape=[jax.ShapeDtypeStruct((k, 1, ROWS), jnp.float32) for k in ((8, 4) if last else (8,))],
+        out_shape=jax.ShapeDtypeStruct((4 if last else 8, 1, ROWS), jnp.float32),
         in_specs=[vmem] * (len(masks) + len(others) + len(prev)),
-        out_specs=[vmem] * (2 if last else 1),
+        out_specs=vmem,
         scratch_shapes=[pltpu.VMEM((columns, ROWS, 128), jnp.int32)] * 2,
         compiler_params=pltpu.CompilerParams(vmem_limit_bytes=GRANT),
         cost_estimate=SMALL,
     )(*[mine[m] for m in masks], *[theirs[n] for n in others], *prev)
-    return found if last else found[0]
 
 
 def fold_kernel(row, *refs):
@@ -247,7 +245,7 @@
     best, mine[7] = lax.optimization_barrier((best, mine[7]))
     theirs[7] = swap(pack(mine[7])[0])
     best = match((7,), (*near, *far), mine, theirs, best)
-    best, send = match((4, 6, 5, 7), (7,), mine, theirs, best, last=True)
+    send = match((4, 6, 5, 7), (7,), mine, theirs, best, last=True)
     send, mine[0] = lax.optimization_barrier((send, mine[0]))
     first = exchange(send, 4)
     send = fold(2, match((2, 3), every, mine, theirs), first)

time: 51.9 us -> 51.5 us (level)
  Pallas kernels: 14.2 us -> 13.6 us
    pallas_call x7, Pallas kernels: 12 us -> 11.4 us  [match(): pl.pallas_call(functools.partial(match_kernel, queries, keys, masks, not...]
where the time goes in v8:
time: 51.5 us; the launch traced here: 51.4 us
  starting transfers between devices  32.2 us (63%)
  Pallas kernels  13.6 us (26%)
  waiting for transfers between devices  5.47 us (11%)
    ppermute x10, starting transfers between devices, exchange(): return lax.ppermute(array, AXES, pairs)  29 us
    pallas_call x7, Pallas kernels, match(): pl.pallas_call(functools.partial(match_kernel, queries, keys, masks, not...  11.4 us
    ppermute x10, waiting for transfers between devices, exchange(): return lax.ppermute(array, AXES, pairs)  3.18 us
    ppermute x8, starting transfers between devices, swap(): return lax.ppermute(array, AXES, pairs)  3.15 us
    ppermute x8, waiting for transfers between devices, swap(): return lax.ppermute(array, AXES, pairs)  2.29 us
    pallas_call x1, Pallas kernels, payload(): pl.pallas_call(unit_kernel, out_shape=jax.ShapeDtypeStruct((PAY, E), jnp....  1.23 us
  transfers between devices with their start and end apart: 18, of which 6 were waited for; matrix products, arithmetic and copies ran while one was open for 0% of the time, Pallas kernels for 21%

profile of v8, /device:TPU:1, one launch (start us, length us, event | category | flops | bytes accessed | tf_op | source)
XLA Modules:
  0.0 51.4 jit_solution(13315977284744987655)
XLA Ops:
  0.0 1.2 %shard_map.37.first_ref = bf16[272,512]{1,0:T(8,128)(2,1)S(1)} custom-call(f32[256,512]{1,0:T(8,128)} %emb_hbm.1, s32[1,256]{1,0:T(1,128)} %bitcast.3, s32[1,256]{1,0:T(1,128)} %bitcast.4), custom_call_target="tpu_custom_call" | custom-call | flops 1000 | bytes 1000 | tf_op jit(solution)/shard_map/pallas_call | solution.py:72
  1.2 1.5 %collective-permute-start = (bf16[272,512]{1,0:T(8,128)(2,1)S(1)}, bf16[272,512]{1,0:T(8,128)(2,1)S(1)}, u32[]{:S(2)}, u32[]{:S(2)}) collective-permute-start(bf16[272,512]{1,0:T(8,128)(2,1)S(1)} %shard_map.37.first_ref), channel_id=1, source_target_pairs={{16,0},{0,16},{48,32},{32,48},{80,64},{64,80},{112,96},{96,112},{2... | collective-permute-start | bytes 835592 | tf_op jit(solution)/shard_map/ppermute | solution.py:45
  2.7 1.2 %collective-permute-done.second_ref = bf16[272,512]{1,0:T(8,128)(2,1)S(1)} collective-permute-done((bf16[272,512]{1,0:T(8,128)(2,1)S(1)}, bf16[272,512]{1,0:T(8,128)(2,1)S(1)}, u32[]{:S(2)}, u32[]{:S(2)}) %collective-permute-start) | collective-permute-done | bytes 278560 | tf_op jit(solution)/shard_map/ppermute | solution.py:45
  4.0 2.6 %collective-permute-start.5 = (bf16[2,272,512]{2,1,0:T(8,128)(2,1)S(1)}, bf16[2,272,512]{2,1,0:T(8,128)(2,1)S(1)}, u32[]{:S(2)}, u32[]{:S(2)}) collective-permute-start(bf16[2,272,512]{2,1,0:T(8,128)(2,1)S(1)} %shard_map.38.refs_0_), channel_id=1, source_target_pairs={{1,0},{19,16},{33,32},{51,48},{65,64},{83,80},{97,96},{115,112},{5... | collective-permute-start | bytes 1671176 | tf_op jit(solution)/shard_map/ppermute | solution.py:40
  6.6 2.7 %collective-permute-start.3 = (bf16[2,272,512]{2,1,0:T(8,128)(2,1)S(1)}, bf16[2,272,512]{2,1,0:T(8,128)(2,1)S(1)}, u32[]{:S(2)}, u32[]{:S(2)}) collective-permute-start(bf16[2,272,512]{2,1,0:T(8,128)(2,1)S(1)} %shard_map.38.refs_0_), channel_id=1, source_target_pairs={{4,0},{28,16},{36,32},{60,48},{68,64},{92,80},{100,96},{124,112},{... | collective-permute-start | bytes 1671176 | tf_op jit(solution)/shard_map/ppermute | solution.py:40
  9.3 3.8 %collective-permute-start.1 = (bf16[2,272,512]{2,1,0:T(8,128)(2,1)S(1)}, bf16[2,272,512]{2,1,0:T(8,128)(2,1)S(1)}, u32[]{:S(2)}, u32[]{:S(2)}) collective-permute-start(bf16[2,272,512]{2,1,0:T(8,128)(2,1)S(1)} %shard_map.38.refs_0_), channel_id=1, source_target_pairs={{32,0},{112,16},{0,32},{80,48},{96,64},{48,80},{64,96},{16,112},{3... | collective-permute-start | bytes 1671176 | tf_op jit(solution)/shard_map/ppermute | solution.py:40
  13.1 0.5 %collective-permute-done.5.refs_0_.refs_1_ = bf16[2,272,512]{2,1,0:T(8,128)(2,1)S(1)} collective-permute-done((bf16[2,272,512]{2,1,0:T(8,128)(2,1)S(1)}, bf16[2,272,512]{2,1,0:T(8,128)(2,1)S(1)}, u32[]{:S(2)}, u32[]{:S(2)}) %collective-permute-start.5) | collective-permute-done | bytes 557088 | tf_op jit(solution)/shard_map/ppermute | solution.py:40
  13.6 2.8 %collective-permute-start.6 = (bf16[2,272,512]{2,1,0:T(8,128)(2,1)S(1)}, bf16[2,272,512]{2,1,0:T(8,128)(2,1)S(1)}, u32[]{:S(2)}, u32[]{:S(2)}) collective-permute-start(bf16[2,272,512]{2,1,0:T(8,128)(2,1)S(1)} %collective-permute-done.5.refs_0_.refs_1_), channel_id=1, source_target_pairs={{4,0},{28,16},{36,32},{60,48},{68,64},{92,80},{100,96},{124,112},{... | collective-permute-start | bytes 1671176 | tf_op jit(solution)/shard_map/ppermute | solution.py:40
  16.5 3.8 %collective-permute-start.4 = (bf16[2,272,512]{2,1,0:T(8,128)(2,1)S(1)}, bf16[2,272,512]{2,1,0:T(8,128)(2,1)S(1)}, u32[]{:S(2)}, u32[]{:S(2)}) collective-permute-start(bf16[2,272,512]{2,1,0:T(8,128)(2,1)S(1)} %collective-permute-done.3.refs_0_.refs_1_), channel_id=1, source_target_pairs={{32,0},{112,16},{0,32},{80,48},{96,64},{48,80},{64,96},{16,112},{3... | collective-permute-start | bytes 1671176 | tf_op jit(solution)/shard_map/ppermute | solution.py:40
  20.2 2.5 %collective-permute-start.2 = (bf16[2,272,512]{2,1,0:T(8,128)(2,1)S(1)}, bf16[2,272,512]{2,1,0:T(8,128)(2,1)S(1)}, u32[]{:S(2)}, u32[]{:S(2)}) collective-permute-start(bf16[2,272,512]{2,1,0:T(8,128)(2,1)S(1)} %collective-permute-done.1.refs_0_.refs_1_), channel_id=1, source_target_pairs={{1,0},{19,16},{33,32},{51,48},{65,64},{83,80},{97,96},{115,112},{5... | collective-permute-start | bytes 1671176 | tf_op jit(solution)/shard_map/ppermute | solution.py:40
  22.7 0.1 collective-permute-start.10
  22.9 0.6 %collective-permute-start.11 = (bf16[528,512]{1,0:T(8,128)(2,1)S(1)}, bf16[528,512]{1,0:T(8,128)(2,1)S(1)}, u32[]{:S(2)}, u32[]{:S(2)}) collective-permute-start(bf16[528,512]{1,0:T(8,128)(2,1)S(1)} %shard_map.43), channel_id=1, source_target_pairs={{16,0},{0,16},{48,32},{32,48},{80,64},{64,80},{112,96},{96,112},{2... | collective-permute-start | bytes 1622024 | tf_op jit(solution)/shard_map/ppermute | solution.py:45
  23.5 3.7 %collective-permute-start.13 = (bf16[2,272,512]{2,1,0:T(8,128)(2,1)S(1)}, bf16[2,272,512]{2,1,0:T(8,128)(2,1)S(1)}, u32[]{:S(2)}, u32[]{:S(2)}) collective-permute-start(bf16[2,272,512]{2,1,0:T(8,128)(2,1)S(1)} %collective-permute-done.6.refs_0_.refs_2_), channel_id=1, source_target_pairs={{32,0},{112,16},{0,32},{80,48},{96,64},{48,80},{64,96},{16,112},{3... | collective-permute-start | bytes 1671176 | tf_op jit(solution)/shard_map/ppermute | solution.py:40
  27.2 0.1 collective-permute-start.12
  27.4 2.4 %collective-permute-done.2.refs_0_.refs_2_.refs_1_ = bf16[2,272,512]{2,1,0:T(8,128)(2,1)S(1)} collective-permute-done((bf16[2,272,512]{2,1,0:T(8,128)(2,1)S(1)}, bf16[2,272,512]{2,1,0:T(8,128)(2,1)S(1)}, u32[]{:S(2)}, u32[]{:S(2)}) %collective-permute-start.2) | collective-permute-done | bytes 557088 | tf_op jit(solution)/shard_map/ppermute | solution.py:40
  29.9 0.6 %collective-permute-start.8 = (bf16[528,512]{1,0:T(8,128)(2,1)S(1)}, bf16[528,512]{1,0:T(8,128)(2,1)S(1)}, u32[]{:S(2)}, u32[]{:S(2)}) collective-permute-start(bf16[528,512]{1,0:T(8,128)(2,1)S(1)} %shard_map.40), channel_id=1, source_target_pairs={{16,0},{0,16},{48,32},{32,48},{80,64},{64,80},{112,96},{96,112},{2... | collective-permute-start | bytes 1622024 | tf_op jit(solution)/shard_map/ppermute | solution.py:45
  30.5 0.1 collective-permute-start.9
  30.6 2.1 %shard_map.45.refs_6_ = f32[8,1,256]{2,1,0:T(1,128)S(1)} custom-call(bf16[2,272,512]{2,1,0:T(8,128)(2,1)S(1)} %shard_map.38.refs_0_, bf16[2,272,512]{2,1,0:T(8,128)(2,1)S(1)} %collective-permute-done.1.refs_0_.refs_1_, bf16[2,272,512]{2,1,0:T(8,128)(2,1)S(1)} %collective-permute-done.2.refs_0_.refs_2_.refs_1_, ...), custom_call_target="tpu_custom_call" | custom-call | flops 1000 | bytes 1000 | tf_op jit(solution)/shard_map/pallas_call | solution.py:198
  32.7 0.6 %collective-permute-done.9.refs_5_.refs_7_.refs_8_.refs_6_ = bf16[528,512]{1,0:T(8,128)(2,1)S(1)} collective-permute-done((bf16[528,512]{1,0:T(8,128)(2,1)S(1)}, bf16[528,512]{1,0:T(8,128)(2,1)S(1)}, u32[]{:S(2)}, u32[]{:S(2)}) %collective-permute-start.9) | collective-permute-done | bytes 540704 | tf_op jit(solution)/shard_map/ppermute | solution.py:45
  33.3 1.6 %shard_map.46.refs_8_ = f32[8,1,256]{2,1,0:T(1,128)S(1)} custom-call(bf16[2,272,512]{2,1,0:T(8,128)(2,1)S(1)} %collective-permute-done.1.refs_0_.refs_1_, bf16[2,272,512]{2,1,0:T(8,128)(2,1)S(1)} %collective-permute-done.2.refs_0_.refs_2_.refs_1_, bf16[2,272,512]{2,1,0:T(8,128)(2,1)S(1)} %collective-permute-done.4.refs_0_.refs_3_.refs_2_, ...), custom_call_target="tpu_custom_call" | custom-call | flops 1000 | bytes 1000 | tf_op jit(solution)/shard_map/pallas_call | solution.py:198
  35.0 0.2 collective-permute-start.14
  35.2 1.3 %shard_map.48.refs_5_ = f32[8,1,256]{2,1,0:T(1,128)S(1)} custom-call(bf16[2,272,512]{2,1,0:T(8,128)(2,1)S(1)} %shard_map.38.refs_0_, bf16[2,272,512]{2,1,0:T(8,128)(2,1)S(1)} %collective-permute-done.13.refs_0_.refs_1_.refs_3_, bf16[528,512]{1,0:T(8,128)(2,1)S(1)} %collective-permute-done.10.refs_4_.refs_2_.refs_3_.refs_1_, ...), custom_call_target="tpu_custom_call" | custom-call | flops 1000 | bytes 1000 | tf_op jit(solution)/shard_map/pallas_call | solution.py:198
  36.5 0.5 collective-permute-done.14.refs_4_.refs_9_.refs_8_.refs_7_
  37.0 0.9 %shard_map.49 = f32[4,1,256]{2,1,0:T(1,128)S(1)} custom-call(bf16[2,272,512]{2,1,0:T(8,128)(2,1)S(1)} %collective-permute-done.1.refs_0_.refs_1_, bf16[2,272,512]{2,1,0:T(8,128)(2,1)S(1)} %collective-permute-done.2.refs_0_.refs_2_.refs_1_, bf16[2,272,512]{2,1,0:T(8,128)(2,1)S(1)} %collective-permute-done.4.refs_0_.refs_3_.refs_2_, ...), custom_call_target="tpu_custom_call" | custom-call | flops 1000 | bytes 1000 | tf_op jit(solution)/shard_map/pallas_call | solution.py:198
  37.9 2.7 %collective-permute-start.15 = (f32[4,1,256]{2,1,0:T(1,128)S(1)}, f32[4,1,256]{2,1,0:T(1,128)S(1)}, u32[]{:S(2)}, u32[]{:S(2)}) collective-permute-start(f32[4,1,256]{2,1,0:T(1,128)S(1)} %shard_map.49), channel_id=1, source_target_pairs={{32,0},{112,16},{0,32},{80,48},{96,64},{48,80},{64,96},{16,112},{3... | collective-permute-start | bytes 12296 | tf_op jit(solution)/shard_map/ppermute | solution.py:40
  40.6 2.6 %shard_map.50.refs_0_ = f32[8,1,256]{2,1,0:T(1,128)S(1)} custom-call(bf16[2,272,512]{2,1,0:T(8,128)(2,1)S(1)} %shard_map.38.refs_0_, bf16[2,272,512]{2,1,0:T(8,128)(2,1)S(1)} %collective-permute-done.3.refs_0_.refs_1_, bf16[2,272,512]{2,1,0:T(8,128)(2,1)S(1)} %collective-permute-done.6.refs_0_.refs_2_, ...), custom_call_target="tpu_custom_call" | custom-call | flops 1000 | bytes 1000 | tf_op jit(solution)/shard_map/pallas_call | solution.py:198
  43.2 2.1 %collective-permute-start.16 = (f32[2,1,256]{2,1,0:T(1,128)S(1)}, f32[2,1,256]{2,1,0:T(1,128)S(1)}, u32[]{:S(2)}, u32[]{:S(2)}) collective-permute-start(f32[2,1,256]{2,1,0:T(1,128)S(1)} %shard_map.51), channel_id=1, source_target_pairs={{4,0},{28,16},{36,32},{60,48},{68,64},{92,80},{100,96},{124,112},{... | collective-permute-start | bytes 6152 | tf_op jit(solution)/shard_map/ppermute | solution.py:40
  45.3 1.5 %shard_map.52.refs_0_ = f32[8,1,256]{2,1,0:T(1,128)S(1)} custom-call(bf16[2,272,512]{2,1,0:T(8,128)(2,1)S(1)} %shard_map.38.refs_0_, bf16[2,272,512]{2,1,0:T(8,128)(2,1)S(1)} %collective-permute-done.5.refs_0_.refs_1_, bf16[528,512]{1,0:T(8,128)(2,1)S(1)} %collective-permute-done.10.refs_4_.refs_2_.refs_3_.refs_1_, ...), custom_call_target="tpu_custom_call" | custom-call | flops 1000 | bytes 1000 | tf_op jit(solution)/shard_map/pallas_call | solution.py:198
  46.8 0.2 collective-permute-done.16.refs_2_
  47.0 2.4 %collective-permute-start.17 = (f32[1,1,256]{2,1,0:T(1,128)S(1)}, f32[1,1,256]{2,1,0:T(1,128)S(1)}, u32[]{:S(2)}, u32[]{:S(2)}) collective-permute-start(f32[1,1,256]{2,1,0:T(1,128)S(1)} %shard_map.53), channel_id=1, source_target_pairs={{1,0},{19,16},{33,32},{51,48},{65,64},{83,80},{97,96},{115,112},{5... | collective-permute-start | bytes 3080 | tf_op jit(solution)/shard_map/ppermute | solution.py:40
  49.4 1.5 %shard_map.54.refs_0_ = f32[8,1,256]{2,1,0:T(1,128)S(1)} custom-call(bf16[2,272,512]{2,1,0:T(8,128)(2,1)S(1)} %shard_map.38.refs_0_, bf16[528,512]{1,0:T(8,128)(2,1)S(1)} %collective-permute-done.10.refs_4_.refs_2_.refs_3_.refs_1_, bf16[528,512]{1,0:T(8,128)(2,1)S(1)} %collective-permute-done.11.refs_5_.refs_3_.refs_4_.refs_2_, ...), custom_call_target="tpu_custom_call" | custom-call | flops 1000 | bytes 1000 | tf_op jit(solution)/shard_map/pallas_call | solution.py:198
  50.8 0.6 %shard_map.55 = f32[1,256]{1,0:T(1,128)} custom-call(f32[8,1,256]{2,1,0:T(1,128)S(1)} %shard_map.54.refs_0_, f32[4,1,256]{2,1,0:T(1,128)S(1)} %collective-permute-done.15.refs_1_, f32[2,1,256]{2,1,0:T(1,128)S(1)} %collective-permute-done.16.refs_2_, f32[1,1,256]{2,1,0:T(1,128)S(1)} %collective-permute-done.17.refs_3_), custom_call_target="tpu_custom_call" | custom-call | flops 1000 | bytes 1000 | tf_op jit(solution)/shard_map/pallas_call | solution.py:220
  (23 shorter events, 0.4 us)
Async XLA Ops:
  1.2 2.7 %collective-permute-start = (bf16[272,512]{1,0:T(8,128)(2,1)S(1)}, bf16[272,512]{1,0:T(8,128)(2,1)S(1)}, u32[]{:S(2)}, u32[]{:S(2)}) collective-permute-start(bf16[272,512]{1,0:T(8,128)(2,1)S(1)} %shard_map.37.first_ref), channel_id=1, source_target_pairs={{16,0},{0,16},{48,32},{32,48},{80,64},{64,80},{112,96},{96,112},{2... | collective-permute-start | bytes 835592 | tf_op jit(solution)/shard_map/ppermute | solution.py:45
  4.0 9.7 %collective-permute-start.5 = (bf16[2,272,512]{2,1,0:T(8,128)(2,1)S(1)}, bf16[2,272,512]{2,1,0:T(8,128)(2,1)S(1)}, u32[]{:S(2)}, u32[]{:S(2)}) collective-permute-start(bf16[2,272,512]{2,1,0:T(8,128)(2,1)S(1)} %shard_map.38.refs_0_), channel_id=1, source_target_pairs={{1,0},{19,16},{33,32},{51,48},{65,64},{83,80},{97,96},{115,112},{5... | collective-permute-start | bytes 1671176 | tf_op jit(solution)/shard_map/ppermute | solution.py:40
  6.6 9.9 %collective-permute-start.3 = (bf16[2,272,512]{2,1,0:T(8,128)(2,1)S(1)}, bf16[2,272,512]{2,1,0:T(8,128)(2,1)S(1)}, u32[]{:S(2)}, u32[]{:S(2)}) collective-permute-start(bf16[2,272,512]{2,1,0:T(8,128)(2,1)S(1)} %shard_map.38.refs_0_), channel_id=1, source_target_pairs={{4,0},{28,16},{36,32},{60,48},{68,64},{92,80},{100,96},{124,112},{... | collective-permute-start | bytes 1671176 | tf_op jit(solution)/shard_map/ppermute | solution.py:40
  9.3 10.9 %collective-permute-start.1 = (bf16[2,272,512]{2,1,0:T(8,128)(2,1)S(1)}, bf16[2,272,512]{2,1,0:T(8,128)(2,1)S(1)}, u32[]{:S(2)}, u32[]{:S(2)}) collective-permute-start(bf16[2,272,512]{2,1,0:T(8,128)(2,1)S(1)} %shard_map.38.refs_0_), channel_id=1, source_target_pairs={{32,0},{112,16},{0,32},{80,48},{96,64},{48,80},{64,96},{16,112},{3... | collective-permute-start | bytes 1671176 | tf_op jit(solution)/shard_map/ppermute | solution.py:40
  13.6 9.8 %collective-permute-start.6 = (bf16[2,272,512]{2,1,0:T(8,128)(2,1)S(1)}, bf16[2,272,512]{2,1,0:T(8,128)(2,1)S(1)}, u32[]{:S(2)}, u32[]{:S(2)}) collective-permute-start(bf16[2,272,512]{2,1,0:T(8,128)(2,1)S(1)} %collective-permute-done.5.refs_0_.refs_1_), channel_id=1, source_target_pairs={{4,0},{28,16},{36,32},{60,48},{68,64},{92,80},{100,96},{124,112},{... | collective-permute-start | bytes 1671176 | tf_op jit(solution)/shard_map/ppermute | solution.py:40
  16.5 10.8 %collective-permute-start.4 = (bf16[2,272,512]{2,1,0:T(8,128)(2,1)S(1)}, bf16[2,272,512]{2,1,0:T(8,128)(2,1)S(1)}, u32[]{:S(2)}, u32[]{:S(2)}) collective-permute-start(bf16[2,272,512]{2,1,0:T(8,128)(2,1)S(1)} %collective-permute-done.3.refs_0_.refs_1_), channel_id=1, source_target_pairs={{32,0},{112,16},{0,32},{80,48},{96,64},{48,80},{64,96},{16,112},{3... | collective-permute-start | bytes 1671176 | tf_op jit(solution)/shard_map/ppermute | solution.py:40
  20.2 9.6 %collective-permute-start.2 = (bf16[2,272,512]{2,1,0:T(8,128)(2,1)S(1)}, bf16[2,272,512]{2,1,0:T(8,128)(2,1)S(1)}, u32[]{:S(2)}, u32[]{:S(2)}) collective-permute-start(bf16[2,272,512]{2,1,0:T(8,128)(2,1)S(1)} %collective-permute-done.1.refs_0_.refs_1_), channel_id=1, source_target_pairs={{1,0},{19,16},{33,32},{51,48},{65,64},{83,80},{97,96},{115,112},{5... | collective-permute-start | bytes 1671176 | tf_op jit(solution)/shard_map/ppermute | solution.py:40
  22.7 7.1 %collective-permute-start.10 = (bf16[528,512]{1,0:T(8,128)(2,1)S(1)}, bf16[528,512]{1,0:T(8,128)(2,1)S(1)}, u32[]{:S(2)}, u32[]{:S(2)}) collective-permute-start(bf16[528,512]{1,0:T(8,128)(2,1)S(1)} %shard_map.42), channel_id=1, source_target_pairs={{16,0},{0,16},{48,32},{32,48},{80,64},{64,80},{112,96},{96,112},{2... | collective-permute-start | bytes 1622024 | tf_op jit(solution)/shard_map/ppermute | solution.py:45
  22.9 7.6 %collective-permute-start.11 = (bf16[528,512]{1,0:T(8,128)(2,1)S(1)}, bf16[528,512]{1,0:T(8,128)(2,1)S(1)}, u32[]{:S(2)}, u32[]{:S(2)}) collective-permute-start(bf16[528,512]{1,0:T(8,128)(2,1)S(1)} %shard_map.43), channel_id=1, source_target_pairs={{16,0},{0,16},{48,32},{32,48},{80,64},{64,80},{112,96},{96,112},{2... | collective-permute-start | bytes 1622024 | tf_op jit(solution)/shard_map/ppermute | solution.py:45
  23.5 11.5 %collective-permute-start.13 = (bf16[2,272,512]{2,1,0:T(8,128)(2,1)S(1)}, bf16[2,272,512]{2,1,0:T(8,128)(2,1)S(1)}, u32[]{:S(2)}, u32[]{:S(2)}) collective-permute-start(bf16[2,272,512]{2,1,0:T(8,128)(2,1)S(1)} %collective-permute-done.6.refs_0_.refs_2_), channel_id=1, source_target_pairs={{32,0},{112,16},{0,32},{80,48},{96,64},{48,80},{64,96},{16,112},{3... | collective-permute-start | bytes 1671176 | tf_op jit(solution)/shard_map/ppermute | solution.py:40
  27.2 3.3 %collective-permute-start.12 = (bf16[528,512]{1,0:T(8,128)(2,1)S(1)}, bf16[528,512]{1,0:T(8,128)(2,1)S(1)}, u32[]{:S(2)}, u32[]{:S(2)}) collective-permute-start(bf16[528,512]{1,0:T(8,128)(2,1)S(1)} %shard_map.44), channel_id=1, source_target_pairs={{16,0},{0,16},{48,32},{32,48},{80,64},{64,80},{112,96},{96,112},{2... | collective-permute-start | bytes 1622024 | tf_op jit(solution)/shard_map/ppermute | solution.py:45
  29.8 2.9 %collective-permute-start.7 = (bf16[528,512]{1,0:T(8,128)(2,1)S(1)}, bf16[528,512]{1,0:T(8,128)(2,1)S(1)}, u32[]{:S(2)}, u32[]{:S(2)}) collective-permute-start(bf16[528,512]{1,0:T(8,128)(2,1)S(1)} %shard_map.39), channel_id=1, source_target_pairs={{16,0},{0,16},{48,32},{32,48},{80,64},{64,80},{112,96},{96,112},{2... | collective-permute-start | bytes 1622024 | tf_op jit(solution)/shard_map/ppermute | solution.py:45
  29.9 2.8 %collective-permute-start.8 = (bf16[528,512]{1,0:T(8,128)(2,1)S(1)}, bf16[528,512]{1,0:T(8,128)(2,1)S(1)}, u32[]{:S(2)}, u32[]{:S(2)}) collective-permute-start(bf16[528,512]{1,0:T(8,128)(2,1)S(1)} %shard_map.40), channel_id=1, source_target_pairs={{16,0},{0,16},{48,32},{32,48},{80,64},{64,80},{112,96},{96,112},{2... | collective-permute-start | bytes 1622024 | tf_op jit(solution)/shard_map/ppermute | solution.py:45
  30.5 2.8 %collective-permute-start.9 = (bf16[528,512]{1,0:T(8,128)(2,1)S(1)}, bf16[528,512]{1,0:T(8,128)(2,1)S(1)}, u32[]{:S(2)}, u32[]{:S(2)}) collective-permute-start(bf16[528,512]{1,0:T(8,128)(2,1)S(1)} %shard_map.41), channel_id=1, source_target_pairs={{16,0},{0,16},{48,32},{32,48},{80,64},{64,80},{112,96},{96,112},{2... | collective-permute-start | bytes 1622024 | tf_op jit(solution)/shard_map/ppermute | solution.py:45
  35.0 2.0 %collective-permute-start.14 = (bf16[528,512]{1,0:T(8,128)(2,1)S(1)}, bf16[528,512]{1,0:T(8,128)(2,1)S(1)}, u32[]{:S(2)}, u32[]{:S(2)}) collective-permute-start(bf16[528,512]{1,0:T(8,128)(2,1)S(1)} %shard_map.47), channel_id=1, source_target_pairs={{16,0},{0,16},{48,32},{32,48},{80,64},{64,80},{112,96},{96,112},{2... | collective-permute-start | bytes 1622024 | tf_op jit(solution)/shard_map/ppermute | solution.py:45
  37.9 5.4 %collective-permute-start.15 = (f32[4,1,256]{2,1,0:T(1,128)S(1)}, f32[4,1,256]{2,1,0:T(1,128)S(1)}, u32[]{:S(2)}, u32[]{:S(2)}) collective-permute-start(f32[4,1,256]{2,1,0:T(1,128)S(1)} %shard_map.49), channel_id=1, source_target_pairs={{32,0},{112,16},{0,32},{80,48},{96,64},{48,80},{64,96},{16,112},{3... | collective-permute-start | bytes 12296 | tf_op jit(solution)/shard_map/ppermute | solution.py:40
  43.2 3.7 %collective-permute-start.16 = (f32[2,1,256]{2,1,0:T(1,128)S(1)}, f32[2,1,256]{2,1,0:T(1,128)S(1)}, u32[]{:S(2)}, u32[]{:S(2)}) collective-permute-start(f32[2,1,256]{2,1,0:T(1,128)S(1)} %shard_map.51), channel_id=1, source_target_pairs={{4,0},{28,16},{36,32},{60,48},{68,64},{92,80},{100,96},{124,112},{... | collective-permute-start | bytes 6152 | tf_op jit(solution)/shard_map/ppermute | solution.py:40
  47.0 3.9 %collective-permute-start.17 = (f32[1,1,256]{2,1,0:T(1,128)S(1)}, f32[1,1,256]{2,1,0:T(1,128)S(1)}, u32[]{:S(2)}, u32[]{:S(2)}) collective-permute-start(f32[1,1,256]{2,1,0:T(1,128)S(1)} %shard_map.53), channel_id=1, source_target_pairs={{1,0},{19,16},{33,32},{51,48},{65,64},{83,80},{97,96},{115,112},{5... | collective-permute-start | bytes 3080 | tf_op jit(solution)/shard_map/ppermute | solution.py:40

commit v9 on v8

--- a/solution.py
+++ b/solution.py
@@ -242,13 +242,14 @@
     every = (*near, *far, 7)
     best = match((4, 6, 5), near, mine, theirs)
     best = match((4, 6, 5), far, mine, theirs, best)
-    best, mine[7] = lax.optimization_barrier((best, mine[7]))
+    part = match((2, 3), near, mine, theirs)
+    part, best, mine[7] = lax.optimization_barrier((part, best, mine[7]))
     theirs[7] = swap(pack(mine[7])[0])
     best = match((7,), (*near, *far), mine, theirs, best)
     send = match((4, 6, 5, 7), (7,), mine, theirs, best, last=True)
     send, mine[0] = lax.optimization_barrier((send, mine[0]))
     first = exchange(send, 4)
-    send = fold(2, match((2, 3), every, mine, theirs), first)
+    send = fold(2, match((2, 3), (*far, 7), mine, theirs, part), first)
     send, mine[0] = lax.optimization_barrier((send, mine[0]))
     second = exchange(send, 2)
     send = fold(1, match((1,), every, mine, theirs), first, second)

time: 51.5 us -> 51.1 us (level)
  starting transfers between devices: 32.2 us -> 27.4 us
  waiting for transfers between devices: 5.47 us -> 9.54 us
    ppermute x10, starting transfers between devices: 29 us -> 23.9 us  [exchange(): return lax.ppermute(array, AXES, pairs)]
    ppermute x10, waiting for transfers between devices: 3.18 us -> 8.1 us  [exchange(): return lax.ppermute(array, AXES, pairs)]
    ppermute x8, waiting for transfers between devices: 2.29 us -> 1.44 us  [swap(): return lax.ppermute(array, AXES, pairs)]
    pallas_call x7 -> x8, Pallas kernels: 11.4 us -> 11.8 us  [match(): pl.pallas_call(functools.partial(match_kernel, queries, keys, masks, not...]
  transfers between devices with their start and end apart: 18 -> 18, of which waited for: 6 -> 9; matrix products, arithmetic and copies ran while one was open for 0% -> 0% of each run, Pallas kernels for 21% -> 22%
where the time goes in v9:
time: 51.1 us; the launch traced here: 51 us
  starting transfers between devices  27.4 us (54%)
  Pallas kernels  13.9 us (27%)
  waiting for transfers between devices  9.54 us (19%)
    ppermute x10, starting transfers between devices, exchange(): return lax.ppermute(array, AXES, pairs)  23.9 us
    pallas_call x8, Pallas kernels, match(): pl.pallas_call(functools.partial(match_kernel, queries, keys, masks, not...  11.8 us
    ppermute x10, waiting for transfers between devices, exchange(): return lax.ppermute(array, AXES, pairs)  8.1 us
    ppermute x8, starting transfers between devices, swap(): return lax.ppermute(array, AXES, pairs)  3.42 us
    ppermute x8, waiting for transfers between devices, swap(): return lax.ppermute(array, AXES, pairs)  1.44 us
    pallas_call x1, Pallas kernels, payload(): pl.pallas_call(unit_kernel, out_shape=jax.ShapeDtypeStruct((PAY, E), jnp....  1.23 us
  transfers between devices with their start and end apart: 18, of which 9 were waited for; matrix products, arithmetic and copies ran while one was open for 0% of the time, Pallas kernels for 22%

profile of v9, /device:TPU:1, one launch (start us, length us, event | category | flops | bytes accessed | tf_op | source)
XLA Modules:
  0.0 51.0 jit_solution(1956113639182521096)
XLA Ops:
  0.0 1.2 %shard_map.37.first_ref = bf16[272,512]{1,0:T(8,128)(2,1)S(1)} custom-call(f32[256,512]{1,0:T(8,128)} %emb_hbm.1, s32[1,256]{1,0:T(1,128)} %bitcast.3, s32[1,256]{1,0:T(1,128)} %bitcast.4), custom_call_target="tpu_custom_call" | custom-call | flops 1000 | bytes 1000 | tf_op jit(solution)/shard_map/pallas_call | solution.py:72
  1.2 1.5 %collective-permute-start = (bf16[272,512]{1,0:T(8,128)(2,1)S(1)}, bf16[272,512]{1,0:T(8,128)(2,1)S(1)}, u32[]{:S(2)}, u32[]{:S(2)}) collective-permute-start(bf16[272,512]{1,0:T(8,128)(2,1)S(1)} %shard_map.37.first_ref), channel_id=1, source_target_pairs={{16,0},{0,16},{48,32},{32,48},{80,64},{64,80},{112,96},{96,112},{2... | collective-permute-start | bytes 835592 | tf_op jit(solution)/shard_map/ppermute | solution.py:45
  2.7 1.2 %collective-permute-done.second_ref = bf16[272,512]{1,0:T(8,128)(2,1)S(1)} collective-permute-done((bf16[272,512]{1,0:T(8,128)(2,1)S(1)}, bf16[272,512]{1,0:T(8,128)(2,1)S(1)}, u32[]{:S(2)}, u32[]{:S(2)}) %collective-permute-start) | collective-permute-done | bytes 278560 | tf_op jit(solution)/shard_map/ppermute | solution.py:45
  4.0 2.6 %collective-permute-start.2 = (bf16[2,272,512]{2,1,0:T(8,128)(2,1)S(1)}, bf16[2,272,512]{2,1,0:T(8,128)(2,1)S(1)}, u32[]{:S(2)}, u32[]{:S(2)}) collective-permute-start(bf16[2,272,512]{2,1,0:T(8,128)(2,1)S(1)} %shard_map.38.refs_0_), channel_id=1, source_target_pairs={{1,0},{19,16},{33,32},{51,48},{65,64},{83,80},{97,96},{115,112},{5... | collective-permute-start | bytes 1671176 | tf_op jit(solution)/shard_map/ppermute | solution.py:40
  6.6 3.8 %collective-permute-start.7 = (bf16[2,272,512]{2,1,0:T(8,128)(2,1)S(1)}, bf16[2,272,512]{2,1,0:T(8,128)(2,1)S(1)}, u32[]{:S(2)}, u32[]{:S(2)}) collective-permute-start(bf16[2,272,512]{2,1,0:T(8,128)(2,1)S(1)} %shard_map.38.refs_0_), channel_id=1, source_target_pairs={{32,0},{112,16},{0,32},{80,48},{96,64},{48,80},{64,96},{16,112},{3... | collective-permute-start | bytes 1671176 | tf_op jit(solution)/shard_map/ppermute | solution.py:40
  10.4 2.7 %collective-permute-start.1 = (bf16[2,272,512]{2,1,0:T(8,128)(2,1)S(1)}, bf16[2,272,512]{2,1,0:T(8,128)(2,1)S(1)}, u32[]{:S(2)}, u32[]{:S(2)}) collective-permute-start(bf16[2,272,512]{2,1,0:T(8,128)(2,1)S(1)} %shard_map.38.refs_0_), channel_id=1, source_target_pairs={{4,0},{28,16},{36,32},{60,48},{68,64},{92,80},{100,96},{124,112},{... | collective-permute-start | bytes 1671176 | tf_op jit(solution)/shard_map/ppermute | solution.py:40
  13.1 0.5 %collective-permute-done.2.refs_0_.refs_1_ = bf16[2,272,512]{2,1,0:T(8,128)(2,1)S(1)} collective-permute-done((bf16[2,272,512]{2,1,0:T(8,128)(2,1)S(1)}, bf16[2,272,512]{2,1,0:T(8,128)(2,1)S(1)}, u32[]{:S(2)}, u32[]{:S(2)}) %collective-permute-start.2) | collective-permute-done | bytes 557088 | tf_op jit(solution)/shard_map/ppermute | solution.py:40
  13.6 2.8 %collective-permute-start.3 = (bf16[2,272,512]{2,1,0:T(8,128)(2,1)S(1)}, bf16[2,272,512]{2,1,0:T(8,128)(2,1)S(1)}, u32[]{:S(2)}, u32[]{:S(2)}) collective-permute-start(bf16[2,272,512]{2,1,0:T(8,128)(2,1)S(1)} %collective-permute-done.2.refs_0_.refs_1_), channel_id=1, source_target_pairs={{4,0},{28,16},{36,32},{60,48},{68,64},{92,80},{100,96},{124,112},{... | collective-permute-start | bytes 1671176 | tf_op jit(solution)/shard_map/ppermute | solution.py:40
  16.5 0.8 %collective-permute-done.7.refs_0_.refs_1_ = bf16[2,272,512]{2,1,0:T(8,128)(2,1)S(1)} collective-permute-done((bf16[2,272,512]{2,1,0:T(8,128)(2,1)S(1)}, bf16[2,272,512]{2,1,0:T(8,128)(2,1)S(1)}, u32[]{:S(2)}, u32[]{:S(2)}) %collective-permute-start.7) | collective-permute-done | bytes 557088 | tf_op jit(solution)/shard_map/ppermute | solution.py:40
  17.3 1.7 %collective-permute-start.8 = (bf16[2,272,512]{2,1,0:T(8,128)(2,1)S(1)}, bf16[2,272,512]{2,1,0:T(8,128)(2,1)S(1)}, u32[]{:S(2)}, u32[]{:S(2)}) collective-permute-start(bf16[2,272,512]{2,1,0:T(8,128)(2,1)S(1)} %collective-permute-done.7.refs_0_.refs_1_), channel_id=1, source_target_pairs={{1,0},{19,16},{33,32},{51,48},{65,64},{83,80},{97,96},{115,112},{5... | collective-permute-start | bytes 1671176 | tf_op jit(solution)/shard_map/ppermute | solution.py:40
  18.9 1.1 %collective-permute-done.1.refs_0_.refs_1_ = bf16[2,272,512]{2,1,0:T(8,128)(2,1)S(1)} collective-permute-done((bf16[2,272,512]{2,1,0:T(8,128)(2,1)S(1)}, bf16[2,272,512]{2,1,0:T(8,128)(2,1)S(1)}, u32[]{:S(2)}, u32[]{:S(2)}) %collective-permute-start.1) | collective-permute-done | bytes 557088 | tf_op jit(solution)/shard_map/ppermute | solution.py:40
  20.0 2.7 %collective-permute-start.5 = (bf16[2,272,512]{2,1,0:T(8,128)(2,1)S(1)}, bf16[2,272,512]{2,1,0:T(8,128)(2,1)S(1)}, u32[]{:S(2)}, u32[]{:S(2)}) collective-permute-start(bf16[2,272,512]{2,1,0:T(8,128)(2,1)S(1)} %collective-permute-done.1.refs_0_.refs_1_), channel_id=1, source_target_pairs={{32,0},{112,16},{0,32},{80,48},{96,64},{48,80},{64,96},{16,112},{3... | collective-permute-start | bytes 1671176 | tf_op jit(solution)/shard_map/ppermute | solution.py:40
  22.9 0.6 %collective-permute-start.10 = (bf16[528,512]{1,0:T(8,128)(2,1)S(1)}, bf16[528,512]{1,0:T(8,128)(2,1)S(1)}, u32[]{:S(2)}, u32[]{:S(2)}) collective-permute-start(bf16[528,512]{1,0:T(8,128)(2,1)S(1)} %shard_map.42), channel_id=1, source_target_pairs={{16,0},{0,16},{48,32},{32,48},{80,64},{64,80},{112,96},{96,112},{2... | collective-permute-start | bytes 1622024 | tf_op jit(solution)/shard_map/ppermute | solution.py:45
  23.5 2.5 %collective-permute-done.3.refs_0_.refs_2_.refs_1_ = bf16[2,272,512]{2,1,0:T(8,128)(2,1)S(1)} collective-permute-done((bf16[2,272,512]{2,1,0:T(8,128)(2,1)S(1)}, bf16[2,272,512]{2,1,0:T(8,128)(2,1)S(1)}, u32[]{:S(2)}, u32[]{:S(2)}) %collective-permute-start.3) | collective-permute-done | bytes 557088 | tf_op jit(solution)/shard_map/ppermute | solution.py:40
  26.0 1.1 %collective-permute-start.13 = (bf16[2,272,512]{2,1,0:T(8,128)(2,1)S(1)}, bf16[2,272,512]{2,1,0:T(8,128)(2,1)S(1)}, u32[]{:S(2)}, u32[]{:S(2)}) collective-permute-start(bf16[2,272,512]{2,1,0:T(8,128)(2,1)S(1)} %collective-permute-done.3.refs_0_.refs_2_.refs_1_), channel_id=1, source_target_pairs={{32,0},{112,16},{0,32},{80,48},{96,64},{48,80},{64,96},{16,112},{3... | collective-permute-start | bytes 1671176 | tf_op jit(solution)/shard_map/ppermute | solution.py:40
  27.4 2.2 %collective-permute-done.5.refs_0_.refs_3_.refs_2_ = bf16[2,272,512]{2,1,0:T(8,128)(2,1)S(1)} collective-permute-done((bf16[2,272,512]{2,1,0:T(8,128)(2,1)S(1)}, bf16[2,272,512]{2,1,0:T(8,128)(2,1)S(1)}, u32[]{:S(2)}, u32[]{:S(2)}) %collective-permute-start.5) | collective-permute-done | bytes 557088 | tf_op jit(solution)/shard_map/ppermute | solution.py:40
  29.7 0.6 %collective-permute-start.4 = (bf16[528,512]{1,0:T(8,128)(2,1)S(1)}, bf16[528,512]{1,0:T(8,128)(2,1)S(1)}, u32[]{:S(2)}, u32[]{:S(2)}) collective-permute-start(bf16[528,512]{1,0:T(8,128)(2,1)S(1)} %shard_map.39), channel_id=1, source_target_pairs={{16,0},{0,16},{48,32},{32,48},{80,64},{64,80},{112,96},{96,112},{2... | collective-permute-start | bytes 1622024 | tf_op jit(solution)/shard_map/ppermute | solution.py:45
  30.4 1.5 %shard_map.45.refs_6_ = f32[8,1,256]{2,1,0:T(1,128)S(1)} custom-call(bf16[2,272,512]{2,1,0:T(8,128)(2,1)S(1)} %shard_map.38.refs_0_, bf16[2,272,512]{2,1,0:T(8,128)(2,1)S(1)} %collective-permute-done.1.refs_0_.refs_1_, bf16[2,272,512]{2,1,0:T(8,128)(2,1)S(1)} %collective-permute-done.3.refs_0_.refs_2_.refs_1_, ...), custom_call_target="tpu_custom_call" | custom-call | flops 1000 | bytes 1000 | tf_op jit(solution)/shard_map/pallas_call | solution.py:198
  31.9 2.1 %shard_map.46.refs_6_ = f32[8,1,256]{2,1,0:T(1,128)S(1)} custom-call(bf16[2,272,512]{2,1,0:T(8,128)(2,1)S(1)} %shard_map.38.refs_0_, bf16[2,272,512]{2,1,0:T(8,128)(2,1)S(1)} %collective-permute-done.7.refs_0_.refs_1_, bf16[2,272,512]{2,1,0:T(8,128)(2,1)S(1)} %collective-permute-done.8.refs_0_.refs_2_.refs_1_, ...), custom_call_target="tpu_custom_call" | custom-call | flops 1000 | bytes 1000 | tf_op jit(solution)/shard_map/pallas_call | solution.py:198
  34.0 1.6 %shard_map.47.refs_8_ = f32[8,1,256]{2,1,0:T(1,128)S(1)} custom-call(bf16[2,272,512]{2,1,0:T(8,128)(2,1)S(1)} %collective-permute-done.7.refs_0_.refs_1_, bf16[2,272,512]{2,1,0:T(8,128)(2,1)S(1)} %collective-permute-done.8.refs_0_.refs_2_.refs_1_, bf16[2,272,512]{2,1,0:T(8,128)(2,1)S(1)} %collective-permute-done.5.refs_0_.refs_3_.refs_2_, ...), custom_call_target="tpu_custom_call" | custom-call | flops 1000 | bytes 1000 | tf_op jit(solution)/shard_map/pallas_call | solution.py:198
  35.7 0.5 collective-permute-start.14
  36.2 1.3 %shard_map.50.refs_5_ = f32[8,1,256]{2,1,0:T(1,128)S(1)} custom-call(bf16[2,272,512]{2,1,0:T(8,128)(2,1)S(1)} %shard_map.38.refs_0_, bf16[2,272,512]{2,1,0:T(8,128)(2,1)S(1)} %collective-permute-done.13.refs_0_.refs_1_.refs_3_, bf16[528,512]{1,0:T(8,128)(2,1)S(1)} %collective-permute-done.10.refs_3_.refs_4_.refs_2_.refs_1_, ...), custom_call_target="tpu_custom_call" | custom-call | flops 1000 | bytes 1000 | tf_op jit(solution)/shard_map/pallas_call | solution.py:198
  37.5 0.2 collective-permute-done.14.refs_5_.refs_4_.refs_8_.refs_7_
  37.7 0.8 %shard_map.51 = f32[4,1,256]{2,1,0:T(1,128)S(1)} custom-call(bf16[2,272,512]{2,1,0:T(8,128)(2,1)S(1)} %collective-permute-done.7.refs_0_.refs_1_, bf16[2,272,512]{2,1,0:T(8,128)(2,1)S(1)} %collective-permute-done.8.refs_0_.refs_2_.refs_1_, bf16[2,272,512]{2,1,0:T(8,128)(2,1)S(1)} %collective-permute-done.5.refs_0_.refs_3_.refs_2_, ...), custom_call_target="tpu_custom_call" | custom-call | flops 1000 | bytes 1000 | tf_op jit(solution)/shard_map/pallas_call | solution.py:198
  38.6 2.9 %collective-permute-start.15 = (f32[4,1,256]{2,1,0:T(1,128)S(1)}, f32[4,1,256]{2,1,0:T(1,128)S(1)}, u32[]{:S(2)}, u32[]{:S(2)}) collective-permute-start(f32[4,1,256]{2,1,0:T(1,128)S(1)} %shard_map.51), channel_id=1, source_target_pairs={{32,0},{112,16},{0,32},{80,48},{96,64},{48,80},{64,96},{16,112},{3... | collective-permute-start | bytes 12296 | tf_op jit(solution)/shard_map/ppermute | solution.py:40
  41.5 1.5 %shard_map.49.refs_0_ = f32[8,1,256]{2,1,0:T(1,128)S(1)} custom-call(bf16[2,272,512]{2,1,0:T(8,128)(2,1)S(1)} %collective-permute-done.1.refs_0_.refs_1_, bf16[2,272,512]{2,1,0:T(8,128)(2,1)S(1)} %collective-permute-done.3.refs_0_.refs_2_.refs_1_, bf16[528,512]{1,0:T(8,128)(2,1)S(1)} %collective-permute-done.4.refs_3_.refs_2_.refs_5_.refs_4_, ...), custom_call_target="tpu_custom_call" | custom-call | flops 1000 | bytes 1000 | tf_op jit(solution)/shard_map/pallas_call | solution.py:198
  43.0 2.1 %collective-permute-start.16 = (f32[2,1,256]{2,1,0:T(1,128)S(1)}, f32[2,1,256]{2,1,0:T(1,128)S(1)}, u32[]{:S(2)}, u32[]{:S(2)}) collective-permute-start(f32[2,1,256]{2,1,0:T(1,128)S(1)} %shard_map.52), channel_id=1, source_target_pairs={{4,0},{28,16},{36,32},{60,48},{68,64},{92,80},{100,96},{124,112},{... | collective-permute-start | bytes 6152 | tf_op jit(solution)/shard_map/ppermute | solution.py:40
  45.2 1.4 %shard_map.53.refs_0_ = f32[8,1,256]{2,1,0:T(1,128)S(1)} custom-call(bf16[2,272,512]{2,1,0:T(8,128)(2,1)S(1)} %shard_map.38.refs_0_, bf16[2,272,512]{2,1,0:T(8,128)(2,1)S(1)} %collective-permute-done.2.refs_0_.refs_1_, bf16[528,512]{1,0:T(8,128)(2,1)S(1)} %collective-permute-done.10.refs_3_.refs_4_.refs_2_.refs_1_, ...), custom_call_target="tpu_custom_call" | custom-call | flops 1000 | bytes 1000 | tf_op jit(solution)/shard_map/pallas_call | solution.py:198
  46.8 1.4 %collective-permute-start.17 = (f32[1,1,256]{2,1,0:T(1,128)S(1)}, f32[1,1,256]{2,1,0:T(1,128)S(1)}, u32[]{:S(2)}, u32[]{:S(2)}) collective-permute-start(f32[1,1,256]{2,1,0:T(1,128)S(1)} %shard_map.54), channel_id=1, source_target_pairs={{1,0},{19,16},{33,32},{51,48},{65,64},{83,80},{97,96},{115,112},{5... | collective-permute-start | bytes 3080 | tf_op jit(solution)/shard_map/ppermute | solution.py:40
  48.2 1.4 %shard_map.55.refs_0_ = f32[8,1,256]{2,1,0:T(1,128)S(1)} custom-call(bf16[2,272,512]{2,1,0:T(8,128)(2,1)S(1)} %shard_map.38.refs_0_, bf16[528,512]{1,0:T(8,128)(2,1)S(1)} %collective-permute-done.10.refs_3_.refs_4_.refs_2_.refs_1_, bf16[528,512]{1,0:T(8,128)(2,1)S(1)} %collective-permute-done.11.refs_4_.refs_5_.refs_3_.refs_2_, ...), custom_call_target="tpu_custom_call" | custom-call | flops 1000 | bytes 1000 | tf_op jit(solution)/shard_map/pallas_call | solution.py:198
  49.7 0.7 %collective-permute-done.17.refs_3_ = f32[1,1,256]{2,1,0:T(1,128)S(1)} collective-permute-done((f32[1,1,256]{2,1,0:T(1,128)S(1)}, f32[1,1,256]{2,1,0:T(1,128)S(1)}, u32[]{:S(2)}, u32[]{:S(2)}) %collective-permute-start.17) | collective-permute-done | bytes 1056 | tf_op jit(solution)/shard_map/ppermute | solution.py:40
  50.4 0.6 %shard_map.56 = f32[1,256]{1,0:T(1,128)} custom-call(f32[8,1,256]{2,1,0:T(1,128)S(1)} %shard_map.55.refs_0_, f32[4,1,256]{2,1,0:T(1,128)S(1)} %collective-permute-done.15.refs_1_, f32[2,1,256]{2,1,0:T(1,128)S(1)} %collective-permute-done.16.refs_2_, f32[1,1,256]{2,1,0:T(1,128)S(1)} %collective-permute-done.17.refs_3_), custom_call_target="tpu_custom_call" | custom-call | flops 1000 | bytes 1000 | tf_op jit(solution)/shard_map/pallas_call | solution.py:220
  (24 shorter events, 0.8 us)
Async XLA Ops:
  1.2 2.7 %collective-permute-start = (bf16[272,512]{1,0:T(8,128)(2,1)S(1)}, bf16[272,512]{1,0:T(8,128)(2,1)S(1)}, u32[]{:S(2)}, u32[]{:S(2)}) collective-permute-start(bf16[272,512]{1,0:T(8,128)(2,1)S(1)} %shard_map.37.first_ref), channel_id=1, source_target_pairs={{16,0},{0,16},{48,32},{32,48},{80,64},{64,80},{112,96},{96,112},{2... | collective-permute-start | bytes 835592 | tf_op jit(solution)/shard_map/ppermute | solution.py:45
  4.0 9.7 %collective-permute-start.2 = (bf16[2,272,512]{2,1,0:T(8,128)(2,1)S(1)}, bf16[2,272,512]{2,1,0:T(8,128)(2,1)S(1)}, u32[]{:S(2)}, u32[]{:S(2)}) collective-permute-start(bf16[2,272,512]{2,1,0:T(8,128)(2,1)S(1)} %shard_map.38.refs_0_), channel_id=1, source_target_pairs={{1,0},{19,16},{33,32},{51,48},{65,64},{83,80},{97,96},{115,112},{5... | collective-permute-start | bytes 1671176 | tf_op jit(solution)/shard_map/ppermute | solution.py:40
  6.6 10.7 %collective-permute-start.7 = (bf16[2,272,512]{2,1,0:T(8,128)(2,1)S(1)}, bf16[2,272,512]{2,1,0:T(8,128)(2,1)S(1)}, u32[]{:S(2)}, u32[]{:S(2)}) collective-permute-start(bf16[2,272,512]{2,1,0:T(8,128)(2,1)S(1)} %shard_map.38.refs_0_), channel_id=1, source_target_pairs={{32,0},{112,16},{0,32},{80,48},{96,64},{48,80},{64,96},{16,112},{3... | collective-permute-start | bytes 1671176 | tf_op jit(solution)/shard_map/ppermute | solution.py:40
  10.4 9.7 %collective-permute-start.1 = (bf16[2,272,512]{2,1,0:T(8,128)(2,1)S(1)}, bf16[2,272,512]{2,1,0:T(8,128)(2,1)S(1)}, u32[]{:S(2)}, u32[]{:S(2)}) collective-permute-start(bf16[2,272,512]{2,1,0:T(8,128)(2,1)S(1)} %shard_map.38.refs_0_), channel_id=1, source_target_pairs={{4,0},{28,16},{36,32},{60,48},{68,64},{92,80},{100,96},{124,112},{... | collective-permute-start | bytes 1671176 | tf_op jit(solution)/shard_map/ppermute | solution.py:40
  13.6 12.3 %collective-permute-start.3 = (bf16[2,272,512]{2,1,0:T(8,128)(2,1)S(1)}, bf16[2,272,512]{2,1,0:T(8,128)(2,1)S(1)}, u32[]{:S(2)}, u32[]{:S(2)}) collective-permute-start(bf16[2,272,512]{2,1,0:T(8,128)(2,1)S(1)} %collective-permute-done.2.refs_0_.refs_1_), channel_id=1, source_target_pairs={{4,0},{28,16},{36,32},{60,48},{68,64},{92,80},{100,96},{124,112},{... | collective-permute-start | bytes 1671176 | tf_op jit(solution)/shard_map/ppermute | solution.py:40
  17.3 9.9 %collective-permute-start.8 = (bf16[2,272,512]{2,1,0:T(8,128)(2,1)S(1)}, bf16[2,272,512]{2,1,0:T(8,128)(2,1)S(1)}, u32[]{:S(2)}, u32[]{:S(2)}) collective-permute-start(bf16[2,272,512]{2,1,0:T(8,128)(2,1)S(1)} %collective-permute-done.7.refs_0_.refs_1_), channel_id=1, source_target_pairs={{1,0},{19,16},{33,32},{51,48},{65,64},{83,80},{97,96},{115,112},{5... | collective-permute-start | bytes 1671176 | tf_op jit(solution)/shard_map/ppermute | solution.py:40
  20.0 9.6 %collective-permute-start.5 = (bf16[2,272,512]{2,1,0:T(8,128)(2,1)S(1)}, bf16[2,272,512]{2,1,0:T(8,128)(2,1)S(1)}, u32[]{:S(2)}, u32[]{:S(2)}) collective-permute-start(bf16[2,272,512]{2,1,0:T(8,128)(2,1)S(1)} %collective-permute-done.1.refs_0_.refs_1_), channel_id=1, source_target_pairs={{32,0},{112,16},{0,32},{80,48},{96,64},{48,80},{64,96},{16,112},{3... | collective-permute-start | bytes 1671176 | tf_op jit(solution)/shard_map/ppermute | solution.py:40
  22.7 6.9 %collective-permute-start.12 = (bf16[528,512]{1,0:T(8,128)(2,1)S(1)}, bf16[528,512]{1,0:T(8,128)(2,1)S(1)}, u32[]{:S(2)}, u32[]{:S(2)}) collective-permute-start(bf16[528,512]{1,0:T(8,128)(2,1)S(1)} %shard_map.44), channel_id=1, source_target_pairs={{16,0},{0,16},{48,32},{32,48},{80,64},{64,80},{112,96},{96,112},{2... | collective-permute-start | bytes 1622024 | tf_op jit(solution)/shard_map/ppermute | solution.py:45
  22.9 7.4 %collective-permute-start.10 = (bf16[528,512]{1,0:T(8,128)(2,1)S(1)}, bf16[528,512]{1,0:T(8,128)(2,1)S(1)}, u32[]{:S(2)}, u32[]{:S(2)}) collective-permute-start(bf16[528,512]{1,0:T(8,128)(2,1)S(1)} %shard_map.42), channel_id=1, source_target_pairs={{16,0},{0,16},{48,32},{32,48},{80,64},{64,80},{112,96},{96,112},{2... | collective-permute-start | bytes 1622024 | tf_op jit(solution)/shard_map/ppermute | solution.py:45
  26.0 9.6 %collective-permute-start.13 = (bf16[2,272,512]{2,1,0:T(8,128)(2,1)S(1)}, bf16[2,272,512]{2,1,0:T(8,128)(2,1)S(1)}, u32[]{:S(2)}, u32[]{:S(2)}) collective-permute-start(bf16[2,272,512]{2,1,0:T(8,128)(2,1)S(1)} %collective-permute-done.3.refs_0_.refs_2_.refs_1_), channel_id=1, source_target_pairs={{32,0},{112,16},{0,32},{80,48},{96,64},{48,80},{64,96},{16,112},{3... | collective-permute-start | bytes 1671176 | tf_op jit(solution)/shard_map/ppermute | solution.py:40
  27.2 3.1 %collective-permute-start.11 = (bf16[528,512]{1,0:T(8,128)(2,1)S(1)}, bf16[528,512]{1,0:T(8,128)(2,1)S(1)}, u32[]{:S(2)}, u32[]{:S(2)}) collective-permute-start(bf16[528,512]{1,0:T(8,128)(2,1)S(1)} %shard_map.43), channel_id=1, source_target_pairs={{16,0},{0,16},{48,32},{32,48},{80,64},{64,80},{112,96},{96,112},{2... | collective-permute-start | bytes 1622024 | tf_op jit(solution)/shard_map/ppermute | solution.py:45
  29.6 4.3 %collective-permute-start.9 = (bf16[528,512]{1,0:T(8,128)(2,1)S(1)}, bf16[528,512]{1,0:T(8,128)(2,1)S(1)}, u32[]{:S(2)}, u32[]{:S(2)}) collective-permute-start(bf16[528,512]{1,0:T(8,128)(2,1)S(1)} %shard_map.41), channel_id=1, source_target_pairs={{16,0},{0,16},{48,32},{32,48},{80,64},{64,80},{112,96},{96,112},{2... | collective-permute-start | bytes 1622024 | tf_op jit(solution)/shard_map/ppermute | solution.py:45
  29.7 4.3 %collective-permute-start.4 = (bf16[528,512]{1,0:T(8,128)(2,1)S(1)}, bf16[528,512]{1,0:T(8,128)(2,1)S(1)}, u32[]{:S(2)}, u32[]{:S(2)}) collective-permute-start(bf16[528,512]{1,0:T(8,128)(2,1)S(1)} %shard_map.39), channel_id=1, source_target_pairs={{16,0},{0,16},{48,32},{32,48},{80,64},{64,80},{112,96},{96,112},{2... | collective-permute-start | bytes 1622024 | tf_op jit(solution)/shard_map/ppermute | solution.py:45
  30.3 3.7 %collective-permute-start.6 = (bf16[528,512]{1,0:T(8,128)(2,1)S(1)}, bf16[528,512]{1,0:T(8,128)(2,1)S(1)}, u32[]{:S(2)}, u32[]{:S(2)}) collective-permute-start(bf16[528,512]{1,0:T(8,128)(2,1)S(1)} %shard_map.40), channel_id=1, source_target_pairs={{16,0},{0,16},{48,32},{32,48},{80,64},{64,80},{112,96},{96,112},{2... | collective-permute-start | bytes 1622024 | tf_op jit(solution)/shard_map/ppermute | solution.py:45
  35.7 2.0 %collective-permute-start.14 = (bf16[528,512]{1,0:T(8,128)(2,1)S(1)}, bf16[528,512]{1,0:T(8,128)(2,1)S(1)}, u32[]{:S(2)}, u32[]{:S(2)}) collective-permute-start(bf16[528,512]{1,0:T(8,128)(2,1)S(1)} %shard_map.48), channel_id=1, source_target_pairs={{16,0},{0,16},{48,32},{32,48},{80,64},{64,80},{112,96},{96,112},{2... | collective-permute-start | bytes 1622024 | tf_op jit(solution)/shard_map/ppermute | solution.py:45
  38.6 4.4 %collective-permute-start.15 = (f32[4,1,256]{2,1,0:T(1,128)S(1)}, f32[4,1,256]{2,1,0:T(1,128)S(1)}, u32[]{:S(2)}, u32[]{:S(2)}) collective-permute-start(f32[4,1,256]{2,1,0:T(1,128)S(1)} %shard_map.51), channel_id=1, source_target_pairs={{32,0},{112,16},{0,32},{80,48},{96,64},{48,80},{64,96},{16,112},{3... | collective-permute-start | bytes 12296 | tf_op jit(solution)/shard_map/ppermute | solution.py:40
  43.0 3.7 %collective-permute-start.16 = (f32[2,1,256]{2,1,0:T(1,128)S(1)}, f32[2,1,256]{2,1,0:T(1,128)S(1)}, u32[]{:S(2)}, u32[]{:S(2)}) collective-permute-start(f32[2,1,256]{2,1,0:T(1,128)S(1)} %shard_map.52), channel_id=1, source_target_pairs={{4,0},{28,16},{36,32},{60,48},{68,64},{92,80},{100,96},{124,112},{... | collective-permute-start | bytes 6152 | tf_op jit(solution)/shard_map/ppermute | solution.py:40
  46.8 3.6 %collective-permute-start.17 = (f32[1,1,256]{2,1,0:T(1,128)S(1)}, f32[1,1,256]{2,1,0:T(1,128)S(1)}, u32[]{:S(2)}, u32[]{:S(2)}) collective-permute-start(f32[1,1,256]{2,1,0:T(1,128)S(1)} %shard_map.54), channel_id=1, source_target_pairs={{1,0},{19,16},{33,32},{51,48},{65,64},{83,80},{97,96},{115,112},{5... | collective-permute-start | bytes 3080 | tf_op jit(solution)/shard_map/ppermute | solution.py:40

commit v10 on v9

--- a/solution.py
+++ b/solution.py
@@ -10,6 +10,7 @@
 AXES = ("group", "tile")
 ROWS = 256
 META = 16
+PIECES = 2
 PAY = ROWS + META
 E = 512
 LOW = -(2**31)
@@ -46,16 +47,22 @@
 
 
 def unit_kernel(emb_hbm, cluster_hbm, rank_hbm, out_ref, emb_ref, cluster_ref, rank_ref, sem):
-    sources = (cluster_hbm, rank_hbm, emb_hbm)
-    targets = (cluster_ref, rank_ref, emb_ref)
-    copies = [pltpu.make_async_copy(a, b, sem.at[i]) for i, (a, b) in enumerate(zip(sources, targets))]
-    for copy in copies:
+    small = [
+        pltpu.make_async_copy(cluster_hbm, cluster_ref, sem.at[PIECES]),
+        pltpu.make_async_copy(rank_hbm, rank_ref, sem.at[PIECES + 1]),
+    ]
+    size = ROWS // PIECES
+    pieces = [pl.ds(i * size, size) for i in range(PIECES)]
+    large = [pltpu.make_async_copy(emb_hbm.at[p], emb_ref.at[p], sem.at[i]) for i, p in enumerate(pieces)]
+    for copy in large + small:
         copy.start()
-    for copy in copies:
+    for piece, copy in zip(pieces, large):
         copy.wait()
-    emb = emb_ref[...]
-    sums = jnp.sum(emb * emb, axis=1, keepdims=True)
-    out_ref[0:ROWS, :] = (emb * lax.rsqrt(sums + 1e-06)).astype(jnp.bfloat16)
+        emb = emb_ref[piece, :]
+        sums = jnp.sum(emb * emb, axis=1, keepdims=True)
+        out_ref[piece, :] = (emb * lax.rsqrt(sums + 1e-06)).astype(jnp.bfloat16)
+    for copy in small:
+        copy.wait()
     rank = rank_ref[...]
     high = (rank >> 8).astype(jnp.float32)
     low = (rank & 255).astype(jnp.float32)
@@ -78,7 +85,7 @@
             pltpu.VMEM((ROWS, E), jnp.float32),
             pltpu.VMEM((1, ROWS), jnp.int32),
             pltpu.VMEM((1, ROWS), jnp.int32),
-            pltpu.SemaphoreType.DMA((3,)),
+            pltpu.SemaphoreType.DMA((PIECES + 2,)),
         ],
         compiler_params=pltpu.CompilerParams(vmem_limit_bytes=GRANT),
         cost_estimate=SMALL,

time: 51.1 us -> 51.1 us (level)
  no operation moved by 1% of the time
where the time goes in v10:
time: 51.1 us; the launch traced here: 51 us
  starting transfers between devices  27.3 us (53%)
  Pallas kernels  13.9 us (27%)
  waiting for transfers between devices  9.55 us (19%)
    ppermute x10, starting transfers between devices, exchange(): return lax.ppermute(array, AXES, pairs)  23.9 us
    pallas_call x8, Pallas kernels, match(): pl.pallas_call(functools.partial(match_kernel, queries, keys, masks, not...  11.8 us
    ppermute x10, waiting for transfers between devices, exchange(): return lax.ppermute(array, AXES, pairs)  8.11 us
    ppermute x8, starting transfers between devices, swap(): return lax.ppermute(array, AXES, pairs)  3.42 us
    ppermute x8, waiting for transfers between devices, swap(): return lax.ppermute(array, AXES, pairs)  1.44 us
    pallas_call x1, Pallas kernels, payload(): pl.pallas_call(unit_kernel, out_shape=jax.ShapeDtypeStruct((PAY, E), jnp....  1.21 us
  transfers between devices with their start and end apart: 18, of which 9 were waited for; matrix products, arithmetic and copies ran while one was open for 0% of the time, Pallas kernels for 22%

profile of v10, /device:TPU:1, one launch (start us, length us, event | category | flops | bytes accessed | tf_op | source)
XLA Modules:
  0.0 51.0 jit_solution(11135534464048155770)
XLA Ops:
  0.0 1.2 %shard_map.37.first_ref = bf16[272,512]{1,0:T(8,128)(2,1)S(1)} custom-call(f32[256,512]{1,0:T(8,128)} %emb_hbm.1, s32[1,256]{1,0:T(1,128)} %bitcast.3, s32[1,256]{1,0:T(1,128)} %bitcast.4), custom_call_target="tpu_custom_call" | custom-call | flops 1000 | bytes 1000 | tf_op jit(solution)/shard_map/pallas_call | solution.py:79
  1.2 1.5 %collective-permute-start = (bf16[272,512]{1,0:T(8,128)(2,1)S(1)}, bf16[272,512]{1,0:T(8,128)(2,1)S(1)}, u32[]{:S(2)}, u32[]{:S(2)}) collective-permute-start(bf16[272,512]{1,0:T(8,128)(2,1)S(1)} %shard_map.37.first_ref), channel_id=1, source_target_pairs={{16,0},{0,16},{48,32},{32,48},{80,64},{64,80},{112,96},{96,112},{2... | collective-permute-start | bytes 835592 | tf_op jit(solution)/shard_map/ppermute | solution.py:46
  2.7 1.2 %collective-permute-done.second_ref = bf16[272,512]{1,0:T(8,128)(2,1)S(1)} collective-permute-done((bf16[272,512]{1,0:T(8,128)(2,1)S(1)}, bf16[272,512]{1,0:T(8,128)(2,1)S(1)}, u32[]{:S(2)}, u32[]{:S(2)}) %collective-permute-start) | collective-permute-done | bytes 278560 | tf_op jit(solution)/shard_map/ppermute | solution.py:46
  3.9 2.6 %collective-permute-start.2 = (bf16[2,272,512]{2,1,0:T(8,128)(2,1)S(1)}, bf16[2,272,512]{2,1,0:T(8,128)(2,1)S(1)}, u32[]{:S(2)}, u32[]{:S(2)}) collective-permute-start(bf16[2,272,512]{2,1,0:T(8,128)(2,1)S(1)} %shard_map.38.refs_0_), channel_id=1, source_target_pairs={{1,0},{19,16},{33,32},{51,48},{65,64},{83,80},{97,96},{115,112},{5... | collective-permute-start | bytes 1671176 | tf_op jit(solution)/shard_map/ppermute | solution.py:41
  6.6 3.8 %collective-permute-start.7 = (bf16[2,272,512]{2,1,0:T(8,128)(2,1)S(1)}, bf16[2,272,512]{2,1,0:T(8,128)(2,1)S(1)}, u32[]{:S(2)}, u32[]{:S(2)}) collective-permute-start(bf16[2,272,512]{2,1,0:T(8,128)(2,1)S(1)} %shard_map.38.refs_0_), channel_id=1, source_target_pairs={{32,0},{112,16},{0,32},{80,48},{96,64},{48,80},{64,96},{16,112},{3... | collective-permute-start | bytes 1671176 | tf_op jit(solution)/shard_map/ppermute | solution.py:41
  10.3 2.7 %collective-permute-start.1 = (bf16[2,272,512]{2,1,0:T(8,128)(2,1)S(1)}, bf16[2,272,512]{2,1,0:T(8,128)(2,1)S(1)}, u32[]{:S(2)}, u32[]{:S(2)}) collective-permute-start(bf16[2,272,512]{2,1,0:T(8,128)(2,1)S(1)} %shard_map.38.refs_0_), channel_id=1, source_target_pairs={{4,0},{28,16},{36,32},{60,48},{68,64},{92,80},{100,96},{124,112},{... | collective-permute-start | bytes 1671176 | tf_op jit(solution)/shard_map/ppermute | solution.py:41
  13.1 0.5 %collective-permute-done.2.refs_0_.refs_1_ = bf16[2,272,512]{2,1,0:T(8,128)(2,1)S(1)} collective-permute-done((bf16[2,272,512]{2,1,0:T(8,128)(2,1)S(1)}, bf16[2,272,512]{2,1,0:T(8,128)(2,1)S(1)}, u32[]{:S(2)}, u32[]{:S(2)}) %collective-permute-start.2) | collective-permute-done | bytes 557088 | tf_op jit(solution)/shard_map/ppermute | solution.py:41
  13.6 2.8 %collective-permute-start.3 = (bf16[2,272,512]{2,1,0:T(8,128)(2,1)S(1)}, bf16[2,272,512]{2,1,0:T(8,128)(2,1)S(1)}, u32[]{:S(2)}, u32[]{:S(2)}) collective-permute-start(bf16[2,272,512]{2,1,0:T(8,128)(2,1)S(1)} %collective-permute-done.2.refs_0_.refs_1_), channel_id=1, source_target_pairs={{4,0},{28,16},{36,32},{60,48},{68,64},{92,80},{100,96},{124,112},{... | collective-permute-start | bytes 1671176 | tf_op jit(solution)/shard_map/ppermute | solution.py:41
  16.4 0.8 %collective-permute-done.7.refs_0_.refs_1_ = bf16[2,272,512]{2,1,0:T(8,128)(2,1)S(1)} collective-permute-done((bf16[2,272,512]{2,1,0:T(8,128)(2,1)S(1)}, bf16[2,272,512]{2,1,0:T(8,128)(2,1)S(1)}, u32[]{:S(2)}, u32[]{:S(2)}) %collective-permute-start.7) | collective-permute-done | bytes 557088 | tf_op jit(solution)/shard_map/ppermute | solution.py:41
  17.3 1.7 %collective-permute-start.8 = (bf16[2,272,512]{2,1,0:T(8,128)(2,1)S(1)}, bf16[2,272,512]{2,1,0:T(8,128)(2,1)S(1)}, u32[]{:S(2)}, u32[]{:S(2)}) collective-permute-start(bf16[2,272,512]{2,1,0:T(8,128)(2,1)S(1)} %collective-permute-done.7.refs_0_.refs_1_), channel_id=1, source_target_pairs={{1,0},{19,16},{33,32},{51,48},{65,64},{83,80},{97,96},{115,112},{5... | collective-permute-start | bytes 1671176 | tf_op jit(solution)/shard_map/ppermute | solution.py:41
  18.9 1.1 %collective-permute-done.1.refs_0_.refs_1_ = bf16[2,272,512]{2,1,0:T(8,128)(2,1)S(1)} collective-permute-done((bf16[2,272,512]{2,1,0:T(8,128)(2,1)S(1)}, bf16[2,272,512]{2,1,0:T(8,128)(2,1)S(1)}, u32[]{:S(2)}, u32[]{:S(2)}) %collective-permute-start.1) | collective-permute-done | bytes 557088 | tf_op jit(solution)/shard_map/ppermute | solution.py:41
  20.0 2.7 %collective-permute-start.5 = (bf16[2,272,512]{2,1,0:T(8,128)(2,1)S(1)}, bf16[2,272,512]{2,1,0:T(8,128)(2,1)S(1)}, u32[]{:S(2)}, u32[]{:S(2)}) collective-permute-start(bf16[2,272,512]{2,1,0:T(8,128)(2,1)S(1)} %collective-permute-done.1.refs_0_.refs_1_), channel_id=1, source_target_pairs={{32,0},{112,16},{0,32},{80,48},{96,64},{48,80},{64,96},{16,112},{3... | collective-permute-start | bytes 1671176 | tf_op jit(solution)/shard_map/ppermute | solution.py:41
  22.9 0.6 %collective-permute-start.10 = (bf16[528,512]{1,0:T(8,128)(2,1)S(1)}, bf16[528,512]{1,0:T(8,128)(2,1)S(1)}, u32[]{:S(2)}, u32[]{:S(2)}) collective-permute-start(bf16[528,512]{1,0:T(8,128)(2,1)S(1)} %shard_map.42), channel_id=1, source_target_pairs={{16,0},{0,16},{48,32},{32,48},{80,64},{64,80},{112,96},{96,112},{2... | collective-permute-start | bytes 1622024 | tf_op jit(solution)/shard_map/ppermute | solution.py:46
  23.4 2.5 %collective-permute-done.3.refs_0_.refs_2_.refs_1_ = bf16[2,272,512]{2,1,0:T(8,128)(2,1)S(1)} collective-permute-done((bf16[2,272,512]{2,1,0:T(8,128)(2,1)S(1)}, bf16[2,272,512]{2,1,0:T(8,128)(2,1)S(1)}, u32[]{:S(2)}, u32[]{:S(2)}) %collective-permute-start.3) | collective-permute-done | bytes 557088 | tf_op jit(solution)/shard_map/ppermute | solution.py:41
  26.0 1.1 %collective-permute-start.13 = (bf16[2,272,512]{2,1,0:T(8,128)(2,1)S(1)}, bf16[2,272,512]{2,1,0:T(8,128)(2,1)S(1)}, u32[]{:S(2)}, u32[]{:S(2)}) collective-permute-start(bf16[2,272,512]{2,1,0:T(8,128)(2,1)S(1)} %collective-permute-done.3.refs_0_.refs_2_.refs_1_), channel_id=1, source_target_pairs={{32,0},{112,16},{0,32},{80,48},{96,64},{48,80},{64,96},{16,112},{3... | collective-permute-start | bytes 1671176 | tf_op jit(solution)/shard_map/ppermute | solution.py:41
  27.4 2.2 %collective-permute-done.5.refs_0_.refs_3_.refs_2_ = bf16[2,272,512]{2,1,0:T(8,128)(2,1)S(1)} collective-permute-done((bf16[2,272,512]{2,1,0:T(8,128)(2,1)S(1)}, bf16[2,272,512]{2,1,0:T(8,128)(2,1)S(1)}, u32[]{:S(2)}, u32[]{:S(2)}) %collective-permute-start.5) | collective-permute-done | bytes 557088 | tf_op jit(solution)/shard_map/ppermute | solution.py:41
  29.7 0.6 %collective-permute-start.4 = (bf16[528,512]{1,0:T(8,128)(2,1)S(1)}, bf16[528,512]{1,0:T(8,128)(2,1)S(1)}, u32[]{:S(2)}, u32[]{:S(2)}) collective-permute-start(bf16[528,512]{1,0:T(8,128)(2,1)S(1)} %shard_map.39), channel_id=1, source_target_pairs={{16,0},{0,16},{48,32},{32,48},{80,64},{64,80},{112,96},{96,112},{2... | collective-permute-start | bytes 1622024 | tf_op jit(solution)/shard_map/ppermute | solution.py:46
  30.3 1.5 %shard_map.45.refs_6_ = f32[8,1,256]{2,1,0:T(1,128)S(1)} custom-call(bf16[2,272,512]{2,1,0:T(8,128)(2,1)S(1)} %shard_map.38.refs_0_, bf16[2,272,512]{2,1,0:T(8,128)(2,1)S(1)} %collective-permute-done.1.refs_0_.refs_1_, bf16[2,272,512]{2,1,0:T(8,128)(2,1)S(1)} %collective-permute-done.3.refs_0_.refs_2_.refs_1_, ...), custom_call_target="tpu_custom_call" | custom-call | flops 1000 | bytes 1000 | tf_op jit(solution)/shard_map/pallas_call | solution.py:205
  31.9 2.1 %shard_map.46.refs_6_ = f32[8,1,256]{2,1,0:T(1,128)S(1)} custom-call(bf16[2,272,512]{2,1,0:T(8,128)(2,1)S(1)} %shard_map.38.refs_0_, bf16[2,272,512]{2,1,0:T(8,128)(2,1)S(1)} %collective-permute-done.7.refs_0_.refs_1_, bf16[2,272,512]{2,1,0:T(8,128)(2,1)S(1)} %collective-permute-done.8.refs_0_.refs_2_.refs_1_, ...), custom_call_target="tpu_custom_call" | custom-call | flops 1000 | bytes 1000 | tf_op jit(solution)/shard_map/pallas_call | solution.py:205
  34.0 1.6 %shard_map.47.refs_8_ = f32[8,1,256]{2,1,0:T(1,128)S(1)} custom-call(bf16[2,272,512]{2,1,0:T(8,128)(2,1)S(1)} %collective-permute-done.7.refs_0_.refs_1_, bf16[2,272,512]{2,1,0:T(8,128)(2,1)S(1)} %collective-permute-done.8.refs_0_.refs_2_.refs_1_, bf16[2,272,512]{2,1,0:T(8,128)(2,1)S(1)} %collective-permute-done.5.refs_0_.refs_3_.refs_2_, ...), custom_call_target="tpu_custom_call" | custom-call | flops 1000 | bytes 1000 | tf_op jit(solution)/shard_map/pallas_call | solution.py:205
  35.7 0.5 collective-permute-start.14
  36.2 1.3 %shard_map.50.refs_5_ = f32[8,1,256]{2,1,0:T(1,128)S(1)} custom-call(bf16[2,272,512]{2,1,0:T(8,128)(2,1)S(1)} %shard_map.38.refs_0_, bf16[2,272,512]{2,1,0:T(8,128)(2,1)S(1)} %collective-permute-done.13.refs_0_.refs_1_.refs_3_, bf16[528,512]{1,0:T(8,128)(2,1)S(1)} %collective-permute-done.10.refs_3_.refs_4_.refs_2_.refs_1_, ...), custom_call_target="tpu_custom_call" | custom-call | flops 1000 | bytes 1000 | tf_op jit(solution)/shard_map/pallas_call | solution.py:205
  37.5 0.2 collective-permute-done.14.refs_5_.refs_4_.refs_8_.refs_7_
  37.7 0.8 %shard_map.51 = f32[4,1,256]{2,1,0:T(1,128)S(1)} custom-call(bf16[2,272,512]{2,1,0:T(8,128)(2,1)S(1)} %collective-permute-done.7.refs_0_.refs_1_, bf16[2,272,512]{2,1,0:T(8,128)(2,1)S(1)} %collective-permute-done.8.refs_0_.refs_2_.refs_1_, bf16[2,272,512]{2,1,0:T(8,128)(2,1)S(1)} %collective-permute-done.5.refs_0_.refs_3_.refs_2_, ...), custom_call_target="tpu_custom_call" | custom-call | flops 1000 | bytes 1000 | tf_op jit(solution)/shard_map/pallas_call | solution.py:205
  38.6 2.9 %collective-permute-start.15 = (f32[4,1,256]{2,1,0:T(1,128)S(1)}, f32[4,1,256]{2,1,0:T(1,128)S(1)}, u32[]{:S(2)}, u32[]{:S(2)}) collective-permute-start(f32[4,1,256]{2,1,0:T(1,128)S(1)} %shard_map.51), channel_id=1, source_target_pairs={{32,0},{112,16},{0,32},{80,48},{96,64},{48,80},{64,96},{16,112},{3... | collective-permute-start | bytes 12296 | tf_op jit(solution)/shard_map/ppermute | solution.py:41
  41.5 1.5 %shard_map.49.refs_0_ = f32[8,1,256]{2,1,0:T(1,128)S(1)} custom-call(bf16[2,272,512]{2,1,0:T(8,128)(2,1)S(1)} %collective-permute-done.1.refs_0_.refs_1_, bf16[2,272,512]{2,1,0:T(8,128)(2,1)S(1)} %collective-permute-done.3.refs_0_.refs_2_.refs_1_, bf16[528,512]{1,0:T(8,128)(2,1)S(1)} %collective-permute-done.4.refs_3_.refs_2_.refs_5_.refs_4_, ...), custom_call_target="tpu_custom_call" | custom-call | flops 1000 | bytes 1000 | tf_op jit(solution)/shard_map/pallas_call | solution.py:205
  43.0 2.1 %collective-permute-start.16 = (f32[2,1,256]{2,1,0:T(1,128)S(1)}, f32[2,1,256]{2,1,0:T(1,128)S(1)}, u32[]{:S(2)}, u32[]{:S(2)}) collective-permute-start(f32[2,1,256]{2,1,0:T(1,128)S(1)} %shard_map.52), channel_id=1, source_target_pairs={{4,0},{28,16},{36,32},{60,48},{68,64},{92,80},{100,96},{124,112},{... | collective-permute-start | bytes 6152 | tf_op jit(solution)/shard_map/ppermute | solution.py:41
  45.2 1.4 %shard_map.53.refs_0_ = f32[8,1,256]{2,1,0:T(1,128)S(1)} custom-call(bf16[2,272,512]{2,1,0:T(8,128)(2,1)S(1)} %shard_map.38.refs_0_, bf16[2,272,512]{2,1,0:T(8,128)(2,1)S(1)} %collective-permute-done.2.refs_0_.refs_1_, bf16[528,512]{1,0:T(8,128)(2,1)S(1)} %collective-permute-done.10.refs_3_.refs_4_.refs_2_.refs_1_, ...), custom_call_target="tpu_custom_call" | custom-call | flops 1000 | bytes 1000 | tf_op jit(solution)/shard_map/pallas_call | solution.py:205
  46.8 1.4 %collective-permute-start.17 = (f32[1,1,256]{2,1,0:T(1,128)S(1)}, f32[1,1,256]{2,1,0:T(1,128)S(1)}, u32[]{:S(2)}, u32[]{:S(2)}) collective-permute-start(f32[1,1,256]{2,1,0:T(1,128)S(1)} %shard_map.54), channel_id=1, source_target_pairs={{1,0},{19,16},{33,32},{51,48},{65,64},{83,80},{97,96},{115,112},{5... | collective-permute-start | bytes 3080 | tf_op jit(solution)/shard_map/ppermute | solution.py:41
  48.2 1.4 %shard_map.55.refs_0_ = f32[8,1,256]{2,1,0:T(1,128)S(1)} custom-call(bf16[2,272,512]{2,1,0:T(8,128)(2,1)S(1)} %shard_map.38.refs_0_, bf16[528,512]{1,0:T(8,128)(2,1)S(1)} %collective-permute-done.10.refs_3_.refs_4_.refs_2_.refs_1_, bf16[528,512]{1,0:T(8,128)(2,1)S(1)} %collective-permute-done.11.refs_4_.refs_5_.refs_3_.refs_2_, ...), custom_call_target="tpu_custom_call" | custom-call | flops 1000 | bytes 1000 | tf_op jit(solution)/shard_map/pallas_call | solution.py:205
  49.6 0.7 %collective-permute-done.17.refs_3_ = f32[1,1,256]{2,1,0:T(1,128)S(1)} collective-permute-done((f32[1,1,256]{2,1,0:T(1,128)S(1)}, f32[1,1,256]{2,1,0:T(1,128)S(1)}, u32[]{:S(2)}, u32[]{:S(2)}) %collective-permute-start.17) | collective-permute-done | bytes 1056 | tf_op jit(solution)/shard_map/ppermute | solution.py:41
  50.4 0.6 %shard_map.56 = f32[1,256]{1,0:T(1,128)} custom-call(f32[8,1,256]{2,1,0:T(1,128)S(1)} %shard_map.55.refs_0_, f32[4,1,256]{2,1,0:T(1,128)S(1)} %collective-permute-done.15.refs_1_, f32[2,1,256]{2,1,0:T(1,128)S(1)} %collective-permute-done.16.refs_2_, f32[1,1,256]{2,1,0:T(1,128)S(1)} %collective-permute-done.17.refs_3_), custom_call_target="tpu_custom_call" | custom-call | flops 1000 | bytes 1000 | tf_op jit(solution)/shard_map/pallas_call | solution.py:227
  (24 shorter events, 0.8 us)
Async XLA Ops:
  1.2 2.7 %collective-permute-start = (bf16[272,512]{1,0:T(8,128)(2,1)S(1)}, bf16[272,512]{1,0:T(8,128)(2,1)S(1)}, u32[]{:S(2)}, u32[]{:S(2)}) collective-permute-start(bf16[272,512]{1,0:T(8,128)(2,1)S(1)} %shard_map.37.first_ref), channel_id=1, source_target_pairs={{16,0},{0,16},{48,32},{32,48},{80,64},{64,80},{112,96},{96,112},{2... | collective-permute-start | bytes 835592 | tf_op jit(solution)/shard_map/ppermute | solution.py:46
  3.9 9.7 %collective-permute-start.2 = (bf16[2,272,512]{2,1,0:T(8,128)(2,1)S(1)}, bf16[2,272,512]{2,1,0:T(8,128)(2,1)S(1)}, u32[]{:S(2)}, u32[]{:S(2)}) collective-permute-start(bf16[2,272,512]{2,1,0:T(8,128)(2,1)S(1)} %shard_map.38.refs_0_), channel_id=1, source_target_pairs={{1,0},{19,16},{33,32},{51,48},{65,64},{83,80},{97,96},{115,112},{5... | collective-permute-start | bytes 1671176 | tf_op jit(solution)/shard_map/ppermute | solution.py:41
  6.6 10.7 %collective-permute-start.7 = (bf16[2,272,512]{2,1,0:T(8,128)(2,1)S(1)}, bf16[2,272,512]{2,1,0:T(8,128)(2,1)S(1)}, u32[]{:S(2)}, u32[]{:S(2)}) collective-permute-start(bf16[2,272,512]{2,1,0:T(8,128)(2,1)S(1)} %shard_map.38.refs_0_), channel_id=1, source_target_pairs={{32,0},{112,16},{0,32},{80,48},{96,64},{48,80},{64,96},{16,112},{3... | collective-permute-start | bytes 1671176 | tf_op jit(solution)/shard_map/ppermute | solution.py:41
  10.3 9.7 %collective-permute-start.1 = (bf16[2,272,512]{2,1,0:T(8,128)(2,1)S(1)}, bf16[2,272,512]{2,1,0:T(8,128)(2,1)S(1)}, u32[]{:S(2)}, u32[]{:S(2)}) collective-permute-start(bf16[2,272,512]{2,1,0:T(8,128)(2,1)S(1)} %shard_map.38.refs_0_), channel_id=1, source_target_pairs={{4,0},{28,16},{36,32},{60,48},{68,64},{92,80},{100,96},{124,112},{... | collective-permute-start | bytes 1671176 | tf_op jit(solution)/shard_map/ppermute | solution.py:41
  13.6 12.3 %collective-permute-start.3 = (bf16[2,272,512]{2,1,0:T(8,128)(2,1)S(1)}, bf16[2,272,512]{2,1,0:T(8,128)(2,1)S(1)}, u32[]{:S(2)}, u32[]{:S(2)}) collective-permute-start(bf16[2,272,512]{2,1,0:T(8,128)(2,1)S(1)} %collective-permute-done.2.refs_0_.refs_1_), channel_id=1, source_target_pairs={{4,0},{28,16},{36,32},{60,48},{68,64},{92,80},{100,96},{124,112},{... | collective-permute-start | bytes 1671176 | tf_op jit(solution)/shard_map/ppermute | solution.py:41
  17.3 9.9 %collective-permute-start.8 = (bf16[2,272,512]{2,1,0:T(8,128)(2,1)S(1)}, bf16[2,272,512]{2,1,0:T(8,128)(2,1)S(1)}, u32[]{:S(2)}, u32[]{:S(2)}) collective-permute-start(bf16[2,272,512]{2,1,0:T(8,128)(2,1)S(1)} %collective-permute-done.7.refs_0_.refs_1_), channel_id=1, source_target_pairs={{1,0},{19,16},{33,32},{51,48},{65,64},{83,80},{97,96},{115,112},{5... | collective-permute-start | bytes 1671176 | tf_op jit(solution)/shard_map/ppermute | solution.py:41
  20.0 9.6 %collective-permute-start.5 = (bf16[2,272,512]{2,1,0:T(8,128)(2,1)S(1)}, bf16[2,272,512]{2,1,0:T(8,128)(2,1)S(1)}, u32[]{:S(2)}, u32[]{:S(2)}) collective-permute-start(bf16[2,272,512]{2,1,0:T(8,128)(2,1)S(1)} %collective-permute-done.1.refs_0_.refs_1_), channel_id=1, source_target_pairs={{32,0},{112,16},{0,32},{80,48},{96,64},{48,80},{64,96},{16,112},{3... | collective-permute-start | bytes 1671176 | tf_op jit(solution)/shard_map/ppermute | solution.py:41
  22.7 6.9 %collective-permute-start.12 = (bf16[528,512]{1,0:T(8,128)(2,1)S(1)}, bf16[528,512]{1,0:T(8,128)(2,1)S(1)}, u32[]{:S(2)}, u32[]{:S(2)}) collective-permute-start(bf16[528,512]{1,0:T(8,128)(2,1)S(1)} %shard_map.44), channel_id=1, source_target_pairs={{16,0},{0,16},{48,32},{32,48},{80,64},{64,80},{112,96},{96,112},{2... | collective-permute-start | bytes 1622024 | tf_op jit(solution)/shard_map/ppermute | solution.py:46
  22.9 7.4 %collective-permute-start.10 = (bf16[528,512]{1,0:T(8,128)(2,1)S(1)}, bf16[528,512]{1,0:T(8,128)(2,1)S(1)}, u32[]{:S(2)}, u32[]{:S(2)}) collective-permute-start(bf16[528,512]{1,0:T(8,128)(2,1)S(1)} %shard_map.42), channel_id=1, source_target_pairs={{16,0},{0,16},{48,32},{32,48},{80,64},{64,80},{112,96},{96,112},{2... | collective-permute-start | bytes 1622024 | tf_op jit(solution)/shard_map/ppermute | solution.py:46
  26.0 9.7 %collective-permute-start.13 = (bf16[2,272,512]{2,1,0:T(8,128)(2,1)S(1)}, bf16[2,272,512]{2,1,0:T(8,128)(2,1)S(1)}, u32[]{:S(2)}, u32[]{:S(2)}) collective-permute-start(bf16[2,272,512]{2,1,0:T(8,128)(2,1)S(1)} %collective-permute-done.3.refs_0_.refs_2_.refs_1_), channel_id=1, source_target_pairs={{32,0},{112,16},{0,32},{80,48},{96,64},{48,80},{64,96},{16,112},{3... | collective-permute-start | bytes 1671176 | tf_op jit(solution)/shard_map/ppermute | solution.py:41
  27.2 3.1 %collective-permute-start.11 = (bf16[528,512]{1,0:T(8,128)(2,1)S(1)}, bf16[528,512]{1,0:T(8,128)(2,1)S(1)}, u32[]{:S(2)}, u32[]{:S(2)}) collective-permute-start(bf16[528,512]{1,0:T(8,128)(2,1)S(1)} %shard_map.43), channel_id=1, source_target_pairs={{16,0},{0,16},{48,32},{32,48},{80,64},{64,80},{112,96},{96,112},{2... | collective-permute-start | bytes 1622024 | tf_op jit(solution)/shard_map/ppermute | solution.py:46
  29.6 4.4 %collective-permute-start.9 = (bf16[528,512]{1,0:T(8,128)(2,1)S(1)}, bf16[528,512]{1,0:T(8,128)(2,1)S(1)}, u32[]{:S(2)}, u32[]{:S(2)}) collective-permute-start(bf16[528,512]{1,0:T(8,128)(2,1)S(1)} %shard_map.41), channel_id=1, source_target_pairs={{16,0},{0,16},{48,32},{32,48},{80,64},{64,80},{112,96},{96,112},{2... | collective-permute-start | bytes 1622024 | tf_op jit(solution)/shard_map/ppermute | solution.py:46
  29.7 4.3 %collective-permute-start.4 = (bf16[528,512]{1,0:T(8,128)(2,1)S(1)}, bf16[528,512]{1,0:T(8,128)(2,1)S(1)}, u32[]{:S(2)}, u32[]{:S(2)}) collective-permute-start(bf16[528,512]{1,0:T(8,128)(2,1)S(1)} %shard_map.39), channel_id=1, source_target_pairs={{16,0},{0,16},{48,32},{32,48},{80,64},{64,80},{112,96},{96,112},{2... | collective-permute-start | bytes 1622024 | tf_op jit(solution)/shard_map/ppermute | solution.py:46
  30.2 3.7 %collective-permute-start.6 = (bf16[528,512]{1,0:T(8,128)(2,1)S(1)}, bf16[528,512]{1,0:T(8,128)(2,1)S(1)}, u32[]{:S(2)}, u32[]{:S(2)}) collective-permute-start(bf16[528,512]{1,0:T(8,128)(2,1)S(1)} %shard_map.40), channel_id=1, source_target_pairs={{16,0},{0,16},{48,32},{32,48},{80,64},{64,80},{112,96},{96,112},{2... | collective-permute-start | bytes 1622024 | tf_op jit(solution)/shard_map/ppermute | solution.py:46
  35.7 2.1 %collective-permute-start.14 = (bf16[528,512]{1,0:T(8,128)(2,1)S(1)}, bf16[528,512]{1,0:T(8,128)(2,1)S(1)}, u32[]{:S(2)}, u32[]{:S(2)}) collective-permute-start(bf16[528,512]{1,0:T(8,128)(2,1)S(1)} %shard_map.48), channel_id=1, source_target_pairs={{16,0},{0,16},{48,32},{32,48},{80,64},{64,80},{112,96},{96,112},{2... | collective-permute-start | bytes 1622024 | tf_op jit(solution)/shard_map/ppermute | solution.py:46
  38.6 4.4 %collective-permute-start.15 = (f32[4,1,256]{2,1,0:T(1,128)S(1)}, f32[4,1,256]{2,1,0:T(1,128)S(1)}, u32[]{:S(2)}, u32[]{:S(2)}) collective-permute-start(f32[4,1,256]{2,1,0:T(1,128)S(1)} %shard_map.51), channel_id=1, source_target_pairs={{32,0},{112,16},{0,32},{80,48},{96,64},{48,80},{64,96},{16,112},{3... | collective-permute-start | bytes 12296 | tf_op jit(solution)/shard_map/ppermute | solution.py:41
  43.0 3.7 %collective-permute-start.16 = (f32[2,1,256]{2,1,0:T(1,128)S(1)}, f32[2,1,256]{2,1,0:T(1,128)S(1)}, u32[]{:S(2)}, u32[]{:S(2)}) collective-permute-start(f32[2,1,256]{2,1,0:T(1,128)S(1)} %shard_map.52), channel_id=1, source_target_pairs={{4,0},{28,16},{36,32},{60,48},{68,64},{92,80},{100,96},{124,112},{... | collective-permute-start | bytes 6152 | tf_op jit(solution)/shard_map/ppermute | solution.py:41
  46.8 3.6 %collective-permute-start.17 = (f32[1,1,256]{2,1,0:T(1,128)S(1)}, f32[1,1,256]{2,1,0:T(1,128)S(1)}, u32[]{:S(2)}, u32[]{:S(2)}) collective-permute-start(f32[1,1,256]{2,1,0:T(1,128)S(1)} %shard_map.54), channel_id=1, source_target_pairs={{1,0},{19,16},{33,32},{51,48},{65,64},{83,80},{97,96},{115,112},{5... | collective-permute-start | bytes 3080 | tf_op jit(solution)/shard_map/ppermute | solution.py:41

commit v11 on v9

--- a/solution.py
+++ b/solution.py
@@ -242,13 +242,14 @@
     every = (*near, *far, 7)
     best = match((4, 6, 5), near, mine, theirs)
     best = match((4, 6, 5), far, mine, theirs, best)
-    part = match((2, 3), near, mine, theirs)
+    part = match((2,), near, mine, theirs)
     part, best, mine[7] = lax.optimization_barrier((part, best, mine[7]))
     theirs[7] = swap(pack(mine[7])[0])
     best = match((7,), (*near, *far), mine, theirs, best)
     send = match((4, 6, 5, 7), (7,), mine, theirs, best, last=True)
     send, mine[0] = lax.optimization_barrier((send, mine[0]))
     first = exchange(send, 4)
+    part = match((3,), near, mine, theirs, part)
     send = fold(2, match((2, 3), (*far, 7), mine, theirs, part), first)
     send, mine[0] = lax.optimization_barrier((send, mine[0]))
     second = exchange(send, 2)

time: 51.1 us -> 51.9 us (1.016)
  waiting for transfers between devices: 9.54 us -> 11.3 us
  starting transfers between devices: 27.4 us -> 26.1 us
    ppermute x10, waiting for transfers between devices: 8.1 us -> 9.5 us  [exchange(): return lax.ppermute(array, AXES, pairs)]
    ppermute x10, starting transfers between devices: 23.9 us -> 23.1 us  [exchange(): return lax.ppermute(array, AXES, pairs)]
    pallas_call x8 -> x9, Pallas kernels: 11.8 us -> 12 us  [match(): pl.pallas_call(functools.partial(match_kernel, queries, keys, masks, not...]
  transfers between devices with their start and end apart: 18 -> 18, of which waited for: 9 -> 10; matrix products, arithmetic and copies ran while one was open for 0% -> 0% of each run, Pallas kernels for 22% -> 22%
where the time goes in v11:
time: 51.9 us; the launch traced here: 51.8 us
  starting transfers between devices  26.1 us (50%)
  Pallas kernels  14.2 us (27%)
  waiting for transfers between devices  11.3 us (22%)
    ppermute x10, starting transfers between devices, exchange(): return lax.ppermute(array, AXES, pairs)  23.1 us
    pallas_call x9, Pallas kernels, match(): pl.pallas_call(functools.partial(match_kernel, queries, keys, masks, not...  12 us
    ppermute x10, waiting for transfers between devices, exchange(): return lax.ppermute(array, AXES, pairs)  9.5 us
    ppermute x8, starting transfers between devices, swap(): return lax.ppermute(array, AXES, pairs)  3.02 us
    ppermute x8, waiting for transfers between devices, swap(): return lax.ppermute(array, AXES, pairs)  1.81 us
    pallas_call x1, Pallas kernels, payload(): pl.pallas_call(unit_kernel, out_shape=jax.ShapeDtypeStruct((PAY, E), jnp....  1.23 us
  transfers between devices with their start and end apart: 18, of which 10 were waited for; matrix products, arithmetic and copies ran while one was open for 0% of the time, Pallas kernels for 22%

profile of v11, /device:TPU:1, one launch (start us, length us, event | category | flops | bytes accessed | tf_op | source)
XLA Modules:
  0.0 51.8 jit_solution(6935726639639336992)
XLA Ops:
  0.0 1.2 %shard_map.37.first_ref = bf16[272,512]{1,0:T(8,128)(2,1)S(1)} custom-call(f32[256,512]{1,0:T(8,128)} %emb_hbm.1, s32[1,256]{1,0:T(1,128)} %bitcast.3, s32[1,256]{1,0:T(1,128)} %bitcast.4), custom_call_target="tpu_custom_call" | custom-call | flops 1000 | bytes 1000 | tf_op jit(solution)/shard_map/pallas_call | solution.py:72
  1.2 1.5 %collective-permute-start = (bf16[272,512]{1,0:T(8,128)(2,1)S(1)}, bf16[272,512]{1,0:T(8,128)(2,1)S(1)}, u32[]{:S(2)}, u32[]{:S(2)}) collective-permute-start(bf16[272,512]{1,0:T(8,128)(2,1)S(1)} %shard_map.37.first_ref), channel_id=1, source_target_pairs={{16,0},{0,16},{48,32},{32,48},{80,64},{64,80},{112,96},{96,112},{2... | collective-permute-start | bytes 835592 | tf_op jit(solution)/shard_map/ppermute | solution.py:45
  2.7 1.2 %collective-permute-done.second_ref = bf16[272,512]{1,0:T(8,128)(2,1)S(1)} collective-permute-done((bf16[272,512]{1,0:T(8,128)(2,1)S(1)}, bf16[272,512]{1,0:T(8,128)(2,1)S(1)}, u32[]{:S(2)}, u32[]{:S(2)}) %collective-permute-start) | collective-permute-done | bytes 278560 | tf_op jit(solution)/shard_map/ppermute | solution.py:45
  4.0 2.6 %collective-permute-start.2 = (bf16[2,272,512]{2,1,0:T(8,128)(2,1)S(1)}, bf16[2,272,512]{2,1,0:T(8,128)(2,1)S(1)}, u32[]{:S(2)}, u32[]{:S(2)}) collective-permute-start(bf16[2,272,512]{2,1,0:T(8,128)(2,1)S(1)} %shard_map.38.refs_0_), channel_id=1, source_target_pairs={{1,0},{19,16},{33,32},{51,48},{65,64},{83,80},{97,96},{115,112},{5... | collective-permute-start | bytes 1671176 | tf_op jit(solution)/shard_map/ppermute | solution.py:40
  6.6 3.8 %collective-permute-start.7 = (bf16[2,272,512]{2,1,0:T(8,128)(2,1)S(1)}, bf16[2,272,512]{2,1,0:T(8,128)(2,1)S(1)}, u32[]{:S(2)}, u32[]{:S(2)}) collective-permute-start(bf16[2,272,512]{2,1,0:T(8,128)(2,1)S(1)} %shard_map.38.refs_0_), channel_id=1, source_target_pairs={{32,0},{112,16},{0,32},{80,48},{96,64},{48,80},{64,96},{16,112},{3... | collective-permute-start | bytes 1671176 | tf_op jit(solution)/shard_map/ppermute | solution.py:40
  10.4 2.7 %collective-permute-start.1 = (bf16[2,272,512]{2,1,0:T(8,128)(2,1)S(1)}, bf16[2,272,512]{2,1,0:T(8,128)(2,1)S(1)}, u32[]{:S(2)}, u32[]{:S(2)}) collective-permute-start(bf16[2,272,512]{2,1,0:T(8,128)(2,1)S(1)} %shard_map.38.refs_0_), channel_id=1, source_target_pairs={{4,0},{28,16},{36,32},{60,48},{68,64},{92,80},{100,96},{124,112},{... | collective-permute-start | bytes 1671176 | tf_op jit(solution)/shard_map/ppermute | solution.py:40
  13.6 2.8 %collective-permute-start.3 = (bf16[2,272,512]{2,1,0:T(8,128)(2,1)S(1)}, bf16[2,272,512]{2,1,0:T(8,128)(2,1)S(1)}, u32[]{:S(2)}, u32[]{:S(2)}) collective-permute-start(bf16[2,272,512]{2,1,0:T(8,128)(2,1)S(1)} %collective-permute-done.2.refs_0_.refs_1_), channel_id=1, source_target_pairs={{4,0},{28,16},{36,32},{60,48},{68,64},{92,80},{100,96},{124,112},{... | collective-permute-start | bytes 1671176 | tf_op jit(solution)/shard_map/ppermute | solution.py:40
  16.5 0.8 %collective-permute-done.7.refs_0_.refs_1_ = bf16[2,272,512]{2,1,0:T(8,128)(2,1)S(1)} collective-permute-done((bf16[2,272,512]{2,1,0:T(8,128)(2,1)S(1)}, bf16[2,272,512]{2,1,0:T(8,128)(2,1)S(1)}, u32[]{:S(2)}, u32[]{:S(2)}) %collective-permute-start.7) | collective-permute-done | bytes 557088 | tf_op jit(solution)/shard_map/ppermute | solution.py:40
  17.3 1.7 %collective-permute-start.8 = (bf16[2,272,512]{2,1,0:T(8,128)(2,1)S(1)}, bf16[2,272,512]{2,1,0:T(8,128)(2,1)S(1)}, u32[]{:S(2)}, u32[]{:S(2)}) collective-permute-start(bf16[2,272,512]{2,1,0:T(8,128)(2,1)S(1)} %collective-permute-done.7.refs_0_.refs_1_), channel_id=1, source_target_pairs={{1,0},{19,16},{33,32},{51,48},{65,64},{83,80},{97,96},{115,112},{5... | collective-permute-start | bytes 1671176 | tf_op jit(solution)/shard_map/ppermute | solution.py:40
  18.9 1.1 %collective-permute-done.1.refs_0_.refs_1_ = bf16[2,272,512]{2,1,0:T(8,128)(2,1)S(1)} collective-permute-done((bf16[2,272,512]{2,1,0:T(8,128)(2,1)S(1)}, bf16[2,272,512]{2,1,0:T(8,128)(2,1)S(1)}, u32[]{:S(2)}, u32[]{:S(2)}) %collective-permute-start.1) | collective-permute-done | bytes 557088 | tf_op jit(solution)/shard_map/ppermute | solution.py:40
  20.0 2.7 %collective-permute-start.5 = (bf16[2,272,512]{2,1,0:T(8,128)(2,1)S(1)}, bf16[2,272,512]{2,1,0:T(8,128)(2,1)S(1)}, u32[]{:S(2)}, u32[]{:S(2)}) collective-permute-start(bf16[2,272,512]{2,1,0:T(8,128)(2,1)S(1)} %collective-permute-done.1.refs_0_.refs_1_), channel_id=1, source_target_pairs={{32,0},{112,16},{0,32},{80,48},{96,64},{48,80},{64,96},{16,112},{3... | collective-permute-start | bytes 1671176 | tf_op jit(solution)/shard_map/ppermute | solution.py:40
  22.9 0.6 %collective-permute-start.10 = (bf16[528,512]{1,0:T(8,128)(2,1)S(1)}, bf16[528,512]{1,0:T(8,128)(2,1)S(1)}, u32[]{:S(2)}, u32[]{:S(2)}) collective-permute-start(bf16[528,512]{1,0:T(8,128)(2,1)S(1)} %shard_map.42), channel_id=1, source_target_pairs={{16,0},{0,16},{48,32},{32,48},{80,64},{64,80},{112,96},{96,112},{2... | collective-permute-start | bytes 1622024 | tf_op jit(solution)/shard_map/ppermute | solution.py:45
  23.5 2.5 %collective-permute-done.3.refs_0_.refs_1_ = bf16[2,272,512]{2,1,0:T(8,128)(2,1)S(1)} collective-permute-done((bf16[2,272,512]{2,1,0:T(8,128)(2,1)S(1)}, bf16[2,272,512]{2,1,0:T(8,128)(2,1)S(1)}, u32[]{:S(2)}, u32[]{:S(2)}) %collective-permute-start.3) | collective-permute-done | bytes 557088 | tf_op jit(solution)/shard_map/ppermute | solution.py:40
  26.0 1.1 %collective-permute-start.13 = (bf16[2,272,512]{2,1,0:T(8,128)(2,1)S(1)}, bf16[2,272,512]{2,1,0:T(8,128)(2,1)S(1)}, u32[]{:S(2)}, u32[]{:S(2)}) collective-permute-start(bf16[2,272,512]{2,1,0:T(8,128)(2,1)S(1)} %collective-permute-done.3.refs_0_.refs_1_), channel_id=1, source_target_pairs={{32,0},{112,16},{0,32},{80,48},{96,64},{48,80},{64,96},{16,112},{3... | collective-permute-start | bytes 1671176 | tf_op jit(solution)/shard_map/ppermute | solution.py:40
  27.4 2.2 %collective-permute-done.5.refs_0_.refs_3_.refs_2_ = bf16[2,272,512]{2,1,0:T(8,128)(2,1)S(1)} collective-permute-done((bf16[2,272,512]{2,1,0:T(8,128)(2,1)S(1)}, bf16[2,272,512]{2,1,0:T(8,128)(2,1)S(1)}, u32[]{:S(2)}, u32[]{:S(2)}) %collective-permute-start.5) | collective-permute-done | bytes 557088 | tf_op jit(solution)/shard_map/ppermute | solution.py:40
  29.7 0.6 %collective-permute-start.4 = (bf16[528,512]{1,0:T(8,128)(2,1)S(1)}, bf16[528,512]{1,0:T(8,128)(2,1)S(1)}, u32[]{:S(2)}, u32[]{:S(2)}) collective-permute-start(bf16[528,512]{1,0:T(8,128)(2,1)S(1)} %shard_map.39), channel_id=1, source_target_pairs={{16,0},{0,16},{48,32},{32,48},{80,64},{64,80},{112,96},{96,112},{2... | collective-permute-start | bytes 1622024 | tf_op jit(solution)/shard_map/ppermute | solution.py:45
  30.4 0.9 %shard_map.45.refs_5_ = f32[8,1,256]{2,1,0:T(1,128)S(1)} custom-call(bf16[2,272,512]{2,1,0:T(8,128)(2,1)S(1)} %shard_map.38.refs_0_, bf16[2,272,512]{2,1,0:T(8,128)(2,1)S(1)} %collective-permute-done.1.refs_0_.refs_1_, bf16[528,512]{1,0:T(8,128)(2,1)S(1)} %collective-permute-done.10.refs_2_.refs_4_.refs_1_, ...), custom_call_target="tpu_custom_call" | custom-call | flops 1000 | bytes 1000 | tf_op jit(solution)/shard_map/pallas_call | solution.py:198
  31.3 2.1 %shard_map.46.refs_6_ = f32[8,1,256]{2,1,0:T(1,128)S(1)} custom-call(bf16[2,272,512]{2,1,0:T(8,128)(2,1)S(1)} %shard_map.38.refs_0_, bf16[2,272,512]{2,1,0:T(8,128)(2,1)S(1)} %collective-permute-done.7.refs_0_.refs_1_, bf16[2,272,512]{2,1,0:T(8,128)(2,1)S(1)} %collective-permute-done.8.refs_0_.refs_2_.refs_1_, ...), custom_call_target="tpu_custom_call" | custom-call | flops 1000 | bytes 1000 | tf_op jit(solution)/shard_map/pallas_call | solution.py:198
  33.4 1.6 %shard_map.47.refs_8_ = f32[8,1,256]{2,1,0:T(1,128)S(1)} custom-call(bf16[2,272,512]{2,1,0:T(8,128)(2,1)S(1)} %collective-permute-done.7.refs_0_.refs_1_, bf16[2,272,512]{2,1,0:T(8,128)(2,1)S(1)} %collective-permute-done.8.refs_0_.refs_2_.refs_1_, bf16[2,272,512]{2,1,0:T(8,128)(2,1)S(1)} %collective-permute-done.5.refs_0_.refs_3_.refs_2_, ...), custom_call_target="tpu_custom_call" | custom-call | flops 1000 | bytes 1000 | tf_op jit(solution)/shard_map/pallas_call | solution.py:198
  35.0 0.6 %collective-permute-done.13.refs_0_.refs_1_.refs_3_ = bf16[2,272,512]{2,1,0:T(8,128)(2,1)S(1)} collective-permute-done((bf16[2,272,512]{2,1,0:T(8,128)(2,1)S(1)}, bf16[2,272,512]{2,1,0:T(8,128)(2,1)S(1)}, u32[]{:S(2)}, u32[]{:S(2)}) %collective-permute-start.13) | collective-permute-done | bytes 557088 | tf_op jit(solution)/shard_map/ppermute | solution.py:40
  35.7 1.3 %shard_map.49.refs_5_ = f32[8,1,256]{2,1,0:T(1,128)S(1)} custom-call(bf16[2,272,512]{2,1,0:T(8,128)(2,1)S(1)} %shard_map.38.refs_0_, bf16[2,272,512]{2,1,0:T(8,128)(2,1)S(1)} %collective-permute-done.13.refs_0_.refs_1_.refs_3_, bf16[528,512]{1,0:T(8,128)(2,1)S(1)} %collective-permute-done.10.refs_2_.refs_4_.refs_1_, ...), custom_call_target="tpu_custom_call" | custom-call | flops 1000 | bytes 1000 | tf_op jit(solution)/shard_map/pallas_call | solution.py:198
  37.0 0.6 %collective-permute-done.14.refs_4_.refs_5_.refs_8_.refs_7_ = bf16[528,512]{1,0:T(8,128)(2,1)S(1)} collective-permute-done((bf16[528,512]{1,0:T(8,128)(2,1)S(1)}, bf16[528,512]{1,0:T(8,128)(2,1)S(1)}, u32[]{:S(2)}, u32[]{:S(2)}) %collective-permute-start.14) | collective-permute-done | bytes 540704 | tf_op jit(solution)/shard_map/ppermute | solution.py:45
  37.6 0.8 %shard_map.50 = f32[4,1,256]{2,1,0:T(1,128)S(1)} custom-call(bf16[2,272,512]{2,1,0:T(8,128)(2,1)S(1)} %collective-permute-done.7.refs_0_.refs_1_, bf16[2,272,512]{2,1,0:T(8,128)(2,1)S(1)} %collective-permute-done.8.refs_0_.refs_2_.refs_1_, bf16[2,272,512]{2,1,0:T(8,128)(2,1)S(1)} %collective-permute-done.5.refs_0_.refs_3_.refs_2_, ...), custom_call_target="tpu_custom_call" | custom-call | flops 1000 | bytes 1000 | tf_op jit(solution)/shard_map/pallas_call | solution.py:198
  38.5 2.9 %collective-permute-start.15 = (f32[4,1,256]{2,1,0:T(1,128)S(1)}, f32[4,1,256]{2,1,0:T(1,128)S(1)}, u32[]{:S(2)}, u32[]{:S(2)}) collective-permute-start(f32[4,1,256]{2,1,0:T(1,128)S(1)} %shard_map.50), channel_id=1, source_target_pairs={{32,0},{112,16},{0,32},{80,48},{96,64},{48,80},{64,96},{16,112},{3... | collective-permute-start | bytes 12296 | tf_op jit(solution)/shard_map/ppermute | solution.py:40
  41.4 0.9 %shard_map.51.refs_6_ = f32[8,1,256]{2,1,0:T(1,128)S(1)} custom-call(bf16[2,272,512]{2,1,0:T(8,128)(2,1)S(1)} %shard_map.38.refs_0_, bf16[2,272,512]{2,1,0:T(8,128)(2,1)S(1)} %collective-permute-done.3.refs_0_.refs_1_, bf16[528,512]{1,0:T(8,128)(2,1)S(1)} %collective-permute-done.10.refs_2_.refs_4_.refs_1_, ...), custom_call_target="tpu_custom_call" | custom-call | flops 1000 | bytes 1000 | tf_op jit(solution)/shard_map/pallas_call | solution.py:198
  42.3 1.5 %shard_map.52.refs_0_ = f32[8,1,256]{2,1,0:T(1,128)S(1)} custom-call(bf16[2,272,512]{2,1,0:T(8,128)(2,1)S(1)} %collective-permute-done.1.refs_0_.refs_1_, bf16[2,272,512]{2,1,0:T(8,128)(2,1)S(1)} %collective-permute-done.3.refs_0_.refs_1_, bf16[528,512]{1,0:T(8,128)(2,1)S(1)} %collective-permute-done.4.refs_3_.refs_5_.refs_2_.refs_4_, ...), custom_call_target="tpu_custom_call" | custom-call | flops 1000 | bytes 1000 | tf_op jit(solution)/shard_map/pallas_call | solution.py:198
  43.9 1.2 %collective-permute-start.16 = (f32[2,1,256]{2,1,0:T(1,128)S(1)}, f32[2,1,256]{2,1,0:T(1,128)S(1)}, u32[]{:S(2)}, u32[]{:S(2)}) collective-permute-start(f32[2,1,256]{2,1,0:T(1,128)S(1)} %shard_map.53), channel_id=1, source_target_pairs={{4,0},{28,16},{36,32},{60,48},{68,64},{92,80},{100,96},{124,112},{... | collective-permute-start | bytes 6152 | tf_op jit(solution)/shard_map/ppermute | solution.py:40
  45.1 1.4 %shard_map.54.refs_0_ = f32[8,1,256]{2,1,0:T(1,128)S(1)} custom-call(bf16[2,272,512]{2,1,0:T(8,128)(2,1)S(1)} %shard_map.38.refs_0_, bf16[2,272,512]{2,1,0:T(8,128)(2,1)S(1)} %collective-permute-done.2.refs_0_.refs_1_, bf16[528,512]{1,0:T(8,128)(2,1)S(1)} %collective-permute-done.10.refs_2_.refs_4_.refs_1_, ...), custom_call_target="tpu_custom_call" | custom-call | flops 1000 | bytes 1000 | tf_op jit(solution)/shard_map/pallas_call | solution.py:198
  46.5 1.0 %collective-permute-done.16.refs_2_ = f32[2,1,256]{2,1,0:T(1,128)S(1)} collective-permute-done((f32[2,1,256]{2,1,0:T(1,128)S(1)}, f32[2,1,256]{2,1,0:T(1,128)S(1)}, u32[]{:S(2)}, u32[]{:S(2)}) %collective-permute-start.16) | collective-permute-done | bytes 2080 | tf_op jit(solution)/shard_map/ppermute | solution.py:40
  47.6 1.5 %collective-permute-start.17 = (f32[1,1,256]{2,1,0:T(1,128)S(1)}, f32[1,1,256]{2,1,0:T(1,128)S(1)}, u32[]{:S(2)}, u32[]{:S(2)}) collective-permute-start(f32[1,1,256]{2,1,0:T(1,128)S(1)} %shard_map.55), channel_id=1, source_target_pairs={{1,0},{19,16},{33,32},{51,48},{65,64},{83,80},{97,96},{115,112},{5... | collective-permute-start | bytes 3080 | tf_op jit(solution)/shard_map/ppermute | solution.py:40
  49.1 1.4 %shard_map.56.refs_0_ = f32[8,1,256]{2,1,0:T(1,128)S(1)} custom-call(bf16[2,272,512]{2,1,0:T(8,128)(2,1)S(1)} %shard_map.38.refs_0_, bf16[528,512]{1,0:T(8,128)(2,1)S(1)} %collective-permute-done.10.refs_2_.refs_4_.refs_1_, bf16[528,512]{1,0:T(8,128)(2,1)S(1)} %collective-permute-done.11.refs_3_.refs_5_.refs_2_, ...), custom_call_target="tpu_custom_call" | custom-call | flops 1000 | bytes 1000 | tf_op jit(solution)/shard_map/pallas_call | solution.py:198
  50.6 0.7 %collective-permute-done.17.refs_3_ = f32[1,1,256]{2,1,0:T(1,128)S(1)} collective-permute-done((f32[1,1,256]{2,1,0:T(1,128)S(1)}, f32[1,1,256]{2,1,0:T(1,128)S(1)}, u32[]{:S(2)}, u32[]{:S(2)}) %collective-permute-start.17) | collective-permute-done | bytes 1056 | tf_op jit(solution)/shard_map/ppermute | solution.py:40
  (25 shorter events, 1.8 us)
Async XLA Ops:
  1.2 2.7 %collective-permute-start = (bf16[272,512]{1,0:T(8,128)(2,1)S(1)}, bf16[272,512]{1,0:T(8,128)(2,1)S(1)}, u32[]{:S(2)}, u32[]{:S(2)}) collective-permute-start(bf16[272,512]{1,0:T(8,128)(2,1)S(1)} %shard_map.37.first_ref), channel_id=1, source_target_pairs={{16,0},{0,16},{48,32},{32,48},{80,64},{64,80},{112,96},{96,112},{2... | collective-permute-start | bytes 835592 | tf_op jit(solution)/shard_map/ppermute | solution.py:45
  4.0 9.7 %collective-permute-start.2 = (bf16[2,272,512]{2,1,0:T(8,128)(2,1)S(1)}, bf16[2,272,512]{2,1,0:T(8,128)(2,1)S(1)}, u32[]{:S(2)}, u32[]{:S(2)}) collective-permute-start(bf16[2,272,512]{2,1,0:T(8,128)(2,1)S(1)} %shard_map.38.refs_0_), channel_id=1, source_target_pairs={{1,0},{19,16},{33,32},{51,48},{65,64},{83,80},{97,96},{115,112},{5... | collective-permute-start | bytes 1671176 | tf_op jit(solution)/shard_map/ppermute | solution.py:40
  6.6 10.7 %collective-permute-start.7 = (bf16[2,272,512]{2,1,0:T(8,128)(2,1)S(1)}, bf16[2,272,512]{2,1,0:T(8,128)(2,1)S(1)}, u32[]{:S(2)}, u32[]{:S(2)}) collective-permute-start(bf16[2,272,512]{2,1,0:T(8,128)(2,1)S(1)} %shard_map.38.refs_0_), channel_id=1, source_target_pairs={{32,0},{112,16},{0,32},{80,48},{96,64},{48,80},{64,96},{16,112},{3... | collective-permute-start | bytes 1671176 | tf_op jit(solution)/shard_map/ppermute | solution.py:40
  10.4 9.7 %collective-permute-start.1 = (bf16[2,272,512]{2,1,0:T(8,128)(2,1)S(1)}, bf16[2,272,512]{2,1,0:T(8,128)(2,1)S(1)}, u32[]{:S(2)}, u32[]{:S(2)}) collective-permute-start(bf16[2,272,512]{2,1,0:T(8,128)(2,1)S(1)} %shard_map.38.refs_0_), channel_id=1, source_target_pairs={{4,0},{28,16},{36,32},{60,48},{68,64},{92,80},{100,96},{124,112},{... | collective-permute-start | bytes 1671176 | tf_op jit(solution)/shard_map/ppermute | solution.py:40
  13.6 12.3 %collective-permute-start.3 = (bf16[2,272,512]{2,1,0:T(8,128)(2,1)S(1)}, bf16[2,272,512]{2,1,0:T(8,128)(2,1)S(1)}, u32[]{:S(2)}, u32[]{:S(2)}) collective-permute-start(bf16[2,272,512]{2,1,0:T(8,128)(2,1)S(1)} %collective-permute-done.2.refs_0_.refs_1_), channel_id=1, source_target_pairs={{4,0},{28,16},{36,32},{60,48},{68,64},{92,80},{100,96},{124,112},{... | collective-permute-start | bytes 1671176 | tf_op jit(solution)/shard_map/ppermute | solution.py:40
  17.3 9.9 %collective-permute-start.8 = (bf16[2,272,512]{2,1,0:T(8,128)(2,1)S(1)}, bf16[2,272,512]{2,1,0:T(8,128)(2,1)S(1)}, u32[]{:S(2)}, u32[]{:S(2)}) collective-permute-start(bf16[2,272,512]{2,1,0:T(8,128)(2,1)S(1)} %collective-permute-done.7.refs_0_.refs_1_), channel_id=1, source_target_pairs={{1,0},{19,16},{33,32},{51,48},{65,64},{83,80},{97,96},{115,112},{5... | collective-permute-start | bytes 1671176 | tf_op jit(solution)/shard_map/ppermute | solution.py:40
  20.0 9.6 %collective-permute-start.5 = (bf16[2,272,512]{2,1,0:T(8,128)(2,1)S(1)}, bf16[2,272,512]{2,1,0:T(8,128)(2,1)S(1)}, u32[]{:S(2)}, u32[]{:S(2)}) collective-permute-start(bf16[2,272,512]{2,1,0:T(8,128)(2,1)S(1)} %collective-permute-done.1.refs_0_.refs_1_), channel_id=1, source_target_pairs={{32,0},{112,16},{0,32},{80,48},{96,64},{48,80},{64,96},{16,112},{3... | collective-permute-start | bytes 1671176 | tf_op jit(solution)/shard_map/ppermute | solution.py:40
  22.7 6.9 %collective-permute-start.12 = (bf16[528,512]{1,0:T(8,128)(2,1)S(1)}, bf16[528,512]{1,0:T(8,128)(2,1)S(1)}, u32[]{:S(2)}, u32[]{:S(2)}) collective-permute-start(bf16[528,512]{1,0:T(8,128)(2,1)S(1)} %shard_map.44), channel_id=1, source_target_pairs={{16,0},{0,16},{48,32},{32,48},{80,64},{64,80},{112,96},{96,112},{2... | collective-permute-start | bytes 1622024 | tf_op jit(solution)/shard_map/ppermute | solution.py:45
  22.9 7.4 %collective-permute-start.10 = (bf16[528,512]{1,0:T(8,128)(2,1)S(1)}, bf16[528,512]{1,0:T(8,128)(2,1)S(1)}, u32[]{:S(2)}, u32[]{:S(2)}) collective-permute-start(bf16[528,512]{1,0:T(8,128)(2,1)S(1)} %shard_map.42), channel_id=1, source_target_pairs={{16,0},{0,16},{48,32},{32,48},{80,64},{64,80},{112,96},{96,112},{2... | collective-permute-start | bytes 1622024 | tf_op jit(solution)/shard_map/ppermute | solution.py:45
  26.0 9.6 %collective-permute-start.13 = (bf16[2,272,512]{2,1,0:T(8,128)(2,1)S(1)}, bf16[2,272,512]{2,1,0:T(8,128)(2,1)S(1)}, u32[]{:S(2)}, u32[]{:S(2)}) collective-permute-start(bf16[2,272,512]{2,1,0:T(8,128)(2,1)S(1)} %collective-permute-done.3.refs_0_.refs_1_), channel_id=1, source_target_pairs={{32,0},{112,16},{0,32},{80,48},{96,64},{48,80},{64,96},{16,112},{3... | collective-permute-start | bytes 1671176 | tf_op jit(solution)/shard_map/ppermute | solution.py:40
  27.2 3.1 %collective-permute-start.11 = (bf16[528,512]{1,0:T(8,128)(2,1)S(1)}, bf16[528,512]{1,0:T(8,128)(2,1)S(1)}, u32[]{:S(2)}, u32[]{:S(2)}) collective-permute-start(bf16[528,512]{1,0:T(8,128)(2,1)S(1)} %shard_map.43), channel_id=1, source_target_pairs={{16,0},{0,16},{48,32},{32,48},{80,64},{64,80},{112,96},{96,112},{2... | collective-permute-start | bytes 1622024 | tf_op jit(solution)/shard_map/ppermute | solution.py:45
  29.6 3.7 %collective-permute-start.9 = (bf16[528,512]{1,0:T(8,128)(2,1)S(1)}, bf16[528,512]{1,0:T(8,128)(2,1)S(1)}, u32[]{:S(2)}, u32[]{:S(2)}) collective-permute-start(bf16[528,512]{1,0:T(8,128)(2,1)S(1)} %shard_map.41), channel_id=1, source_target_pairs={{16,0},{0,16},{48,32},{32,48},{80,64},{64,80},{112,96},{96,112},{2... | collective-permute-start | bytes 1622024 | tf_op jit(solution)/shard_map/ppermute | solution.py:45
  29.7 3.7 %collective-permute-start.4 = (bf16[528,512]{1,0:T(8,128)(2,1)S(1)}, bf16[528,512]{1,0:T(8,128)(2,1)S(1)}, u32[]{:S(2)}, u32[]{:S(2)}) collective-permute-start(bf16[528,512]{1,0:T(8,128)(2,1)S(1)} %shard_map.39), channel_id=1, source_target_pairs={{16,0},{0,16},{48,32},{32,48},{80,64},{64,80},{112,96},{96,112},{2... | collective-permute-start | bytes 1622024 | tf_op jit(solution)/shard_map/ppermute | solution.py:45
  30.3 3.1 %collective-permute-start.6 = (bf16[528,512]{1,0:T(8,128)(2,1)S(1)}, bf16[528,512]{1,0:T(8,128)(2,1)S(1)}, u32[]{:S(2)}, u32[]{:S(2)}) collective-permute-start(bf16[528,512]{1,0:T(8,128)(2,1)S(1)} %shard_map.40), channel_id=1, source_target_pairs={{16,0},{0,16},{48,32},{32,48},{80,64},{64,80},{112,96},{96,112},{2... | collective-permute-start | bytes 1622024 | tf_op jit(solution)/shard_map/ppermute | solution.py:45
  35.6 2.0 %collective-permute-start.14 = (bf16[528,512]{1,0:T(8,128)(2,1)S(1)}, bf16[528,512]{1,0:T(8,128)(2,1)S(1)}, u32[]{:S(2)}, u32[]{:S(2)}) collective-permute-start(bf16[528,512]{1,0:T(8,128)(2,1)S(1)} %shard_map.48), channel_id=1, source_target_pairs={{16,0},{0,16},{48,32},{32,48},{80,64},{64,80},{112,96},{96,112},{2... | collective-permute-start | bytes 1622024 | tf_op jit(solution)/shard_map/ppermute | solution.py:45
  38.5 5.4 %collective-permute-start.15 = (f32[4,1,256]{2,1,0:T(1,128)S(1)}, f32[4,1,256]{2,1,0:T(1,128)S(1)}, u32[]{:S(2)}, u32[]{:S(2)}) collective-permute-start(f32[4,1,256]{2,1,0:T(1,128)S(1)} %shard_map.50), channel_id=1, source_target_pairs={{32,0},{112,16},{0,32},{80,48},{96,64},{48,80},{64,96},{16,112},{3... | collective-permute-start | bytes 12296 | tf_op jit(solution)/shard_map/ppermute | solution.py:40
  43.9 3.7 %collective-permute-start.16 = (f32[2,1,256]{2,1,0:T(1,128)S(1)}, f32[2,1,256]{2,1,0:T(1,128)S(1)}, u32[]{:S(2)}, u32[]{:S(2)}) collective-permute-start(f32[2,1,256]{2,1,0:T(1,128)S(1)} %shard_map.53), channel_id=1, source_target_pairs={{4,0},{28,16},{36,32},{60,48},{68,64},{92,80},{100,96},{124,112},{... | collective-permute-start | bytes 6152 | tf_op jit(solution)/shard_map/ppermute | solution.py:40
  47.6 3.6 %collective-permute-start.17 = (f32[1,1,256]{2,1,0:T(1,128)S(1)}, f32[1,1,256]{2,1,0:T(1,128)S(1)}, u32[]{:S(2)}, u32[]{:S(2)}) collective-permute-start(f32[1,1,256]{2,1,0:T(1,128)S(1)} %shard_map.55), channel_id=1, source_target_pairs={{1,0},{19,16},{33,32},{51,48},{65,64},{83,80},{97,96},{115,112},{5... | collective-permute-start | bytes 3080 | tf_op jit(solution)/shard_map/ppermute | solution.py:40
